TPU v7x, 32 devices: a whole 2x2x4 slice. The times are simulated.
32 devices in a mesh: tile: 8 (over z, y), layer: 4 (over x, core).
Axes of the slice: x: 2, y: 2, z: 4, core: 2. Of those that a mesh axis runs over, the one named last changes fastest.
Arguments:
- newton_rhs: float32 [3, 12, 128, 2048], P(None, 'layer', 'tile'), may hold values from -6 to 6
- weights: float32 [3, 12, 128, 2048], P(None, 'layer', 'tile'), may hold values from 0.2 to 1
- block_diag: float32 [3, 3, 12, 128, 2048], P(None, None, 'layer', 'tile'), as said below
- block_inv: float32 [3, 3, 12, 128, 2048], P(None, None, 'layer', 'tile'), as said below
- trans_x: float32 [12, 128, 2048], P('layer', 'tile'), may hold values from 0.2 to 1
- trans_y: float32 [12, 128, 2048], P('layer', 'tile'), may hold values from 0.2 to 1
- trans_z: float32 [12, 128, 2048], P('layer', 'tile'), may hold values from 0.2 to 1
- storage: float32 [12, 128, 2048], P('layer', 'tile'), may hold values from 0.05 to 0.5
- perf_cell: int32 [8192], P(('tile', 'layer')), may hold values from 0 to 98303
- perf_front: int32 [8192], P(('tile', 'layer')), may hold values from 0 to 8191
- productivity: float32 [8192], P(('tile', 'layer')), may hold values from 0.5 to 2
- front_inverse: float32 [8192, 8192], P(('tile', 'layer')), may hold values from -0.0625 to 0.0625
Outputs:
- update: float32 [3, 12, 128, 2048], P(None, 'layer', 'tile')
- lin_res: float32 [3, 12, 128, 2048], P(None, 'layer', 'tile')
- ratio: float32 [], replicated
Inputs may be any that keep to these rules, and one draw needn't show every extreme that they name: perf_cell indexes the [3, 16, 2048] block of the device that holds the perforation; cells may hold several perforations. `perf_front`: front unknowns may receive several perforations from many devices. Diagonal entries of block_diag lie between 6 and 9. Diagonal entries of block_inv lie between 0.1 and 0.2.
All inputs are finite; a program needn't handle non-finite values.
Results may differ from a plain program's by a relative error of at most 0.000098.
Values sent between devices are 32-bit elements; how exact they have to be, the bound alone decides.
No kernel may reach another device: no remote copies, remote signals or barrier semaphores. Data moves between devices by JAX's collectives and lax.ppermute only.
A program may use at most 128 MiB of HBM per device.

v0:
```python
import jax
import jax.numpy as jnp
from jax import lax
from jax.sharding import PartitionSpec as P


def shifted(block, axis, distance):
    devices = range(lax.axis_size(axis))
    route = [(i - distance, i) for i in devices if i - distance in devices]
    return lax.ppermute(block, axis, route)


def with_halo(array, sides, width):
    for axis, dim in sides:
        size, length = (lax.axis_size(axis), array.shape[dim])
        up = [(i, (i + 1) % size) for i in range(size - 1)]
        down = [(j, i) for i, j in up]
        last = lax.slice_in_dim(array, length - width, length, axis=dim)
        initial = lax.slice_in_dim(array, 0, width, axis=dim)
        before = lax.ppermute(last, axis, up)
        after = lax.ppermute(initial, axis, down)
        array = jnp.concatenate([before, array, after], axis=dim)
    return array


def couple(padded, coeffs, trans_y):
    tx_here, tx_before, tz_here, tz_before = coeffs
    centre = padded[..., 1:-1, 1:-1, :]
    total = tx_here * padded[..., 1:-1, 2:, :] + tx_before * padded[..., 1:-1, :-2, :]
    total = total + tz_here * padded[..., 2:, 1:-1, :] + tz_before * padded[..., :-2, 1:-1, :]
    lead = centre.ndim - 1
    ypad = jnp.pad(centre, [(0, 0)] * lead + [(1, 1)])
    ty_pad = jnp.pad(trans_y, ((0, 0), (0, 0), (1, 1)))
    total = total + trans_y * ypad[..., 2:] + ty_pad[..., :-2] * ypad[..., :-2]
    return (centre, total)


def block_apply(matrix, vector):
    return (
        matrix[:, 0] * vector[0][None]
        + matrix[:, 1] * vector[1][None]
        + matrix[:, 2] * vector[2][None]
    )


def line_solve(rhs, upper_raw, store):
    depth = rhs.shape[0]
    live = (lax.iota(jnp.int32, depth) < depth - 1).astype(jnp.float32)[:, None, None]
    upper = upper_raw * live
    lower = jnp.concatenate([jnp.zeros_like(upper[:1]), upper[:-1]], 0)
    diag = lower + upper + store

    def forward(carry, item):
        gprev, dprev = carry
        low, up, dia, rh = item
        pivot = dia - low * gprev
        gnow = up / pivot
        dnow = (rh + low * dprev) / pivot
        return ((gnow, dnow), (gnow, dnow))

    zero = jnp.zeros_like(rhs[0])
    _, (gall, dall) = lax.scan(forward, (zero, zero), (lower, upper, diag, rhs))

    def backward(carry, item):
        gnow, dnow = item
        value = dnow + gnow * carry
        return (value, value)

    _, sol = lax.scan(backward, zero, (gall, dall), reverse=True)
    return sol


def shards(
    newton_rhs,
    weights,
    block_diag,
    block_inv,
    trans_x,
    trans_y,
    trans_z,
    storage,
    perf_cell,
    perf_front,
    productivity,
    front_inverse,
):
    prev_row = shifted(trans_x[:, -1:, :], "tile", 1)
    prev_layer = shifted(trans_z[-1:], "layer", 1)
    tx_before = jnp.concatenate([prev_row, trans_x[:, :-1, :]], 1)
    tz_before = jnp.concatenate([prev_layer, trans_z[:-1]], 0)
    coeffs = (trans_x, tx_before, trans_z, tz_before)
    pres_rhs = jnp.sum(weights * newton_rhs, axis=0)
    flat = pres_rhs.reshape(-1)
    local_front = jax.ops.segment_sum(
        productivity * flat[perf_cell], perf_front, num_segments=front_inverse.shape[1]
    )
    front_rhs = lax.psum(local_front, ("tile", "layer"))
    front_rows = jnp.dot(front_inverse, front_rhs, precision=lax.Precision.HIGHEST)
    front_sol = lax.all_gather(front_rows, ("tile", "layer"), axis=0, tiled=True)
    adjusted = flat.at[perf_cell].add(-productivity * front_sol[perf_front]).reshape(pres_rhs.shape)
    solved = line_solve(
        lax.all_to_all(adjusted, "layer", split_axis=2, concat_axis=0, tiled=True),
        lax.all_to_all(trans_z, "layer", split_axis=2, concat_axis=0, tiled=True),
        lax.all_to_all(storage, "layer", split_axis=2, concat_axis=0, tiled=True),
    )
    pressure = lax.all_to_all(solved, "layer", split_axis=0, concat_axis=2, tiled=True)
    press_pad = with_halo(pressure, (("tile", 1), ("layer", 0)), 1)
    _, near_press = couple(press_pad, coeffs, trans_y)
    zeros_two = jnp.zeros((2,) + pressure.shape, jnp.float32)
    pe0 = jnp.concatenate([pressure[None], zeros_two], 0)
    image_press = block_apply(block_diag, pe0) - jnp.concatenate([near_press[None], zeros_two], 0)
    remain = newton_rhs - image_press
    search = pe0 + block_apply(block_inv, remain)
    search_pad = with_halo(search, (("tile", 2), ("layer", 1)), 1)
    centre, near_search = couple(search_pad, coeffs, trans_y)
    image = block_apply(block_diag, centre) - near_search
    along, power, start_sq = lax.psum(
        (jnp.sum(image * newton_rhs), jnp.sum(image * image), jnp.sum(newton_rhs * newton_rhs)),
        ("tile", "layer"),
    )
    omega = along / power
    update = omega * search
    lin_res = newton_rhs - omega * image
    end_sq = lax.psum(jnp.sum(lin_res * lin_res), ("tile", "layer"))
    ratio = jnp.sqrt(end_sq / start_sq)
    return (update, lin_res, ratio)


def solution(mesh):
    return jax.shard_map(
        shards,
        mesh=mesh,
        in_specs=(
            P(None, "layer", "tile", None),
            P(None, "layer", "tile", None),
            P(None, None, "layer", "tile", None),
            P(None, None, "layer", "tile", None),
            P("layer", "tile", None),
            P("layer", "tile", None),
            P("layer", "tile", None),
            P("layer", "tile", None),
            P(("tile", "layer")),
            P(("tile", "layer")),
            P(("tile", "layer")),
            P(("tile", "layer"), None),
        ),
        out_specs=(P(None, "layer", "tile", None), P(None, "layer", "tile", None), P()),
        check_vma=False,
    )
```

profile of v0, /device:TPU:0, one launch (start us, length us, event | category | flops | bytes accessed | tf_op | source)
XLA Modules:
  0.0 341.2 jit_solution(14199775917796376466)
XLA Ops:
  0.6 4.5 %copy.93 = f32[3,16,2048]{1,0,2:T(4,128)} copy(f32[3,16,2048]{2,1,0:T(8,128)} %param.22) | data formatting | bytes 786432 | tf_op args[6]
  5.1 5.3 %reshape.69 = f32[4,1,24576]{2,1,0:T(1,128)} reshape(f32[2048,3,16]{2,1,0:T(4,128)} %bitcast.174) | data formatting | bytes 786432
  10.4 4.2 %all-to-all-start = ((f32[4,1,24576]{2,1,0:T(1,128)}), f32[4,1,24576]{2,1,0:T(1,128)S(1)}, u32[]{:S(2)}, u32[]{:S(2)}) async-start(f32[4,1,24576]{2,1,0:T(1,128)} %reshape.69), calls=%async_computation | async-start | bytes 786432 | tf_op jit(solution)/shard_map/all_to_all | solution.py:103
  17.1 2.0 scatter_custom_fusion
  19.0 41.9 %psum.35 = f32[8192]{0:T(1024)S(1)} all-reduce(f32[8192]{0:T(1024)S(1)} %scatter_custom_fusion), channel_id=1, replica_groups=mesh['tile'=8,'layer'=4] {'tile','layer'}, use_global_device_ids=true, to_apply=%region_2.0 | all-reduce | flops 8192 | bytes 65536 | tf_op jit(solution)/shard_map/psum | solution.py:97
  61.0 8.9 %convolution_bitcast_fusion = f32[1,1,256]{2,1,0:T(1,128)S(1)} fusion(f32[8192,1]{0,1:T(1,128)S(1)} %bitcast.182, f32[256,8192]{1,0:T(8,128)} %param.27), kind=kOutput, calls=%fused_computation.61 | convolution fusion | flops 25165824 | bytes 8422400 | tf_op jit(solution)/shard_map/dot_general | solution.py:98
  69.9 3.1 copy.95
  73.0 5.1 %reshape.71 = f32[4,1,24576]{2,1,0:T(1,128)} reshape(f32[2048,3,16]{2,1,0:T(4,128)} %bitcast.175) | data formatting | bytes 786432
  78.1 40.2 %all-gather = f32[32,1,256]{2,1,0:T(1,128)S(1)} all-gather(f32[1,1,256]{2,1,0:T(1,128)S(1)} %convolution_bitcast_fusion), channel_id=1, replica_groups=mesh['tile'=8,'layer'=4] {'tile','layer'}, dimensions={0}, use_global_device_ids=true | all-gather | bytes 33792 | tf_op jit(solution)/shard_map/all_gather | solution.py:99
  118.3 3.5 %all-to-all-start.1 = ((f32[4,1,24576]{2,1,0:T(1,128)}), f32[4,1,24576]{2,1,0:T(1,128)S(1)}, u32[]{:S(2)}, u32[]{:S(2)}) async-start(f32[4,1,24576]{2,1,0:T(1,128)} %reshape.71), calls=%async_computation.1 | async-start | bytes 786432 | tf_op jit(solution)/shard_map/all_to_all | solution.py:104
  123.5 2.1 scatter_fusion
  125.7 3.1 copy.97
  128.8 5.1 %reshape.73 = f32[4,1,24576]{2,1,0:T(1,128)} reshape(f32[2048,3,16]{2,1,0:T(4,128)} %bitcast.170) | data formatting | bytes 786432
  134.0 3.6 %all-to-all-start.2 = ((f32[4,1,24576]{2,1,0:T(1,128)}), f32[4,1,24576]{2,1,0:T(1,128)S(1)}, u32[]{:S(2)}, u32[]{:S(2)}) async-start(f32[4,1,24576]{2,1,0:T(1,128)} %reshape.73), calls=%async_computation.2 | async-start | bytes 786432 | tf_op jit(solution)/shard_map/all_to_all | solution.py:102
  139.9 4.7 %reshape.70 = f32[2048,3,16]{2,1,0:T(4,128)} reshape(f32[4,24576]{1,0:T(4,128)S(1)} %reduce) | data formatting | bytes 786432
  144.6 3.3 copy.94
  149.8 4.7 %reshape.72 = f32[2048,3,16]{2,1,0:T(4,128)} reshape(f32[4,24576]{1,0:T(4,128)S(1)} %reduce.1) | data formatting | bytes 786432
  154.5 3.3 copy.96
  159.6 4.7 %reshape.74 = f32[2048,3,16]{2,1,0:T(4,128)} reshape(f32[4,24576]{1,0:T(4,128)S(1)} %reduce.2) | data formatting | bytes 786432
  164.3 3.4 copy.99
  168.8 9.8 %while.34 = (s32[]{:T(128)}, f32[16,512]{1,0:T(8,128)S(1)}, f32[16,512]{1,0:T(8,128)S(1)}, f32[12,16,512]{2,1,0:T(8,128)S(1)}, f32[12,16,512]{2,1,0:T(8,128)S(1)...) while((s32[]{:T(128)}, f32[16,512]{1,0:T(8,128)S(1)}, ...), condition=%wide.region_5.6_spmd.clone, body=%wide.region_4.5_spmd.clone.sunk | while | flops 65539 | bytes 327803 | solution.py:62
  179.5 9.5 %while.35 = (s32[]{:T(128)}, f32[16,512]{1,0:T(8,128)S(1)}, f32[12,16,512]{2,1,0:T(8,128)S(1)}, f32[12,16,512]{2,1,0:T(8,128)}, f32[12,16,512]{2,1,0:T(8,128)S(1)}, /*index=5*/s32[]{:T(128)}, s32[]{:T(128)}, s32[]{:T(128)}) while((s32[]{:T(128)}, f32[16,512]{1,0:T(8,128)S(1)}, f32[12,16,512]{2,1,0:T(8,128)S(1)}, ...), condition=%wide.region_7.8_spmd.clone, body=%wide.region_6.7_spmd.clone.sunk | while | flops 24580 | bytes 163951 | solution.py:69
  189.0 10.6 %all_to_all.69 = f32[12,16,512]{2,1,0:T(8,128)S(1)} all-to-all(f32[12,16,512]{2,1,0:T(8,128)S(1)} %get-tuple-element.156), channel_id=1, replica_groups=mesh['tile'=8,'layer'=4] {'layer'}, dimensions={0} | all-to-all | bytes 786432 | tf_op jit(solution)/shard_map/all_to_all | solution.py:106
  201.5 4.5 %collective-permute-start.2 = (f32[3,1,2048]{2,1,0:T(1,128)S(1)}, f32[3,1,2048]{2,1,0:T(1,128)S(1)}, u32[]{:S(2)}, u32[]{:S(2)}) collective-permute-start(f32[3,1,2048]{2,1,0:T(1,128)S(1)} %get-tuple-element.268), channel_id=1, source_target_pairs={{0,4},{4,8},{8,12},{12,16},{16,20},{20,24},{24,28},{1,5},{5,9},{9,... | collective-permute-start | bytes 73736 | tf_op jit(solution)/shard_map/ppermute | solution.py:20
  209.3 2.5 collective-permute-start.1
  213.9 3.7 %collective-permute-start.5 = (f32[1,18,2048]{2,1,0:T(8,128)}, f32[1,18,2048]{2,1,0:T(8,128)}, u32[]{:S(2)}, u32[]{:S(2)}) collective-permute-start(f32[1,18,2048]{2,1,0:T(8,128)} %get-tuple-element.267), channel_id=1, source_target_pairs={{0,1},{1,2},{2,3},{4,5},{5,6},{6,7},{8,9},{9,10},{10,11},{12,13},{... | collective-permute-start | bytes 442376 | tf_op jit(solution)/shard_map/ppermute | solution.py:20
  226.4 4.6 %collective-permute-start.7 = (f32[3,3,1,2048]{3,1,2,0:T(4,128)S(1)}, f32[3,3,1,2048]{3,1,2,0:T(4,128)S(1)}, u32[]{:S(2)}, u32[]{:S(2)}) collective-permute-start(f32[3,3,1,2048]{3,1,2,0:T(4,128)S(1)} %copy.108), channel_id=1, source_target_pairs={{0,4},{4,8},{8,12},{12,16},{16,20},{20,24},{24,28},{1,5},{5,9},{9,... | collective-permute-start | bytes 221192 | tf_op jit(solution)/shard_map/ppermute | solution.py:20
  236.3 3.1 collective-permute-start.9
  241.0 2.8 multiply_reduce_fusion
  243.7 47.6 %all-reduce.7 = (f32[]{:T(128)}, f32[]{:T(128)}) all-reduce(f32[]{:T(128)} %get-tuple-element.209, f32[]{:T(128)} %get-tuple-element.210), channel_id=1, replica_groups=mesh['tile'=8,'layer'=4] {'tile','layer'}, use_global_device_ids=true, to_apply=%region_9.10 | all-reduce | flops 2 | bytes 16 | tf_op jit(solution)/shard_map/psum | solution.py:117
  292.6 3.8 %broadcast_multiply_fusion = f32[3,3,16,2048]{3,2,1,0:T(8,128)} fusion(f32[]{:T(128)S(6)} %div.12, f32[3,16,2048]{2,1,0:T(8,128)} %copy-done.7, f32[3,3,3,16,2048]{4,3,2,1,0:T(8,128)} %param.19, f32[3,16,2048]{2,1,0:T(8,128)} %copy-done.8, f32[3,16,2048]{2,1,0:T(8,128)S(1)} %get-tuple-element.263, f32[1,3,16,2048]{3,2,1,0:T(8,128)} %copy-done.9), kind=kLoop, calls=%fused_computation.65 | loop fusion | flops 2064384 | bytes 6291460 | tf_op jit(solution)/shard_map/mul | solution.py:122
  298.3 40.4 %all-reduce.6 = (f32[]{:T(128)}, f32[]{:T(128)}) all-reduce(f32[]{:T(128)} %get-tuple-element.249, f32[]{:T(128)} %get-tuple-element.208), channel_id=1, replica_groups=mesh['tile'=8,'layer'=4] {'tile','layer'}, use_global_device_ids=true, to_apply=%region_13.14 | all-reduce | flops 2 | bytes 16 | tf_op jit(solution)/shard_map/psum | solution.py:124
  (138 shorter events, 55.4 us)
Async XLA Ops:
  5.1 9.5 %copy-start = (f32[3,3,16,2048]{3,2,1,0:T(8,128)S(1)}, f32[3,3,16,2048]{3,2,1,0:T(8,128)}, u32[]{:S(2)}) copy-start(f32[3,3,16,2048]{3,2,1,0:T(8,128)} %param.16) | copy-start | bytes 3538948
  5.1 9.5 %copy-start.14 = (f32[3,3,16,2048]{3,2,1,0:T(8,128)S(1)}, f32[3,3,16,2048]{3,2,1,0:T(8,128)}, u32[]{:S(2)}) copy-start(f32[3,3,16,2048]{3,2,1,0:T(8,128)} %param.17) | copy-start | bytes 3538948
  10.4 107.9 %all-to-all-start = ((f32[4,1,24576]{2,1,0:T(1,128)}), f32[4,1,24576]{2,1,0:T(1,128)S(1)}, u32[]{:S(2)}, u32[]{:S(2)}) async-start(f32[4,1,24576]{2,1,0:T(1,128)} %reshape.69), calls=%async_computation | async-start | bytes 786432 | tf_op jit(solution)/shard_map/all_to_all | solution.py:103
  14.7 2.3 copy-start.19
  14.8 2.3 copy-start.21
  60.9 9.0 %copy-start.16 = (f32[3,16,2048]{2,1,0:T(8,128)S(1)}, f32[3,16,2048]{2,1,0:T(8,128)}, u32[]{:S(2)}) copy-start(f32[3,16,2048]{2,1,0:T(8,128)} %param.23) | copy-start | bytes 1179652
  118.3 15.6 %all-to-all-start.1 = ((f32[4,1,24576]{2,1,0:T(1,128)}), f32[4,1,24576]{2,1,0:T(1,128)S(1)}, u32[]{:S(2)}, u32[]{:S(2)}) async-start(f32[4,1,24576]{2,1,0:T(1,128)} %reshape.71), calls=%async_computation.1 | async-start | bytes 786432 | tf_op jit(solution)/shard_map/all_to_all | solution.py:104
  134.0 23.9 %all-to-all-start.2 = ((f32[4,1,24576]{2,1,0:T(1,128)}), f32[4,1,24576]{2,1,0:T(1,128)S(1)}, u32[]{:S(2)}, u32[]{:S(2)}) async-start(f32[4,1,24576]{2,1,0:T(1,128)} %reshape.73), calls=%async_computation.2 | async-start | bytes 786432 | tf_op jit(solution)/shard_map/all_to_all | solution.py:102
  148.0 6.5 %copy-start.11 = (f32[12,16,512]{2,1,0:T(8,128)}, f32[12,16,512]{2,1,0:T(8,128)S(1)}, u32[]{:S(2)}) copy-start(f32[12,16,512]{2,1,0:T(8,128)S(1)} %bitcast_multiply_fusion.12) | copy-start | bytes 1179652
  164.3 3.4 slice-start
  189.0 17.1 %copy-start.3 = (f32[3,16,2048]{2,1,0:T(8,128)S(1)}, f32[3,16,2048]{2,1,0:T(8,128)}, u32[]{:S(2)}) copy-start(f32[3,16,2048]{2,1,0:T(8,128)} %param.22) | copy-start | bytes 1179652
  189.0 19.7 %copy-start.4 = (f32[3,16,2048]{2,1,0:T(8,128)S(1)}, f32[3,16,2048]{2,1,0:T(8,128)}, u32[]{:S(2)}) copy-start(f32[3,16,2048]{2,1,0:T(8,128)} %param.20) | copy-start | bytes 1179652
  199.9 17.8 %copy-start.5 = (f32[3,16,2048]{2,1,0:T(8,128)S(1)}, f32[3,16,2048]{2,1,0:T(8,128)}, u32[]{:S(2)}) copy-start(f32[3,16,2048]{2,1,0:T(8,128)} %param.21) | copy-start | bytes 1179652
  200.2 11.6 %collective-permute-start = (f32[3,1,2048]{2,1,0:T(1,128)S(1)}, f32[3,1,2048]{2,1,0:T(1,128)S(1)}, u32[]{:S(2)}, u32[]{:S(2)}) collective-permute-start(f32[3,1,2048]{2,1,0:T(1,128)S(1)} %get-tuple-element.269), channel_id=1, source_target_pairs={{4,0},{8,4},{12,8},{16,12},{20,16},{24,20},{28,24},{5,1},{9,5},{13... | collective-permute-start | bytes 73736 | tf_op jit(solution)/shard_map/ppermute | solution.py:21
  201.5 10.3 %collective-permute-start.2 = (f32[3,1,2048]{2,1,0:T(1,128)S(1)}, f32[3,1,2048]{2,1,0:T(1,128)S(1)}, u32[]{:S(2)}, u32[]{:S(2)}) collective-permute-start(f32[3,1,2048]{2,1,0:T(1,128)S(1)} %get-tuple-element.268), channel_id=1, source_target_pairs={{0,4},{4,8},{8,12},{12,16},{16,20},{20,24},{24,28},{1,5},{5,9},{9,... | collective-permute-start | bytes 73736 | tf_op jit(solution)/shard_map/ppermute | solution.py:20
  206.8 12.8 %collective-permute-start.4 = (f32[1,16,2048]{2,1,0:T(8,128)}, f32[1,16,2048]{2,1,0:T(8,128)}, u32[]{:S(2)}, u32[]{:S(2)}) collective-permute-start(f32[1,16,2048]{2,1,0:T(8,128)} %slice.139), channel_id=1, source_target_pairs={{0,1},{1,2},{2,3},{4,5},{5,6},{6,7},{8,9},{9,10},{10,11},{12,13},{... | collective-permute-start | bytes 393224 | tf_op jit(solution)/shard_map/ppermute | solution.py:10
  209.3 10.3 %collective-permute-start.1 = (f32[3,1,2048]{2,1,0:T(1,128)}, f32[3,1,2048]{2,1,0:T(1,128)}, u32[]{:S(2)}, u32[]{:S(2)}) collective-permute-start(f32[3,1,2048]{2,1,0:T(1,128)} %slice.133), channel_id=1, source_target_pairs={{0,4},{4,8},{8,12},{12,16},{16,20},{20,24},{24,28},{1,5},{5,9},{9,... | collective-permute-start | bytes 73736 | tf_op jit(solution)/shard_map/ppermute | solution.py:10
  211.8 6.7 %copy-start.17 = (f32[3,1,2048]{2,1,0:T(1,128)}, f32[3,1,2048]{2,1,0:T(1,128)S(1)}, u32[]{:S(2)}) copy-start(f32[3,1,2048]{2,1,0:T(1,128)S(1)} %collective-permute-done) | copy-start | bytes 73732
  211.8 6.7 %copy-start.18 = (f32[3,1,2048]{2,1,0:T(1,128)}, f32[3,1,2048]{2,1,0:T(1,128)S(1)}, u32[]{:S(2)}) copy-start(f32[3,1,2048]{2,1,0:T(1,128)S(1)} %collective-permute-done.2) | copy-start | bytes 73732
  212.7 6.9 %collective-permute-start.3 = (f32[1,18,2048]{2,1,0:T(8,128)}, f32[1,18,2048]{2,1,0:T(8,128)}, u32[]{:S(2)}, u32[]{:S(2)}) collective-permute-start(f32[1,18,2048]{2,1,0:T(8,128)} %get-tuple-element.266), channel_id=1, source_target_pairs={{1,0},{2,1},{3,2},{5,4},{6,5},{7,6},{9,8},{10,9},{11,10},{13,12},{... | collective-permute-start | bytes 442376 | tf_op jit(solution)/shard_map/ppermute | solution.py:21
  213.9 5.7 %collective-permute-start.5 = (f32[1,18,2048]{2,1,0:T(8,128)}, f32[1,18,2048]{2,1,0:T(8,128)}, u32[]{:S(2)}, u32[]{:S(2)}) collective-permute-start(f32[1,18,2048]{2,1,0:T(8,128)} %get-tuple-element.267), channel_id=1, source_target_pairs={{0,1},{1,2},{2,3},{4,5},{5,6},{6,7},{8,9},{9,10},{10,11},{12,13},{... | collective-permute-start | bytes 442376 | tf_op jit(solution)/shard_map/ppermute | solution.py:20
  219.6 3.2 copy-start.9
  219.6 2.5 copy-start.1
  222.1 2.3 copy-start.2
  222.8 2.1 copy-start.7
  222.8 2.1 copy-start.8
  224.4 6.6 %copy-start.10 = (f32[2,16,2048]{2,1,0:T(8,128)S(1)}, f32[2,16,2048]{2,1,0:T(8,128)}, u32[]{:S(2)}) copy-start(f32[2,16,2048]{2,1,0:T(8,128)} %slice.140) | copy-start | bytes 786436
  225.1 7.0 %collective-permute-start.6 = (f32[3,3,1,2048]{3,1,2,0:T(4,128)S(1)}, f32[3,3,1,2048]{3,1,2,0:T(4,128)S(1)}, u32[]{:S(2)}, u32[]{:S(2)}) collective-permute-start(f32[3,3,1,2048]{3,1,2,0:T(4,128)S(1)} %copy.106), channel_id=1, source_target_pairs={{4,0},{8,4},{12,8},{16,12},{20,16},{24,20},{28,24},{5,1},{9,5},{13... | collective-permute-start | bytes 221192 | tf_op jit(solution)/shard_map/ppermute | solution.py:21
  226.4 7.4 %collective-permute-start.7 = (f32[3,3,1,2048]{3,1,2,0:T(4,128)S(1)}, f32[3,3,1,2048]{3,1,2,0:T(4,128)S(1)}, u32[]{:S(2)}, u32[]{:S(2)}) collective-permute-start(f32[3,3,1,2048]{3,1,2,0:T(4,128)S(1)} %copy.108), channel_id=1, source_target_pairs={{0,4},{4,8},{8,12},{12,16},{16,20},{20,24},{24,28},{1,5},{5,9},{9,... | collective-permute-start | bytes 221192 | tf_op jit(solution)/shard_map/ppermute | solution.py:20
  234.6 5.0 %collective-permute-start.8 = (f32[3,1,18,2048]{3,1,2,0:T(1,128)S(1)}, f32[3,1,18,2048]{3,1,2,0:T(1,128)S(1)}, u32[]{:S(2)}, u32[]{:S(2)}) collective-permute-start(f32[3,1,18,2048]{3,1,2,0:T(1,128)S(1)} %copy.112), channel_id=1, source_target_pairs={{1,0},{2,1},{3,2},{5,4},{6,5},{7,6},{9,8},{10,9},{11,10},{13,12},{... | collective-permute-start | bytes 1327112 | tf_op jit(solution)/shard_map/ppermute | solution.py:21
  236.3 4.4 %collective-permute-start.9 = (f32[3,1,18,2048]{3,1,2,0:T(1,128)S(1)}, f32[3,1,18,2048]{3,1,2,0:T(1,128)S(1)}, u32[]{:S(2)}, u32[]{:S(2)}) collective-permute-start(f32[3,1,18,2048]{3,1,2,0:T(1,128)S(1)} %copy.114), channel_id=1, source_target_pairs={{0,1},{1,2},{2,3},{4,5},{5,6},{6,7},{8,9},{9,10},{10,11},{12,13},{... | collective-permute-start | bytes 1327112 | tf_op jit(solution)/shard_map/ppermute | solution.py:20
  239.5 1.4 copy-start.6
  (4 other events, 4.0 us)
where the time goes:
time: 344 us; the launch traced here: 341 us
  blocking collectives  181 us (53%)
  local copies, waits for them, and re-layouts  63.7 us (19%)
  other arithmetic  42.6 us (12%)
  starting transfers between devices  36.8 us (11%)
  matrix products  8.94 us (3%)
  between operations  5.16 us (2%)
    psum x1, blocking collectives, shards(): lax.psum((jnp.sum(image * newton_rhs), jnp.sum(image * image), jnp.sum(ne...  47.6 us
    psum x1, blocking collectives, shards(): front_rhs = lax.psum(local_front, ('tile', 'layer'))  41.9 us
    unnamed x53, local copies, waits for them, and re-layouts  41 us
    psum x1, blocking collectives, shards(): end_sq = lax.psum(jnp.sum(lin_res * lin_res), ('tile', 'layer'))  40.4 us
    all_gather x1, blocking collectives, shards(): lax.all_gather(front_rows, ('tile', 'layer'), axis=0, tiled=True)  40.2 us
    dynamic_update_slice x24, other arithmetic, line_solve(): _, (gall, dall) = lax.scan(forward, (zero, zero), (lower, upper, diag, rhs))  18.9 us
    ppermute x4, starting transfers between devices, with_halo(): before = lax.ppermute(last, axis, up)  15.9 us
    all_to_all x1, blocking collectives, shards(): lax.all_to_all(solved, 'layer', split_axis=0, concat_axis=2, tiled=True)  10.6 us
  transfers between devices with their start and end apart: 13, of which 3 were waited for; matrix products, arithmetic and copies ran while one was open for 17% of the time, Pallas kernels for 0%

commit v1 on v0

v1 whole, which is shorter than its diff:
```python
import functools
import jax
import jax.numpy as jnp
from jax import lax
from jax.experimental import pallas as pl
from jax.experimental.pallas import tpu as pltpu
from jax.sharding import PartitionSpec as P

F32 = jnp.float32
BF16 = jnp.bfloat16
I32 = jnp.int32
BOTH = ("tile", "layer")
VM = pl.BlockSpec(memory_space=pltpu.VMEM)
LIMIT = 16 << 20


def hbm(shape):
    return jax.ShapeDtypeStruct(shape, F32)


def vmem(shape, dtype=F32):
    return pltpu.VMEM(shape, dtype)


def call(kernel, outs, args, flops=0, limit=LIMIT):
    args = [pltpu.with_memory_space_constraint(a, pltpu.VMEM) for a in args]
    size = 4 * sum(a.size for a in args)
    return pl.pallas_call(
        kernel,
        out_shape=outs,
        in_specs=[VM] * len(args),
        out_specs=jax.tree.map(lambda _: VM, outs),
        compiler_params=pltpu.CompilerParams(vmem_limit_bytes=limit),
        cost_estimate=pl.CostEstimate(flops=flops, bytes_accessed=size, transcendentals=0),
    )(*args)


def iota(shape, dim):
    return lax.broadcasted_iota(I32, shape, dim)


def split(x):
    one = x.astype(BF16)
    rest = x - one.astype(F32)
    two = rest.astype(BF16)
    three = (rest - two.astype(F32)).astype(BF16)
    return [one, two, three]


def fold(x):
    n = x.shape[0] // 3
    return x[:n] + (x[n : 2 * n] + x[2 * n :])


def onehot(index, size):
    return jnp.where(iota((size, index.shape[1]), 0) == index, 1.0, 0.0)


def dot(a, b):
    return lax.dot_general(a, b, (((1,), (0,)), ((), ())), preferred_element_type=F32)


def dot_nt(a, b):
    return lax.dot_general(a, b, (((1,), (1,)), ((), ())), preferred_element_type=F32)


def pick(table, hi, lo):
    rows, cols = table.shape
    parts = jnp.concatenate(split(table), 0)
    got = fold(dot(parts, onehot(lo, cols).astype(BF16)))
    return jnp.sum(got * onehot(hi, rows), axis=0, keepdims=True)


def spread(value, hi, lo, rows, cols):
    parts = [jnp.where(iota((rows, hi.shape[1]), 0) == hi, v.astype(F32), 0.0).astype(BF16) for v in split(value)]
    return fold(dot_nt(jnp.concatenate(parts, 0), onehot(lo, cols).astype(BF16)))


def pres_kernel(rhs, wts, cell, front, prod, pres, send):
    depth, width, long = pres.shape
    for z in range(depth):
        pres[z] = wts[0, z] * rhs[0, z] + wts[1, z] * rhs[1, z] + wts[2, z] * rhs[2, z]
    where = cell[...]
    table = pres[...].reshape(depth * width, long)
    value = prod[...] * pick(table, lax.div(where, long), lax.rem(where, long))
    both = jnp.concatenate([value, front[...].astype(F32)], 1)
    send[...] = jnp.broadcast_to(both, send.shape)


def front_kernel(recv, inverse, send):
    devices = recv.shape[0]
    count = recv.shape[1] // 2
    rows, length = inverse.shape
    lanes = 128
    total = jnp.zeros((length // lanes, lanes), F32)
    group = 8
    for first in range(0, devices, group):
        lefts, rights = ([], [])
        for d in range(first, first + group):
            value = recv[d : d + 1, :count]
            index = recv[d : d + 1, count:].astype(I32)
            hi, lo = lax.div(index, lanes), lax.rem(index, lanes)
            hit = iota((length // lanes, count), 0) == hi
            lefts.append(jnp.concatenate([jnp.where(hit, v.astype(F32), 0.0).astype(BF16) for v in split(value)], 0))
            rights.append(onehot(lo, lanes).astype(BF16))
        total = total + fold(dot_nt(jnp.concatenate(lefts, 1), jnp.concatenate(rights, 1)))
    acc = jnp.zeros((rows, lanes), F32)
    for r in range(length // lanes):
        acc = acc + inverse[:, r * lanes : (r + 1) * lanes] * total[r : r + 1]
    parts = jnp.concatenate(split(acc), 1)
    out = dot_nt(jnp.ones((8, parts.shape[1]), BF16), parts)
    send[...] = jnp.broadcast_to(out[0:1], send.shape)


def coef_kernel(last, tz, store, tz_prev, upper, inv, sides, ends):
    depth = tz.shape[0]
    is_last = lax.axis_index("layer") == last
    low = tz_prev[0]
    gs, invs, lows = ([], [], [])
    g = jnp.zeros_like(low)
    before = low
    for z in range(depth):
        up = tz[z]
        if z == depth - 1:
            up = jnp.where(is_last, 0.0, up)
        pivot = before + up + store[z]
        if z:
            pivot = pivot - before * g
        ipv = 1.0 / pivot
        g = up * ipv
        inv[z] = ipv
        upper[z] = g
        gs.append(g)
        invs.append(ipv)
        lows.append(before)
        before = up
    a = [low * invs[0]]
    for z in range(1, depth):
        a.append(lows[z] * a[-1] * invs[z])
    b = [None] * depth
    b[-1] = gs[-1]
    for z in range(depth - 2, -1, -1):
        a[z] = a[z] + gs[z] * a[z + 1]
        b[z] = gs[z] * b[z + 1]
    for z in range(depth):
        sides[0, z] = a[z]
        sides[1, z] = b[z]
    ends[0], ends[1], ends[2], ends[3] = (a[0], a[-1], b[0], b[-1])


def is_right(level):
    return (lax.axis_index("layer") >> level) % 2 == 1


def choose(level, mine, other):
    right = is_right(level)
    return (jnp.where(right, other, mine), jnp.where(right, mine, other))


def join_coef_kernel(level, own, sib, out):
    af, af_ = choose(level, own[0], sib[0])
    al, al_ = choose(level, own[1], sib[1])
    bf, bf_ = choose(level, own[2], sib[2])
    bl, bl_ = choose(level, own[3], sib[3])
    den = 1.0 / (1.0 - bl * af_)
    out[0] = af + bf * af_ * al * den
    out[1] = al_ * al * den
    out[2] = bf * bf_ * den
    out[3] = bl_ + al_ * bl * bf_ * den


def local_solve(rhs, upper, inv, tz):
    depth = len(rhs)
    y = [rhs[0] * inv[0]]
    for z in range(1, depth):
        y.append((rhs[z] + tz[z - 1] * y[-1]) * inv[z])
    for z in range(depth - 2, -1, -1):
        y[z] = y[z] + upper[z] * y[z + 1]
    return y


def adjust_kernel(sol, cell, front, prod, pres, upper, inv, tz, y_out, ends):
    depth, width, long = pres.shape
    where, index = (cell[...], front[...])
    rows = sol.shape[1]
    value = prod[...] * pick(sol[...], lax.div(index, rows), lax.rem(index, rows))
    change = spread(value, lax.div(where, long), lax.rem(where, long), depth * width, long)
    change = change.reshape(depth, width, long)
    y = local_solve([pres[z] - change[z] for z in range(depth)], upper, inv, tz)
    for z in range(depth):
        y_out[z] = y[z]
    ends[0] = y[0]
    ends[1] = y[-1]


def join_kernel(level, own, sib, ocoef, scoef, out):
    yf, yf_ = choose(level, own[0], sib[0])
    yl, yl_ = choose(level, own[1], sib[1])
    af, af_ = choose(level, ocoef[0], scoef[0])
    al, al_ = choose(level, ocoef[1], scoef[1])
    bf, bf_ = choose(level, ocoef[2], scoef[2])
    bl, bl_ = choose(level, ocoef[3], scoef[3])
    den = 1.0 / (1.0 - bl * af_)
    out[0] = yf + bf * (yf_ + af_ * yl) * den
    out[1] = yl_ + al_ * (yl + bl * yf_) * den


def pressure_kernel(levels, *refs):
    groups = [refs[4 * i : 4 * i + 4] for i in range(levels)]
    y, sides, p, outer, row_first, row_last = refs[4 * levels :]
    zero = jnp.zeros(y.shape[1:], F32)
    above, below = (zero, zero)
    for level in range(levels - 1, -1, -1):
        own, sib, ocoef, scoef = groups[level]
        if level == levels - 1:
            yl, yf_ = choose(level, own[1], sib[0])[0], choose(level, own[0], sib[0])[1]
            bl, af_ = choose(level, ocoef[3], scoef[0])[0], choose(level, ocoef[0], scoef[0])[1]
            den = 1.0 / (1.0 - bl * af_)
            ml = (yl + bl * yf_) * den
            mr = (yf_ + af_ * yl) * den
        else:
            yl, _ = choose(level, own[1], sib[1])
            _, yf_ = choose(level, own[0], sib[0])
            _, af_ = choose(level, ocoef[0], scoef[0])
            al, _ = choose(level, ocoef[1], scoef[1])
            _, bf_ = choose(level, ocoef[2], scoef[2])
            bl, _ = choose(level, ocoef[3], scoef[3])
            den = 1.0 / (1.0 - bl * af_)
            one = yl + al * above
            two = yf_ + bf_ * below
            ml = (one + bl * two) * den
            mr = (two + af_ * one) * den
        right = is_right(level)
        above, below = (jnp.where(right, ml, above), jnp.where(right, below, mr))
    outer[0] = above
    outer[1] = below
    width = y.shape[1]
    for z in range(y.shape[0]):
        value = y[z] + sides[0, z] * above + sides[1, z] * below
        p[z] = value
        row_first[z] = value[0:1]
        row_last[z] = value[width - 1 : width]


def near(centre, above, below, row_before, row_after, tx, tx_row, ty, tz, tz_above):
    width, long = centre.shape
    row, col = (iota(centre.shape, 0), iota(centre.shape, 1))
    total = tz * below + tz_above * above
    after = jnp.where(row == width - 1, row_after, pltpu.roll(centre, width - 1, 0))
    total = total + tx * after
    total = total + jnp.where(row == 0, tx_row * row_before, pltpu.roll(tx * centre, 1, 0))
    total = total + ty * jnp.where(col == long - 1, 0.0, pltpu.roll(centre, long - 1, 1))
    total = total + jnp.where(col == 0, 0.0, pltpu.roll(ty * centre, 1, 1))
    return total


def search_kernel(p, outer, before, after, rhs, dcol, binv, tx, tx_row, ty, tz, tz_prev, s, s_first, s_last, s_top, s_bottom):
    depth, width, _ = p.shape
    for z in range(depth):
        above = outer[0] if z == 0 else p[z - 1]
        below = outer[1] if z == depth - 1 else p[z + 1]
        tza = tz_prev[0] if z == 0 else tz[z - 1]
        centre = p[z]
        coupled = near(centre, above, below, before[z], after[z], tx[z], tx_row[z], ty[z], tz[z], tza)
        remain = [rhs[c, z] - dcol[c, z] * centre for c in range(3)]
        remain[0] = remain[0] + coupled
        for c in range(3):
            value = binv[c, 0, z] * remain[0] + binv[c, 1, z] * remain[1] + binv[c, 2, z] * remain[2]
            if c == 0:
                value = centre + value
            s[c, z] = value
            s_first[c, z] = value[0:1]
            s_last[c, z] = value[width - 1 : width]
            if z == 0:
                s_top[c] = value
            if z == depth - 1:
                s_bottom[c] = value


def image_kernel(s, before, after, above_s, below_s, rhs, diag, tx, tx_row, ty, tz, tz_prev, image, send):
    depth = s.shape[1]
    along = power = start = 0.0
    for z in range(depth):
        tza = tz_prev[0] if z == 0 else tz[z - 1]
        for c in range(3):
            above = above_s[c] if z == 0 else s[c, z - 1]
            below = below_s[c] if z == depth - 1 else s[c, z + 1]
            coupled = near(s[c, z], above, below, before[c, z], after[c, z], tx[z], tx_row[z], ty[z], tz[z], tza)
            value = diag[c, 0, z] * s[0, z] + diag[c, 1, z] * s[1, z] + diag[c, 2, z] * s[2, z] - coupled
            image[c, z] = value
            right = rhs[c, z]
            along = along + value * right
            power = power + value * value
            start = start + right * right
    along, power, start = (jnp.sum(along), jnp.sum(power), jnp.sum(start))
    omega = along / jnp.where(power > 0.0, power, 1.0)
    square = cross = 0.0
    for z in range(depth):
        for c in range(3):
            value = image[c, z]
            left = rhs[c, z] - omega * value
            square = square + left * left
            cross = cross + left * value
    lane = iota((1, send.shape[1]), 1)
    out = jnp.zeros((1, send.shape[1]), F32)
    for i, value in enumerate((along, power, start, jnp.sum(square), jnp.sum(cross), omega)):
        out = jnp.where(lane == i, value, out)
    send[...] = jnp.broadcast_to(out, send.shape)


def finish_kernel(recv, s, image, rhs, update, lin_res, ratio):
    sums = recv[...]
    whole = jnp.sum(sums, axis=0, keepdims=True)
    omega = whole[:, 0:1] / whole[:, 1:2]
    shift = sums[:, 5:6] - omega
    square = sums[:, 3:4] + 2.0 * shift * sums[:, 4:5] + shift * shift * sums[:, 1:2]
    ratio[...] = jnp.sqrt(jnp.sum(square, axis=0, keepdims=True) / whole[:, 2:3])
    for c in range(3):
        for z in range(s.shape[1]):
            update[c, z] = omega * s[c, z]
            lin_res[c, z] = rhs[c, z] - omega * image[c, z]


def up(x, axis):
    return lax.ppermute(x, axis, [(i, i + 1) for i in range(lax.axis_size(axis) - 1)])


def down(x, axis):
    return lax.ppermute(x, axis, [(i + 1, i) for i in range(lax.axis_size(axis) - 1)])


def flip(x, level):
    return lax.ppermute(x, "layer", [(i, i ^ (1 << level)) for i in range(lax.axis_size("layer"))])


def everywhere(x):
    return lax.all_to_all(x, BOTH, split_axis=0, concat_axis=0, tiled=True)


def shards(rhs, weights, block_diag, block_inv, tx, ty, tz, store, cell, front, prod, inverse):
    devices = lax.axis_size("tile") * lax.axis_size("layer")
    layers = lax.axis_size("layer")
    levels = layers.bit_length() - 1
    depth, width, long = tx.shape
    plane = (width, long)
    count = cell.shape[0]
    rows = inverse.shape[0]
    cell, front, prod = (cell.reshape(1, -1), front.reshape(1, -1), prod.reshape(1, -1))

    tz_prev = up(tz[-1:], "layer")
    tx_row = up(tx[:, -1:], "tile")
    pres, send = call(
        pres_kernel, (vmem(tx.shape), vmem((devices, 2 * count))), (rhs, weights, cell, front, prod)
    )
    terms = everywhere(send)

    field = vmem(tx.shape)
    upper, inv, sides, ends = call(
        functools.partial(coef_kernel, layers - 1),
        (field, field, vmem((2,) + tx.shape), vmem((4,) + plane)),
        (tz, store, tz_prev),
    )
    coefs = []
    right = lambda level: (lax.axis_index("layer") >> level) % 2 == 1
    for level in range(levels):
        if level == levels - 1:
            face = jnp.where(right(level), ends[0], ends[3])[None]
            coefs.append((ends, flip(face, level)))
        else:
            sib = flip(ends, level)
            coefs.append((ends, sib))
            ends = call(functools.partial(join_coef_kernel, level), vmem((4,) + plane), (ends, sib))

    rows_sol = call(front_kernel, vmem((devices, rows)), (terms, inverse))
    sol = everywhere(rows_sol)

    y, yends = call(
        adjust_kernel, (field, vmem((2,) + plane)), (sol, cell, front, prod, pres, upper, inv, tz)
    )
    args = []
    for level in range(levels):
        own, scoef = coefs[level]
        if level == levels - 1:
            face = jnp.where(right(level), yends[0], yends[1])[None]
            args += [yends, flip(face, level), own, scoef]
        else:
            sib = flip(yends, level)
            args += [yends, sib, own, scoef]
            yends = call(functools.partial(join_kernel, level), vmem((2,) + plane), (yends, sib, own, scoef))
    row3 = vmem((depth, 1, long))
    p, outer, p_first, p_last = call(
        functools.partial(pressure_kernel, levels), (field, vmem((2,) + plane), row3, row3), (*args, y, sides)
    )
    before, after = (up(p_last, "tile"), down(p_first, "tile"))
    row9 = vmem((3, depth, 1, long))
    plane3 = vmem((3,) + plane)
    s, s_first, s_last, s_top, s_bottom = call(
        search_kernel,
        (vmem(rhs.shape), row9, row9, plane3, plane3),
        (p, outer, before, after, rhs, block_diag[:, 0], block_inv, tx, tx_row, ty, tz, tz_prev),
    )
    above, below = (up(s_bottom, "layer"), down(s_top, "layer"))
    before, after = (up(s_last, "tile"), down(s_first, "tile"))
    image, send = call(
        image_kernel,
        (vmem(rhs.shape), vmem((devices, 128))),
        (s, before, after, above, below, rhs, block_diag, tx, tx_row, ty, tz, tz_prev),
    )
    sums = everywhere(send)
    update, lin_res, ratio = call(
        finish_kernel, (hbm(rhs.shape), hbm(rhs.shape), hbm((1, 1))), (sums, s, image, rhs)
    )
    return (update, lin_res, ratio.reshape(()))


def solution(mesh):
    return jax.shard_map(
        shards,
        mesh=mesh,
        in_specs=(
            P(None, "layer", "tile", None),
            P(None, "layer", "tile", None),
            P(None, None, "layer", "tile", None),
            P(None, None, "layer", "tile", None),
            P("layer", "tile", None),
            P("layer", "tile", None),
            P("layer", "tile", None),
            P("layer", "tile", None),
            P(("tile", "layer")),
            P(("tile", "layer")),
            P(("tile", "layer")),
            P(("tile", "layer"), None),
        ),
        out_specs=(P(None, "layer", "tile", None), P(None, "layer", "tile", None), P()),
        check_vma=False,
    )
```

time: 344 us -> 96.3 us (0.28)
  blocking collectives: 181 us -> 33.9 us
  local copies, waits for them, and re-layouts: 63.7 us -> 13.7 us
  other arithmetic: 42.6 us -> 0.03 us
  starting transfers between devices: 36.8 us -> 23 us
  waiting for transfers between devices: 2.92 us -> 15.5 us
  matrix products: 8.94 us -> 0 us
  Pallas kernels: 0 us -> 8.68 us
  between operations: 5.16 us -> 0.9 us
    psum x3 -> x0, blocking collectives: 130 us -> none  [the longest x1 47.6 us: shards(): lax.psum((jnp.sum(image * newton_rhs), jnp.sum(image * image), jnp.sum(ne...]
    all_gather x1 -> x0, blocking collectives: 40.2 us -> none  [shards(): lax.all_gather(front_rows, ('tile', 'layer'), axis=0, tiled=True)]
    unnamed x53 -> x42, local copies, waits for them, and re-layouts: 41 us -> 12.5 us
    all_to_all x1 -> x3, blocking collectives: 10.6 us -> 33.9 us  [everywhere(): return lax.all_to_all(x, BOTH, split_axis=0, concat_axis=0, tiled=True)]
    dynamic_update_slice x24 -> x0, other arithmetic: 18.9 us -> none  [line_solve(): _, (gall, dall) = lax.scan(forward, (zero, zero), (lower, upper, diag, rhs))]
    ppermute x10 -> x12, waiting for transfers between devices: 2.91 us -> 15.5 us  [the longest x3 8.86 us: down(): lax.ppermute(x, axis, [(i + 1, i) for i in range(lax.axis_size(axis) - 1)])]
    all_to_all x3 -> x0, starting transfers between devices: 11.3 us -> none  [the longest x1 4.21 us: shards(): lax.all_to_all(trans_z, 'layer', split_axis=2, concat_axis=0, tiled=True)]
    all_to_all x5 -> x2, local copies, waits for them, and re-layouts: 10.7 us -> 0.13 us  [everywhere(): return lax.all_to_all(x, BOTH, split_axis=0, concat_axis=0, tiled=True)]
  transfers between devices with their start and end apart: 13 -> 12, of which waited for: 3 -> 7; matrix products, arithmetic and copies ran while one was open for 17% -> 0% of each run, Pallas kernels for 0% -> 3%
where the time goes in v1:
time: 96.3 us; the launch traced here: 95.7 us
  blocking collectives  33.9 us (35%)
  starting transfers between devices  23 us (24%)
  waiting for transfers between devices  15.5 us (16%)
  local copies, waits for them, and re-layouts  13.7 us (14%)
  Pallas kernels  8.68 us (9%)
    all_to_all x3, blocking collectives, everywhere(): return lax.all_to_all(x, BOTH, split_axis=0, concat_axis=0, tiled=True)  33.9 us
    ppermute x5, starting transfers between devices, up(): lax.ppermute(x, axis, [(i, i + 1) for i in range(lax.axis_size(axis) - 1)])  13.2 us
    unnamed x42, local copies, waits for them, and re-layouts  12.5 us
    ppermute x3, waiting for transfers between devices, down(): lax.ppermute(x, axis, [(i + 1, i) for i in range(lax.axis_size(axis) - 1)])  8.86 us
    pallas_call x10, Pallas kernels, call(): pl.pallas_call(kernel, out_shape=outs, in_specs=[VM] * len(args), out_spe...  8.68 us
    ppermute x4, starting transfers between devices, flip(): lax.ppermute(x, 'layer', [(i, i ^ 1 << level) for i in range(lax.axis_siz...  5.83 us
    ppermute x4, waiting for transfers between devices, flip(): lax.ppermute(x, 'layer', [(i, i ^ 1 << level) for i in range(lax.axis_siz...  5 us
    ppermute x3, starting transfers between devices, down(): lax.ppermute(x, axis, [(i + 1, i) for i in range(lax.axis_size(axis) - 1)])  4.01 us
  transfers between devices with their start and end apart: 12, of which 7 were waited for; matrix products, arithmetic and copies ran while one was open for 0% of the time, Pallas kernels for 3%

profile of v1, /device:TPU:0, one launch (start us, length us, event | category | flops | bytes accessed | tf_op | source)
XLA Modules:
  0.0 95.7 jit_solution(8959374220872682604)
XLA Ops:
  0.6 1.0 %slice.21 = f32[1,16,2048]{2,1,0:T(8,128)S(1)} slice(f32[3,16,2048]{2,1,0:T(8,128)} %tz.7), slice={[2:3], [0:16], [0:2048]} | slice | bytes 262144 | tf_op jit(solution)/shard_map/slice | solution.py:350
  1.7 2.4 %collective-permute-start = (f32[1,16,2048]{2,1,0:T(8,128)S(1)}, f32[1,16,2048]{2,1,0:T(8,128)S(1)}, u32[]{:S(2)}, u32[]{:S(2)}) collective-permute-start(f32[1,16,2048]{2,1,0:T(8,128)S(1)} %slice.21), channel_id=1, source_target_pairs={{0,1},{1,2},{2,3},{4,5},{5,6},{6,7},{8,9},{9,10},{10,11},{12,13},{... | collective-permute-start | bytes 393224 | tf_op jit(solution)/shard_map/ppermute | solution.py:325
  4.0 1.0 %collective-permute-done.tz_prev = f32[1,16,2048]{2,1,0:T(8,128)S(1)} collective-permute-done((f32[1,16,2048]{2,1,0:T(8,128)S(1)}, f32[1,16,2048]{2,1,0:T(8,128)S(1)}, u32[]{:S(2)}, u32[]{:S(2)}) %collective-permute-start) | collective-permute-done | bytes 131104 | tf_op jit(solution)/shard_map/ppermute | solution.py:325
  5.0 1.0 %copy-done.2 = f32[3,16,2048]{2,1,0:T(8,128)S(1)} copy-done((f32[3,16,2048]{2,1,0:T(8,128)S(1)}, f32[3,16,2048]{2,1,0:T(8,128)}, u32[]{:S(2)}) %copy-start.2) | copy-done | bytes 393240
  6.0 1.0 %copy-done.11 = f32[3,16,2048]{2,1,0:T(8,128)S(1)} copy-done((f32[3,16,2048]{2,1,0:T(8,128)S(1)}, f32[3,16,2048]{2,1,0:T(8,128)}, u32[]{:S(2)}) %copy-start.11) | copy-done | bytes 393240
  7.2 0.9 copy-done.9
  8.0 3.6 %collective-permute-start.2 = (f32[4,16,2048]{2,1,0:T(8,128)S(1)}, f32[4,16,2048]{2,1,0:T(8,128)S(1)}, u32[]{:S(2)}, u32[]{:S(2)}) collective-permute-start(f32[4,16,2048]{2,1,0:T(8,128)S(1)} %get-tuple-element.30.ocoef.own.refs_2_), channel_id=1, source_target_pairs={{0,1},{1,0},{2,3},{3,2},{4,5},{5,4},{6,7},{7,6},{8,9},{9,8},{10,11... | collective-permute-start | bytes 1572872 | tf_op jit(solution)/shard_map/ppermute | solution.py:333
  11.6 1.3 %copy-done.8 = f32[3,3,16,2048]{3,2,1,0:T(8,128)S(1)} copy-done((f32[3,3,16,2048]{3,2,1,0:T(8,128)S(1)}, f32[3,3,16,2048]{3,2,1,0:T(8,128)}, u32[]{:S(2)}) %copy-start.8) | copy-done | bytes 1179672
  15.5 14.0 %all_to_all.33 = f32[32,1,512]{2,1,0:T(1,128)S(1)} all-to-all(f32[32,1,512]{2,1,0:T(1,128)S(1)} %copy.16), channel_id=1, replica_groups=mesh['tile'=8,'layer'=4] {'tile','layer'}, dimensions={0} | all-to-all | bytes 131072 | tf_op jit(solution)/shard_map/all_to_all | solution.py:337
  29.5 3.4 %copy-done.1 = f32[256,8192]{1,0:T(8,128)S(1)} copy-done((f32[256,8192]{1,0:T(8,128)S(1)}, f32[256,8192]{1,0:T(8,128)}, u32[]{:S(2)}) %copy-start.1) | copy-done | bytes 8388632
  32.9 1.7 %shard_map.140 = f32[32,256]{1,0:T(8,128)S(1)} custom-call(f32[32,512]{1,0:T(8,128)S(1)} %bitcast.20, f32[256,8192]{1,0:T(8,128)S(1)} %copy-done.1), custom_call_target="tpu_custom_call" | custom-call | bytes 8454144 | tf_op jit(solution)/shard_map/pallas_call | solution.py:28
  34.7 8.9 %all_to_all.34 = f32[32,1,256]{2,1,0:T(1,128)S(1)} all-to-all(f32[32,1,256]{2,1,0:T(1,128)S(1)} %copy.17), channel_id=1, replica_groups=mesh['tile'=8,'layer'=4] {'tile','layer'}, dimensions={0} | all-to-all | bytes 65536 | tf_op jit(solution)/shard_map/all_to_all | solution.py:337
  44.4 0.7 copy-done.12
  45.2 1.4 %collective-permute-done.1.sib.refs_1_ = f32[2,16,2048]{2,1,0:T(8,128)S(1)} collective-permute-done((f32[2,16,2048]{2,1,0:T(8,128)S(1)}, f32[2,16,2048]{2,1,0:T(8,128)S(1)}, u32[]{:S(2)}, u32[]{:S(2)}) %collective-permute-start.1) | collective-permute-done | bytes 262176 | tf_op jit(solution)/shard_map/ppermute | solution.py:333
  47.5 1.6 %collective-permute-start.4 = (f32[1,16,2048]{2,1,0:T(8,128)S(1)}, f32[1,16,2048]{2,1,0:T(8,128)S(1)}, u32[]{:S(2)}, u32[]{:S(2)}) collective-permute-start(f32[1,16,2048]{2,1,0:T(8,128)S(1)} %slice_select_fusion), channel_id=1, source_target_pairs={{0,2},{1,3},{2,0},{3,1},{4,6},{5,7},{6,4},{7,5},{8,10},{9,11},{10,... | collective-permute-start | bytes 393224 | tf_op jit(solution)/shard_map/ppermute | solution.py:333
  49.2 2.5 %collective-permute-start.7 = (f32[3,1,2048]{2,1,0:T(1,128)S(1)}, f32[3,1,2048]{2,1,0:T(1,128)S(1)}, u32[]{:S(2)}, u32[]{:S(2)}) collective-permute-start(f32[3,1,2048]{2,1,0:T(1,128)S(1)} %slice.27), channel_id=1, source_target_pairs={{0,4},{4,8},{8,12},{12,16},{16,20},{20,24},{24,28},{1,5},{5,9},{9,... | collective-permute-start | bytes 73736 | tf_op jit(solution)/shard_map/ppermute | solution.py:325
  51.6 1.6 %collective-permute-done.3.refs_5_ = f32[1,16,2048]{2,1,0:T(8,128)S(1)} collective-permute-done((f32[1,16,2048]{2,1,0:T(8,128)S(1)}, f32[1,16,2048]{2,1,0:T(8,128)S(1)}, u32[]{:S(2)}, u32[]{:S(2)}) %collective-permute-start.3) | collective-permute-done | bytes 131104 | tf_op jit(solution)/shard_map/ppermute | solution.py:333
  53.2 2.0 %collective-permute-done.4.refs_7_ = f32[1,16,2048]{2,1,0:T(8,128)S(1)} collective-permute-done((f32[1,16,2048]{2,1,0:T(8,128)S(1)}, f32[1,16,2048]{2,1,0:T(8,128)S(1)}, u32[]{:S(2)}, u32[]{:S(2)}) %collective-permute-start.4) | collective-permute-done | bytes 131104 | tf_op jit(solution)/shard_map/ppermute | solution.py:333
  55.2 1.1 %copy-done.10 = f32[2,3,16,2048]{3,2,1,0:T(8,128)S(1)} copy-done((f32[2,3,16,2048]{3,2,1,0:T(8,128)S(1)}, f32[2,3,16,2048]{3,2,1,0:T(8,128)}, u32[]{:S(2)}) %copy-start.10) | copy-done | bytes 786456
  56.3 1.0 %copy-done.13 = f32[3,16,2048]{2,1,0:T(8,128)S(1)} copy-done((f32[3,16,2048]{2,1,0:T(8,128)S(1)}, f32[3,16,2048]{2,1,0:T(8,128)}, u32[]{:S(2)}) %copy-start.13) | copy-done | bytes 393240
  57.6 2.7 %collective-permute-start.5 = (f32[3,1,2048]{2,1,0:T(1,128)S(1)}, f32[3,1,2048]{2,1,0:T(1,128)S(1)}, u32[]{:S(2)}, u32[]{:S(2)}) collective-permute-start(f32[3,1,2048]{2,1,0:T(1,128)S(1)} %get-tuple-element.35), channel_id=1, source_target_pairs={{0,4},{4,8},{8,12},{12,16},{16,20},{20,24},{24,28},{1,5},{5,9},{9,... | collective-permute-start | bytes 73736 | tf_op jit(solution)/shard_map/ppermute | solution.py:325
  60.4 1.4 %collective-permute-start.6 = (f32[3,1,2048]{2,1,0:T(1,128)S(1)}, f32[3,1,2048]{2,1,0:T(1,128)S(1)}, u32[]{:S(2)}, u32[]{:S(2)}) collective-permute-start(f32[3,1,2048]{2,1,0:T(1,128)S(1)} %get-tuple-element.36), channel_id=1, source_target_pairs={{4,0},{8,4},{12,8},{16,12},{20,16},{24,20},{28,24},{5,1},{9,5},{13... | collective-permute-start | bytes 73736 | tf_op jit(solution)/shard_map/ppermute | solution.py:329
  61.9 4.3 %collective-permute-done.6.after = f32[3,1,2048]{2,1,0:T(1,128)S(1)} collective-permute-done((f32[3,1,2048]{2,1,0:T(1,128)S(1)}, f32[3,1,2048]{2,1,0:T(1,128)S(1)}, u32[]{:S(2)}, u32[]{:S(2)}) %collective-permute-start.6) | collective-permute-done | bytes 24608 | tf_op jit(solution)/shard_map/ppermute | solution.py:329
  66.2 0.9 shard_map.146
  67.1 1.3 %collective-permute-start.10 = (f32[3,16,2048]{2,1,0:T(8,128)S(1)}, f32[3,16,2048]{2,1,0:T(8,128)S(1)}, u32[]{:S(2)}, u32[]{:S(2)}) collective-permute-start(f32[3,16,2048]{2,1,0:T(8,128)S(1)} %get-tuple-element.40), channel_id=1, source_target_pairs={{0,1},{1,2},{2,3},{4,5},{5,6},{6,7},{8,9},{9,10},{10,11},{12,13},{... | collective-permute-start | bytes 1179656 | tf_op jit(solution)/shard_map/ppermute | solution.py:325
  68.4 1.3 %collective-permute-start.11 = (f32[3,16,2048]{2,1,0:T(8,128)S(1)}, f32[3,16,2048]{2,1,0:T(8,128)S(1)}, u32[]{:S(2)}, u32[]{:S(2)}) collective-permute-start(f32[3,16,2048]{2,1,0:T(8,128)S(1)} %get-tuple-element.41), channel_id=1, source_target_pairs={{1,0},{2,1},{3,2},{5,4},{6,5},{7,6},{9,8},{10,9},{11,10},{13,12},{... | collective-permute-start | bytes 1179656 | tf_op jit(solution)/shard_map/ppermute | solution.py:329
  69.7 4.3 %collective-permute-start.8 = (f32[3,3,1,2048]{3,2,1,0:T(1,128)S(1)}, f32[3,3,1,2048]{3,2,1,0:T(1,128)S(1)}, u32[]{:S(2)}, u32[]{:S(2)}) collective-permute-start(f32[3,3,1,2048]{3,2,1,0:T(1,128)S(1)} %get-tuple-element.38), channel_id=1, source_target_pairs={{0,4},{4,8},{8,12},{12,16},{16,20},{20,24},{24,28},{1,5},{5,9},{9,... | collective-permute-start | bytes 221192 | tf_op jit(solution)/shard_map/ppermute | solution.py:325
  74.0 1.3 %collective-permute-start.9 = (f32[3,3,1,2048]{3,2,1,0:T(1,128)S(1)}, f32[3,3,1,2048]{3,2,1,0:T(1,128)S(1)}, u32[]{:S(2)}, u32[]{:S(2)}) collective-permute-start(f32[3,3,1,2048]{3,2,1,0:T(1,128)S(1)} %get-tuple-element.39), channel_id=1, source_target_pairs={{4,0},{8,4},{12,8},{16,12},{20,16},{24,20},{28,24},{5,1},{9,5},{13... | collective-permute-start | bytes 221192 | tf_op jit(solution)/shard_map/ppermute | solution.py:329
  76.0 4.5 %collective-permute-done.9.after = f32[3,3,1,2048]{3,2,1,0:T(1,128)S(1)} collective-permute-done((f32[3,3,1,2048]{3,2,1,0:T(1,128)S(1)}, f32[3,3,1,2048]{3,2,1,0:T(1,128)S(1)}, u32[]{:S(2)}, u32[]{:S(2)}) %collective-permute-start.9) | collective-permute-done | bytes 73760 | tf_op jit(solution)/shard_map/ppermute | solution.py:329
  80.5 2.5 %shard_map.147 = (f32[3,3,16,2048]{3,2,1,0:T(8,128)S(1)}, f32[32,128]{1,0:T(8,128)S(1)}) custom-call(f32[3,3,16,2048]{3,2,1,0:T(8,128)S(1)} %get-tuple-element.37.s, f32[3,3,1,2048]{3,2,1,0:T(1,128)S(1)} %collective-permute-done.8.before, f32[3,3,1,2048]{3,2,1,0:T(1,128)S(1)} %collective-permute-done.9.after, ...), custom_call_target="tpu_custom_call" | custom-call | bytes 8167424 | tf_op jit(solution)/shard_map/pallas_call | solution.py:28
  83.1 10.9 %all_to_all.35 = f32[32,1,128]{2,1,0:T(1,128)S(1)} all-to-all(f32[32,1,128]{2,1,0:T(1,128)S(1)} %bitcast.25), channel_id=1, replica_groups=mesh['tile'=8,'layer'=4] {'tile','layer'}, dimensions={0} | all-to-all | bytes 32768 | tf_op jit(solution)/shard_map/all_to_all | solution.py:337
  94.0 1.7 %shard_map.148 = (f32[3,3,16,2048]{3,2,1,0:T(8,128)}, f32[3,3,16,2048]{3,2,1,0:T(8,128)}, f32[1,1]{1,0:T(1,128)}) custom-call(f32[32,128]{1,0:T(8,128)S(1)} %bitcast.23, f32[3,3,16,2048]{3,2,1,0:T(8,128)S(1)} %get-tuple-element.37.s, f32[3,3,16,2048]{3,2,1,0:T(8,128)S(1)} %get-tuple-element.43.image, f32[3,3,16,2048]{3,2,1,0:T(8,128)S(1)} %copy-done), custom_call_target="tpu_custom_call" | custom-call | bytes 3555328 | tf_op jit(solution)/shard_map/pallas_call | solution.py:28
  (54 shorter events, 5.5 us)
Async XLA Ops:
  0.6 11.0 %copy-start = (f32[3,3,16,2048]{3,2,1,0:T(8,128)S(1)}, f32[3,3,16,2048]{3,2,1,0:T(8,128)}, u32[]{:S(2)}) copy-start(f32[3,3,16,2048]{3,2,1,0:T(8,128)} %rhs.7) | copy-start | bytes 3538948
  1.7 3.3 %collective-permute-start = (f32[1,16,2048]{2,1,0:T(8,128)S(1)}, f32[1,16,2048]{2,1,0:T(8,128)S(1)}, u32[]{:S(2)}, u32[]{:S(2)}) collective-permute-start(f32[1,16,2048]{2,1,0:T(8,128)S(1)} %slice.21), channel_id=1, source_target_pairs={{0,1},{1,2},{2,3},{4,5},{5,6},{6,7},{8,9},{9,10},{10,11},{12,13},{... | collective-permute-start | bytes 393224 | tf_op jit(solution)/shard_map/ppermute | solution.py:325
  5.0 1.0 %copy-start.2 = (f32[3,16,2048]{2,1,0:T(8,128)S(1)}, f32[3,16,2048]{2,1,0:T(8,128)}, u32[]{:S(2)}) copy-start(f32[3,16,2048]{2,1,0:T(8,128)} %tz.7) | copy-start | bytes 1179652
  6.0 1.0 %copy-start.11 = (f32[3,16,2048]{2,1,0:T(8,128)S(1)}, f32[3,16,2048]{2,1,0:T(8,128)}, u32[]{:S(2)}) copy-start(f32[3,16,2048]{2,1,0:T(8,128)} %store.1) | copy-start | bytes 1179652
  7.2 0.9 copy-start.9
  8.0 38.6 %collective-permute-start.2 = (f32[4,16,2048]{2,1,0:T(8,128)S(1)}, f32[4,16,2048]{2,1,0:T(8,128)S(1)}, u32[]{:S(2)}, u32[]{:S(2)}) collective-permute-start(f32[4,16,2048]{2,1,0:T(8,128)S(1)} %get-tuple-element.30.ocoef.own.refs_2_), channel_id=1, source_target_pairs={{0,1},{1,0},{2,3},{3,2},{4,5},{5,4},{6,7},{7,6},{8,9},{9,8},{10,11... | collective-permute-start | bytes 1572872 | tf_op jit(solution)/shard_map/ppermute | solution.py:333
  11.6 1.3 %copy-start.8 = (f32[3,3,16,2048]{3,2,1,0:T(8,128)S(1)}, f32[3,3,16,2048]{3,2,1,0:T(8,128)}, u32[]{:S(2)}) copy-start(f32[3,3,16,2048]{3,2,1,0:T(8,128)} %wts.1) | copy-start | bytes 3538948
  12.9 0.7 copy-start.14
  13.6 0.7 copy-start.16
  14.2 0.7 copy-start.18
  29.5 3.4 %copy-start.1 = (f32[256,8192]{1,0:T(8,128)S(1)}, f32[256,8192]{1,0:T(8,128)}, u32[]{:S(2)}) copy-start(f32[256,8192]{1,0:T(8,128)} %inverse.1) | copy-start | bytes 25165828
  32.9 10.8 %copy-start.3 = (f32[3,16,2048]{2,1,0:T(8,128)S(1)}, f32[3,16,2048]{2,1,0:T(8,128)}, u32[]{:S(2)}) copy-start(f32[3,16,2048]{2,1,0:T(8,128)} %tz.7) | copy-start | bytes 1179652
  32.9 10.8 %copy-start.15 = (s32[256]{0:T(256)S(1)}, s32[256]{0:T(256)}, u32[]{:S(2)}) copy-start(s32[256]{0:T(256)} %param.20) | copy-start | bytes 3076
  32.9 10.8 %copy-start.17 = (s32[256]{0:T(256)S(1)}, s32[256]{0:T(256)}, u32[]{:S(2)}) copy-start(s32[256]{0:T(256)} %param.21) | copy-start | bytes 3076
  32.9 10.8 %copy-start.19 = (f32[256]{0:T(256)S(1)}, f32[256]{0:T(256)}, u32[]{:S(2)}) copy-start(f32[256]{0:T(256)} %param.22) | copy-start | bytes 3076
  44.3 0.7 copy-start.12
  45.1 1.5 %collective-permute-start.1 = (f32[2,16,2048]{2,1,0:T(8,128)S(1)}, f32[2,16,2048]{2,1,0:T(8,128)S(1)}, u32[]{:S(2)}, u32[]{:S(2)}) collective-permute-start(f32[2,16,2048]{2,1,0:T(8,128)S(1)} %get-tuple-element.29.own.refs_0_), channel_id=1, source_target_pairs={{0,1},{1,0},{2,3},{3,2},{4,5},{5,4},{6,7},{7,6},{8,9},{9,8},{10,11... | collective-permute-start | bytes 786440 | tf_op jit(solution)/shard_map/ppermute | solution.py:333
  46.6 19.6 %copy-start.5 = (f32[3,3,3,16,2048]{4,3,2,1,0:T(8,128)S(1)}, f32[3,3,3,16,2048]{4,3,2,1,0:T(8,128)}, u32[]{:S(2)}) copy-start(f32[3,3,3,16,2048]{4,3,2,1,0:T(8,128)} %binv.1) | copy-start | bytes 10616836
  46.8 2.4 %copy-start.6 = (f32[3,16,2048]{2,1,0:T(8,128)S(1)}, f32[3,16,2048]{2,1,0:T(8,128)}, u32[]{:S(2)}) copy-start(f32[3,16,2048]{2,1,0:T(8,128)} %tx.3) | copy-start | bytes 1179652
  46.8 6.4 %collective-permute-start.3 = (f32[1,16,2048]{2,1,0:T(8,128)S(1)}, f32[1,16,2048]{2,1,0:T(8,128)S(1)}, u32[]{:S(2)}, u32[]{:S(2)}) collective-permute-start(f32[1,16,2048]{2,1,0:T(8,128)S(1)} %slice_select_fusion.1), channel_id=1, source_target_pairs={{0,2},{1,3},{2,0},{3,1},{4,6},{5,7},{6,4},{7,5},{8,10},{9,11},{10,... | collective-permute-start | bytes 393224 | tf_op jit(solution)/shard_map/ppermute | solution.py:333
  47.5 7.7 %collective-permute-start.4 = (f32[1,16,2048]{2,1,0:T(8,128)S(1)}, f32[1,16,2048]{2,1,0:T(8,128)S(1)}, u32[]{:S(2)}, u32[]{:S(2)}) collective-permute-start(f32[1,16,2048]{2,1,0:T(8,128)S(1)} %slice_select_fusion), channel_id=1, source_target_pairs={{0,2},{1,3},{2,0},{3,1},{4,6},{5,7},{6,4},{7,5},{8,10},{9,11},{10,... | collective-permute-start | bytes 393224 | tf_op jit(solution)/shard_map/ppermute | solution.py:333
  49.2 12.8 %collective-permute-start.7 = (f32[3,1,2048]{2,1,0:T(1,128)S(1)}, f32[3,1,2048]{2,1,0:T(1,128)S(1)}, u32[]{:S(2)}, u32[]{:S(2)}) collective-permute-start(f32[3,1,2048]{2,1,0:T(1,128)S(1)} %slice.27), channel_id=1, source_target_pairs={{0,4},{4,8},{8,12},{12,16},{16,20},{20,24},{24,28},{1,5},{5,9},{9,... | collective-permute-start | bytes 73736 | tf_op jit(solution)/shard_map/ppermute | solution.py:325
  55.2 1.1 %copy-start.10 = (f32[2,3,16,2048]{3,2,1,0:T(8,128)S(1)}, f32[2,3,16,2048]{3,2,1,0:T(8,128)}, u32[]{:S(2)}) copy-start(f32[2,3,16,2048]{3,2,1,0:T(8,128)} %copy-done.9) | copy-start | bytes 2359300
  56.3 1.0 %copy-start.13 = (f32[3,16,2048]{2,1,0:T(8,128)S(1)}, f32[3,16,2048]{2,1,0:T(8,128)}, u32[]{:S(2)}) copy-start(f32[3,16,2048]{2,1,0:T(8,128)} %copy-done.12) | copy-start | bytes 1179652
  57.3 4.5 %copy-start.4 = (f32[3,3,3,16,2048]{4,3,2,1,0:T(8,128)S(1)}, f32[3,3,3,16,2048]{4,3,2,1,0:T(8,128)}, u32[]{:S(2)}) copy-start(f32[3,3,3,16,2048]{4,3,2,1,0:T(8,128)} %diag.1) | copy-start | bytes 10616836
  57.6 4.3 %collective-permute-start.5 = (f32[3,1,2048]{2,1,0:T(1,128)S(1)}, f32[3,1,2048]{2,1,0:T(1,128)S(1)}, u32[]{:S(2)}, u32[]{:S(2)}) collective-permute-start(f32[3,1,2048]{2,1,0:T(1,128)S(1)} %get-tuple-element.35), channel_id=1, source_target_pairs={{0,4},{4,8},{8,12},{12,16},{16,20},{20,24},{24,28},{1,5},{5,9},{9,... | collective-permute-start | bytes 73736 | tf_op jit(solution)/shard_map/ppermute | solution.py:325
  60.4 5.9 %copy-start.7 = (f32[3,16,2048]{2,1,0:T(8,128)S(1)}, f32[3,16,2048]{2,1,0:T(8,128)}, u32[]{:S(2)}) copy-start(f32[3,16,2048]{2,1,0:T(8,128)} %ty.3) | copy-start | bytes 1179652
  60.4 5.9 %collective-permute-start.6 = (f32[3,1,2048]{2,1,0:T(1,128)S(1)}, f32[3,1,2048]{2,1,0:T(1,128)S(1)}, u32[]{:S(2)}, u32[]{:S(2)}) collective-permute-start(f32[3,1,2048]{2,1,0:T(1,128)S(1)} %get-tuple-element.36), channel_id=1, source_target_pairs={{4,0},{8,4},{12,8},{16,12},{20,16},{24,20},{28,24},{5,1},{9,5},{13... | collective-permute-start | bytes 73736 | tf_op jit(solution)/shard_map/ppermute | solution.py:329
  67.1 13.4 %collective-permute-start.10 = (f32[3,16,2048]{2,1,0:T(8,128)S(1)}, f32[3,16,2048]{2,1,0:T(8,128)S(1)}, u32[]{:S(2)}, u32[]{:S(2)}) collective-permute-start(f32[3,16,2048]{2,1,0:T(8,128)S(1)} %get-tuple-element.40), channel_id=1, source_target_pairs={{0,1},{1,2},{2,3},{4,5},{5,6},{6,7},{8,9},{9,10},{10,11},{12,13},{... | collective-permute-start | bytes 1179656 | tf_op jit(solution)/shard_map/ppermute | solution.py:325
  68.4 12.1 %collective-permute-start.11 = (f32[3,16,2048]{2,1,0:T(8,128)S(1)}, f32[3,16,2048]{2,1,0:T(8,128)S(1)}, u32[]{:S(2)}, u32[]{:S(2)}) collective-permute-start(f32[3,16,2048]{2,1,0:T(8,128)S(1)} %get-tuple-element.41), channel_id=1, source_target_pairs={{1,0},{2,1},{3,2},{5,4},{6,5},{7,6},{9,8},{10,9},{11,10},{13,12},{... | collective-permute-start | bytes 1179656 | tf_op jit(solution)/shard_map/ppermute | solution.py:329
  69.7 6.3 %collective-permute-start.8 = (f32[3,3,1,2048]{3,2,1,0:T(1,128)S(1)}, f32[3,3,1,2048]{3,2,1,0:T(1,128)S(1)}, u32[]{:S(2)}, u32[]{:S(2)}) collective-permute-start(f32[3,3,1,2048]{3,2,1,0:T(1,128)S(1)} %get-tuple-element.38), channel_id=1, source_target_pairs={{0,4},{4,8},{8,12},{12,16},{16,20},{20,24},{24,28},{1,5},{5,9},{9,... | collective-permute-start | bytes 221192 | tf_op jit(solution)/shard_map/ppermute | solution.py:325
  74.0 6.5 %collective-permute-start.9 = (f32[3,3,1,2048]{3,2,1,0:T(1,128)S(1)}, f32[3,3,1,2048]{3,2,1,0:T(1,128)S(1)}, u32[]{:S(2)}, u32[]{:S(2)}) collective-permute-start(f32[3,3,1,2048]{3,2,1,0:T(1,128)S(1)} %get-tuple-element.39), channel_id=1, source_target_pairs={{4,0},{8,4},{12,8},{16,12},{20,16},{24,20},{28,24},{5,1},{9,5},{13... | collective-permute-start | bytes 221192 | tf_op jit(solution)/shard_map/ppermute | solution.py:329

commit v2 on v1

--- a/solution.py
+++ b/solution.py
@@ -22,17 +22,36 @@
     return pltpu.VMEM(shape, dtype)
 
 
-def call(kernel, outs, args, flops=0, limit=LIMIT):
-    args = [pltpu.with_memory_space_constraint(a, pltpu.VMEM) for a in args]
-    size = 4 * sum(a.size for a in args)
+def staged(kernel, where, outs, *refs):
+    count, sems = len(where), refs[-1]
+    held = list(refs[count + outs : -1])
+    operands, copies = ([], [])
+    for i, far in enumerate(where):
+        if far:
+            copies.append(pltpu.make_async_copy(refs[i], held[len(copies)], sems.at[len(copies)]))
+            operands.append(held[len(copies) - 1])
+        else:
+            operands.append(refs[i])
+    for copy in copies:
+        copy.start()
+    for copy in copies:
+        copy.wait()
+    kernel(*operands, *refs[count : count + outs])
+
+
+def call(kernel, outs, args, far=(), limit=LIMIT):
+    where = [i in far for i in range(len(args))]
+    spaces = [pltpu.HBM if w else pltpu.VMEM for w in where]
+    count = len(jax.tree.leaves(outs, is_leaf=lambda x: hasattr(x, "shape")))
     return pl.pallas_call(
-        kernel,
+        functools.partial(staged, kernel, where, count),
         out_shape=outs,
-        in_specs=[VM] * len(args),
-        out_specs=jax.tree.map(lambda _: VM, outs),
+        in_specs=[pl.BlockSpec(memory_space=s) for s in spaces],
+        out_specs=VM if not isinstance(outs, tuple) else (VM,) * count,
+        scratch_shapes=[vmem(a.shape, a.dtype) for a, w in zip(args, where) if w]
+        + [pltpu.SemaphoreType.DMA((max(1, sum(where)),))],
         compiler_params=pltpu.CompilerParams(vmem_limit_bytes=limit),
-        cost_estimate=pl.CostEstimate(flops=flops, bytes_accessed=size, transcendentals=0),
-    )(*args)
+    )(*[pltpu.with_memory_space_constraint(a, s) for a, s in zip(args, spaces)])
 
 
 def iota(shape, dim):
@@ -76,6 +95,28 @@
     return fold(dot_nt(jnp.concatenate(parts, 0), onehot(lo, cols).astype(BF16)))
 
 
+def load_kernel(count, *refs):
+    sems = refs[-1]
+    copies = [pltpu.make_async_copy(refs[i], refs[count + i], sems.at[i]) for i in range(count)]
+    for copy in copies:
+        copy.start()
+    for copy in copies:
+        copy.wait()
+
+
+def load(*args):
+    count = len(args)
+    args = [pltpu.with_memory_space_constraint(a, pltpu.HBM) for a in args]
+    return pl.pallas_call(
+        functools.partial(load_kernel, count),
+        out_shape=tuple(vmem(a.shape, a.dtype) for a in args),
+        in_specs=[pl.BlockSpec(memory_space=pltpu.HBM)] * count,
+        out_specs=tuple(VM for _ in args),
+        scratch_shapes=[pltpu.SemaphoreType.DMA((count,))],
+        compiler_params=pltpu.CompilerParams(vmem_limit_bytes=1 << 20),
+    )(*args)
+
+
 def pres_kernel(rhs, wts, cell, front, prod, pres, send):
     depth, width, long = pres.shape
     for z in range(depth):
@@ -84,35 +125,45 @@
     table = pres[...].reshape(depth * width, long)
     value = prod[...] * pick(table, lax.div(where, long), lax.rem(where, long))
     both = jnp.concatenate([value, front[...].astype(F32)], 1)
-    send[...] = jnp.broadcast_to(both, send.shape)
-
-
-def front_kernel(recv, inverse, send):
+    send[...] = jnp.broadcast_to(both[:, None], send.shape)
+
+
+def front_kernel(recv, inverse, send, held, sems):
     devices = recv.shape[0]
-    count = recv.shape[1] // 2
+    count = recv.shape[2] // 2
     rows, length = inverse.shape
     lanes = 128
+    chunks = sems.shape[0]
+    wide = length // chunks
+    copies = [
+        pltpu.make_async_copy(inverse.at[:, pl.ds(i * wide, wide)], held.at[:, pl.ds(i * wide, wide)], sems.at[i])
+        for i in range(chunks)
+    ]
+    for copy in copies:
+        copy.start()
     total = jnp.zeros((length // lanes, lanes), F32)
     group = 8
     for first in range(0, devices, group):
         lefts, rights = ([], [])
         for d in range(first, first + group):
-            value = recv[d : d + 1, :count]
-            index = recv[d : d + 1, count:].astype(I32)
+            value = recv[d, :, :count]
+            index = recv[d, :, count:].astype(I32)
             hi, lo = lax.div(index, lanes), lax.rem(index, lanes)
             hit = iota((length // lanes, count), 0) == hi
             lefts.append(jnp.concatenate([jnp.where(hit, v.astype(F32), 0.0).astype(BF16) for v in split(value)], 0))
             rights.append(onehot(lo, lanes).astype(BF16))
         total = total + fold(dot_nt(jnp.concatenate(lefts, 1), jnp.concatenate(rights, 1)))
     acc = jnp.zeros((rows, lanes), F32)
-    for r in range(length // lanes):
-        acc = acc + inverse[:, r * lanes : (r + 1) * lanes] * total[r : r + 1]
+    for i in range(chunks):
+        copies[i].wait()
+        for r in range(i * wide // lanes, (i + 1) * wide // lanes):
+            acc = acc + held[:, r * lanes : (r + 1) * lanes] * total[r : r + 1]
     parts = jnp.concatenate(split(acc), 1)
     out = dot_nt(jnp.ones((8, parts.shape[1]), BF16), parts)
-    send[...] = jnp.broadcast_to(out[0:1], send.shape)
-
-
-def coef_kernel(last, tz, store, tz_prev, upper, inv, sides, ends):
+    send[...] = jnp.broadcast_to(out[0:1][:, None], send.shape)
+
+
+def coef_kernel(last, tz, store, tz_prev, upper, inv, sides, ends, face):
     depth = tz.shape[0]
     is_last = lax.axis_index("layer") == last
     low = tz_prev[0]
@@ -146,6 +197,7 @@
         sides[0, z] = a[z]
         sides[1, z] = b[z]
     ends[0], ends[1], ends[2], ends[3] = (a[0], a[-1], b[0], b[-1])
+    face[0] = jnp.where(is_right(0), a[0], b[-1])
 
 
 def is_right(level):
@@ -157,16 +209,19 @@
     return (jnp.where(right, other, mine), jnp.where(right, mine, other))
 
 
-def join_coef_kernel(level, own, sib, out):
+def join_coef_kernel(level, own, sib, out, face):
     af, af_ = choose(level, own[0], sib[0])
     al, al_ = choose(level, own[1], sib[1])
     bf, bf_ = choose(level, own[2], sib[2])
     bl, bl_ = choose(level, own[3], sib[3])
     den = 1.0 / (1.0 - bl * af_)
-    out[0] = af + bf * af_ * al * den
+    first = af + bf * af_ * al * den
+    last = bl_ + al_ * bl * bf_ * den
+    out[0] = first
     out[1] = al_ * al * den
     out[2] = bf * bf_ * den
-    out[3] = bl_ + al_ * bl * bf_ * den
+    out[3] = last
+    face[0] = jnp.where(is_right(level + 1), first, last)
 
 
 def local_solve(rhs, upper, inv, tz):
@@ -179,11 +234,11 @@
     return y
 
 
-def adjust_kernel(sol, cell, front, prod, pres, upper, inv, tz, y_out, ends):
+def adjust_kernel(sol, cell, front, prod, pres, upper, inv, tz, y_out, ends, face):
     depth, width, long = pres.shape
     where, index = (cell[...], front[...])
-    rows = sol.shape[1]
-    value = prod[...] * pick(sol[...], lax.div(index, rows), lax.rem(index, rows))
+    rows = sol.shape[2]
+    value = prod[...] * pick(sol[...].reshape(sol.shape[0], rows), lax.div(index, rows), lax.rem(index, rows))
     change = spread(value, lax.div(where, long), lax.rem(where, long), depth * width, long)
     change = change.reshape(depth, width, long)
     y = local_solve([pres[z] - change[z] for z in range(depth)], upper, inv, tz)
@@ -191,9 +246,10 @@
         y_out[z] = y[z]
     ends[0] = y[0]
     ends[1] = y[-1]
-
-
-def join_kernel(level, own, sib, ocoef, scoef, out):
+    face[0] = jnp.where(is_right(0), y[0], y[-1])
+
+
+def join_kernel(level, own, sib, ocoef, scoef, out, face):
     yf, yf_ = choose(level, own[0], sib[0])
     yl, yl_ = choose(level, own[1], sib[1])
     af, af_ = choose(level, ocoef[0], scoef[0])
@@ -201,8 +257,11 @@
     bf, bf_ = choose(level, ocoef[2], scoef[2])
     bl, bl_ = choose(level, ocoef[3], scoef[3])
     den = 1.0 / (1.0 - bl * af_)
-    out[0] = yf + bf * (yf_ + af_ * yl) * den
-    out[1] = yl_ + al_ * (yl + bl * yf_) * den
+    first = yf + bf * (yf_ + af_ * yl) * den
+    last = yl_ + al_ * (yl + bl * yf_) * den
+    out[0] = first
+    out[1] = last
+    face[0] = jnp.where(is_right(level + 1), first, last)
 
 
 def pressure_kernel(levels, *refs):
@@ -254,7 +313,7 @@
     return total
 
 
-def search_kernel(p, outer, before, after, rhs, dcol, binv, tx, tx_row, ty, tz, tz_prev, s, s_first, s_last, s_top, s_bottom):
+def search_kernel(p, outer, before, after, rhs, diag, binv, tx, tx_row, ty, tz, tz_prev, s, s_first, s_last, s_top, s_bottom):
     depth, width, _ = p.shape
     for z in range(depth):
         above = outer[0] if z == 0 else p[z - 1]
@@ -262,7 +321,7 @@
         tza = tz_prev[0] if z == 0 else tz[z - 1]
         centre = p[z]
         coupled = near(centre, above, below, before[z], after[z], tx[z], tx_row[z], ty[z], tz[z], tza)
-        remain = [rhs[c, z] - dcol[c, z] * centre for c in range(3)]
+        remain = [rhs[c, z] - diag[c, 0, z] * centre for c in range(3)]
         remain[0] = remain[0] + coupled
         for c in range(3):
             value = binv[c, 0, z] * remain[0] + binv[c, 1, z] * remain[1] + binv[c, 2, z] * remain[2]
@@ -277,16 +336,28 @@
                 s_bottom[c] = value
 
 
-def image_kernel(s, before, after, above_s, below_s, rhs, diag, tx, tx_row, ty, tz, tz_prev, image, send):
+def inner_kernel(s, before, after, diag, tx, tx_row, ty, tz, image):
     depth = s.shape[1]
+    zero = jnp.zeros(s.shape[2:], F32)
+    for z in range(depth):
+        tza = zero if z == 0 else tz[z - 1]
+        for c in range(3):
+            above = zero if z == 0 else s[c, z - 1]
+            below = zero if z == depth - 1 else s[c, z + 1]
+            coupled = near(s[c, z], above, below, before[c, z], after[c, z], tx[z], tx_row[z], ty[z], tz[z], tza)
+            image[c, z] = diag[c, 0, z] * s[0, z] + diag[c, 1, z] * s[1, z] + diag[c, 2, z] * s[2, z] - coupled
+
+
+def image_kernel(part, above_s, below_s, rhs, tz, tz_prev, image, send):
+    depth = part.shape[1]
     along = power = start = 0.0
     for z in range(depth):
-        tza = tz_prev[0] if z == 0 else tz[z - 1]
         for c in range(3):
-            above = above_s[c] if z == 0 else s[c, z - 1]
-            below = below_s[c] if z == depth - 1 else s[c, z + 1]
-            coupled = near(s[c, z], above, below, before[c, z], after[c, z], tx[z], tx_row[z], ty[z], tz[z], tza)
-            value = diag[c, 0, z] * s[0, z] + diag[c, 1, z] * s[1, z] + diag[c, 2, z] * s[2, z] - coupled
+            value = part[c, z]
+            if z == 0:
+                value = value - tz_prev[0] * above_s[c]
+            if z == depth - 1:
+                value = value - tz[z] * below_s[c]
             image[c, z] = value
             right = rhs[c, z]
             along = along + value * right
@@ -301,15 +372,15 @@
             left = rhs[c, z] - omega * value
             square = square + left * left
             cross = cross + left * value
-    lane = iota((1, send.shape[1]), 1)
-    out = jnp.zeros((1, send.shape[1]), F32)
+    lane = iota((1, send.shape[2]), 1)
+    out = jnp.zeros((1, send.shape[2]), F32)
     for i, value in enumerate((along, power, start, jnp.sum(square), jnp.sum(cross), omega)):
         out = jnp.where(lane == i, value, out)
-    send[...] = jnp.broadcast_to(out, send.shape)
+    send[...] = jnp.broadcast_to(out[:, None], send.shape)
 
 
 def finish_kernel(recv, s, image, rhs, update, lin_res, ratio):
-    sums = recv[...]
+    sums = recv[...].reshape(recv.shape[0], recv.shape[2])
     whole = jnp.sum(sums, axis=0, keepdims=True)
     omega = whole[:, 0:1] / whole[:, 1:2]
     shift = sums[:, 5:6] - omega
@@ -347,49 +418,71 @@
     rows = inverse.shape[0]
     cell, front, prod = (cell.reshape(1, -1), front.reshape(1, -1), prod.reshape(1, -1))
 
+    pres, send = call(
+        pres_kernel,
+        (vmem(tx.shape), vmem((devices, 1, 2 * count))),
+        (rhs, weights, cell, front, prod),
+        far=range(5),
+    )
+    send, tz, store, tx = lax.optimization_barrier((send, tz, store, tx))
     tz_prev = up(tz[-1:], "layer")
     tx_row = up(tx[:, -1:], "tile")
-    pres, send = call(
-        pres_kernel, (vmem(tx.shape), vmem((devices, 2 * count))), (rhs, weights, cell, front, prod)
-    )
     terms = everywhere(send)
+    terms, store, tz_prev = lax.optimization_barrier((terms, store, tz_prev))
 
     field = vmem(tx.shape)
-    upper, inv, sides, ends = call(
+    one, two, four = (vmem((k,) + plane) for k in (1, 2, 4))
+    upper, inv, sides, ends, face = call(
         functools.partial(coef_kernel, layers - 1),
-        (field, field, vmem((2,) + tx.shape), vmem((4,) + plane)),
+        (field, field, vmem((2,) + tx.shape), four, one),
         (tz, store, tz_prev),
+        far=(0, 1),
     )
     coefs = []
-    right = lambda level: (lax.axis_index("layer") >> level) % 2 == 1
     for level in range(levels):
         if level == levels - 1:
-            face = jnp.where(right(level), ends[0], ends[3])[None]
             coefs.append((ends, flip(face, level)))
         else:
             sib = flip(ends, level)
             coefs.append((ends, sib))
-            ends = call(functools.partial(join_coef_kernel, level), vmem((4,) + plane), (ends, sib))
-
-    rows_sol = call(front_kernel, vmem((devices, rows)), (terms, inverse))
-    sol = everywhere(rows_sol)
-
-    y, yends = call(
-        adjust_kernel, (field, vmem((2,) + plane)), (sol, cell, front, prod, pres, upper, inv, tz)
-    )
+            ends, face = call(functools.partial(join_coef_kernel, level), (four, one), (ends, sib))
+
+    chunks = 8
+    solved = pl.pallas_call(
+        front_kernel,
+        out_shape=vmem((devices, 1, rows)),
+        in_specs=[VM, pl.BlockSpec(memory_space=pltpu.HBM)],
+        out_specs=VM,
+        scratch_shapes=[vmem(inverse.shape), pltpu.SemaphoreType.DMA((chunks,))],
+        compiler_params=pltpu.CompilerParams(vmem_limit_bytes=LIMIT),
+    )(terms, pltpu.with_memory_space_constraint(inverse, pltpu.HBM))
+    solved, coefs = lax.optimization_barrier((solved, coefs))
+    sol = everywhere(solved)
+
+    y, yends, yface = call(
+        adjust_kernel,
+        (field, two, one),
+        (sol, cell, front, prod, pres, upper, inv, tz),
+        far=(1, 2, 3, 7),
+    )
+    tz_prev_v = tz_prev
+    diag, binv, rhs_v, tx_v, ty_v, tz_v = load(block_diag, block_inv, rhs, tx, ty, tz)
     args = []
     for level in range(levels):
         own, scoef = coefs[level]
         if level == levels - 1:
-            face = jnp.where(right(level), yends[0], yends[1])[None]
-            args += [yends, flip(face, level), own, scoef]
+            args += [yends, flip(yface, level), own, scoef]
         else:
             sib = flip(yends, level)
             args += [yends, sib, own, scoef]
-            yends = call(functools.partial(join_kernel, level), vmem((2,) + plane), (yends, sib, own, scoef))
+            yends, yface = call(
+                functools.partial(join_kernel, level), (two, one), (yends, sib, own, scoef)
+            )
     row3 = vmem((depth, 1, long))
     p, outer, p_first, p_last = call(
-        functools.partial(pressure_kernel, levels), (field, vmem((2,) + plane), row3, row3), (*args, y, sides)
+        functools.partial(pressure_kernel, levels),
+        (field, two, row3, row3),
+        (*args, y, sides),
     )
     before, after = (up(p_last, "tile"), down(p_first, "tile"))
     row9 = vmem((3, depth, 1, long))
@@ -397,18 +490,19 @@
     s, s_first, s_last, s_top, s_bottom = call(
         search_kernel,
         (vmem(rhs.shape), row9, row9, plane3, plane3),
-        (p, outer, before, after, rhs, block_diag[:, 0], block_inv, tx, tx_row, ty, tz, tz_prev),
+        (p, outer, before, after, rhs_v, diag, binv, tx_v, tx_row, ty_v, tz_v, tz_prev_v),
     )
     above, below = (up(s_bottom, "layer"), down(s_top, "layer"))
     before, after = (up(s_last, "tile"), down(s_first, "tile"))
+    part = call(inner_kernel, vmem(rhs.shape), (s, before, after, diag, tx_v, tx_row, ty_v, tz_v))
     image, send = call(
         image_kernel,
-        (vmem(rhs.shape), vmem((devices, 128))),
-        (s, before, after, above, below, rhs, block_diag, tx, tx_row, ty, tz, tz_prev),
+        (vmem(rhs.shape), vmem((devices, 1, 128))),
+        (part, above, below, rhs_v, tz_v, tz_prev_v),
     )
     sums = everywhere(send)
     update, lin_res, ratio = call(
-        finish_kernel, (hbm(rhs.shape), hbm(rhs.shape), hbm((1, 1))), (sums, s, image, rhs)
+        finish_kernel, (hbm(rhs.shape), hbm(rhs.shape), hbm((1, 1))), (sums, s, image, rhs_v)
     )
     return (update, lin_res, ratio.reshape(()))
 

time: 96.3 us -> 89.3 us (0.927)
  local copies, waits for them, and re-layouts: 13.7 us -> 1.87 us
  Pallas kernels: 8.68 us -> 20.5 us
  waiting for transfers between devices: 15.5 us -> 10.8 us
  starting transfers between devices: 23 us -> 18.4 us
  blocking collectives: 33.9 us -> 36.4 us
    unnamed x42 -> x0, local copies, waits for them, and re-layouts: 12.5 us -> none
    pallas_call x10 -> x12, Pallas kernels: 8.68 us -> 20.5 us  [the longest x10 12.3 us: call(): pl.pallas_call(functools.partial(staged, kernel, where, count), out_shape...]
    ppermute x4, starting transfers between devices: 5.83 us -> 1.42 us  [flip(): lax.ppermute(x, 'layer', [(i, i ^ 1 << level) for i in range(lax.axis_siz...]
    ppermute x3, waiting for transfers between devices: 8.86 us -> 4.99 us  [down(): lax.ppermute(x, axis, [(i + 1, i) for i in range(lax.axis_size(axis) - 1)])]
    all_to_all x3, blocking collectives: 33.9 us -> 36.4 us  [everywhere(): return lax.all_to_all(x, BOTH, split_axis=0, concat_axis=0, tiled=True)]
  transfers between devices with their start and end apart: 12 -> 12, of which waited for: 7 -> 7; matrix products, arithmetic and copies ran while one was open for 0% -> 1% of each run, Pallas kernels for 3% -> 11%
where the time goes in v2:
time: 89.3 us; the launch traced here: 88.8 us
  blocking collectives  36.4 us (41%)
  Pallas kernels  20.5 us (23%)
  starting transfers between devices  18.4 us (21%)
  waiting for transfers between devices  10.8 us (12%)
  local copies, waits for them, and re-layouts  1.87 us (2%)
    all_to_all x3, blocking collectives, everywhere(): return lax.all_to_all(x, BOTH, split_axis=0, concat_axis=0, tiled=True)  36.4 us
    ppermute x5, starting transfers between devices, up(): lax.ppermute(x, axis, [(i, i + 1) for i in range(lax.axis_size(axis) - 1)])  13.1 us
    pallas_call x10, Pallas kernels, call(): pl.pallas_call(functools.partial(staged, kernel, where, count), out_shape...  12.3 us
    ppermute x4, waiting for transfers between devices, flip(): lax.ppermute(x, 'layer', [(i, i ^ 1 << level) for i in range(lax.axis_siz...  5.19 us
    ppermute x3, waiting for transfers between devices, down(): lax.ppermute(x, axis, [(i + 1, i) for i in range(lax.axis_size(axis) - 1)])  4.99 us
    pallas_call x1, Pallas kernels, shards(): pl.pallas_call(front_kernel, out_shape=vmem((devices, 1, rows)), in_specs...  4.6 us
    ppermute x3, starting transfers between devices, down(): lax.ppermute(x, axis, [(i + 1, i) for i in range(lax.axis_size(axis) - 1)])  3.88 us
    pallas_call x1, Pallas kernels, load(): pl.pallas_call(functools.partial(load_kernel, count), out_shape=tuple((vm...  3.69 us
  transfers between devices with their start and end apart: 12, of which 7 were waited for; matrix products, arithmetic and copies ran while one was open for 1% of the time, Pallas kernels for 11%

profile of v2, /device:TPU:0, one launch (start us, length us, event | category | flops | bytes accessed | tf_op | source)
XLA Modules:
  0.0 88.8 jit_solution(18225583930233119613)
XLA Ops:
  0.6 2.2 %shard_map.139 = (f32[3,16,2048]{2,1,0:T(8,128)S(1)}, f32[32,1,512]{2,1,0:T(1,128)S(1)}) custom-call(f32[3,3,16,2048]{3,2,1,0:T(8,128)} %refs_2_.1, f32[3,3,16,2048]{3,2,1,0:T(8,128)} %refs_1_.2, s32[1,256]{1,0:T(1,128)} %bitcast.4, s32[1,256]{1,0:T(1,128)} %bitcast.6, f32[1,256]{1,0:T(1,128)} %bitcast.8), custom_call_target="tpu_custom_call" | custom-call | tf_op jit(solution)/shard_map/pallas_call | solution.py:46
  2.8 0.9 %slice.6 = f32[1,16,2048]{2,1,0:T(8,128)S(1)} slice(f32[3,16,2048]{2,1,0:T(8,128)} %refs_5_), slice={[2:3], [0:16], [0:2048]} | slice | bytes 262144 | tf_op jit(solution)/shard_map/slice | solution.py:428
  3.7 2.4 %collective-permute-start = (f32[1,16,2048]{2,1,0:T(8,128)S(1)}, f32[1,16,2048]{2,1,0:T(8,128)S(1)}, u32[]{:S(2)}, u32[]{:S(2)}) collective-permute-start(f32[1,16,2048]{2,1,0:T(8,128)S(1)} %slice.6), channel_id=1, source_target_pairs={{0,1},{1,2},{2,3},{4,5},{5,6},{6,7},{8,9},{9,10},{10,11},{12,13},{... | collective-permute-start | bytes 393224 | tf_op jit(solution)/shard_map/ppermute | solution.py:396
  6.1 14.3 %all_to_all.15.recv = f32[32,1,512]{2,1,0:T(1,128)S(1)} all-to-all(f32[32,1,512]{2,1,0:T(1,128)S(1)} %get-tuple-element.48), channel_id=1, replica_groups=mesh['tile'=8,'layer'=4] {'tile','layer'}, dimensions={0} | all-to-all | bytes 131072 | tf_op jit(solution)/shard_map/all_to_all | solution.py:408
  20.4 2.0 %shard_map.141 = (f32[3,16,2048]{2,1,0:T(8,128)S(1)}, f32[3,16,2048]{2,1,0:T(8,128)S(1)}, f32[2,3,16,2048]{3,2,1,0:T(8,128)S(1)}, f32[4,16,2048]{2,1,0:T(8,128)S(1)}, f32[1,16,2048]{2,1,0:T(8,128)}) custom-call(f32[3,16,2048]{2,1,0:T(8,128)} %refs_5_, f32[3,16,2048]{2,1,0:T(8,128)} %refs_1_.3, f32[1,16,2048]{2,1,0:T(8,128)S(1)} %collective-permute-done.refs_2_.refs_11_.refs_5_), custom_call_target="tpu_custom_call" | custom-call | tf_op jit(solution)/shard_map/pallas_call | solution.py:46
  22.6 1.8 %collective-permute-done.1.refs_1_.refs_3_ = f32[4,16,2048]{2,1,0:T(8,128)S(1)} collective-permute-done((f32[4,16,2048]{2,1,0:T(8,128)S(1)}, f32[4,16,2048]{2,1,0:T(8,128)S(1)}, u32[]{:S(2)}, u32[]{:S(2)}) %collective-permute-start.1) | collective-permute-done | bytes 524320 | tf_op jit(solution)/shard_map/ppermute | solution.py:404
  24.6 0.5 collective-permute-start.2
  25.1 4.6 %shard_map.140 = f32[32,1,256]{2,1,0:T(1,128)S(1)} custom-call(f32[32,1,512]{2,1,0:T(1,128)S(1)} %all_to_all.15.recv, f32[256,8192]{1,0:T(8,128)} %inverse.1), custom_call_target="tpu_custom_call" | custom-call | tf_op jit(solution)/shard_map/pallas_call | solution.py:451
  29.7 0.5 collective-permute-done.2.refs_7_
  30.2 8.9 %all_to_all.16.refs_0_ = f32[32,1,256]{2,1,0:T(1,128)S(1)} all-to-all(f32[32,1,256]{2,1,0:T(1,128)S(1)} %shard_map.140), channel_id=1, replica_groups=mesh['tile'=8,'layer'=4] {'tile','layer'}, dimensions={0} | all-to-all | bytes 65536 | tf_op jit(solution)/shard_map/all_to_all | solution.py:408
  39.1 2.5 %shard_map.143 = (f32[3,16,2048]{2,1,0:T(8,128)S(1)}, f32[2,16,2048]{2,1,0:T(8,128)S(1)}, f32[1,16,2048]{2,1,0:T(8,128)}) custom-call(f32[32,1,256]{2,1,0:T(1,128)S(1)} %all_to_all.16.refs_0_, s32[1,256]{1,0:T(1,128)} %bitcast.5, s32[1,256]{1,0:T(1,128)} %bitcast.7, f32[1,256]{1,0:T(1,128)} %bitcast.9, f32[3,16,2048]{2,1,0:T(8,128)S(1)} %get-tuple-element.58.refs_4_, ...), custom_call_target="tpu_custom_call" | custom-call | tf_op jit(solution)/shard_map/pallas_call | solution.py:46
  41.8 1.4 %collective-permute-done.3.refs_1_ = f32[2,16,2048]{2,1,0:T(8,128)S(1)} collective-permute-done((f32[2,16,2048]{2,1,0:T(8,128)S(1)}, f32[2,16,2048]{2,1,0:T(8,128)S(1)}, u32[]{:S(2)}, u32[]{:S(2)}) %collective-permute-start.3) | collective-permute-done | bytes 262176 | tf_op jit(solution)/shard_map/ppermute | solution.py:404
  43.4 0.6 collective-permute-start.4
  43.9 0.9 %slice.7 = f32[3,1,2048]{2,1,0:T(1,128)S(1)} slice(f32[3,16,2048]{2,1,0:T(8,128)} %refs_3_), slice={[0:3], [15:16], [0:2048]} | slice | bytes 49152 | tf_op jit(solution)/shard_map/slice | solution.py:429
  44.9 2.6 %collective-permute-start.7 = (f32[3,1,2048]{2,1,0:T(1,128)S(1)}, f32[3,1,2048]{2,1,0:T(1,128)S(1)}, u32[]{:S(2)}, u32[]{:S(2)}) collective-permute-start(f32[3,1,2048]{2,1,0:T(1,128)S(1)} %slice.7), channel_id=1, source_target_pairs={{0,4},{4,8},{8,12},{12,16},{16,20},{20,24},{24,28},{1,5},{5,9},{9,... | collective-permute-start | bytes 73736 | tf_op jit(solution)/shard_map/ppermute | solution.py:396
  47.5 1.5 %collective-permute-done.4.refs_5_ = f32[1,16,2048]{2,1,0:T(8,128)S(1)} collective-permute-done((f32[1,16,2048]{2,1,0:T(8,128)S(1)}, f32[1,16,2048]{2,1,0:T(8,128)S(1)}, u32[]{:S(2)}, u32[]{:S(2)}) %collective-permute-start.4) | collective-permute-done | bytes 131104 | tf_op jit(solution)/shard_map/ppermute | solution.py:404
  49.0 0.3 shard_map.145
  49.2 2.5 %collective-permute-start.5 = (f32[3,1,2048]{2,1,0:T(1,128)S(1)}, f32[3,1,2048]{2,1,0:T(1,128)S(1)}, u32[]{:S(2)}, u32[]{:S(2)}) collective-permute-start(f32[3,1,2048]{2,1,0:T(1,128)S(1)} %get-tuple-element.72), channel_id=1, source_target_pairs={{0,4},{4,8},{8,12},{12,16},{16,20},{20,24},{24,28},{1,5},{5,9},{9,... | collective-permute-start | bytes 73736 | tf_op jit(solution)/shard_map/ppermute | solution.py:396
  51.7 1.3 %collective-permute-start.6 = (f32[3,1,2048]{2,1,0:T(1,128)S(1)}, f32[3,1,2048]{2,1,0:T(1,128)S(1)}, u32[]{:S(2)}, u32[]{:S(2)}) collective-permute-start(f32[3,1,2048]{2,1,0:T(1,128)S(1)} %get-tuple-element.73), channel_id=1, source_target_pairs={{4,0},{8,4},{12,8},{16,12},{20,16},{24,20},{28,24},{5,1},{9,5},{13... | collective-permute-start | bytes 73736 | tf_op jit(solution)/shard_map/ppermute | solution.py:400
  53.0 3.7 %shard_map.146 = (f32[3,3,3,16,2048]{4,3,2,1,0:T(8,128)S(1)}, f32[3,3,3,16,2048]{4,3,2,1,0:T(8,128)S(1)}, f32[3,3,16,2048]{3,2,1,0:T(8,128)S(1)}, f32[3,16,2048]...) custom-call(f32[3,3,3,16,2048]{4,3,2,1,0:T(8,128)} %refs_0_.4, ...), custom_call_target="tpu_custom_call" | custom-call | tf_op jit(solution)/shard_map/pallas_call | solution.py:110
  56.7 0.7 collective-permute-done.6.refs_3_
  57.4 0.9 shard_map.147
  58.3 1.3 %collective-permute-start.10 = (f32[3,16,2048]{2,1,0:T(8,128)S(1)}, f32[3,16,2048]{2,1,0:T(8,128)S(1)}, u32[]{:S(2)}, u32[]{:S(2)}) collective-permute-start(f32[3,16,2048]{2,1,0:T(8,128)S(1)} %get-tuple-element.84), channel_id=1, source_target_pairs={{0,1},{1,2},{2,3},{4,5},{5,6},{6,7},{8,9},{9,10},{10,11},{12,13},{... | collective-permute-start | bytes 1179656 | tf_op jit(solution)/shard_map/ppermute | solution.py:396
  59.6 1.3 %collective-permute-start.11 = (f32[3,16,2048]{2,1,0:T(8,128)S(1)}, f32[3,16,2048]{2,1,0:T(8,128)S(1)}, u32[]{:S(2)}, u32[]{:S(2)}) collective-permute-start(f32[3,16,2048]{2,1,0:T(8,128)S(1)} %get-tuple-element.85), channel_id=1, source_target_pairs={{1,0},{2,1},{3,2},{5,4},{6,5},{7,6},{9,8},{10,9},{11,10},{13,12},{... | collective-permute-start | bytes 1179656 | tf_op jit(solution)/shard_map/ppermute | solution.py:400
  60.9 4.3 %collective-permute-start.8 = (f32[3,3,1,2048]{3,2,1,0:T(1,128)S(1)}, f32[3,3,1,2048]{3,2,1,0:T(1,128)S(1)}, u32[]{:S(2)}, u32[]{:S(2)}) collective-permute-start(f32[3,3,1,2048]{3,2,1,0:T(1,128)S(1)} %get-tuple-element.82), channel_id=1, source_target_pairs={{0,4},{4,8},{8,12},{12,16},{16,20},{20,24},{24,28},{1,5},{5,9},{9,... | collective-permute-start | bytes 221192 | tf_op jit(solution)/shard_map/ppermute | solution.py:396
  65.3 1.3 %collective-permute-start.9 = (f32[3,3,1,2048]{3,2,1,0:T(1,128)S(1)}, f32[3,3,1,2048]{3,2,1,0:T(1,128)S(1)}, u32[]{:S(2)}, u32[]{:S(2)}) collective-permute-start(f32[3,3,1,2048]{3,2,1,0:T(1,128)S(1)} %get-tuple-element.83), channel_id=1, source_target_pairs={{4,0},{8,4},{12,8},{16,12},{20,16},{24,20},{28,24},{5,1},{9,5},{13... | collective-permute-start | bytes 221192 | tf_op jit(solution)/shard_map/ppermute | solution.py:400
  66.6 0.7 collective-permute-done.8.refs_1_
  67.2 4.3 %collective-permute-done.9.refs_2_ = f32[3,3,1,2048]{3,2,1,0:T(1,128)S(1)} collective-permute-done((f32[3,3,1,2048]{3,2,1,0:T(1,128)S(1)}, f32[3,3,1,2048]{3,2,1,0:T(1,128)S(1)}, u32[]{:S(2)}, u32[]{:S(2)}) %collective-permute-start.9) | collective-permute-done | bytes 73760 | tf_op jit(solution)/shard_map/ppermute | solution.py:400
  71.5 1.5 %shard_map.148.refs_0_ = f32[3,3,16,2048]{3,2,1,0:T(8,128)S(1)} custom-call(f32[3,3,16,2048]{3,2,1,0:T(8,128)S(1)} %get-tuple-element.81.refs_0_.refs_1_, f32[3,3,1,2048]{3,2,1,0:T(1,128)S(1)} %collective-permute-done.8.refs_1_, f32[3,3,1,2048]{3,2,1,0:T(1,128)S(1)} %collective-permute-done.9.refs_2_, ...), custom_call_target="tpu_custom_call" | custom-call | tf_op jit(solution)/shard_map/pallas_call | solution.py:46
  73.0 1.0 %shard_map.149 = (f32[3,3,16,2048]{3,2,1,0:T(8,128)S(1)}, f32[32,1,128]{2,1,0:T(1,128)S(1)}) custom-call(f32[3,3,16,2048]{3,2,1,0:T(8,128)S(1)} %shard_map.148.refs_0_, f32[3,16,2048]{2,1,0:T(8,128)S(1)} %collective-permute-done.10.refs_1_, f32[3,16,2048]{2,1,0:T(8,128)S(1)} %collective-permute-done.11.refs_2_, ...), custom_call_target="tpu_custom_call" | custom-call | tf_op jit(solution)/shard_map/pallas_call | solution.py:46
  74.0 13.1 %all_to_all.17.refs_0_ = f32[32,1,128]{2,1,0:T(1,128)S(1)} all-to-all(f32[32,1,128]{2,1,0:T(1,128)S(1)} %get-tuple-element.86), channel_id=1, replica_groups=mesh['tile'=8,'layer'=4] {'tile','layer'}, dimensions={0} | all-to-all | bytes 32768 | tf_op jit(solution)/shard_map/all_to_all | solution.py:408
  87.1 1.7 %shard_map.150 = (f32[3,3,16,2048]{3,2,1,0:T(8,128)}, f32[3,3,16,2048]{3,2,1,0:T(8,128)}, f32[1,1]{1,0:T(1,128)}) custom-call(f32[32,1,128]{2,1,0:T(1,128)S(1)} %all_to_all.17.refs_0_, f32[3,3,16,2048]{3,2,1,0:T(8,128)S(1)} %get-tuple-element.81.refs_0_.refs_1_, f32[3,3,16,2048]{3,2,1,0:T(8,128)S(1)} %get-tuple-element.87.refs_2_, ...), custom_call_target="tpu_custom_call" | custom-call | tf_op jit(solution)/shard_map/pallas_call | solution.py:46
  (9 shorter events, 0.7 us)
Async XLA Ops:
  3.7 16.7 %collective-permute-start = (f32[1,16,2048]{2,1,0:T(8,128)S(1)}, f32[1,16,2048]{2,1,0:T(8,128)S(1)}, u32[]{:S(2)}, u32[]{:S(2)}) collective-permute-start(f32[1,16,2048]{2,1,0:T(8,128)S(1)} %slice.6), channel_id=1, source_target_pairs={{0,1},{1,2},{2,3},{4,5},{5,6},{6,7},{8,9},{9,10},{10,11},{12,13},{... | collective-permute-start | bytes 393224 | tf_op jit(solution)/shard_map/ppermute | solution.py:396
  22.4 2.0 %collective-permute-start.1 = (f32[4,16,2048]{2,1,0:T(8,128)S(1)}, f32[4,16,2048]{2,1,0:T(8,128)S(1)}, u32[]{:S(2)}, u32[]{:S(2)}) collective-permute-start(f32[4,16,2048]{2,1,0:T(8,128)S(1)} %get-tuple-element.62.refs_0_.refs_2_), channel_id=1, source_target_pairs={{0,1},{1,0},{2,3},{3,2},{4,5},{5,4},{6,7},{7,6},{8,9},{9,8},{10,11... | collective-permute-start | bytes 1572872 | tf_op jit(solution)/shard_map/ppermute | solution.py:404
  24.6 5.6 %collective-permute-start.2 = (f32[1,16,2048]{2,1,0:T(8,128)S(1)}, f32[1,16,2048]{2,1,0:T(8,128)S(1)}, u32[]{:S(2)}, u32[]{:S(2)}) collective-permute-start(f32[1,16,2048]{2,1,0:T(8,128)S(1)} %get-tuple-element.56), channel_id=1, source_target_pairs={{0,2},{1,3},{2,0},{3,1},{4,6},{5,7},{6,4},{7,5},{8,10},{9,11},{10,... | collective-permute-start | bytes 393224 | tf_op jit(solution)/shard_map/ppermute | solution.py:404
  41.6 1.6 %collective-permute-start.3 = (f32[2,16,2048]{2,1,0:T(8,128)S(1)}, f32[2,16,2048]{2,1,0:T(8,128)S(1)}, u32[]{:S(2)}, u32[]{:S(2)}) collective-permute-start(f32[2,16,2048]{2,1,0:T(8,128)S(1)} %get-tuple-element.61.refs_0_), channel_id=1, source_target_pairs={{0,1},{1,0},{2,3},{3,2},{4,5},{5,4},{6,7},{7,6},{8,9},{9,8},{10,11... | collective-permute-start | bytes 786440 | tf_op jit(solution)/shard_map/ppermute | solution.py:404
  43.4 5.6 %collective-permute-start.4 = (f32[1,16,2048]{2,1,0:T(8,128)S(1)}, f32[1,16,2048]{2,1,0:T(8,128)S(1)}, u32[]{:S(2)}, u32[]{:S(2)}) collective-permute-start(f32[1,16,2048]{2,1,0:T(8,128)S(1)} %get-tuple-element.65), channel_id=1, source_target_pairs={{0,2},{1,3},{2,0},{3,1},{4,6},{5,7},{6,4},{7,5},{8,10},{9,11},{10,... | collective-permute-start | bytes 393224 | tf_op jit(solution)/shard_map/ppermute | solution.py:404
  44.9 11.9 %collective-permute-start.7 = (f32[3,1,2048]{2,1,0:T(1,128)S(1)}, f32[3,1,2048]{2,1,0:T(1,128)S(1)}, u32[]{:S(2)}, u32[]{:S(2)}) collective-permute-start(f32[3,1,2048]{2,1,0:T(1,128)S(1)} %slice.7), channel_id=1, source_target_pairs={{0,4},{4,8},{8,12},{12,16},{16,20},{20,24},{24,28},{1,5},{5,9},{9,... | collective-permute-start | bytes 73736 | tf_op jit(solution)/shard_map/ppermute | solution.py:396
  49.2 7.5 %collective-permute-start.5 = (f32[3,1,2048]{2,1,0:T(1,128)S(1)}, f32[3,1,2048]{2,1,0:T(1,128)S(1)}, u32[]{:S(2)}, u32[]{:S(2)}) collective-permute-start(f32[3,1,2048]{2,1,0:T(1,128)S(1)} %get-tuple-element.72), channel_id=1, source_target_pairs={{0,4},{4,8},{8,12},{12,16},{16,20},{20,24},{24,28},{1,5},{5,9},{9,... | collective-permute-start | bytes 73736 | tf_op jit(solution)/shard_map/ppermute | solution.py:396
  51.7 5.7 %collective-permute-start.6 = (f32[3,1,2048]{2,1,0:T(1,128)S(1)}, f32[3,1,2048]{2,1,0:T(1,128)S(1)}, u32[]{:S(2)}, u32[]{:S(2)}) collective-permute-start(f32[3,1,2048]{2,1,0:T(1,128)S(1)} %get-tuple-element.73), channel_id=1, source_target_pairs={{4,0},{8,4},{12,8},{16,12},{20,16},{24,20},{28,24},{5,1},{9,5},{13... | collective-permute-start | bytes 73736 | tf_op jit(solution)/shard_map/ppermute | solution.py:400
  58.3 14.7 %collective-permute-start.10 = (f32[3,16,2048]{2,1,0:T(8,128)S(1)}, f32[3,16,2048]{2,1,0:T(8,128)S(1)}, u32[]{:S(2)}, u32[]{:S(2)}) collective-permute-start(f32[3,16,2048]{2,1,0:T(8,128)S(1)} %get-tuple-element.84), channel_id=1, source_target_pairs={{0,1},{1,2},{2,3},{4,5},{5,6},{6,7},{8,9},{9,10},{10,11},{12,13},{... | collective-permute-start | bytes 1179656 | tf_op jit(solution)/shard_map/ppermute | solution.py:396
  59.6 13.4 %collective-permute-start.11 = (f32[3,16,2048]{2,1,0:T(8,128)S(1)}, f32[3,16,2048]{2,1,0:T(8,128)S(1)}, u32[]{:S(2)}, u32[]{:S(2)}) collective-permute-start(f32[3,16,2048]{2,1,0:T(8,128)S(1)} %get-tuple-element.85), channel_id=1, source_target_pairs={{1,0},{2,1},{3,2},{5,4},{6,5},{7,6},{9,8},{10,9},{11,10},{13,12},{... | collective-permute-start | bytes 1179656 | tf_op jit(solution)/shard_map/ppermute | solution.py:400
  60.9 6.3 %collective-permute-start.8 = (f32[3,3,1,2048]{3,2,1,0:T(1,128)S(1)}, f32[3,3,1,2048]{3,2,1,0:T(1,128)S(1)}, u32[]{:S(2)}, u32[]{:S(2)}) collective-permute-start(f32[3,3,1,2048]{3,2,1,0:T(1,128)S(1)} %get-tuple-element.82), channel_id=1, source_target_pairs={{0,4},{4,8},{8,12},{12,16},{16,20},{20,24},{24,28},{1,5},{5,9},{9,... | collective-permute-start | bytes 221192 | tf_op jit(solution)/shard_map/ppermute | solution.py:396
  65.3 6.2 %collective-permute-start.9 = (f32[3,3,1,2048]{3,2,1,0:T(1,128)S(1)}, f32[3,3,1,2048]{3,2,1,0:T(1,128)S(1)}, u32[]{:S(2)}, u32[]{:S(2)}) collective-permute-start(f32[3,3,1,2048]{3,2,1,0:T(1,128)S(1)} %get-tuple-element.83), channel_id=1, source_target_pairs={{4,0},{8,4},{12,8},{16,12},{20,16},{24,20},{28,24},{5,1},{9,5},{13... | collective-permute-start | bytes 221192 | tf_op jit(solution)/shard_map/ppermute | solution.py:400

commit v3 on v2

v3 whole, which is shorter than its diff:
```python
import functools
import jax
import jax.numpy as jnp
from jax import lax
from jax.experimental import pallas as pl
from jax.experimental.pallas import tpu as pltpu
from jax.sharding import PartitionSpec as P

F32 = jnp.float32
BF16 = jnp.bfloat16
I32 = jnp.int32
BOTH = ("tile", "layer")
VM = pl.BlockSpec(memory_space=pltpu.VMEM)
LIMIT = 16 << 20


def hbm(shape):
    return jax.ShapeDtypeStruct(shape, F32)


def vmem(shape, dtype=F32):
    return pltpu.VMEM(shape, dtype)


def staged(kernel, where, outs, kept, *refs):
    count, sems = (len(where), refs[-1])
    held = list(refs[count + outs + len(kept) : -1])
    target = dict(zip(kept, refs[count + outs : count + outs + len(kept)]))
    operands, copies = ([], [])
    for i, far in enumerate(where):
        if far:
            to = target[i] if i in target else held.pop(0)
            copies.append(pltpu.make_async_copy(refs[i], to, sems.at[len(copies)]))
            operands.append(to)
        else:
            operands.append(refs[i])
    for copy in copies:
        copy.start()
    for copy in copies:
        copy.wait()
    kernel(*operands, *refs[count : count + outs])


def call(kernel, outs, args, far=(), keep=(), limit=LIMIT):
    where = [i in far for i in range(len(args))]
    spaces = [pltpu.HBM if w else pltpu.VMEM for w in where]
    every = (*outs, *(vmem(args[i].shape, args[i].dtype) for i in keep))
    return pl.pallas_call(
        functools.partial(staged, kernel, where, len(outs), tuple(keep)),
        out_shape=every,
        in_specs=[pl.BlockSpec(memory_space=s) for s in spaces],
        out_specs=(VM,) * len(every),
        scratch_shapes=[vmem(a.shape, a.dtype) for i, a in enumerate(args) if where[i] and i not in keep]
        + [pltpu.SemaphoreType.DMA((max(1, sum(where)),))],
        compiler_params=pltpu.CompilerParams(vmem_limit_bytes=limit),
    )(*[pltpu.with_memory_space_constraint(a, s) for a, s in zip(args, spaces)])


def iota(shape, dim):
    return lax.broadcasted_iota(I32, shape, dim)


def split(x):
    one = x.astype(BF16)
    rest = x - one.astype(F32)
    two = rest.astype(BF16)
    three = (rest - two.astype(F32)).astype(BF16)
    return [one, two, three]


def fold(x):
    n = x.shape[0] // 3
    return x[:n] + (x[n : 2 * n] + x[2 * n :])


def onehot(index, size):
    return jnp.where(iota((size, index.shape[1]), 0) == index, 1.0, 0.0)


def dot(a, b):
    return lax.dot_general(a, b, (((1,), (0,)), ((), ())), preferred_element_type=F32)


def dot_nt(a, b):
    return lax.dot_general(a, b, (((1,), (1,)), ((), ())), preferred_element_type=F32)


def pick(table, hi, lo):
    rows, cols = table.shape
    parts = jnp.concatenate(split(table), 0)
    got = fold(dot(parts, onehot(lo, cols).astype(BF16)))
    return jnp.sum(got * onehot(hi, rows), axis=0, keepdims=True)


def spread(value, hi, lo, rows, cols):
    parts = [jnp.where(iota((rows, hi.shape[1]), 0) == hi, v.astype(F32), 0.0).astype(BF16) for v in split(value)]
    return fold(dot_nt(jnp.concatenate(parts, 0), onehot(lo, cols).astype(BF16)))


def pres_kernel(rhs, wts, cell, front, prod, tz, pres, send, tz_last):
    depth, width, long = pres.shape
    for z in range(depth):
        pres[z] = wts[0, z] * rhs[0, z] + wts[1, z] * rhs[1, z] + wts[2, z] * rhs[2, z]
    where = cell[...]
    table = pres[...].reshape(depth * width, long)
    value = prod[...] * pick(table, lax.div(where, long), lax.rem(where, long))
    both = jnp.concatenate([value, front[...].astype(F32), where.astype(F32)], 1)
    send[...] = jnp.broadcast_to(both[:, None], send.shape)
    tz_last[0] = tz[depth - 1]


def edge_kernel(rhs, diag, binv, tz, store, tx, ty, pres, tz_prev, low, high):
    depth, width, long = pres.shape
    planes = [ref[z] for ref in (tz, store, pres, tx, ty) for z in range(depth)] + [tz_prev[0]]
    single = 2 * len(planes)
    low[...] = jnp.zeros(low.shape, F32)
    high[...] = jnp.zeros(high.shape, F32)
    for i, plane in enumerate(planes):
        low[2 * i : 2 * i + 2] = plane[0:2]
        high[2 * i : 2 * i + 2] = plane[width - 2 : width]
    for out, rows, at in ((low, slice(0, 8), 0), (high, slice(width - 8, width), 7)):
        for z in range(depth):
            right = [rhs[d, z, rows] for d in range(3)]
            column = [diag[d, 0, z, rows] for d in range(3)]
            for c in range(3):
                m = [binv[c, d, z, rows] for d in range(3)]
                first = m[0] * right[0] + m[1] * right[1] + m[2] * right[2]
                slope = (1.0 if c == 0 else 0.0) - (m[0] * column[0] + m[1] * column[1] + m[2] * column[2])
                for k, value in enumerate((first, slope, m[0])):
                    i = single + (k * 3 + c) * depth + z
                    out[i : i + 1] = value[at : at + 1]


def is_right(level):
    return (lax.axis_index("layer") >> level) % 2 == 1


def choose(level, mine, other):
    right = is_right(level)
    return (jnp.where(right, other, mine), jnp.where(right, mine, other))


def local_solve(rhs, upper, inv, tz):
    depth = len(rhs)
    y = [rhs[0] * inv[0]]
    for z in range(1, depth):
        y.append((rhs[z] + tz[z - 1] * y[-1]) * inv[z])
    for z in range(depth - 2, -1, -1):
        y[z] = y[z] + upper[z] * y[z + 1]
    return y


def coef_kernel(last, tz, store, tx, ty, pres, tz_prev, after, before, fields, halo, upper, inv, answers, sides, ends):
    depth, width, long = pres.shape
    pieces = [(ref, z) for ref in (tz, store, pres, tx, ty) for z in range(depth)] + [(tz_prev, 0)]
    for i, (ref, z) in enumerate(pieces):
        fields[i, :width] = ref[z]
        fields[i, width:] = jnp.zeros((8, long), F32)
        fields[i, width : width + 2] = after[2 * i : 2 * i + 2]
        fields[i, width + 6 :] = before[2 * i : 2 * i + 2]
    single = 2 * len(pieces)
    halo[...] = jnp.zeros(halo.shape, F32)
    for i in range(9 * depth):
        halo[i, 0:1] = after[single + i : single + i + 1]
        halo[i, 7:8] = before[single + i : single + i + 1]
    is_last = lax.axis_index("layer") == last
    tzs = [fields[z] for z in range(depth)]
    low = fields[5 * depth]
    gs, invs = ([], [])
    g, up_last = (None, None)
    above = low
    for z in range(depth):
        up = tzs[z]
        if z == depth - 1:
            up = jnp.where(is_last, 0.0, up)
            up_last = up
        kept = fields[depth + z]
        pivot = above + up + jnp.where(kept == 0.0, 1.0, kept)
        if z:
            pivot = pivot - above * g
        ipv = 1.0 / pivot
        g = up * ipv
        inv[z] = ipv
        upper[z] = g
        gs.append(g)
        invs.append(ipv)
        above = up
    first = [invs[0]]
    for z in range(1, depth):
        first.append(tzs[z - 1] * first[-1] * invs[z])
    final = [None] * depth
    final[-1] = invs[-1]
    for z in range(depth - 2, -1, -1):
        first[z] = first[z] + gs[z] * first[z + 1]
        final[z] = gs[z] * final[z + 1]
    for z in range(depth):
        answers[z] = first[z][:width]
        answers[depth + z] = final[z][:width]
        sides[z] = low * first[z]
        sides[depth + z] = up_last * final[z]
    y = local_solve([fields[2 * depth + z] for z in range(depth)], gs, invs, tzs)
    ends[0], ends[1] = (low * first[0], low * first[-1])
    ends[2], ends[3] = (up_last * final[0], up_last * final[-1])
    ends[4], ends[5] = (y[0], y[-1])


def pair(level, own, sib):
    af, af_ = choose(level, own[0], sib[0])
    al, al_ = choose(level, own[1], sib[1])
    bf, bf_ = choose(level, own[2], sib[2])
    bl, bl_ = choose(level, own[3], sib[3])
    return af, al, bf, bl, af_, al_, bf_, bl_, 1.0 / (1.0 - bl * af_)


def join_ends(level, own, sib, mine, other):
    _, _, bf, bl, af_, al_, _, _, den = pair(level, own, sib)
    yf, yf_ = choose(level, mine[0], other[0])
    yl, yl_ = choose(level, mine[1], other[1])
    return (yf + bf * (yf_ + af_ * yl) * den, yl_ + al_ * (yl + bl * yf_) * den)


def join_kernel(level, own, sib, answers, out, face, more, one):
    depth, width, _ = more.shape
    depth = depth // 2
    af, al, bf, bl, af_, al_, bf_, bl_, den = pair(level, own, sib)
    first = af + bf * af_ * al * den
    last = bl_ + al_ * bl * bf_ * den
    yf, yl = join_ends(level, own, sib, (own[4], own[5]), (sib[4], sib[5]))
    out[0], out[1], out[2], out[3] = (first, al_ * al * den, bf * bf_ * den, last)
    out[4], out[5] = (yf, yl)
    right, later = (is_right(level), is_right(level + 1))
    face[0], face[1] = (jnp.where(later, first, last), jnp.where(later, yf, yl))
    bfd, ald, af_, bl = ((bf * den)[:width], (al_ * den)[:width], af_[:width], bl[:width])
    for z in range(depth):
        kf, kl = (answers[z], answers[depth + z])
        top = jnp.where(right, bfd * kf, kf + bfd * af_ * kl)
        bottom = jnp.where(right, kl + ald * bl * kf, ald * kl)
        more[z] = top
        more[depth + z] = bottom
        one[z] = jnp.where(later, top, bottom)


def groups_of(lists, levels):
    tiles = lax.axis_size("tile")
    layers = lax.axis_size("layer")
    t, l = (lax.axis_index("tile"), lax.axis_index("layer"))
    out = []
    for level in range(-1, levels):
        members = [l] if level < 0 else [(((l >> level) ^ 1) << level) + i for i in range(1 << level)]
        group = []
        for member in members:
            for step in (-1, 0, 1):
                there = jnp.clip(t + step, 0, tiles - 1)
                group.append((there * layers + member, step, there == t + step))
        out.append(group)
    return out


def front_kernel(levels, shape, ext, recv, inverse, solved, rows_hot, lanes_hot, sol_hot, sol_row, layer, held, sems):
    devices = recv.shape[0]
    count = recv.shape[2] // 3
    rows, length = inverse.shape
    depth, width, long = shape
    lanes = 128
    chunks = sems.shape[0]
    wide = length // chunks
    copies = [
        pltpu.make_async_copy(inverse.at[:, pl.ds(i * wide, wide)], held.at[:, pl.ds(i * wide, wide)], sems.at[i])
        for i in range(chunks)
    ]
    for copy in copies:
        copy.start()
    total = jnp.zeros((length // lanes, lanes), F32)
    group = 8
    for first in range(0, devices, group):
        lefts, rights = ([], [])
        for d in range(first, first + group):
            value = recv[d, :, :count]
            index = recv[d, :, count : 2 * count].astype(I32)
            hi, lo = lax.div(index, lanes), lax.rem(index, lanes)
            hit = iota((length // lanes, count), 0) == hi
            lefts.append(jnp.concatenate([jnp.where(hit, v.astype(F32), 0.0).astype(BF16) for v in split(value)], 0))
            rights.append(onehot(lo, lanes).astype(BF16))
        total = total + fold(dot_nt(jnp.concatenate(lefts, 1), jnp.concatenate(rights, 1)))
    at = 0
    for members in groups_of(recv, levels):
        for device, step, valid in members:
            entry = recv[device]
            index = entry[:, count : 2 * count].astype(I32)
            cell = entry[:, 2 * count :].astype(I32)
            y, x = lax.rem(cell, long), lax.rem(lax.div(cell, long), width)
            if step == 1:
                x = jnp.where(x < 2, x + width, -1)
            if step == -1:
                x = jnp.where(x >= width - 2, x - width + ext, -1)
            row = jnp.where(jnp.logical_and(valid, x >= 0), lax.div(y, lanes) * ext + x, -1)
            here = pl.ds(at, count)
            rows_hot[:, here] = onehot(row, rows_hot.shape[0]).astype(BF16)
            lanes_hot[:, here] = onehot(lax.rem(y, lanes), lanes).astype(BF16)
            sol_hot[:, here] = onehot(lax.rem(index, rows), rows).astype(BF16)
            sol_row[:, here] = lax.div(index, rows)
            if at < layer.shape[1]:
                layer[:, here] = lax.div(cell, long * width)
            at += count
    acc = jnp.zeros((rows, lanes), F32)
    for i in range(chunks):
        copies[i].wait()
        for r in range(i * wide // lanes, (i + 1) * wide // lanes):
            acc = acc + held[:, r * lanes : (r + 1) * lanes] * total[r : r + 1]
    parts = jnp.concatenate(split(acc), 1)
    out = dot_nt(jnp.ones((8, parts.shape[1]), BF16), parts)
    solved[...] = out[0:1]


def list_kernel(solved, cell, prod, *refs):
    tables, send = (refs[:-1], refs[-1])
    where, value = (cell[...], prod[...])
    hi, lo = None, None
    depth, width, long = tables[-1].shape
    hi, lo = lax.div(where, long), lax.rem(where, long)
    stack = [t[k * depth : (k + 1) * depth].reshape(depth * width, long) for t in tables for k in range(t.shape[0] // depth)]
    parts = jnp.concatenate([p for table in stack for p in split(table)], 0)
    got = dot(parts, onehot(lo, long).astype(BF16))
    mask = onehot(hi, depth * width)
    n = 3 * depth * width
    found = [value * jnp.sum(fold(got[i * n : (i + 1) * n]) * mask, axis=0, keepdims=True) for i in range(len(stack))]
    send[...] = jnp.broadcast_to(jnp.concatenate([solved[...], value, *found], 1)[:, None], send.shape)


def gathered(values, rows_hot, lanes_hot, start, size, ext, parts):
    hot = lanes_hot[:, start : start + size]
    pieces = [hot * p for v in values for p in split(v)[:parts]]
    got = dot_nt(rows_hot[:, start : start + size], jnp.concatenate(pieces, 0))
    planes = []
    lanes = hot.shape[0]
    for i in range(len(values)):
        plane = got[:, i * parts * lanes : (i * parts + 1) * lanes]
        for k in range(1, parts):
            j = i * parts + k
            plane = plane + got[:, j * lanes : (j + 1) * lanes]
        planes.append(jnp.concatenate([plane[r : r + ext] for r in range(0, plane.shape[0], ext)], 1))
    return planes


def near(centre, above, below, tx, ty, tz, tza):
    high, long = centre.shape
    col = iota(centre.shape, 1)
    total = tz * below + tza * above
    total = total + tx * pltpu.roll(centre, high - 1, 0) + pltpu.roll(tx * centre, 1, 0)
    total = total + ty * jnp.where(col == long - 1, 0.0, pltpu.roll(centre, long - 1, 1))
    return total + jnp.where(col == 0, 0.0, pltpu.roll(ty * centre, 1, 1))


def search_kernel(levels, recv, rows_hot, lanes_hot, sol_hot, sol_row, layer, fields, halo, upper, inv, sides, rhs, diag, binv, *refs):
    own, sib = (refs[:levels], refs[levels : 2 * levels])
    s, inner, outer, p = refs[2 * levels :]
    depth, ext, long = (upper.shape[0], upper.shape[1], upper.shape[2])
    width = ext - 8
    rows, count = (sol_hot.shape[0], layer.shape[1] // 3)
    table = jnp.concatenate(split(recv[...].reshape(recv.shape[0], recv.shape[2])[:, :rows]), 0)
    sol = fold(dot(table, sol_hot[...]))
    sol = jnp.sum(jnp.where(iota(sol.shape, 0) == sol_row[...], sol, 0.0), axis=0, keepdims=True)
    groups = groups_of(recv, levels)

    def listed(group, column):
        at = rows + column * count
        return jnp.concatenate([recv[device][:, at : at + count] for device, _, _ in group], 1)

    start = layer.shape[1]
    value = listed(groups[0], 0) * sol[:, :start]
    which = layer[...]
    change = gathered([jnp.where(which == z, value, 0.0) for z in range(depth)], rows_hot, lanes_hot, 0, start, ext, 3)
    tzs = [fields[z] for z in range(depth)]
    y = local_solve([fields[2 * depth + z] - change[z] for z in range(depth)], upper, inv, tzs)
    mine = (y[0], y[-1])
    steps = []
    for level in range(levels):
        group = groups[level + 1]
        size = len(group) * count
        top = level == levels - 1
        columns = [1 + 2 * level] if top else [1 + 2 * level, 2 + 2 * level]
        values = [listed(group, c) * sol[:, start : start + size] for c in columns]
        change = gathered(values, rows_hot, lanes_hot, start, size, ext, 3)
        start += size
        if top:
            other = sib[level][1] - change[0]
            steps.append((mine, (other, other)))
        else:
            other = (sib[level][4] - change[0], sib[level][5] - change[1])
            steps.append((mine, other))
            mine = join_ends(level, own[level], sib[level], mine, other)
    zero = jnp.zeros((ext, long), F32)
    above, below = (zero, zero)
    for level in range(levels - 1, -1, -1):
        mine, other = steps[level]
        yl, _ = choose(level, mine[1], other[1])
        _, yf_ = choose(level, mine[0], other[0])
        if level == levels - 1:
            bl, _ = choose(level, own[level][3], sib[level][0])
            _, af_ = choose(level, own[level][0], sib[level][0])
            den = 1.0 / (1.0 - bl * af_)
            ml = (yl + bl * yf_) * den
            mr = (yf_ + af_ * yl) * den
        else:
            _, al, _, bl, af_, _, bf_, _, den = pair(level, own[level], sib[level])
            one = yl + al * above
            two = yf_ + bf_ * below
            ml = (one + bl * two) * den
            mr = (two + af_ * one) * den
        right = is_right(level)
        above, below = (jnp.where(right, ml, above), jnp.where(right, below, mr))
    for z in range(depth):
        p[z] = y[z] + sides[z] * above + sides[depth + z] * below
    odd = is_right(0)
    for z in range(depth):
        up = above if z == 0 else p[z - 1]
        down = below if z == depth - 1 else p[z + 1]
        tza = fields[5 * depth] if z == 0 else fields[z - 1]
        centre = p[z]
        coupled = near(centre, up, down, fields[3 * depth + z], fields[4 * depth + z], fields[z], tza)
        c16, n16, c8, n8 = (centre[:width], coupled[:width], centre[width:], coupled[width:])
        remain = [rhs[c, z] - diag[c, 0, z] * c16 for c in range(3)]
        remain[0] = remain[0] + n16
        for c in range(3):
            value = binv[c, 0, z] * remain[0] + binv[c, 1, z] * remain[1] + binv[c, 2, z] * remain[2]
            if c == 0:
                value = c16 + value
            s[c, z, :width] = value
            i = c * depth + z
            s[c, z, width:] = halo[i] + halo[3 * depth + i] * c8 + halo[6 * depth + i] * n8
    for c in range(3):
        top, bottom = (s[c, 0, :width], s[c, depth - 1, :width])
        inner[c] = jnp.where(odd, top, bottom)
        outer[c] = jnp.where(odd, bottom, top)


def inner_kernel(s, diag, fields, image):
    depth, ext, long = s.shape[1:]
    width = ext - 8
    zero = jnp.zeros((ext, long), F32)
    for z in range(depth):
        tza = zero if z == 0 else fields[z - 1]
        for c in range(3):
            above = zero if z == 0 else s[c, z - 1]
            below = zero if z == depth - 1 else s[c, z + 1]
            coupled = near(s[c, z], above, below, fields[3 * depth + z], fields[4 * depth + z], fields[z], tza)
            total = diag[c, 0, z] * s[0, z, :width] + diag[c, 1, z] * s[1, z, :width] + diag[c, 2, z] * s[2, z, :width]
            image[c, z] = total - coupled[:width]


def image_kernel(part, inner, outer, rhs, fields, image, send):
    depth, width = part.shape[1:3]
    odd = is_right(0)
    along = power = start = 0.0
    for z in range(depth):
        for c in range(3):
            value = part[c, z]
            if z == 0:
                value = value - fields[5 * depth, :width] * jnp.where(odd, inner[c], outer[c])
            if z == depth - 1:
                value = value - fields[z, :width] * jnp.where(odd, outer[c], inner[c])
            image[c, z] = value
            right = rhs[c, z]
            along = along + value * right
            power = power + value * value
            start = start + right * right
    along, power, start = (jnp.sum(along), jnp.sum(power), jnp.sum(start))
    omega = along / jnp.where(power > 0.0, power, 1.0)
    square = cross = 0.0
    for z in range(depth):
        for c in range(3):
            value = image[c, z]
            left = rhs[c, z] - omega * value
            square = square + left * left
            cross = cross + left * value
    lane = iota((1, send.shape[2]), 1)
    out = jnp.zeros((1, send.shape[2]), F32)
    for i, value in enumerate((along, power, start, jnp.sum(square), jnp.sum(cross), omega)):
        out = jnp.where(lane == i, value, out)
    send[...] = jnp.broadcast_to(out[:, None], send.shape)


def finish_kernel(recv, s, image, rhs, update, lin_res, ratio):
    sums = recv[...].reshape(recv.shape[0], recv.shape[2])
    whole = jnp.sum(sums, axis=0, keepdims=True)
    omega = whole[:, 0:1] / whole[:, 1:2]
    shift = sums[:, 5:6] - omega
    square = sums[:, 3:4] + 2.0 * shift * sums[:, 4:5] + shift * shift * sums[:, 1:2]
    ratio[...] = jnp.sqrt(jnp.sum(square, axis=0, keepdims=True) / whole[:, 2:3])
    for c in range(3):
        for z in range(s.shape[1]):
            update[c, z] = omega * s[c, z, : rhs.shape[2]]
            lin_res[c, z] = rhs[c, z] - omega * image[c, z]


def up(x, axis):
    return lax.ppermute(x, axis, [(i, i + 1) for i in range(lax.axis_size(axis) - 1)])


def down(x, axis):
    return lax.ppermute(x, axis, [(i + 1, i) for i in range(lax.axis_size(axis) - 1)])


def flip(x, level):
    return lax.ppermute(x, "layer", [(i, i ^ (1 << level)) for i in range(lax.axis_size("layer"))])


def neighbour(x):
    size = lax.axis_size("layer")
    pairs = [(i, i + 1) for i in range(1, size - 1, 2)]
    return lax.ppermute(x, "layer", pairs + [(j, i) for i, j in pairs])


def everywhere(x):
    return lax.all_to_all(x, BOTH, split_axis=0, concat_axis=0, tiled=True)


def shards(rhs, weights, block_diag, block_inv, tx, ty, tz, store, cell, front, prod, inverse):
    layers = lax.axis_size("layer")
    devices = lax.axis_size("tile") * layers
    levels = layers.bit_length() - 1
    depth, width, long = tx.shape
    ext = width + 8
    count = cell.shape[0]
    rows = inverse.shape[0]
    lists = 3 * layers * count
    cell, front, prod = (cell.reshape(1, -1), front.reshape(1, -1), prod.reshape(1, -1))
    field = vmem(tx.shape)

    def planes(n, high=ext):
        return vmem((n, high, long))

    pres, send, tz_last = call(
        pres_kernel,
        (field, vmem((devices, 1, 3 * count)), vmem((1, width, long))),
        (rhs, weights, cell, front, prod, tz),
        far=range(6),
    )
    tz_prev = up(tz_last, "layer")
    terms = everywhere(send)
    terms, tz_prev, rhs, block_diag = lax.optimization_barrier((terms, tz_prev, rhs, block_diag))

    edge = vmem((8 * (-(-(10 * depth + 2 + 9 * depth) // 8)), long))
    low, high, rhs, diag, binv, tz, store, tx, ty = call(
        edge_kernel,
        (edge, edge),
        (rhs, block_diag, block_inv, tz, store, tx, ty, pres, tz_prev),
        far=range(7),
        keep=range(7),
    )
    after, before = (down(low, "tile"), up(high, "tile"))
    six = planes(6)
    fields, halo, upper, inv, answers, sides, ends = call(
        functools.partial(coef_kernel, layers - 1),
        (planes(5 * depth + 1), planes(9 * depth, 8), planes(depth), planes(depth), planes(2 * depth, width), planes(2 * depth), six),
        (tz, store, tx, ty, pres, tz_prev, after, before),
    )
    chunks = 8
    solved, rows_hot, lanes_hot, sol_hot, sol_row, layer = pl.pallas_call(
        functools.partial(front_kernel, levels, (depth, width, long), ext),
        out_shape=(
            vmem((1, rows)),
            vmem((ext * long // 128, lists), BF16),
            vmem((128, lists), BF16),
            vmem((rows, lists), BF16),
            vmem((1, lists), I32),
            vmem((1, 3 * count), I32),
        ),
        in_specs=[VM, pl.BlockSpec(memory_space=pltpu.HBM)],
        out_specs=(VM,) * 6,
        scratch_shapes=[vmem(inverse.shape), pltpu.SemaphoreType.DMA((chunks,))],
        compiler_params=pltpu.CompilerParams(vmem_limit_bytes=LIMIT),
    )(terms, pltpu.with_memory_space_constraint(inverse, pltpu.HBM))
    own, sib, tables = ([ends], [], [])
    face, last = (None, answers)
    for level in range(levels - 1):
        tables.append(answers)
        sib.append(flip(ends, level))
        ends, face, answers, last = call(
            functools.partial(join_kernel, level),
            (six, planes(2), planes(2 * depth, width), planes(depth, width)),
            (ends, sib[-1], answers),
        )
        own.append(ends)
    tables.append(last)
    sib.append(flip(face, levels - 1))
    (send,) = call(
        list_kernel,
        (vmem((devices, 1, rows + 2 * levels * count)),),
        (solved, cell, prod, *tables),
        far=(1, 2),
    )
    send, sib = lax.optimization_barrier((send, sib))
    sol = everywhere(send)
    plane3 = vmem((3, width, long))
    s, inner, outer, _ = call(
        functools.partial(search_kernel, levels),
        (vmem((3, depth, ext, long)), plane3, plane3, planes(depth)),
        (sol, rows_hot, lanes_hot, sol_hot, sol_row, layer, fields, halo, upper, inv, sides, rhs, diag, binv, *own, *sib),
    )
    inner, outer = (flip(inner, 0), neighbour(outer))
    (part,) = call(inner_kernel, (vmem(rhs.shape),), (s, diag, fields))
    image, send = call(
        image_kernel,
        (vmem(rhs.shape), vmem((devices, 1, 128))),
        (part, inner, outer, rhs, fields),
    )
    sums = everywhere(send)
    update, lin_res, ratio = call(
        finish_kernel, (hbm(rhs.shape), hbm(rhs.shape), hbm((1, 1))), (sums, s, image, rhs)
    )
    return (update, lin_res, ratio.reshape(()))


def solution(mesh):
    return jax.shard_map(
        shards,
        mesh=mesh,
        in_specs=(
            P(None, "layer", "tile", None),
            P(None, "layer", "tile", None),
            P(None, None, "layer", "tile", None),
            P(None, None, "layer", "tile", None),
            P("layer", "tile", None),
            P("layer", "tile", None),
            P("layer", "tile", None),
            P("layer", "tile", None),
            P(("tile", "layer")),
            P(("tile", "layer")),
            P(("tile", "layer")),
            P(("tile", "layer"), None),
        ),
        out_specs=(P(None, "layer", "tile", None), P(None, "layer", "tile", None), P()),
        check_vma=False,
    )
```

time: 89.3 us -> 104 us (1.16)
  waiting for transfers between devices: 10.8 us -> 31 us
  blocking collectives: 36.4 us -> 27.8 us
  Pallas kernels: 20.5 us -> 26.8 us
  local copies, waits for them, and re-layouts: 1.87 us -> 0 us
  starting transfers between devices: 18.4 us -> 17.3 us
    ppermute x5 -> x2, waiting for transfers between devices: 0.67 us -> 11.1 us  [up(): lax.ppermute(x, axis, [(i, i + 1) for i in range(lax.axis_size(axis) - 1)])]
    all_to_all x3 -> x2, blocking collectives: 36.4 us -> 27.8 us  [everywhere(): return lax.all_to_all(x, BOTH, split_axis=0, concat_axis=0, tiled=True)]
    all_to_all x0 -> x1, starting transfers between devices: none -> 7.3 us  [everywhere(): return lax.all_to_all(x, BOTH, split_axis=0, concat_axis=0, tiled=True)]
    ppermute x5 -> x2, starting transfers between devices: 13.1 us -> 6.74 us  [up(): lax.ppermute(x, axis, [(i, i + 1) for i in range(lax.axis_size(axis) - 1)])]
    pallas_call x12 -> x10, Pallas kernels: 20.5 us -> 26.8 us  [the longest x9 20.1 us: call(): pl.pallas_call(functools.partial(staged, kernel, where, len(outs), tuple(...]
    ppermute x3 -> x1, waiting for transfers between devices: 4.99 us -> 9.95 us  [down(): lax.ppermute(x, axis, [(i + 1, i) for i in range(lax.axis_size(axis) - 1)])]
    all_to_all x0 -> x1, waiting for transfers between devices: none -> 4.68 us  [everywhere(): return lax.all_to_all(x, BOTH, split_axis=0, concat_axis=0, tiled=True)]
    ppermute x3 -> x1, starting transfers between devices: 3.88 us -> 1.29 us  [down(): lax.ppermute(x, axis, [(i + 1, i) for i in range(lax.axis_size(axis) - 1)])]
  transfers between devices with their start and end apart: 12 -> 8, of which waited for: 7 -> 6; matrix products, arithmetic and copies ran while one was open for 1% -> 0% of each run, Pallas kernels for 11% -> 9%
where the time goes in v3:
time: 104 us
  waiting for transfers between devices  31 us (30%)
  blocking collectives  27.8 us (27%)
  Pallas kernels  26.8 us (26%)
  starting transfers between devices  17.3 us (17%)
    all_to_all x2, blocking collectives, everywhere(): return lax.all_to_all(x, BOTH, split_axis=0, concat_axis=0, tiled=True)  27.8 us
    pallas_call x9, Pallas kernels, call(): pl.pallas_call(functools.partial(staged, kernel, where, len(outs), tuple(...  20.1 us
    ppermute x2, waiting for transfers between devices, up(): lax.ppermute(x, axis, [(i, i + 1) for i in range(lax.axis_size(axis) - 1)])  11.1 us
    ppermute x1, waiting for transfers between devices, down(): lax.ppermute(x, axis, [(i + 1, i) for i in range(lax.axis_size(axis) - 1)])  9.95 us
    all_to_all x1, starting transfers between devices, everywhere(): return lax.all_to_all(x, BOTH, split_axis=0, concat_axis=0, tiled=True)  7.3 us
    ppermute x2, starting transfers between devices, up(): lax.ppermute(x, axis, [(i, i + 1) for i in range(lax.axis_size(axis) - 1)])  6.74 us
    pallas_call x1, Pallas kernels, shards(): pl.pallas_call(functools.partial(front_kernel, levels, (depth, width, lon...  6.64 us
    ppermute x3, waiting for transfers between devices, flip(): lax.ppermute(x, 'layer', [(i, i ^ 1 << level) for i in range(lax.axis_siz...  5.27 us
  transfers between devices with their start and end apart: 8, of which 6 were waited for; matrix products, arithmetic and copies ran while one was open for 0% of the time, Pallas kernels for 9%

profile of v3, /device:TPU:0, one launch (start us, length us, event | category | flops | bytes accessed | tf_op | source)
XLA Modules:
  0.0 103.8 jit_solution(16159881727900814927)
XLA Ops:
  0.6 2.9 %shard_map.139 = (f32[3,16,2048]{2,1,0:T(8,128)S(1)}, f32[32,1,768]{2,1,0:T(1,128)}, f32[1,16,2048]{2,1,0:T(8,128)S(1)}) custom-call(f32[3,3,16,2048]{3,2,1,0:T(8,128)} %refs_0_.2, f32[3,3,16,2048]{3,2,1,0:T(8,128)} %refs_1_.1, s32[1,256]{1,0:T(1,128)} %bitcast.4, s32[1,256]{1,0:T(1,128)} %bitcast.8, f32[1,256]{1,0:T(1,128)} %bitcast.6, f32[3,16,2048]{2,1,0:T(8,128)} %refs_3_.1), custom_call_target="tpu_custom_call" | custom-call | tf_op jit(solution)/shard_map/pallas_call | solution.py:48
  3.6 7.3 %all-to-all-start = ((f32[32,1,768]{2,1,0:T(1,128)}), f32[32,1,768]{2,1,0:T(1,128)S(1)}, u32[]{:S(2)}, u32[]{:S(2)}) async-start(f32[32,1,768]{2,1,0:T(1,128)} %get-tuple-element.46), calls=%async_computation | async-start | bytes 196608 | tf_op jit(solution)/shard_map/all_to_all | solution.py:515
  10.9 2.2 %collective-permute-start = (f32[1,16,2048]{2,1,0:T(8,128)S(1)}, f32[1,16,2048]{2,1,0:T(8,128)S(1)}, u32[]{:S(2)}, u32[]{:S(2)}) collective-permute-start(f32[1,16,2048]{2,1,0:T(8,128)S(1)} %get-tuple-element.47), channel_id=1, source_target_pairs={{0,1},{1,2},{2,3},{4,5},{5,6},{6,7},{8,9},{9,10},{10,11},{12,13},{... | collective-permute-start | bytes 393224 | tf_op jit(solution)/shard_map/ppermute | solution.py:497
  13.1 1.0 collective-permute-done.refs_8_.refs_5_
  14.0 4.7 %all-to-all-done.recv = f32[32,1,768]{2,1,0:T(1,128)S(1)} async-done(((f32[32,1,768]{2,1,0:T(1,128)}), f32[32,1,768]{2,1,0:T(1,128)S(1)}, u32[]{:S(2)}, u32[]{:S(2)}) %all-to-all-start) | async-done | bytes 98336 | tf_op jit(solution)/shard_map/all_to_all | solution.py:515
  18.7 4.7 %shard_map.141 = (f32[64,2048]{1,0:T(8,128)S(1)}, f32[64,2048]{1,0:T(8,128)S(1)}, f32[3,3,16,2048]{3,2,1,0:T(8,128)S(1)}, f32[3,3,3,16,2048]{4,3,2,1,0:T(8,128)S...) custom-call(f32[3,3,16,2048]{3,2,1,0:T(8,128)} %refs_0_.2, ...), custom_call_target="tpu_custom_call" | custom-call | tf_op jit(solution)/shard_map/pallas_call | solution.py:48
  23.4 1.3 %collective-permute-start.1 = (f32[64,2048]{1,0:T(8,128)S(1)}, f32[64,2048]{1,0:T(8,128)S(1)}, u32[]{:S(2)}, u32[]{:S(2)}) collective-permute-start(f32[64,2048]{1,0:T(8,128)S(1)} %get-tuple-element.58), channel_id=1, source_target_pairs={{4,0},{8,4},{12,8},{16,12},{20,16},{24,20},{28,24},{5,1},{9,5},{13... | collective-permute-start | bytes 1572872 | tf_op jit(solution)/shard_map/ppermute | solution.py:501
  24.7 4.6 %collective-permute-start.2 = (f32[64,2048]{1,0:T(8,128)S(1)}, f32[64,2048]{1,0:T(8,128)S(1)}, u32[]{:S(2)}, u32[]{:S(2)}) collective-permute-start(f32[64,2048]{1,0:T(8,128)S(1)} %get-tuple-element.59), channel_id=1, source_target_pairs={{0,4},{4,8},{8,12},{12,16},{16,20},{20,24},{24,28},{1,5},{5,9},{9,... | collective-permute-start | bytes 1572872 | tf_op jit(solution)/shard_map/ppermute | solution.py:497
  29.3 10.0 %collective-permute-done.1.refs_6_ = f32[64,2048]{1,0:T(8,128)S(1)} collective-permute-done((f32[64,2048]{1,0:T(8,128)S(1)}, f32[64,2048]{1,0:T(8,128)S(1)}, u32[]{:S(2)}, u32[]{:S(2)}) %collective-permute-start.1) | collective-permute-done | bytes 524320 | tf_op jit(solution)/shard_map/ppermute | solution.py:501
  39.3 10.1 %collective-permute-done.2.refs_7_ = f32[64,2048]{1,0:T(8,128)S(1)} collective-permute-done((f32[64,2048]{1,0:T(8,128)S(1)}, f32[64,2048]{1,0:T(8,128)S(1)}, u32[]{:S(2)}, u32[]{:S(2)}) %collective-permute-start.2) | collective-permute-done | bytes 524320 | tf_op jit(solution)/shard_map/ppermute | solution.py:497
  49.4 1.3 %shard_map.142 = (f32[16,24,2048]{2,1,0:T(8,128)S(1)}, f32[27,8,2048]{2,1,0:T(8,128)S(1)}, f32[3,24,2048]{2,1,0:T(8,128)S(1)}, f32[3,24,2048]{2,1,0:T(8,128)S(1)...) custom-call(f32[3,16,2048]{2,1,0:T(8,128)S(1)} %get-tuple-element.54.refs_0_, ...), custom_call_target="tpu_custom_call" | custom-call | tf_op jit(solution)/shard_map/pallas_call | solution.py:48
  50.7 0.1 collective-permute-start.3
  50.8 2.8 %collective-permute-done.3.refs_1_.refs_16_ = f32[6,24,2048]{2,1,0:T(8,128)S(1)} collective-permute-done((f32[6,24,2048]{2,1,0:T(8,128)S(1)}, f32[6,24,2048]{2,1,0:T(8,128)S(1)}, u32[]{:S(2)}, u32[]{:S(2)}) %collective-permute-start.3) | collective-permute-done | bytes 1179680 | tf_op jit(solution)/shard_map/ppermute | solution.py:505
  53.6 1.2 %shard_map.143 = (f32[6,24,2048]{2,1,0:T(8,128)S(1)}, f32[2,24,2048]{2,1,0:T(8,128)S(1)}, f32[6,16,2048]{2,1,0:T(8,128)}, f32[3,16,2048]{2,1,0:T(8,128)S(1)}) custom-call(f32[6,24,2048]{2,1,0:T(8,128)S(1)} %get-tuple-element.61.refs_0_.refs_14_, f32[6,24,2048]{2,1,0:T(8,128)S(1)} %collective-permute-done.3.refs_1_.refs_16_, ...), custom_call_target="tpu_custom_call" | custom-call | tf_op jit(solution)/shard_map/pallas_call | solution.py:48
  54.8 0.7 collective-permute-start.4
  55.6 6.6 %shard_map.140 = (f32[1,256]{1,0:T(1,128)S(1)}, bf16[384,3072]{1,0:T(8,128)(2,1)S(1)}, bf16[128,3072]{1,0:T(8,128)(2,1)S(1)}, bf16[256,3072]{1,0:T(8,128)(2,1)S(...) custom-call(f32[32,1,768]{2,1,0:T(1,128)S(1)} %all-to-all-done.recv, f32[256,8192]{1,0:T(8,128)} %inverse.1), custom_call_target="tpu_custom_call" | custom-call | tf_op jit(solution)/shard_map/pallas_call | solution.py:559
  62.2 1.4 %shard_map.144 = f32[32,1,1280]{2,1,0:T(1,128)S(1)} custom-call(f32[1,256]{1,0:T(1,128)S(1)} %get-tuple-element.49.refs_0_, s32[1,256]{1,0:T(1,128)} %bitcast.5, f32[1,256]{1,0:T(1,128)} %bitcast.7, f32[6,16,2048]{2,1,0:T(8,128)S(1)} %get-tuple-element.60.refs_2_.refs_3_, f32[3,16,2048]{2,1,0:T(8,128)S(1)} %get-tuple-element.62.refs_4_), custom_call_target="tpu_custom_call" | custom-call | tf_op jit(solution)/shard_map/pallas_call | solution.py:48
  63.6 2.4 %collective-permute-done.4.refs_17_ = f32[2,24,2048]{2,1,0:T(8,128)S(1)} collective-permute-done((f32[2,24,2048]{2,1,0:T(8,128)S(1)}, f32[2,24,2048]{2,1,0:T(8,128)S(1)}, u32[]{:S(2)}, u32[]{:S(2)}) %collective-permute-start.4) | collective-permute-done | bytes 393248 | tf_op jit(solution)/shard_map/ppermute | solution.py:505
  66.1 11.8 %all_to_all.15.refs_0_ = f32[32,1,1280]{2,1,0:T(1,128)S(1)} all-to-all(f32[32,1,1280]{2,1,0:T(1,128)S(1)} %shard_map.144), channel_id=1, replica_groups=mesh['tile'=8,'layer'=4] {'tile','layer'}, dimensions={0} | all-to-all | bytes 327680 | tf_op jit(solution)/shard_map/all_to_all | solution.py:515
  77.9 4.5 %shard_map.145 = (f32[3,3,24,2048]{3,2,1,0:T(8,128)S(1)}, f32[3,16,2048]{2,1,0:T(8,128)S(1)}, f32[3,16,2048]{2,1,0:T(8,128)S(1)}, f32[3,24,2048]{2,1,0:T(8,128)}) custom-call(f32[32,1,1280]{2,1,0:T(1,128)S(1)} %all_to_all.15.refs_0_, bf16[384,3072]{1,0:T(8,128)(2,1)S(1)} %get-tuple-element.65.refs_1_, bf16[128,3072]{1,0:T(8,128)(2,1)S(1)} %get-tuple-element.66.refs_2_, ...), custom_call_target="tpu_custom_call" | custom-call | tf_op jit(solution)/shard_map/pallas_call | solution.py:48
  82.4 0.5 collective-permute-start.5
  82.9 0.7 collective-permute-start.6
  83.6 1.3 %shard_map.146.refs_0_ = f32[3,3,16,2048]{3,2,1,0:T(8,128)S(1)} custom-call(f32[3,3,24,2048]{3,2,1,0:T(8,128)S(1)} %get-tuple-element.81.refs_0_.refs_1_, f32[3,3,3,16,2048]{4,3,2,1,0:T(8,128)S(1)} %get-tuple-element.76.refs_12_.refs_1_, f32[16,24,2048]{2,1,0:T(8,128)S(1)} %get-tuple-element.70.refs_6_.refs_2_.refs_4_), custom_call_target="tpu_custom_call" | custom-call | tf_op jit(solution)/shard_map/pallas_call | solution.py:48
  84.9 0.0 collective-permute-done.5.refs_1_
  84.9 0.0 collective-permute-done.6.refs_2_
  84.9 1.1 %shard_map.147 = (f32[3,3,16,2048]{3,2,1,0:T(8,128)S(1)}, f32[32,1,128]{2,1,0:T(1,128)S(1)}) custom-call(f32[3,3,16,2048]{3,2,1,0:T(8,128)S(1)} %shard_map.146.refs_0_, f32[3,16,2048]{2,1,0:T(8,128)S(1)} %collective-permute-done.5.refs_1_, f32[3,16,2048]{2,1,0:T(8,128)S(1)} %collective-permute-done.6.refs_2_, ...), custom_call_target="tpu_custom_call" | custom-call | tf_op jit(solution)/shard_map/pallas_call | solution.py:48
  86.0 16.0 %all_to_all.16.refs_0_ = f32[32,1,128]{2,1,0:T(1,128)S(1)} all-to-all(f32[32,1,128]{2,1,0:T(1,128)S(1)} %get-tuple-element.84), channel_id=1, replica_groups=mesh['tile'=8,'layer'=4] {'tile','layer'}, dimensions={0} | all-to-all | bytes 32768 | tf_op jit(solution)/shard_map/all_to_all | solution.py:515
  101.9 1.7 %shard_map.148 = (f32[3,3,16,2048]{3,2,1,0:T(8,128)}, f32[3,3,16,2048]{3,2,1,0:T(8,128)}, f32[1,1]{1,0:T(1,128)}) custom-call(f32[32,1,128]{2,1,0:T(1,128)S(1)} %all_to_all.16.refs_0_, f32[3,3,24,2048]{3,2,1,0:T(8,128)S(1)} %get-tuple-element.81.refs_0_.refs_1_, f32[3,3,16,2048]{3,2,1,0:T(8,128)S(1)} %get-tuple-element.85.refs_2_, ...), custom_call_target="tpu_custom_call" | custom-call | tf_op jit(solution)/shard_map/pallas_call | solution.py:48
Async XLA Ops:
  3.6 15.1 %all-to-all-start = ((f32[32,1,768]{2,1,0:T(1,128)}), f32[32,1,768]{2,1,0:T(1,128)S(1)}, u32[]{:S(2)}, u32[]{:S(2)}) async-start(f32[32,1,768]{2,1,0:T(1,128)} %get-tuple-element.46), calls=%async_computation | async-start | bytes 196608 | tf_op jit(solution)/shard_map/all_to_all | solution.py:515
  10.9 3.1 %collective-permute-start = (f32[1,16,2048]{2,1,0:T(8,128)S(1)}, f32[1,16,2048]{2,1,0:T(8,128)S(1)}, u32[]{:S(2)}, u32[]{:S(2)}) collective-permute-start(f32[1,16,2048]{2,1,0:T(8,128)S(1)} %get-tuple-element.47), channel_id=1, source_target_pairs={{0,1},{1,2},{2,3},{4,5},{5,6},{6,7},{8,9},{9,10},{10,11},{12,13},{... | collective-permute-start | bytes 393224 | tf_op jit(solution)/shard_map/ppermute | solution.py:497
  23.4 15.8 %collective-permute-start.1 = (f32[64,2048]{1,0:T(8,128)S(1)}, f32[64,2048]{1,0:T(8,128)S(1)}, u32[]{:S(2)}, u32[]{:S(2)}) collective-permute-start(f32[64,2048]{1,0:T(8,128)S(1)} %get-tuple-element.58), channel_id=1, source_target_pairs={{4,0},{8,4},{12,8},{16,12},{20,16},{24,20},{28,24},{5,1},{9,5},{13... | collective-permute-start | bytes 1572872 | tf_op jit(solution)/shard_map/ppermute | solution.py:501
  24.7 24.7 %collective-permute-start.2 = (f32[64,2048]{1,0:T(8,128)S(1)}, f32[64,2048]{1,0:T(8,128)S(1)}, u32[]{:S(2)}, u32[]{:S(2)}) collective-permute-start(f32[64,2048]{1,0:T(8,128)S(1)} %get-tuple-element.59), channel_id=1, source_target_pairs={{0,4},{4,8},{8,12},{12,16},{16,20},{20,24},{24,28},{1,5},{5,9},{9,... | collective-permute-start | bytes 1572872 | tf_op jit(solution)/shard_map/ppermute | solution.py:497
  50.7 2.9 %collective-permute-start.3 = (f32[6,24,2048]{2,1,0:T(8,128)S(1)}, f32[6,24,2048]{2,1,0:T(8,128)S(1)}, u32[]{:S(2)}, u32[]{:S(2)}) collective-permute-start(f32[6,24,2048]{2,1,0:T(8,128)S(1)} %get-tuple-element.61.refs_0_.refs_14_), channel_id=1, source_target_pairs={{0,1},{1,0},{2,3},{3,2},{4,5},{5,4},{6,7},{7,6},{8,9},{9,8},{10,11... | collective-permute-start | bytes 3538952 | tf_op jit(solution)/shard_map/ppermute | solution.py:505
  54.8 11.2 %collective-permute-start.4 = (f32[2,24,2048]{2,1,0:T(8,128)S(1)}, f32[2,24,2048]{2,1,0:T(8,128)S(1)}, u32[]{:S(2)}, u32[]{:S(2)}) collective-permute-start(f32[2,24,2048]{2,1,0:T(8,128)S(1)} %get-tuple-element.63), channel_id=1, source_target_pairs={{0,2},{1,3},{2,0},{3,1},{4,6},{5,7},{6,4},{7,5},{8,10},{9,11},{10,... | collective-permute-start | bytes 1179656 | tf_op jit(solution)/shard_map/ppermute | solution.py:505
  82.4 2.5 %collective-permute-start.5 = (f32[3,16,2048]{2,1,0:T(8,128)S(1)}, f32[3,16,2048]{2,1,0:T(8,128)S(1)}, u32[]{:S(2)}, u32[]{:S(2)}) collective-permute-start(f32[3,16,2048]{2,1,0:T(8,128)S(1)} %get-tuple-element.82), channel_id=1, source_target_pairs={{0,1},{1,0},{2,3},{3,2},{4,5},{5,4},{6,7},{7,6},{8,9},{9,8},{10,11... | collective-permute-start | bytes 1179656 | tf_op jit(solution)/shard_map/ppermute | solution.py:505
  82.9 2.0 %collective-permute-start.6 = (f32[3,16,2048]{2,1,0:T(8,128)S(1)}, f32[3,16,2048]{2,1,0:T(8,128)S(1)}, u32[]{:S(2)}, u32[]{:S(2)}) collective-permute-start(f32[3,16,2048]{2,1,0:T(8,128)S(1)} %get-tuple-element.83), channel_id=1, source_target_pairs={{1,2},{2,1},{5,6},{6,5},{9,10},{10,9},{13,14},{14,13},{17,18},{18,... | collective-permute-start | bytes 1179656 | tf_op jit(solution)/shard_map/ppermute | solution.py:511

commit v4 on v3

v4 whole, which is shorter than its diff:
```python
import functools
import jax
import jax.numpy as jnp
from jax import lax
from jax.experimental import pallas as pl
from jax.experimental.pallas import tpu as pltpu
from jax.sharding import PartitionSpec as P

F32 = jnp.float32
BF16 = jnp.bfloat16
I32 = jnp.int32
BOTH = ("tile", "layer")
VM = pl.BlockSpec(memory_space=pltpu.VMEM)
LIMIT = 16 << 20


def hbm(shape):
    return jax.ShapeDtypeStruct(shape, F32)


def vmem(shape, dtype=F32):
    return pltpu.VMEM(shape, dtype)


def staged(kernel, where, outs, kept, column, *refs):
    count, sems = (len(where), refs[-1])
    held = list(refs[count + outs + len(kept) : -1])
    target = dict(zip(kept, refs[count + outs : count + outs + len(kept)]))
    operands, copies = ([], [])
    for i, far in enumerate(where):
        if far:
            to = target[i] if i in target else held.pop(0)
            part = refs[i].at[:, 0] if i in column else refs[i]
            copies.append(pltpu.make_async_copy(part, to, sems.at[len(copies)]))
            operands.append(to)
        else:
            operands.append(refs[i])
    for copy in copies:
        copy.start()
    for copy in copies:
        copy.wait()
    kernel(*operands, *refs[count : count + outs])


def call(kernel, outs, args, far=(), keep=(), column=(), limit=LIMIT):
    where = [i in far for i in range(len(args))]
    spaces = [pltpu.HBM if w else pltpu.VMEM for w in where]
    every = (*outs, *(vmem(args[i].shape, args[i].dtype) for i in keep))
    return pl.pallas_call(
        functools.partial(staged, kernel, where, len(outs), tuple(keep), tuple(column)),
        out_shape=every,
        in_specs=[pl.BlockSpec(memory_space=s) for s in spaces],
        out_specs=(VM,) * len(every),
        scratch_shapes=[
            vmem(a.shape[:1] + a.shape[2:] if i in column else a.shape, a.dtype)
            for i, a in enumerate(args)
            if where[i] and i not in keep
        ]
        + [pltpu.SemaphoreType.DMA((max(1, sum(where)),))],
        compiler_params=pltpu.CompilerParams(vmem_limit_bytes=limit),
    )(*[pltpu.with_memory_space_constraint(a, s) for a, s in zip(args, spaces)])


def iota(shape, dim):
    return lax.broadcasted_iota(I32, shape, dim)


def split(x):
    one = x.astype(BF16)
    rest = x - one.astype(F32)
    two = rest.astype(BF16)
    three = (rest - two.astype(F32)).astype(BF16)
    return [one, two, three]


def fold(x):
    n = x.shape[0] // 3
    return x[:n] + (x[n : 2 * n] + x[2 * n :])


def onehot(index, size):
    return jnp.where(iota((size, index.shape[1]), 0) == index, 1.0, 0.0)


def dot(a, b):
    return lax.dot_general(a, b, (((1,), (0,)), ((), ())), preferred_element_type=F32)


def dot_nt(a, b):
    return lax.dot_general(a, b, (((1,), (1,)), ((), ())), preferred_element_type=F32)


def pick(table, hi, lo):
    rows, cols = table.shape
    parts = jnp.concatenate(split(table), 0)
    got = fold(dot(parts, onehot(lo, cols).astype(BF16)))
    return jnp.sum(got * onehot(hi, rows), axis=0, keepdims=True)


def spread(value, hi, lo, rows, cols):
    parts = [jnp.where(iota((rows, hi.shape[1]), 0) == hi, v.astype(F32), 0.0).astype(BF16) for v in split(value)]
    return fold(dot_nt(jnp.concatenate(parts, 0), onehot(lo, cols).astype(BF16)))


def pres_kernel(rhs, wts, cell, front, prod, tz, store, pres, send, tz_last, low, high):
    depth, width, long = pres.shape
    for z in range(depth):
        pres[z] = wts[0, z] * rhs[0, z] + wts[1, z] * rhs[1, z] + wts[2, z] * rhs[2, z]
    where = cell[...]
    table = pres[...].reshape(depth * width, long)
    value = prod[...] * pick(table, lax.div(where, long), lax.rem(where, long))
    both = jnp.concatenate([value, front[...].astype(F32), where.astype(F32)], 1)
    send[...] = jnp.broadcast_to(both[:, None], send.shape)
    tz_last[0] = tz[depth - 1]
    planes = [(ref, z) for ref in (tz, store, pres) for z in range(depth)]
    for i, (ref, z) in enumerate(planes):
        low[2 * i : 2 * i + 2] = ref[z, 0:2]
        high[2 * i : 2 * i + 2] = ref[z, width - 2 : width]
    for out in (low, high):
        out[2 * len(planes) :] = jnp.zeros((out.shape[0] - 2 * len(planes), long), F32)


def edge_kernel(rhs, column, binv, tx, ty, tz_prev, low, high):
    depth, width, long = tx.shape
    for out, rows, at, two in ((low, slice(0, 8), 0, 0), (high, slice(width - 8, width), 7, 6)):
        out[...] = jnp.zeros(out.shape, F32)
        out[0:1] = tz_prev[0, rows][at : at + 1]
        for z in range(depth):
            out[1 + z : 2 + z] = ty[z, rows][at : at + 1]
            i = 1 + depth + 2 * z
            out[i : i + 2] = tx[z, rows][two : two + 2]
            right = [rhs[d, z, rows] for d in range(3)]
            slope_of = [column[d, z, rows] for d in range(3)]
            for c in range(3):
                m = [binv[c, d, z, rows] for d in range(3)]
                first = m[0] * right[0] + m[1] * right[1] + m[2] * right[2]
                slope = (1.0 if c == 0 else 0.0) - (m[0] * slope_of[0] + m[1] * slope_of[1] + m[2] * slope_of[2])
                for k, value in enumerate((first, slope, m[0])):
                    i = 1 + 3 * depth + (k * 3 + c) * depth + z
                    out[i : i + 1] = value[at : at + 1]


def is_right(level):
    return (lax.axis_index("layer") >> level) % 2 == 1


def choose(level, mine, other):
    right = is_right(level)
    return (jnp.where(right, other, mine), jnp.where(right, mine, other))


def local_solve(rhs, upper, inv, tz):
    depth = len(rhs)
    y = [rhs[0] * inv[0]]
    for z in range(1, depth):
        y.append((rhs[z] + tz[z - 1] * y[-1]) * inv[z])
    for z in range(depth - 2, -1, -1):
        y[z] = y[z] + upper[z] * y[z + 1]
    return y


def factors(tz, store):
    depth = len(tz)
    gs, invs = ([], [])
    own = None
    for z in range(depth):
        own = store[z] if z == 0 else store[z] + gs[-1] * own
        invs.append(1.0 / (own + tz[z] if z < depth - 1 else own))
        gs.append(tz[z] * invs[-1])
    first = [invs[0]]
    for z in range(1, depth):
        first.append(tz[z - 1] * first[-1] * invs[z])
    final = [None] * depth
    final[-1] = invs[-1]
    for z in range(depth - 2, -1, -1):
        first[z] = first[z] + gs[z] * first[z + 1]
        final[z] = gs[z] * final[z + 1]
    return gs, invs, first, final, (first[0], first[-1], final[-1] + 1.0 / jnp.maximum(tz[-1], 1e-30))


def coef_kernel(tz, store, pres, after, before, base, answers, ends):
    depth, width, long = pres.shape
    for k, ref in enumerate((tz, store, pres)):
        for z in range(depth):
            i = k * depth + z
            base[i, :width] = ref[z]
            base[i, width:] = jnp.full((8, long), 1.0 if k == 1 else 0.0, F32)
            for side, at in ((after, width), (before, width + 6)):
                rows = side[2 * i : 2 * i + 2]
                base[i, at : at + 2] = jnp.where(rows == 0.0, 1.0, rows) if k == 1 else rows
    tzs = [base[z] for z in range(depth)]
    gs, invs, first, final, coefs = factors(tzs, [base[depth + z] for z in range(depth)])
    for z in range(depth):
        answers[z] = first[z][:width]
        answers[depth + z] = final[z][:width]
    y = local_solve([base[2 * depth + z] for z in range(depth)], gs, invs, tzs)
    for i, value in enumerate((*coefs, y[0], y[-1])):
        ends[i] = value


def pair(level, own, sib):
    af, af_ = choose(level, own[0], sib[0])
    c, c_ = choose(level, own[1], sib[1])
    b, b_ = choose(level, own[2], sib[2])
    return af, c, b, af_, c_, b_, 1.0 / (b + af_)


def join_coefs(level, own, sib):
    af, c, _, _, c_, b_, g = pair(level, own, sib)
    return (af - c * c * g, c * c_ * g, b_ - c_ * c_ * g)


def join_ends(level, own, sib, mine, other):
    _, c, _, _, c_, _, g = pair(level, own, sib)
    yf, yf_ = choose(level, mine[0], other[0])
    yl, yl_ = choose(level, mine[1], other[1])
    flux = g * (yl - yf_)
    return (yf - c * flux, yl_ + c_ * flux)


def join_kernel(level, own, sib, answers, out, face, more, one):
    depth, width, _ = more.shape
    depth = depth // 2
    _, c, _, _, c_, _, g = pair(level, own, sib)
    first, both, last = join_coefs(level, own, sib)
    yf, yl = join_ends(level, own, sib, (own[3], own[4]), (sib[3], sib[4]))
    out[0], out[1], out[2] = (first, both, last)
    out[3], out[4] = (yf, yl)
    right, later = (is_right(level), is_right(level + 1))
    face[0], face[1] = (jnp.where(later, first, last), jnp.where(later, yf, yl))
    cg, cg_ = ((c * g)[:width], (c_ * g)[:width])
    for z in range(depth):
        kf, kl = (answers[z], answers[depth + z])
        top = jnp.where(right, cg * kf, kf - cg * kl)
        bottom = jnp.where(right, kl - cg_ * kf, cg_ * kl)
        more[z] = top
        more[depth + z] = bottom
        one[z] = jnp.where(later, top, bottom)


def groups_of(lists, levels):
    tiles = lax.axis_size("tile")
    layers = lax.axis_size("layer")
    t, l = (lax.axis_index("tile"), lax.axis_index("layer"))
    out = []
    for level in range(-1, levels):
        members = [l] if level < 0 else [(((l >> level) ^ 1) << level) + i for i in range(1 << level)]
        group = []
        for member in members:
            for step in (-1, 0, 1):
                there = jnp.clip(t + step, 0, tiles - 1)
                group.append((there * layers + member, step, there == t + step))
        out.append(group)
    return out


def front_kernel(recv, inverse, solved, held, sems):
    devices = recv.shape[0]
    count = recv.shape[2] // 3
    rows, length = inverse.shape
    lanes = 128
    chunks = sems.shape[0]
    wide = length // chunks
    copies = [
        pltpu.make_async_copy(inverse.at[:, pl.ds(i * wide, wide)], held.at[:, pl.ds(i * wide, wide)], sems.at[i])
        for i in range(chunks)
    ]
    for copy in copies:
        copy.start()
    total = jnp.zeros((length // lanes, lanes), F32)
    group = 8
    for first in range(0, devices, group):
        lefts, rights = ([], [])
        for d in range(first, first + group):
            value = recv[d, :, :count]
            index = recv[d, :, count : 2 * count].astype(I32)
            hi, lo = lax.div(index, lanes), lax.rem(index, lanes)
            hit = iota((length // lanes, count), 0) == hi
            lefts.append(jnp.concatenate([jnp.where(hit, v.astype(F32), 0.0).astype(BF16) for v in split(value)], 0))
            rights.append(onehot(lo, lanes).astype(BF16))
        total = total + fold(dot_nt(jnp.concatenate(lefts, 1), jnp.concatenate(rights, 1)))
    acc = jnp.zeros((rows, lanes), F32)
    for i in range(chunks):
        copies[i].wait()
        for r in range(i * wide // lanes, (i + 1) * wide // lanes):
            acc = acc + held[:, r * lanes : (r + 1) * lanes] * total[r : r + 1]
    parts = jnp.concatenate(split(acc), 1)
    out = dot_nt(jnp.ones((8, parts.shape[1]), BF16), parts)
    solved[...] = out[0:1]


def list_kernel(solved, cell, prod, *refs):
    tables, send = (refs[:-1], refs[-1])
    where, value = (cell[...], prod[...])
    hi, lo = None, None
    depth, width, long = tables[-1].shape
    hi, lo = lax.div(where, long), lax.rem(where, long)
    stack = [t[k * depth : (k + 1) * depth].reshape(depth * width, long) for t in tables for k in range(t.shape[0] // depth)]
    parts = jnp.concatenate([p for table in stack for p in split(table)], 0)
    got = dot(parts, onehot(lo, long).astype(BF16))
    mask = onehot(hi, depth * width)
    n = 3 * depth * width
    found = [value * jnp.sum(fold(got[i * n : (i + 1) * n]) * mask, axis=0, keepdims=True) for i in range(len(stack))]
    send[...] = jnp.broadcast_to(jnp.concatenate([solved[...], value, *found], 1)[:, None], send.shape)


def gathered(values, rows_hot, lanes_hot, start, size, ext, parts):
    hot = lanes_hot[:, start : start + size]
    pieces = [hot * p for v in values for p in split(v)[:parts]]
    got = dot_nt(rows_hot[:, start : start + size], jnp.concatenate(pieces, 0))
    planes = []
    lanes = hot.shape[0]
    for i in range(len(values)):
        plane = got[:, i * parts * lanes : (i * parts + 1) * lanes]
        for k in range(1, parts):
            j = i * parts + k
            plane = plane + got[:, j * lanes : (j + 1) * lanes]
        planes.append(jnp.concatenate([plane[r : r + ext] for r in range(0, plane.shape[0], ext)], 1))
    return planes


def beside(centre, tx, ty):
    high, long = centre.shape
    col = iota(centre.shape, 1)
    total = tx * pltpu.roll(centre, high - 1, 0) + pltpu.roll(tx * centre, 1, 0)
    total = total + ty * jnp.where(col == long - 1, 0.0, pltpu.roll(centre, long - 1, 1))
    return total + jnp.where(col == 0, 0.0, pltpu.roll(ty * centre, 1, 1))


def search_kernel(levels, *refs):
    (recv, terms, base), refs = (refs[:3], refs[3:])
    far, refs = (refs[: levels + 8], refs[levels + 8 :])
    (s, inner, outer, tx_wide, ty_wide, tzp), near_by, refs = (refs[:6], refs[6:11], refs[11:])
    near_by = [*near_by, *refs[: levels + 3]]
    p, rows_hot, lanes_hot, sol_hot, sol_row, layer, sems = refs[levels + 3 :]
    copies = [pltpu.make_async_copy(a, b, sems.at[i]) for i, (a, b) in enumerate(zip(far, near_by))]
    for copy in copies[5:] + copies[:5]:
        copy.start()
    tx, ty, rhs, diag, binv = near_by[:5]
    sib, (after, before, tz_prev) = (near_by[5 : levels + 5], near_by[levels + 5 :])
    depth = base.shape[0] // 3
    ext, long = base.shape[1:]
    width = ext - 8
    rows = sol_hot.shape[0]
    count = terms.shape[2] // 3
    lanes = 128
    groups = groups_of(recv, levels)
    at = 0
    for members in groups:
        for device, step, valid in members:
            entry = terms[device]
            index = entry[:, count : 2 * count].astype(I32)
            cell = entry[:, 2 * count :].astype(I32)
            y, x = lax.rem(cell, long), lax.rem(lax.div(cell, long), width)
            if step == 1:
                x = jnp.where(x < 2, x + width, -1)
            if step == -1:
                x = jnp.where(x >= width - 2, x - width + ext, -1)
            row = jnp.where(jnp.logical_and(valid, x >= 0), lax.div(y, lanes) * ext + x, -1)
            here = pl.ds(at, count)
            rows_hot[:, here] = onehot(row, rows_hot.shape[0]).astype(BF16)
            lanes_hot[:, here] = onehot(lax.rem(y, lanes), lanes).astype(BF16)
            sol_hot[:, here] = onehot(lax.rem(index, rows), rows).astype(BF16)
            sol_row[:, here] = lax.div(index, rows)
            if at < layer.shape[1]:
                layer[:, here] = lax.div(cell, long * width)
            at += count
    table = jnp.concatenate(split(recv[...].reshape(recv.shape[0], recv.shape[2])[:, :rows]), 0)
    sol = fold(dot(table, sol_hot[...]))
    sol = jnp.sum(jnp.where(iota(sol.shape, 0) == sol_row[...], sol, 0.0), axis=0, keepdims=True)

    def listed(group, column):
        at = rows + column * count
        return jnp.concatenate([recv[device][:, at : at + count] for device, _, _ in group], 1)

    tzs = [base[z] for z in range(depth)]
    gs, invs, first, final, coefs = factors(tzs, [base[depth + z] for z in range(depth)])
    own = [coefs]
    start = layer.shape[1]
    value = listed(groups[0], 0) * sol[:, :start]
    which = layer[...]
    change = gathered([jnp.where(which == z, value, 0.0) for z in range(depth)], rows_hot, lanes_hot, 0, start, ext, 3)
    y = local_solve([base[2 * depth + z] - change[z] for z in range(depth)], gs, invs, tzs)
    for copy in copies[5:]:
        copy.wait()
    mine = (y[0], y[-1])
    steps = []
    for level in range(levels):
        size = len(groups[level + 1]) * count
        top = level == levels - 1
        columns = [1 + 2 * level] if top else [1 + 2 * level, 2 + 2 * level]
        values = [listed(groups[level + 1], c) * sol[:, start : start + size] for c in columns]
        change = gathered(values, rows_hot, lanes_hot, start, size, ext, 3)
        start += size
        if top:
            other = sib[level][1] - change[0]
            steps.append((mine, (other, other)))
        else:
            other = (sib[level][3] - change[0], sib[level][4] - change[1])
            steps.append((mine, other))
            mine = join_ends(level, own[level], sib[level], mine, other)
            own.append(join_coefs(level, own[level], sib[level]))
    zero = jnp.zeros((8, long), F32)
    for z in range(depth):
        tx_wide[z, width:] = zero
        ty_wide[z, width:] = zero
        at = 1 + depth + 2 * z
        tx_wide[z, width : width + 2] = after[at : at + 2]
        tx_wide[z, width + 6 :] = before[at : at + 2]
        ty_wide[z, width : width + 1] = after[1 + z : 2 + z]
        ty_wide[z, width + 7 :] = before[1 + z : 2 + z]
    tzp[0, :width] = tz_prev[0]
    tzp[0, width:] = zero
    tzp[0, width : width + 1] = after[0:1]
    tzp[0, width + 7 :] = before[0:1]
    above = below = None
    for level in range(levels - 1, -1, -1):
        mine, other = steps[level]
        yl, _ = choose(level, mine[1], other[1])
        _, yf_ = choose(level, mine[0], other[0])
        flux = yl - yf_
        if level == levels - 1:
            b, _ = choose(level, own[level][2], sib[level][0])
            _, af_ = choose(level, own[level][0], sib[level][0])
            g = 1.0 / (b + af_)
        else:
            _, c, _, _, c_, _, g = pair(level, own[level], sib[level])
            flux = flux + c * above - c_ * below
        flux = g * flux
        right = is_right(level)
        if above is None:
            above = below = jnp.zeros((ext, long), F32)
        above, below = (jnp.where(right, flux, above), jnp.where(right, below, -flux))
    for z in range(depth):
        p[z] = y[z] + first[z] * above + final[z] * below
    is_last = lax.axis_index("layer") == (1 << levels) - 1
    for copy in copies[:5]:
        copy.wait()
    odd = is_right(0)
    for z in range(depth):
        tx_wide[z, :width] = tx[z]
        ty_wide[z, :width] = ty[z]
        centre = p[z]
        coupled = beside(centre, tx_wide[z], ty_wide[z])
        coupled = coupled + (above + tzp[0] * centre if z == 0 else tzs[z - 1] * p[z - 1])
        if z == depth - 1:
            coupled = coupled + jnp.where(is_last, 0.0, below + tzs[z] * centre)
        else:
            coupled = coupled + tzs[z] * p[z + 1]
        c16, n16, c8, n8 = (centre[:width], coupled[:width], centre[width:], coupled[width:])
        remain = [rhs[c, z] - diag[c, 0, z] * c16 for c in range(3)]
        remain[0] = remain[0] + n16
        for c in range(3):
            value = binv[c, 0, z] * remain[0] + binv[c, 1, z] * remain[1] + binv[c, 2, z] * remain[2]
            if c == 0:
                value = c16 + value
            s[c, z, :width] = value
            s[c, z, width:] = jnp.zeros((8, long), F32)
            for side, at in ((after, 0), (before, 7)):
                i = 1 + 3 * depth + c * depth + z
                j, k = (i + 3 * depth, i + 6 * depth)
                row = side[i : i + 1] + side[j : j + 1] * c8[at : at + 1] + side[k : k + 1] * n8[at : at + 1]
                s[c, z, width + at : width + at + 1] = row
    for c in range(3):
        top, bottom = (s[c, 0, :width], s[c, depth - 1, :width])
        inner[c] = jnp.where(odd, top, bottom)
        outer[c] = jnp.where(odd, bottom, top)


def inner_kernel(s, diag, tzs, tx, ty, image):
    depth, ext, long = s.shape[1:]
    width = ext - 8
    for z in range(depth):
        for c in range(3):
            total = diag[c, 0, z] * s[0, z, :width] + diag[c, 1, z] * s[1, z, :width] + diag[c, 2, z] * s[2, z, :width]
            total = total - beside(s[c, z], tx[z], ty[z])[:width]
            if z:
                total = total - tzs[z - 1, :width] * s[c, z - 1, :width]
            if z < depth - 1:
                total = total - tzs[z, :width] * s[c, z + 1, :width]
            image[c, z] = total


def image_kernel(part, inner, outer, rhs, tzs, tzp, image, send):
    depth, width = part.shape[1:3]
    odd = is_right(0)
    along = power = start = 0.0
    for z in range(depth):
        for c in range(3):
            value = part[c, z]
            if z == 0:
                value = value - tzp[0, :width] * jnp.where(odd, inner[c], outer[c])
            if z == depth - 1:
                value = value - tzs[z, :width] * jnp.where(odd, outer[c], inner[c])
            image[c, z] = value
            right = rhs[c, z]
            along = along + value * right
            power = power + value * value
            start = start + right * right
    along, power, start = (jnp.sum(along), jnp.sum(power), jnp.sum(start))
    omega = along / jnp.where(power > 0.0, power, 1.0)
    square = cross = 0.0
    for z in range(depth):
        for c in range(3):
            value = image[c, z]
            left = rhs[c, z] - omega * value
            square = square + left * left
            cross = cross + left * value
    lane = iota((1, send.shape[2]), 1)
    out = jnp.zeros((1, send.shape[2]), F32)
    for i, value in enumerate((along, power, start, jnp.sum(square), jnp.sum(cross), omega)):
        out = jnp.where(lane == i, value, out)
    send[...] = jnp.broadcast_to(out[:, None], send.shape)


def finish_kernel(recv, s, image, rhs, update, lin_res, ratio):
    sums = recv[...].reshape(recv.shape[0], recv.shape[2])
    whole = jnp.sum(sums, axis=0, keepdims=True)
    omega = whole[:, 0:1] / whole[:, 1:2]
    shift = sums[:, 5:6] - omega
    square = sums[:, 3:4] + 2.0 * shift * sums[:, 4:5] + shift * shift * sums[:, 1:2]
    ratio[...] = jnp.sqrt(jnp.sum(square, axis=0, keepdims=True) / whole[:, 2:3])
    for c in range(3):
        for z in range(s.shape[1]):
            update[c, z] = omega * s[c, z, : rhs.shape[2]]
            lin_res[c, z] = rhs[c, z] - omega * image[c, z]


def up(x, axis):
    return lax.ppermute(x, axis, [(i, i + 1) for i in range(lax.axis_size(axis) - 1)])


def down(x, axis):
    return lax.ppermute(x, axis, [(i + 1, i) for i in range(lax.axis_size(axis) - 1)])


def flip(x, level):
    return lax.ppermute(x, "layer", [(i, i ^ (1 << level)) for i in range(lax.axis_size("layer"))])


def neighbour(x):
    size = lax.axis_size("layer")
    pairs = [(i, i + 1) for i in range(1, size - 1, 2)]
    return lax.ppermute(x, "layer", pairs + [(j, i) for i, j in pairs])


def everywhere(x):
    return lax.all_to_all(x, BOTH, split_axis=0, concat_axis=0, tiled=True)


def shards(rhs, weights, block_diag, block_inv, tx, ty, tz, store, cell, front, prod, inverse):
    layers = lax.axis_size("layer")
    devices = lax.axis_size("tile") * layers
    levels = layers.bit_length() - 1
    depth, width, long = tx.shape
    ext = width + 8
    count = cell.shape[0]
    rows = inverse.shape[0]
    lists = 3 * layers * count
    cell, front, prod = (cell.reshape(1, -1), front.reshape(1, -1), prod.reshape(1, -1))
    field = vmem(tx.shape)

    def planes(n, high=ext):
        return vmem((n, high, long))

    rim = vmem((8 * (-(-6 * depth // 8)), long))
    pres, send, tz_last, low, high, tz, store = call(
        pres_kernel,
        (field, vmem((devices, 1, 3 * count)), vmem((1, width, long)), rim, rim),
        (rhs, weights, cell, front, prod, tz, store),
        far=range(7),
        keep=(5, 6),
    )
    terms = everywhere(send)
    tz_prev = up(tz_last, "layer")
    after, before = (down(low, "tile"), up(high, "tile"))
    terms, after, before = lax.optimization_barrier((terms, after, before))
    five = planes(5)
    base, answers, ends = call(
        coef_kernel, (planes(3 * depth), planes(2 * depth, width), five), (tz, store, pres, after, before)
    )
    rim = vmem((8 * (-(-(1 + 12 * depth) // 8)), long))
    low, high = call(
        edge_kernel, (rim, rim), (rhs, block_diag, block_inv, tx, ty, tz_prev), far=range(5), column=(1,)
    )
    after, before = (down(low, "tile"), up(high, "tile"))
    terms, low, high, ends = lax.optimization_barrier((terms, low, high, ends))
    chunks = 8
    solved = pl.pallas_call(
        front_kernel,
        out_shape=vmem((1, rows)),
        in_specs=[VM, pl.BlockSpec(memory_space=pltpu.HBM)],
        out_specs=VM,
        scratch_shapes=[vmem(inverse.shape), pltpu.SemaphoreType.DMA((chunks,))],
        compiler_params=pltpu.CompilerParams(vmem_limit_bytes=LIMIT),
    )(terms, pltpu.with_memory_space_constraint(inverse, pltpu.HBM))
    sib, tables = ([], [])
    last = answers
    for level in range(levels - 1):
        tables.append(answers)
        got = flip(ends, level)
        solved, got = lax.optimization_barrier((solved, got))
        sib.append(got)
        ends, face, answers, last = call(
            functools.partial(join_kernel, level),
            (five, planes(2), planes(2 * depth, width), planes(depth, width)),
            (ends, sib[-1], answers),
        )
    tables.append(last)
    sib.append(flip(face, levels - 1))
    (send,) = call(
        list_kernel,
        (vmem((devices, 1, rows + 2 * levels * count)),),
        (solved, cell, prod, *tables),
        far=(1, 2),
    )
    sol = everywhere(send)
    plane3 = vmem((3, width, long))
    far = (tx, ty, rhs, block_diag, block_inv, *sib, after, before, tz_prev)
    args = (sol, terms, base)
    s, inner, outer, tx, ty, tzp, _, _, rhs, diag, _ = pl.pallas_call(
        functools.partial(search_kernel, levels),
        out_shape=(vmem((3, depth, ext, long)), plane3, plane3, planes(depth), planes(depth), planes(1))
        + tuple(vmem(a.shape) for a in far[:5]),
        in_specs=[VM] * len(args) + [pl.BlockSpec(memory_space=pltpu.HBM)] * len(far),
        out_specs=(VM,) * 11,
        scratch_shapes=[vmem(a.shape) for a in far[5:]]
        + [
            planes(depth),
            vmem((ext * long // 128, lists), BF16),
            vmem((128, lists), BF16),
            vmem((rows, lists), BF16),
            vmem((1, lists), I32),
            vmem((1, 3 * count), I32),
            pltpu.SemaphoreType.DMA((len(far),)),
        ],
        compiler_params=pltpu.CompilerParams(vmem_limit_bytes=2 * LIMIT),
    )(
        *[pltpu.with_memory_space_constraint(a, pltpu.VMEM) for a in args],
        *[pltpu.with_memory_space_constraint(a, pltpu.HBM) for a in far],
    )
    inner, outer = (flip(inner, 0), neighbour(outer))
    (part,) = call(inner_kernel, (vmem(rhs.shape),), (s, diag, base, tx, ty))
    image, send = call(
        image_kernel,
        (vmem(rhs.shape), vmem((devices, 1, 128))),
        (part, inner, outer, rhs, base, tzp),
    )
    sums = everywhere(send)
    update, lin_res, ratio = call(
        finish_kernel, (hbm(rhs.shape), hbm(rhs.shape), hbm((1, 1))), (sums, s, image, rhs)
    )
    return (update, lin_res, ratio.reshape(()))


def solution(mesh):
    return jax.shard_map(
        shards,
        mesh=mesh,
        in_specs=(
            P(None, "layer", "tile", None),
            P(None, "layer", "tile", None),
            P(None, None, "layer", "tile", None),
            P(None, None, "layer", "tile", None),
            P("layer", "tile", None),
            P("layer", "tile", None),
            P("layer", "tile", None),
            P("layer", "tile", None),
            P(("tile", "layer")),
            P(("tile", "layer")),
            P(("tile", "layer")),
            P(("tile", "layer"), None),
        ),
        out_specs=(P(None, "layer", "tile", None), P(None, "layer", "tile", None), P()),
        check_vma=False,
    )
```

time: 104 us -> 90.1 us (0.87)
  waiting for transfers between devices: 31 us -> 9.79 us
  starting transfers between devices: 17.3 us -> 31.8 us
  blocking collectives: 27.8 us -> 17.8 us
  local copies, waits for them, and re-layouts: 0 us -> 1.61 us
    all_to_all x2 -> x1, blocking collectives: 27.8 us -> 17.8 us  [everywhere(): return lax.all_to_all(x, BOTH, split_axis=0, concat_axis=0, tiled=True)]
    ppermute x1 -> x2, waiting for transfers between devices: 9.95 us -> 0.01 us  [down(): lax.ppermute(x, axis, [(i + 1, i) for i in range(lax.axis_size(axis) - 1)])]
    ppermute x2 -> x3, starting transfers between devices: 6.74 us -> 13 us  [up(): lax.ppermute(x, axis, [(i, i + 1) for i in range(lax.axis_size(axis) - 1)])]
    pallas_call x1 -> x2, Pallas kernels: 6.64 us -> 12 us  [the longest x1 7.45 us: shards(): pl.pallas_call(functools.partial(search_kernel, levels), out_shape=(vmem(...]
    ppermute x3, waiting for transfers between devices: 5.27 us -> 0.01 us  [flip(): lax.ppermute(x, 'layer', [(i, i ^ 1 << level) for i in range(lax.axis_siz...]
    pallas_call x9 -> x8, Pallas kernels: 20.1 us -> 15.8 us  [call(): pl.pallas_call(functools.partial(staged, kernel, where, len(outs), tuple(...]
    ppermute x3, starting transfers between devices: 1.28 us -> 5.49 us  [flip(): lax.ppermute(x, 'layer', [(i, i ^ 1 << level) for i in range(lax.axis_siz...]
    all_to_all x1 -> x2, waiting for transfers between devices: 4.68 us -> 0.56 us  [everywhere(): return lax.all_to_all(x, BOTH, split_axis=0, concat_axis=0, tiled=True)]
  transfers between devices with their start and end apart: 8 -> 11, of which waited for: 6 -> 4; matrix products, arithmetic and copies ran while one was open for 0% -> 0% of each run, Pallas kernels for 9% -> 14%
where the time goes in v4:
time: 90.1 us; the launch traced here: 89.7 us
  starting transfers between devices  31.8 us (35%)
  Pallas kernels  27.8 us (31%)
  blocking collectives  17.8 us (20%)
  waiting for transfers between devices  9.79 us (11%)
  local copies, waits for them, and re-layouts  1.61 us (2%)
  between operations  0.99 us (1%)
    all_to_all x1, blocking collectives, everywhere(): return lax.all_to_all(x, BOTH, split_axis=0, concat_axis=0, tiled=True)  17.8 us
    pallas_call x8, Pallas kernels, call(): pl.pallas_call(functools.partial(staged, kernel, where, len(outs), tuple(...  15.8 us
    ppermute x3, starting transfers between devices, up(): lax.ppermute(x, axis, [(i, i + 1) for i in range(lax.axis_size(axis) - 1)])  13 us
    all_to_all x2, starting transfers between devices, everywhere(): return lax.all_to_all(x, BOTH, split_axis=0, concat_axis=0, tiled=True)  9.88 us
    ppermute x3, waiting for transfers between devices, up(): lax.ppermute(x, axis, [(i, i + 1) for i in range(lax.axis_size(axis) - 1)])  9.22 us
    pallas_call x1, Pallas kernels, shards(): pl.pallas_call(functools.partial(search_kernel, levels), out_shape=(vmem(...  7.45 us
    ppermute x3, starting transfers between devices, flip(): lax.ppermute(x, 'layer', [(i, i ^ 1 << level) for i in range(lax.axis_siz...  5.49 us
    pallas_call x1, Pallas kernels, shards(): pl.pallas_call(front_kernel, out_shape=vmem((1, rows)), in_specs=[VM, pl....  4.59 us
  transfers between devices with their start and end apart: 11, of which 4 were waited for; matrix products, arithmetic and copies ran while one was open for 0% of the time, Pallas kernels for 14%

profile of v4, /device:TPU:0, one launch (start us, length us, event | category | flops | bytes accessed | tf_op | source)
XLA Modules:
  0.0 89.7 jit_solution(2535292077100373200)
XLA Ops:
  0.6 3.2 %shard_map.139 = (f32[3,16,2048]{2,1,0:T(8,128)S(1)}, f32[32,1,768]{2,1,0:T(1,128)}, f32[1,16,2048]{2,1,0:T(8,128)S(1)}, f32[24,2048]{1,0:T(8,128)S(1)}, f32[24,...) custom-call(f32[3,3,16,2048]{3,2,1,0:T(8,128)} %refs_5_.3, f32[3,3,16,2048]{3,2,1,0:T(8,128)} %refs_1_.2, ...), custom_call_target="tpu_custom_call" | custom-call | tf_op jit(solution)/shard_map/pallas_call | solution.py:49
  3.8 1.3 %collective-permute-start = (f32[24,2048]{1,0:T(8,128)S(1)}, f32[24,2048]{1,0:T(8,128)S(1)}, u32[]{:S(2)}, u32[]{:S(2)}) collective-permute-start(f32[24,2048]{1,0:T(8,128)S(1)} %get-tuple-element.38), channel_id=1, source_target_pairs={{4,0},{8,4},{12,8},{16,12},{20,16},{24,20},{28,24},{5,1},{9,5},{13... | collective-permute-start | bytes 589832 | tf_op jit(solution)/shard_map/ppermute | solution.py:534
  5.1 5.5 %collective-permute-start.1 = (f32[24,2048]{1,0:T(8,128)S(1)}, f32[24,2048]{1,0:T(8,128)S(1)}, u32[]{:S(2)}, u32[]{:S(2)}) collective-permute-start(f32[24,2048]{1,0:T(8,128)S(1)} %get-tuple-element.39), channel_id=1, source_target_pairs={{0,4},{4,8},{8,12},{12,16},{16,20},{20,24},{24,28},{1,5},{5,9},{9,... | collective-permute-start | bytes 589832 | tf_op jit(solution)/shard_map/ppermute | solution.py:530
  10.6 6.2 %all-to-all-start = ((f32[32,1,768]{2,1,0:T(1,128)}), f32[32,1,768]{2,1,0:T(1,128)S(1)}, u32[]{:S(2)}, u32[]{:S(2)}) async-start(f32[32,1,768]{2,1,0:T(1,128)} %get-tuple-element.37), calls=%async_computation | async-start | bytes 196608 | tf_op jit(solution)/shard_map/all_to_all | solution.py:548
  16.9 2.2 %collective-permute-start.2 = (f32[1,16,2048]{2,1,0:T(8,128)S(1)}, f32[1,16,2048]{2,1,0:T(8,128)S(1)}, u32[]{:S(2)}, u32[]{:S(2)}) collective-permute-start(f32[1,16,2048]{2,1,0:T(8,128)S(1)} %get-tuple-element.41), channel_id=1, source_target_pairs={{0,1},{1,2},{2,3},{4,5},{5,6},{6,7},{8,9},{9,10},{10,11},{12,13},{... | collective-permute-start | bytes 393224 | tf_op jit(solution)/shard_map/ppermute | solution.py:530
  19.0 1.0 %collective-permute-done.2.refs_5_.refs_12_ = f32[1,16,2048]{2,1,0:T(8,128)S(1)} collective-permute-done((f32[1,16,2048]{2,1,0:T(8,128)S(1)}, f32[1,16,2048]{2,1,0:T(8,128)S(1)}, u32[]{:S(2)}, u32[]{:S(2)}) %collective-permute-start.2) | collective-permute-done | bytes 131104 | tf_op jit(solution)/shard_map/ppermute | solution.py:530
  20.0 4.4 %shard_map.140 = (f32[40,2048]{1,0:T(8,128)}, f32[40,2048]{1,0:T(8,128)}) custom-call(f32[3,3,16,2048]{3,2,1,0:T(8,128)} %refs_5_.3, f32[3,3,3,16,2048]{4,3,2,1,0:T(8,128)} %refs_6_.3, f32[3,3,3,16,2048]{4,3,2,1,0:T(8,128)} %refs_7_.1, f32[3,16,2048]{2,1,0:T(8,128)} %refs_3_.3, f32[3,16,2048]{2,1,0:T(8,128)} %refs_4_.3, ...), custom_call_target="tpu_custom_call" | custom-call | tf_op jit(solution)/shard_map/pallas_call | solution.py:49
  24.4 0.3 all-to-all-done.recv.refs_1_
  24.7 0.7 copy-done.2
  25.4 0.9 %copy-done.3 = f32[24,2048]{1,0:T(8,128)S(1)} copy-done((f32[24,2048]{1,0:T(8,128)S(1)}, f32[24,2048]{1,0:T(8,128)}, u32[]{:S(2)}) %copy-start.3) | copy-done | bytes 196632
  26.3 0.6 shard_map.141
  26.9 2.6 %collective-permute-start.3 = (f32[5,24,2048]{2,1,0:T(8,128)S(1)}, f32[5,24,2048]{2,1,0:T(8,128)S(1)}, u32[]{:S(2)}, u32[]{:S(2)}) collective-permute-start(f32[5,24,2048]{2,1,0:T(8,128)S(1)} %get-tuple-element.51.refs_0_), channel_id=1, source_target_pairs={{0,1},{1,0},{2,3},{3,2},{4,5},{5,4},{6,7},{7,6},{8,9},{9,8},{10,11... | collective-permute-start | bytes 2949128 | tf_op jit(solution)/shard_map/ppermute | solution.py:538
  29.5 4.6 %shard_map.142.refs_0_ = f32[1,256]{1,0:T(1,128)S(1)} custom-call(f32[32,1,768]{2,1,0:T(1,128)S(1)} %all-to-all-done.recv.refs_1_, f32[256,8192]{1,0:T(8,128)} %inverse.1), custom_call_target="tpu_custom_call" | custom-call | tf_op jit(solution)/shard_map/pallas_call | solution.py:589
  34.1 0.0 collective-permute-done.3.refs_1_.refs_8_
  34.1 0.0 copy-start
  34.1 1.5 %shard_map.143 = (f32[5,24,2048]{2,1,0:T(8,128)}, f32[2,24,2048]{2,1,0:T(8,128)S(1)}, f32[6,16,2048]{2,1,0:T(8,128)}, f32[3,16,2048]{2,1,0:T(8,128)S(1)}) custom-call(f32[5,24,2048]{2,1,0:T(8,128)S(1)} %get-tuple-element.51.refs_0_, f32[5,24,2048]{2,1,0:T(8,128)S(1)} %collective-permute-done.3.refs_1_.refs_8_, ...), custom_call_target="tpu_custom_call" | custom-call | tf_op jit(solution)/shard_map/pallas_call | solution.py:49
  35.7 2.4 %collective-permute-start.4 = (f32[2,24,2048]{2,1,0:T(8,128)S(1)}, f32[2,24,2048]{2,1,0:T(8,128)}, u32[]{:S(2)}, u32[]{:S(2)}) collective-permute-start(f32[2,24,2048]{2,1,0:T(8,128)S(1)} %get-tuple-element.57), channel_id=1, source_target_pairs={{0,2},{1,3},{2,0},{3,1},{4,6},{5,7},{6,4},{7,5},{8,10},{9,11},{10,... | collective-permute-start | bytes 1179656 | tf_op jit(solution)/shard_map/ppermute | solution.py:538
  38.1 1.3 %collective-permute-start.5 = (f32[40,2048]{1,0:T(8,128)}, f32[40,2048]{1,0:T(8,128)}, u32[]{:S(2)}, u32[]{:S(2)}) collective-permute-start(f32[40,2048]{1,0:T(8,128)} %get-tuple-element.42), channel_id=1, source_target_pairs={{4,0},{8,4},{12,8},{16,12},{20,16},{24,20},{28,24},{5,1},{9,5},{13... | collective-permute-start | bytes 983048 | tf_op jit(solution)/shard_map/ppermute | solution.py:534
  39.4 5.3 %collective-permute-start.6 = (f32[40,2048]{1,0:T(8,128)}, f32[40,2048]{1,0:T(8,128)}, u32[]{:S(2)}, u32[]{:S(2)}) collective-permute-start(f32[40,2048]{1,0:T(8,128)} %get-tuple-element.43), channel_id=1, source_target_pairs={{0,4},{4,8},{8,12},{12,16},{16,20},{20,24},{24,28},{1,5},{5,9},{9,... | collective-permute-start | bytes 983048 | tf_op jit(solution)/shard_map/ppermute | solution.py:530
  44.7 2.0 %shard_map.144 = f32[32,1,1280]{2,1,0:T(1,128)} custom-call(f32[1,256]{1,0:T(1,128)S(1)} %shard_map.142.refs_0_, s32[1,256]{1,0:T(1,128)} %bitcast.5, f32[1,256]{1,0:T(1,128)} %bitcast.7, f32[6,16,2048]{2,1,0:T(8,128)S(1)} %get-tuple-element.53.refs_2_.refs_3_, f32[3,16,2048]{2,1,0:T(8,128)S(1)} %get-tuple-element.55.refs_4_), custom_call_target="tpu_custom_call" | custom-call | tf_op jit(solution)/shard_map/pallas_call | solution.py:49
  46.8 3.7 %all-to-all-start.1 = ((f32[32,1,1280]{2,1,0:T(1,128)}), f32[32,1,1280]{2,1,0:T(1,128)S(1)}, u32[]{:S(2)}, u32[]{:S(2)}) async-start(f32[32,1,1280]{2,1,0:T(1,128)} %shard_map.144), calls=%async_computation.1 | async-start | bytes 327680 | tf_op jit(solution)/shard_map/all_to_all | solution.py:548
  50.4 8.3 %collective-permute-done.6.refs_11_ = f32[40,2048]{1,0:T(8,128)} collective-permute-done((f32[40,2048]{1,0:T(8,128)}, f32[40,2048]{1,0:T(8,128)}, u32[]{:S(2)}, u32[]{:S(2)}) %collective-permute-start.6) | collective-permute-done | bytes 327712 | tf_op jit(solution)/shard_map/ppermute | solution.py:530
  58.7 0.3 all-to-all-done.1.refs_0_
  59.0 7.4 %shard_map.145 = (f32[3,3,24,2048]{3,2,1,0:T(8,128)S(1)}, f32[3,16,2048]{2,1,0:T(8,128)S(1)}, f32[3,16,2048]{2,1,0:T(8,128)S(1)}, f32[3,24,2048]{2,1,0:T(8,128)S...) custom-call(f32[32,1,1280]{2,1,0:T(1,128)S(1)} %all-to-all-done.1.re, ...), custom_call_target="tpu_custom_call" | custom-call | tf_op jit(solution)/shard_map/pallas_call | solution.py:621
  66.5 0.5 collective-permute-start.7
  66.9 0.9 collective-permute-start.8
  67.8 1.3 %shard_map.146.refs_0_ = f32[3,3,16,2048]{3,2,1,0:T(8,128)S(1)} custom-call(f32[3,3,24,2048]{3,2,1,0:T(8,128)S(1)} %get-tuple-element.58.refs_0_.refs_1_, f32[3,3,3,16,2048]{4,3,2,1,0:T(8,128)S(1)} %get-tuple-element.59.refs_1_, f32[9,24,2048]{2,1,0:T(8,128)S(1)} %get-tuple-element.56.refs_2_.refs_4_, f32[3,24,2048]{2,1,0:T(8,128)S(1)} %get-tuple-element.60.refs_3_, ...), custom_call_target="tpu_custom_call" | custom-call | tf_op jit(solution)/shard_map/pallas_call | solution.py:49
  69.0 0.0 collective-permute-done.7.refs_1_
  69.0 0.0 collective-permute-done.8.refs_2_
  69.1 1.1 %shard_map.147 = (f32[3,3,16,2048]{3,2,1,0:T(8,128)S(1)}, f32[32,1,128]{2,1,0:T(1,128)S(1)}) custom-call(f32[3,3,16,2048]{3,2,1,0:T(8,128)S(1)} %shard_map.146.refs_0_, f32[3,16,2048]{2,1,0:T(8,128)S(1)} %collective-permute-done.7.refs_1_, f32[3,16,2048]{2,1,0:T(8,128)S(1)} %collective-permute-done.8.refs_2_, ...), custom_call_target="tpu_custom_call" | custom-call | tf_op jit(solution)/shard_map/pallas_call | solution.py:49
  70.1 17.8 %all_to_all.15.refs_0_ = f32[32,1,128]{2,1,0:T(1,128)S(1)} all-to-all(f32[32,1,128]{2,1,0:T(1,128)S(1)} %get-tuple-element.66), channel_id=1, replica_groups=mesh['tile'=8,'layer'=4] {'tile','layer'}, dimensions={0} | all-to-all | bytes 32768 | tf_op jit(solution)/shard_map/all_to_all | solution.py:548
  87.9 1.7 %shard_map.148 = (f32[3,3,16,2048]{3,2,1,0:T(8,128)}, f32[3,3,16,2048]{3,2,1,0:T(8,128)}, f32[1,1]{1,0:T(1,128)}) custom-call(f32[32,1,128]{2,1,0:T(1,128)S(1)} %all_to_all.15.refs_0_, f32[3,3,24,2048]{3,2,1,0:T(8,128)S(1)} %get-tuple-element.58.refs_0_.refs_1_, f32[3,3,16,2048]{3,2,1,0:T(8,128)S(1)} %get-tuple-element.67.refs_2_, ...), custom_call_target="tpu_custom_call" | custom-call | tf_op jit(solution)/shard_map/pallas_call | solution.py:49
  (9 shorter events, 0.0 us)
Async XLA Ops:
  3.8 20.9 %collective-permute-start = (f32[24,2048]{1,0:T(8,128)S(1)}, f32[24,2048]{1,0:T(8,128)S(1)}, u32[]{:S(2)}, u32[]{:S(2)}) collective-permute-start(f32[24,2048]{1,0:T(8,128)S(1)} %get-tuple-element.38), channel_id=1, source_target_pairs={{4,0},{8,4},{12,8},{16,12},{20,16},{24,20},{28,24},{5,1},{9,5},{13... | collective-permute-start | bytes 589832 | tf_op jit(solution)/shard_map/ppermute | solution.py:534
  5.1 19.6 %collective-permute-start.1 = (f32[24,2048]{1,0:T(8,128)S(1)}, f32[24,2048]{1,0:T(8,128)S(1)}, u32[]{:S(2)}, u32[]{:S(2)}) collective-permute-start(f32[24,2048]{1,0:T(8,128)S(1)} %get-tuple-element.39), channel_id=1, source_target_pairs={{0,4},{4,8},{8,12},{12,16},{16,20},{20,24},{24,28},{1,5},{5,9},{9,... | collective-permute-start | bytes 589832 | tf_op jit(solution)/shard_map/ppermute | solution.py:530
  10.6 14.0 %all-to-all-start = ((f32[32,1,768]{2,1,0:T(1,128)}), f32[32,1,768]{2,1,0:T(1,128)S(1)}, u32[]{:S(2)}, u32[]{:S(2)}) async-start(f32[32,1,768]{2,1,0:T(1,128)} %get-tuple-element.37), calls=%async_computation | async-start | bytes 196608 | tf_op jit(solution)/shard_map/all_to_all | solution.py:548
  16.9 3.1 %collective-permute-start.2 = (f32[1,16,2048]{2,1,0:T(8,128)S(1)}, f32[1,16,2048]{2,1,0:T(8,128)S(1)}, u32[]{:S(2)}, u32[]{:S(2)}) collective-permute-start(f32[1,16,2048]{2,1,0:T(8,128)S(1)} %get-tuple-element.41), channel_id=1, source_target_pairs={{0,1},{1,2},{2,3},{4,5},{5,6},{6,7},{8,9},{9,10},{10,11},{12,13},{... | collective-permute-start | bytes 393224 | tf_op jit(solution)/shard_map/ppermute | solution.py:530
  20.0 4.4 %copy-start.1 = (f32[1,16,2048]{2,1,0:T(8,128)}, f32[1,16,2048]{2,1,0:T(8,128)S(1)}, u32[]{:S(2)}) copy-start(f32[1,16,2048]{2,1,0:T(8,128)S(1)} %collective-permute-done.2.refs_5_.refs_12_) | copy-start | bytes 393220
  24.7 0.7 copy-start.2
  25.4 0.9 %copy-start.3 = (f32[24,2048]{1,0:T(8,128)S(1)}, f32[24,2048]{1,0:T(8,128)}, u32[]{:S(2)}) copy-start(f32[24,2048]{1,0:T(8,128)} %copy-done.2) | copy-start | bytes 589828
  26.9 7.2 %collective-permute-start.3 = (f32[5,24,2048]{2,1,0:T(8,128)S(1)}, f32[5,24,2048]{2,1,0:T(8,128)S(1)}, u32[]{:S(2)}, u32[]{:S(2)}) collective-permute-start(f32[5,24,2048]{2,1,0:T(8,128)S(1)} %get-tuple-element.51.refs_0_), channel_id=1, source_target_pairs={{0,1},{1,0},{2,3},{3,2},{4,5},{5,4},{6,7},{7,6},{8,9},{9,8},{10,11... | collective-permute-start | bytes 2949128 | tf_op jit(solution)/shard_map/ppermute | solution.py:538
  34.1 12.6 %copy-start = (f32[5,24,2048]{2,1,0:T(8,128)}, f32[5,24,2048]{2,1,0:T(8,128)S(1)}, u32[]{:S(2)}) copy-start(f32[5,24,2048]{2,1,0:T(8,128)S(1)} %collective-permute-done.3.refs_1_.refs_8_) | copy-start | bytes 2949124
  35.7 23.3 %collective-permute-start.4 = (f32[2,24,2048]{2,1,0:T(8,128)S(1)}, f32[2,24,2048]{2,1,0:T(8,128)}, u32[]{:S(2)}, u32[]{:S(2)}) collective-permute-start(f32[2,24,2048]{2,1,0:T(8,128)S(1)} %get-tuple-element.57), channel_id=1, source_target_pairs={{0,2},{1,3},{2,0},{3,1},{4,6},{5,7},{6,4},{7,5},{8,10},{9,11},{10,... | collective-permute-start | bytes 1179656 | tf_op jit(solution)/shard_map/ppermute | solution.py:538
  38.1 12.3 %collective-permute-start.5 = (f32[40,2048]{1,0:T(8,128)}, f32[40,2048]{1,0:T(8,128)}, u32[]{:S(2)}, u32[]{:S(2)}) collective-permute-start(f32[40,2048]{1,0:T(8,128)} %get-tuple-element.42), channel_id=1, source_target_pairs={{4,0},{8,4},{12,8},{16,12},{20,16},{24,20},{28,24},{5,1},{9,5},{13... | collective-permute-start | bytes 983048 | tf_op jit(solution)/shard_map/ppermute | solution.py:534
  39.4 19.3 %collective-permute-start.6 = (f32[40,2048]{1,0:T(8,128)}, f32[40,2048]{1,0:T(8,128)}, u32[]{:S(2)}, u32[]{:S(2)}) collective-permute-start(f32[40,2048]{1,0:T(8,128)} %get-tuple-element.43), channel_id=1, source_target_pairs={{0,4},{4,8},{8,12},{12,16},{16,20},{20,24},{24,28},{1,5},{5,9},{9,... | collective-permute-start | bytes 983048 | tf_op jit(solution)/shard_map/ppermute | solution.py:530
  46.8 12.2 %all-to-all-start.1 = ((f32[32,1,1280]{2,1,0:T(1,128)}), f32[32,1,1280]{2,1,0:T(1,128)S(1)}, u32[]{:S(2)}, u32[]{:S(2)}) async-start(f32[32,1,1280]{2,1,0:T(1,128)} %shard_map.144), calls=%async_computation.1 | async-start | bytes 327680 | tf_op jit(solution)/shard_map/all_to_all | solution.py:548
  66.5 2.6 %collective-permute-start.7 = (f32[3,16,2048]{2,1,0:T(8,128)S(1)}, f32[3,16,2048]{2,1,0:T(8,128)S(1)}, u32[]{:S(2)}, u32[]{:S(2)}) collective-permute-start(f32[3,16,2048]{2,1,0:T(8,128)S(1)} %get-tuple-element.62), channel_id=1, source_target_pairs={{0,1},{1,0},{2,3},{3,2},{4,5},{5,4},{6,7},{7,6},{8,9},{9,8},{10,11... | collective-permute-start | bytes 1179656 | tf_op jit(solution)/shard_map/ppermute | solution.py:538
  66.9 2.1 %collective-permute-start.8 = (f32[3,16,2048]{2,1,0:T(8,128)S(1)}, f32[3,16,2048]{2,1,0:T(8,128)S(1)}, u32[]{:S(2)}, u32[]{:S(2)}) collective-permute-start(f32[3,16,2048]{2,1,0:T(8,128)S(1)} %get-tuple-element.63), channel_id=1, source_target_pairs={{1,2},{2,1},{5,6},{6,5},{9,10},{10,9},{13,14},{14,13},{17,18},{18,... | collective-permute-start | bytes 1179656 | tf_op jit(solution)/shard_map/ppermute | solution.py:544

commit v5 on v4

v5 whole, which is shorter than its diff:
```python
import functools
import jax
import jax.numpy as jnp
from jax import lax
from jax.experimental import pallas as pl
from jax.experimental.pallas import tpu as pltpu
from jax.sharding import PartitionSpec as P

F32 = jnp.float32
BF16 = jnp.bfloat16
I32 = jnp.int32
BOTH = ("tile", "layer")
VM = pl.BlockSpec(memory_space=pltpu.VMEM)
LIMIT = 16 << 20


def hbm(shape):
    return jax.ShapeDtypeStruct(shape, F32)


def vmem(shape, dtype=F32):
    return pltpu.VMEM(shape, dtype)


def staged(kernel, where, outs, kept, column, *refs):
    count, sems = (len(where), refs[-1])
    held = list(refs[count + outs + len(kept) : -1])
    target = dict(zip(kept, refs[count + outs : count + outs + len(kept)]))
    operands, copies = ([], [])
    for i, far in enumerate(where):
        if far:
            to = target[i] if i in target else held.pop(0)
            part = refs[i].at[:, 0] if i in column else refs[i]
            copies.append(pltpu.make_async_copy(part, to, sems.at[len(copies)]))
            operands.append(to)
        else:
            operands.append(refs[i])
    for copy in copies:
        copy.start()
    for copy in copies:
        copy.wait()
    kernel(*operands, *refs[count : count + outs])


def call(kernel, outs, args, far=(), keep=(), column=(), limit=LIMIT):
    where = [i in far for i in range(len(args))]
    spaces = [pltpu.HBM if w else pltpu.VMEM for w in where]
    every = (*outs, *(vmem(args[i].shape, args[i].dtype) for i in keep))
    return pl.pallas_call(
        functools.partial(staged, kernel, where, len(outs), tuple(keep), tuple(column)),
        out_shape=every,
        in_specs=[pl.BlockSpec(memory_space=s) for s in spaces],
        out_specs=(VM,) * len(every),
        scratch_shapes=[
            vmem(a.shape[:1] + a.shape[2:] if i in column else a.shape, a.dtype)
            for i, a in enumerate(args)
            if where[i] and i not in keep
        ]
        + [pltpu.SemaphoreType.DMA((max(1, sum(where)),))],
        compiler_params=pltpu.CompilerParams(vmem_limit_bytes=limit),
    )(*[pltpu.with_memory_space_constraint(a, s) for a, s in zip(args, spaces)])


def iota(shape, dim):
    return lax.broadcasted_iota(I32, shape, dim)


def split(x):
    one = x.astype(BF16)
    rest = x - one.astype(F32)
    two = rest.astype(BF16)
    three = (rest - two.astype(F32)).astype(BF16)
    return [one, two, three]


def fold(x):
    n = x.shape[0] // 3
    return x[:n] + (x[n : 2 * n] + x[2 * n :])


def onehot(index, size):
    return jnp.where(iota((size, index.shape[1]), 0) == index, 1.0, 0.0)


def dot(a, b):
    return lax.dot_general(a, b, (((1,), (0,)), ((), ())), preferred_element_type=F32)


def dot_nt(a, b):
    return lax.dot_general(a, b, (((1,), (1,)), ((), ())), preferred_element_type=F32)


def pick(table, hi, lo):
    rows, cols = table.shape
    parts = jnp.concatenate(split(table), 0)
    got = fold(dot(parts, onehot(lo, cols).astype(BF16)))
    return jnp.sum(got * onehot(hi, rows), axis=0, keepdims=True)


def spread(value, hi, lo, rows, cols):
    parts = [jnp.where(iota((rows, hi.shape[1]), 0) == hi, v.astype(F32), 0.0).astype(BF16) for v in split(value)]
    return fold(dot_nt(jnp.concatenate(parts, 0), onehot(lo, cols).astype(BF16)))


def pres_kernel(rhs, wts, cell, front, prod, pres, send):
    depth, width, long = pres.shape
    for z in range(depth):
        pres[z] = wts[0, z] * rhs[0, z] + wts[1, z] * rhs[1, z] + wts[2, z] * rhs[2, z]
    where = cell[...]
    table = pres[...].reshape(depth * width, long)
    value = prod[...] * pick(table, lax.div(where, long), lax.rem(where, long))
    both = jnp.concatenate([value, front[...].astype(F32), where.astype(F32)], 1)
    send[...] = jnp.broadcast_to(both[:, None], send.shape)


def is_right(level, axis="layer"):
    return (lax.axis_index(axis) >> level) % 2 == 1


def choose(level, mine, other, axis="layer"):
    right = is_right(level, axis)
    return (jnp.where(right, other, mine), jnp.where(right, mine, other))


def local_solve(rhs, upper, inv, tz):
    depth = len(rhs)
    y = [rhs[0] * inv[0]]
    for z in range(1, depth):
        y.append((rhs[z] + tz[z - 1] * y[-1]) * inv[z])
    for z in range(depth - 2, -1, -1):
        y[z] = y[z] + upper[z] * y[z + 1]
    return y


def factors(tz, store):
    depth = len(tz)
    gs, invs = ([], [])
    own = None
    for z in range(depth):
        own = store[z] if z == 0 else store[z] + gs[-1] * own
        invs.append(1.0 / (own + tz[z] if z < depth - 1 else own))
        gs.append(tz[z] * invs[-1])
    first = [invs[0]]
    for z in range(1, depth):
        first.append(tz[z - 1] * first[-1] * invs[z])
    final = [None] * depth
    final[-1] = invs[-1]
    for z in range(depth - 2, -1, -1):
        first[z] = first[z] + gs[z] * first[z + 1]
        final[z] = gs[z] * final[z + 1]
    return gs, invs, first, final, (first[0], first[-1], final[-1] + 1.0 / jnp.maximum(tz[-1], 1e-30))


def coef_kernel(tz, store, pres, answers, ends):
    depth = pres.shape[0]
    tzs = [tz[z] for z in range(depth)]
    gs, invs, first, final, coefs = factors(tzs, [store[z] for z in range(depth)])
    for z in range(depth):
        answers[z] = first[z]
        answers[depth + z] = final[z]
    y = local_solve([pres[z] for z in range(depth)], gs, invs, tzs)
    for i, value in enumerate((*coefs, y[0], y[-1], tzs[-1])):
        ends[i] = value


def pair(level, own, sib):
    af, af_ = choose(level, own[0], sib[0])
    c, c_ = choose(level, own[1], sib[1])
    b, b_ = choose(level, own[2], sib[2])
    return af, c, b, af_, c_, b_, 1.0 / (b + af_)


def join_coefs(level, own, sib):
    af, c, _, _, c_, b_, g = pair(level, own, sib)
    return (af - c * c * g, c * c_ * g, b_ - c_ * c_ * g)


def join_ends(level, own, sib, mine, other):
    _, c, _, _, c_, _, g = pair(level, own, sib)
    yf, yf_ = choose(level, mine[0], other[0])
    yl, yl_ = choose(level, mine[1], other[1])
    flux = g * (yl - yf_)
    return (yf - c * flux, yl_ + c_ * flux)


def join_kernel(level, own, sib, answers, out, face, more, one):
    depth, width, _ = more.shape
    depth = depth // 2
    _, c, _, _, c_, _, g = pair(level, own, sib)
    first, both, last = join_coefs(level, own, sib)
    yf, yl = join_ends(level, own, sib, (own[3], own[4]), (sib[3], sib[4]))
    out[0], out[1], out[2] = (first, both, last)
    out[3], out[4] = (yf, yl)
    lower = choose(level, own[5], sib[5])[1]
    out[5] = lower
    face[2] = lower
    right, later = (is_right(level), is_right(level + 1))
    face[0], face[1] = (jnp.where(later, first, last), jnp.where(later, yf, yl))
    cg, cg_ = (c * g, c_ * g)
    for z in range(depth):
        kf, kl = (answers[z], answers[depth + z])
        top = jnp.where(right, cg * kf, kf - cg * kl)
        bottom = jnp.where(right, kl - cg_ * kf, cg_ * kl)
        more[z] = top
        more[depth + z] = bottom
        one[z] = jnp.where(later, top, bottom)


def groups_of(levels):
    layers = lax.axis_size("layer")
    l = lax.axis_index("layer")
    base = lax.axis_index("tile") * layers
    out = [[base + l]]
    for level in range(levels):
        out.append([base + (((l >> level) ^ 1) << level) + i for i in range(1 << level)])
    return out


def front_kernel(recv, cell, prod, tables, inverse, send, held, sems):
    devices = recv.shape[0]
    count = recv.shape[2] // 3
    rows, length = inverse.shape
    lanes = 128
    chunks = sems.shape[0]
    wide = length // chunks
    cell, prod = (cell[...], prod[...])
    copies = [
        pltpu.make_async_copy(inverse.at[:, pl.ds(i * wide, wide)], held.at[:, pl.ds(i * wide, wide)], sems.at[i])
        for i in range(chunks)
    ]
    for copy in copies:
        copy.start()
    where, value = (cell, prod)
    depth, width, long = tables[-1].shape
    hi, lo = lax.div(where, long), lax.rem(where, long)
    stack = [t[k * depth : (k + 1) * depth].reshape(depth * width, long) for t in tables for k in range(t.shape[0] // depth)]
    parts = jnp.concatenate([p for table in stack for p in split(table)], 0)
    got = dot(parts, onehot(lo, long).astype(BF16))
    mask = onehot(hi, depth * width)
    n = 3 * depth * width
    found = [value * jnp.sum(fold(got[i * n : (i + 1) * n]) * mask, axis=0, keepdims=True) for i in range(len(stack))]
    total = jnp.zeros((length // lanes, lanes), F32)
    group = 8
    for first in range(0, devices, group):
        lefts, rights = ([], [])
        for d in range(first, first + group):
            term = recv[d, :, :count]
            index = recv[d, :, count : 2 * count].astype(I32)
            hi, lo = lax.div(index, lanes), lax.rem(index, lanes)
            hit = iota((length // lanes, count), 0) == hi
            lefts.append(jnp.concatenate([jnp.where(hit, v.astype(F32), 0.0).astype(BF16) for v in split(term)], 0))
            rights.append(onehot(lo, lanes).astype(BF16))
        total = total + fold(dot_nt(jnp.concatenate(lefts, 1), jnp.concatenate(rights, 1)))
    acc = jnp.zeros((rows, lanes), F32)
    for i in range(chunks):
        copies[i].wait()
        for r in range(i * wide // lanes, (i + 1) * wide // lanes):
            acc = acc + held[:, r * lanes : (r + 1) * lanes] * total[r : r + 1]
    parts = jnp.concatenate(split(acc), 1)
    out = dot_nt(jnp.ones((8, parts.shape[1]), BF16), parts)
    send[...] = jnp.broadcast_to(jnp.concatenate([out[0:1], value, *found], 1)[:, None], send.shape)


def gathered(values, rows_hot, lanes_hot, start, size, ext, parts):
    hot = lanes_hot[:, start : start + size]
    pieces = [hot * p for v in values for p in split(v)[:parts]]
    got = dot_nt(rows_hot[:, start : start + size], jnp.concatenate(pieces, 0))
    planes = []
    lanes = hot.shape[0]
    for i in range(len(values)):
        plane = got[:, i * parts * lanes : (i * parts + 1) * lanes]
        for k in range(1, parts):
            j = i * parts + k
            plane = plane + got[:, j * lanes : (j + 1) * lanes]
        planes.append(jnp.concatenate([plane[r : r + ext] for r in range(0, plane.shape[0], ext)], 1))
    return planes


def beside(centre, tx, ty):
    width, long = centre.shape
    row, col = (iota(centre.shape, 0), iota(centre.shape, 1))
    total = tx * jnp.where(row == width - 1, 0.0, pltpu.roll(centre, width - 1, 0))
    total = total + jnp.where(row == 0, 0.0, pltpu.roll(tx * centre, 1, 0))
    total = total + ty * jnp.where(col == long - 1, 0.0, pltpu.roll(centre, long - 1, 1))
    return total + jnp.where(col == 0, 0.0, pltpu.roll(ty * centre, 1, 1))


def tile_rows(first, last, one, two):
    odd = is_right(0, "tile")
    one[...] = jnp.where(odd, first, last)
    two[...] = jnp.where(odd, last, first)


def pressure_kernel(levels, *refs):
    (recv, terms, tz, store, pres), refs = (refs[:5], refs[5:])
    sib, refs = (refs[:levels], refs[levels:])
    far, refs = (refs[:5], refs[5:])
    (p, coupled_z, one, two), near_by, refs = (refs[:4], refs[4:9], refs[9:])
    rows_hot, lanes_hot, sol_hot, sol_row, sems = refs
    copies = [pltpu.make_async_copy(a, b, sems.at[i]) for i, (a, b) in enumerate(zip(far, near_by))]
    for copy in copies:
        copy.start()
    tx = near_by[0]
    depth, width, long = pres.shape
    rows = sol_hot.shape[0]
    count = terms.shape[2] // 3
    lanes = 128
    groups = groups_of(levels)
    at = 0
    layer = None
    for members in groups:
        for device in members:
            entry = terms[device]
            index = entry[:, count : 2 * count].astype(I32)
            cell = entry[:, 2 * count :].astype(I32)
            y, x = lax.rem(cell, long), lax.rem(lax.div(cell, long), width)
            here = pl.ds(at, count)
            rows_hot[:, here] = onehot(lax.div(y, lanes) * width + x, rows_hot.shape[0]).astype(BF16)
            lanes_hot[:, here] = onehot(lax.rem(y, lanes), lanes).astype(BF16)
            sol_hot[:, here] = onehot(lax.rem(index, rows), rows).astype(BF16)
            sol_row[:, here] = lax.div(index, rows)
            if layer is None:
                layer = lax.div(cell, long * width)
            at += count
    table = jnp.concatenate(split(recv[...].reshape(recv.shape[0], recv.shape[2])[:, :rows]), 0)
    sol = fold(dot(table, sol_hot[...]))
    sol = jnp.sum(jnp.where(iota(sol.shape, 0) == sol_row[...], sol, 0.0), axis=0, keepdims=True)

    def listed(group, column):
        at = rows + column * count
        return jnp.concatenate([recv[device][:, at : at + count] for device in group], 1)

    tzs = [tz[z] for z in range(depth)]
    gs, invs, first, final, coefs = factors(tzs, [store[z] for z in range(depth)])
    own = [coefs]
    value = listed(groups[0], 0) * sol[:, :count]
    values = [jnp.where(layer == z, value, 0.0) for z in range(depth)]
    change = gathered(values, rows_hot, lanes_hot, 0, count, width, 3)
    y = local_solve([pres[z] - change[z] for z in range(depth)], gs, invs, tzs)
    mine = (y[0], y[-1])
    steps = []
    start = count
    for level in range(levels):
        size = len(groups[level + 1]) * count
        top = level == levels - 1
        columns = [1 + 2 * level] if top else [1 + 2 * level, 2 + 2 * level]
        values = [listed(groups[level + 1], c) * sol[:, start : start + size] for c in columns]
        change = gathered(values, rows_hot, lanes_hot, start, size, width, 3)
        start += size
        if top:
            other = sib[level][1] - change[0]
            steps.append((mine, (other, other)))
        else:
            other = (sib[level][3] - change[0], sib[level][4] - change[1])
            steps.append((mine, other))
            mine = join_ends(level, own[level], sib[level], mine, other)
            own.append(join_coefs(level, own[level], sib[level]))
    above = below = jnp.zeros((width, long), F32)
    tzp = jnp.zeros((width, long), F32)
    place = lax.axis_index("layer")
    for level in range(levels - 1, -1, -1):
        mine, other = steps[level]
        yl, _ = choose(level, mine[1], other[1])
        _, yf_ = choose(level, mine[0], other[0])
        flux = yl - yf_
        if level == levels - 1:
            b, _ = choose(level, own[level][2], sib[level][0])
            _, af_ = choose(level, own[level][0], sib[level][0])
            g = 1.0 / (b + af_)
            before = sib[level][2]
        else:
            _, c, _, _, c_, _, g = pair(level, own[level], sib[level])
            flux = flux + c * above - c_ * below
            before = sib[level][5]
        tzp = jnp.where(place % (2 << level) == 1 << level, before, tzp)
        flux = g * flux
        right = is_right(level)
        above, below = (jnp.where(right, flux, above), jnp.where(right, below, -flux))
    values = [y[z] + first[z] * above + final[z] * below for z in range(depth)]
    is_last = place == (1 << levels) - 1
    for z in range(depth):
        p[z] = values[z]
        total = above + tzp * values[z] if z == 0 else tzs[z - 1] * values[z - 1]
        if z == depth - 1:
            coupled_z[z] = total + jnp.where(is_last, 0.0, below + tzs[z] * values[z])
        else:
            coupled_z[z] = total + tzs[z] * values[z + 1]
    for copy in copies:
        copy.wait()
    for z in range(depth):
        tile_rows(values[z][0:1], (tx[z] * values[z])[width - 1 :], one.at[z], two.at[z])


def search_kernel(p, coupled_z, one, two, tx, ty, tz, rhs, diag, binv, s, row_one, row_two, inner, outer):
    depth, width, _ = p.shape
    odd = is_right(0, "tile")
    right = is_right(0)
    row = iota(p.shape[1:], 0)
    for z in range(depth):
        centre = p[z]
        after = jnp.where(odd, two[z], one[z])
        before = jnp.where(odd, one[z], two[z])
        coupled = coupled_z[z] + beside(centre, tx[z], ty[z])
        coupled = coupled + jnp.where(row == 0, before, 0.0) + jnp.where(row == width - 1, tx[z] * after, 0.0)
        remain = [rhs[c, z] - diag[c, 0, z] * centre for c in range(3)]
        remain[0] = remain[0] + coupled
        for c in range(3):
            value = binv[c, 0, z] * remain[0] + binv[c, 1, z] * remain[1] + binv[c, 2, z] * remain[2]
            if c == 0:
                value = centre + value
            s[c, z] = value
            tile_rows(value[0:1], (tx[z] * value)[width - 1 :], row_one.at[c, z], row_two.at[c, z])
    for c in range(3):
        top, bottom = (s[c, 0], tz[depth - 1] * s[c, depth - 1])
        inner[c] = jnp.where(right, top, bottom)
        outer[c] = jnp.where(right, bottom, top)


def inner_kernel(s, diag, tz, tx, ty, image):
    depth = s.shape[1]
    for z in range(depth):
        for c in range(3):
            total = diag[c, 0, z] * s[0, z] + diag[c, 1, z] * s[1, z] + diag[c, 2, z] * s[2, z]
            total = total - beside(s[c, z], tx[z], ty[z])
            if z:
                total = total - tz[z - 1] * s[c, z - 1]
            if z < depth - 1:
                total = total - tz[z] * s[c, z + 1]
            image[c, z] = total


def image_kernel(part, row_one, row_two, inner, outer, rhs, tz, tx, image, send):
    depth, width = part.shape[1:3]
    right, odd = (is_right(0), is_right(0, "tile"))
    row = iota(part.shape[2:], 0)
    along = power = start = 0.0
    for z in range(depth):
        for c in range(3):
            value = part[c, z]
            if z == 0:
                value = value - jnp.where(right, inner[c], outer[c])
            if z == depth - 1:
                value = value - tz[z] * jnp.where(right, outer[c], inner[c])
            after = jnp.where(odd, row_two[c, z], row_one[c, z])
            before = jnp.where(odd, row_one[c, z], row_two[c, z])
            value = value - jnp.where(row == 0, before, 0.0) - jnp.where(row == width - 1, tx[z] * after, 0.0)
            image[c, z] = value
            given = rhs[c, z]
            along = along + value * given
            power = power + value * value
            start = start + given * given
    along, power, start = (jnp.sum(along), jnp.sum(power), jnp.sum(start))
    omega = along / jnp.where(power > 0.0, power, 1.0)
    square = cross = 0.0
    for z in range(depth):
        for c in range(3):
            value = image[c, z]
            left = rhs[c, z] - omega * value
            square = square + left * left
            cross = cross + left * value
    lane = iota((1, send.shape[2]), 1)
    out = jnp.zeros((1, send.shape[2]), F32)
    for i, value in enumerate((along, power, start, jnp.sum(square), jnp.sum(cross), omega)):
        out = jnp.where(lane == i, value, out)
    send[...] = jnp.broadcast_to(out[:, None], send.shape)


def finish_kernel(recv, s, image, rhs, update, lin_res, ratio):
    sums = recv[...].reshape(recv.shape[0], recv.shape[2])
    whole = jnp.sum(sums, axis=0, keepdims=True)
    omega = whole[:, 0:1] / whole[:, 1:2]
    shift = sums[:, 5:6] - omega
    square = sums[:, 3:4] + 2.0 * shift * sums[:, 4:5] + shift * shift * sums[:, 1:2]
    ratio[...] = jnp.sqrt(jnp.sum(square, axis=0, keepdims=True) / whole[:, 2:3])
    for c in range(3):
        for z in range(s.shape[1]):
            update[c, z] = omega * s[c, z]
            lin_res[c, z] = rhs[c, z] - omega * image[c, z]


def flip(x, level, axis="layer"):
    return lax.ppermute(x, axis, [(i, i ^ (1 << level)) for i in range(lax.axis_size(axis))])


def neighbour(x, axis="layer"):
    pairs = [(i, i + 1) for i in range(1, lax.axis_size(axis) - 1, 2)]
    return lax.ppermute(x, axis, pairs + [(j, i) for i, j in pairs])


def everywhere(x):
    return lax.all_to_all(x, BOTH, split_axis=0, concat_axis=0, tiled=True)


def shards(rhs, weights, block_diag, block_inv, tx, ty, tz, store, cell, front, prod, inverse):
    layers = lax.axis_size("layer")
    devices = lax.axis_size("tile") * layers
    levels = layers.bit_length() - 1
    depth, width, long = tx.shape
    count = cell.shape[0]
    rows = inverse.shape[0]
    lists = layers * count
    cell, front, prod = (cell.reshape(1, -1), front.reshape(1, -1), prod.reshape(1, -1))
    field = vmem(tx.shape)

    def planes(n):
        return vmem((n, width, long))

    pres, send = call(
        pres_kernel, (field, vmem((devices, 1, 3 * count))), (rhs, weights, cell, front, prod), far=range(5)
    )
    terms = everywhere(send)
    pres, tz, store = lax.optimization_barrier((pres, tz, store))
    answers, ends, tz_v, store_v = call(
        coef_kernel, (planes(2 * depth), planes(6)), (tz, store, pres), far=(0, 1), keep=(0, 1)
    )
    sib, tables = ([], [])
    last = answers
    for level in range(levels - 1):
        tables.append(answers)
        sib.append(flip(ends, level))
        ends, face, answers, last = call(
            functools.partial(join_kernel, level), (planes(6), planes(3), planes(2 * depth), field), (ends, sib[-1], answers)
        )
    tables.append(last)
    sib.append(flip(face, levels - 1))
    chunks = 8
    hbm_spec = pl.BlockSpec(memory_space=pltpu.HBM)
    terms, *tables = lax.optimization_barrier((terms, *tables))
    send = pl.pallas_call(
        front_kernel,
        out_shape=vmem((devices, 1, rows + 2 * levels * count)),
        in_specs=[VM, VM, VM, [VM] * len(tables), hbm_spec],
        out_specs=VM,
        scratch_shapes=[vmem(inverse.shape), pltpu.SemaphoreType.DMA((chunks,))],
        compiler_params=pltpu.CompilerParams(vmem_limit_bytes=LIMIT),
    )(terms, cell, prod, tables, pltpu.with_memory_space_constraint(inverse, pltpu.HBM))
    sol = everywhere(send)
    far = (tx, ty, rhs, block_diag, block_inv)
    args = (sol, terms, tz_v, store_v, pres, *sib)
    row3 = vmem((depth, 1, long))
    p, coupled_z, one, two, tx, ty, rhs, diag, binv = pl.pallas_call(
        functools.partial(pressure_kernel, levels),
        out_shape=(field, field, row3, row3) + tuple(vmem(a.shape) for a in far),
        in_specs=[VM] * len(args) + [hbm_spec] * len(far),
        out_specs=(VM,) * 9,
        scratch_shapes=[
            vmem((width * long // 128, lists), BF16),
            vmem((128, lists), BF16),
            vmem((rows, lists), BF16),
            vmem((1, lists), I32),
            pltpu.SemaphoreType.DMA((len(far),)),
        ],
        compiler_params=pltpu.CompilerParams(vmem_limit_bytes=LIMIT),
    )(
        *[pltpu.with_memory_space_constraint(a, pltpu.VMEM) for a in args],
        *[pltpu.with_memory_space_constraint(a, pltpu.HBM) for a in far],
    )
    one, two = (flip(one, 0, "tile"), neighbour(two, "tile"))
    row9 = vmem((3, depth, 1, long))
    plane3 = planes(3)
    s, row_one, row_two, inner, outer = call(
        search_kernel,
        (vmem(rhs.shape), row9, row9, plane3, plane3),
        (p, coupled_z, one, two, tx, ty, tz_v, rhs, diag, binv),
    )
    inner, outer = (flip(inner, 0), neighbour(outer))
    row_one, row_two = (flip(row_one, 0, "tile"), neighbour(row_two, "tile"))
    (part,) = call(inner_kernel, (vmem(rhs.shape),), (s, diag, tz_v, tx, ty))
    image, send = call(
        image_kernel,
        (vmem(rhs.shape), vmem((devices, 1, 128))),
        (part, row_one, row_two, inner, outer, rhs, tz_v, tx),
    )
    sums = everywhere(send)
    update, lin_res, ratio = call(
        finish_kernel, (hbm(rhs.shape), hbm(rhs.shape), hbm((1, 1))), (sums, s, image, rhs)
    )
    return (update, lin_res, ratio.reshape(()))


def solution(mesh):
    return jax.shard_map(
        shards,
        mesh=mesh,
        in_specs=(
            P(None, "layer", "tile", None),
            P(None, "layer", "tile", None),
            P(None, None, "layer", "tile", None),
            P(None, None, "layer", "tile", None),
            P("layer", "tile", None),
            P("layer", "tile", None),
            P("layer", "tile", None),
            P("layer", "tile", None),
            P(("tile", "layer")),
            P(("tile", "layer")),
            P(("tile", "layer")),
            P(("tile", "layer"), None),
        ),
        out_specs=(P(None, "layer", "tile", None), P(None, "layer", "tile", None), P()),
        check_vma=False,
    )
```

time: 90.1 us -> 73.4 us (0.81)
  starting transfers between devices: 31.8 us -> 16.9 us
  blocking collectives: 17.8 us -> 26.1 us
  Pallas kernels: 27.8 us -> 20 us
  waiting for transfers between devices: 9.79 us -> 6.7 us
    ppermute x9 -> x8, starting transfers between devices: 21.9 us -> 9.98 us  [the longest x5 8 us: flip(): lax.ppermute(x, axis, [(i, i ^ 1 << level) for i in range(lax.axis_size(a...]
    all_to_all x1 -> x2, blocking collectives: 17.8 us -> 26.1 us  [everywhere(): return lax.all_to_all(x, BOTH, split_axis=0, concat_axis=0, tiled=True)]
    ppermute x9 -> x8, waiting for transfers between devices: 9.23 us -> 2.89 us  [the longest x5 2.89 us: flip(): lax.ppermute(x, axis, [(i, i ^ 1 << level) for i in range(lax.axis_size(a...]
    pallas_call x8 -> x7, Pallas kernels: 15.8 us -> 10.5 us  [call(): pl.pallas_call(functools.partial(staged, kernel, where, len(outs), tuple(...]
    all_to_all x2 -> x1, waiting for transfers between devices: 0.56 us -> 3.81 us  [everywhere(): return lax.all_to_all(x, BOTH, split_axis=0, concat_axis=0, tiled=True)]
    all_to_all x2 -> x1, starting transfers between devices: 9.88 us -> 6.96 us  [everywhere(): return lax.all_to_all(x, BOTH, split_axis=0, concat_axis=0, tiled=True)]
    pallas_call x2, Pallas kernels: 12 us -> 9.48 us  [the longest x1 5.05 us: shards(): pl.pallas_call(front_kernel, out_shape=vmem((devices, 1, rows + 2 * level...]
    unnamed x8 -> x12, local copies, waits for them, and re-layouts: 1.61 us -> 2.5 us
  transfers between devices with their start and end apart: 11 -> 9, of which waited for: 4 -> 3; matrix products, arithmetic and copies ran while one was open for 0% -> 0% of each run, Pallas kernels for 14% -> 11%
where the time goes in v5:
time: 73.4 us; the launch traced here: 73.1 us
  blocking collectives  26.1 us (36%)
  Pallas kernels  20 us (27%)
  starting transfers between devices  16.9 us (23%)
  waiting for transfers between devices  6.7 us (9%)
  local copies, waits for them, and re-layouts  2.5 us (3%)
  between operations  0.79 us (1%)
    all_to_all x2, blocking collectives, everywhere(): return lax.all_to_all(x, BOTH, split_axis=0, concat_axis=0, tiled=True)  26.1 us
    pallas_call x7, Pallas kernels, call(): pl.pallas_call(functools.partial(staged, kernel, where, len(outs), tuple(...  10.5 us
    ppermute x5, starting transfers between devices, flip(): lax.ppermute(x, axis, [(i, i ^ 1 << level) for i in range(lax.axis_size(a...  8 us
    all_to_all x1, starting transfers between devices, everywhere(): return lax.all_to_all(x, BOTH, split_axis=0, concat_axis=0, tiled=True)  6.96 us
    pallas_call x1, Pallas kernels, shards(): pl.pallas_call(front_kernel, out_shape=vmem((devices, 1, rows + 2 * level...  5.05 us
    pallas_call x1, Pallas kernels, shards(): pl.pallas_call(functools.partial(pressure_kernel, levels), out_shape=(fie...  4.42 us
    all_to_all x1, waiting for transfers between devices, everywhere(): return lax.all_to_all(x, BOTH, split_axis=0, concat_axis=0, tiled=True)  3.81 us
    ppermute x5, waiting for transfers between devices, flip(): lax.ppermute(x, axis, [(i, i ^ 1 << level) for i in range(lax.axis_size(a...  2.89 us
  transfers between devices with their start and end apart: 9, of which 3 were waited for; matrix products, arithmetic and copies ran while one was open for 0% of the time, Pallas kernels for 11%

profile of v5, /device:TPU:0, one launch (start us, length us, event | category | flops | bytes accessed | tf_op | source)
XLA Modules:
  0.0 73.1 jit_solution(17673947005077056626)
XLA Ops:
  0.6 2.8 %shard_map.139 = (f32[3,16,2048]{2,1,0:T(8,128)S(1)}, f32[32,1,768]{2,1,0:T(1,128)}) custom-call(f32[3,3,16,2048]{3,2,1,0:T(8,128)} %refs_9_.1, f32[3,3,16,2048]{3,2,1,0:T(8,128)} %refs_1_.1, s32[1,256]{1,0:T(1,128)} %bitcast.4, s32[1,256]{1,0:T(1,128)} %bitcast.8, f32[1,256]{1,0:T(1,128)} %bitcast.6), custom_call_target="tpu_custom_call" | custom-call | tf_op jit(solution)/shard_map/pallas_call | solution.py:49
  3.4 1.3 %shard_map.140 = (f32[6,16,2048]{2,1,0:T(8,128)S(1)}, f32[6,16,2048]{2,1,0:T(8,128)S(1)}, f32[3,16,2048]{2,1,0:T(8,128)S(1)}, f32[3,16,2048]{2,1,0:T(8,128)S(1)}) custom-call(f32[3,16,2048]{2,1,0:T(8,128)} %refs_0_.2, f32[3,16,2048]{2,1,0:T(8,128)} %refs_1_.2, f32[3,16,2048]{2,1,0:T(8,128)S(1)} %get-tuple-element.40.refs_2_.refs_4_), custom_call_target="tpu_custom_call" | custom-call | tf_op jit(solution)/shard_map/pallas_call | solution.py:49
  4.8 0.7 %copy-done = f32[3,16,2048]{2,1,0:T(8,128)} copy-done((f32[3,16,2048]{2,1,0:T(8,128)}, f32[3,16,2048]{2,1,0:T(8,128)S(1)}, u32[]{:S(2)}) %copy-start) | copy-done | bytes 393240
  5.5 0.5 collective-permute-start
  6.0 7.0 %all-to-all-start = ((f32[32,1,768]{2,1,0:T(1,128)}), f32[32,1,768]{2,1,0:T(1,128)S(1)}, u32[]{:S(2)}, u32[]{:S(2)}) async-start(f32[32,1,768]{2,1,0:T(1,128)} %get-tuple-element.36), calls=%async_computation | async-start | bytes 196608 | tf_op jit(solution)/shard_map/all_to_all | solution.py:491
  13.0 0.0 collective-permute-done.refs_1_.refs_5_
  13.0 0.0 copy-start.4
  13.0 0.0 copy-start.5
  13.0 1.4 %shard_map.141 = (f32[6,16,2048]{2,1,0:T(8,128)}, f32[3,16,2048]{2,1,0:T(8,128)}, f32[6,16,2048]{2,1,0:T(8,128)}, f32[3,16,2048]{2,1,0:T(8,128)S(1)}) custom-call(f32[6,16,2048]{2,1,0:T(8,128)S(1)} %get-tuple-element.42.refs_0_, f32[6,16,2048]{2,1,0:T(8,128)S(1)} %collective-permute-done.refs_1_.refs_5_, f32[6,16,2048]{2,1,0:T(8,128)S(1)} %get-tuple-element.45.refs_2_.tables_0_), custom_call_target="tpu_custom_call" | custom-call | tf_op jit(solution)/shard_map/pallas_call | solution.py:49
  14.4 0.0 copy-start.2
  14.5 0.7 %copy-done.2 = f32[3,16,2048]{2,1,0:T(8,128)} copy-done((f32[3,16,2048]{2,1,0:T(8,128)}, f32[3,16,2048]{2,1,0:T(8,128)S(1)}, u32[]{:S(2)}) %copy-start.2) | copy-done | bytes 393240
  15.2 1.8 %collective-permute-start.1 = (f32[3,16,2048]{2,1,0:T(8,128)}, f32[3,16,2048]{2,1,0:T(8,128)S(1)}, u32[]{:S(2)}, u32[]{:S(2)}) collective-permute-start(f32[3,16,2048]{2,1,0:T(8,128)} %get-tuple-element.49), channel_id=1, source_target_pairs={{0,2},{1,3},{2,0},{3,1},{4,6},{5,7},{6,4},{7,5},{8,10},{9,11},{10,... | collective-permute-start | bytes 1179656 | tf_op jit(solution)/shard_map/ppermute | solution.py:482
  17.0 3.8 %all-to-all-done.recv.refs_1_ = f32[32,1,768]{2,1,0:T(1,128)S(1)} async-done(((f32[32,1,768]{2,1,0:T(1,128)}), f32[32,1,768]{2,1,0:T(1,128)S(1)}, u32[]{:S(2)}, u32[]{:S(2)}) %all-to-all-start) | async-done | bytes 98336 | tf_op jit(solution)/shard_map/all_to_all | solution.py:491
  20.8 1.0 %copy-done.3 = f32[3,16,2048]{2,1,0:T(8,128)S(1)} copy-done((f32[3,16,2048]{2,1,0:T(8,128)S(1)}, f32[3,16,2048]{2,1,0:T(8,128)}, u32[]{:S(2)}) %copy-start.3) | copy-done | bytes 393240
  21.8 5.1 %shard_map.142 = f32[32,1,1280]{2,1,0:T(1,128)S(1)} custom-call(f32[32,1,768]{2,1,0:T(1,128)S(1)} %all-to-all-done.recv.refs_1_, s32[1,256]{1,0:T(1,128)S(1)} %bitcast.5, f32[1,256]{1,0:T(1,128)S(1)} %bitcast.7, f32[6,16,2048]{2,1,0:T(8,128)S(1)} %get-tuple-element.45.refs_2_.tables_0_, f32[3,16,2048]{2,1,0:T(8,128)S(1)} %copy-done.3, f32[256,8192]{1,0:T(8,128)} %inverse.1), custom_call_target="tpu_custom_call" | custom-call | tf_op jit(solution)/shard_map/pallas_call | solution.py:529
  26.8 10.3 %all_to_all.15.refs_0_ = f32[32,1,1280]{2,1,0:T(1,128)S(1)} all-to-all(f32[32,1,1280]{2,1,0:T(1,128)S(1)} %shard_map.142), channel_id=1, replica_groups=mesh['tile'=8,'layer'=4] {'tile','layer'}, dimensions={0} | all-to-all | bytes 327680 | tf_op jit(solution)/shard_map/all_to_all | solution.py:491
  37.1 0.0 collective-permute-done.1.refs_6_
  37.1 4.4 %shard_map.143 = (f32[3,16,2048]{2,1,0:T(8,128)S(1)}, f32[3,16,2048]{2,1,0:T(8,128)S(1)}, f32[3,1,2048]{2,1,0:T(1,128)S(1)}, f32[3,1,2048]{2,1,0:T(1,128)S(1)}, ...) custom-call(f32[32,1,1280]{2,1,0:T(1,128)S(1)} %all_to_all.15.refs_0, ...), custom_call_target="tpu_custom_call" | custom-call | tf_op jit(solution)/shard_map/pallas_call | solution.py:541
  41.6 0.8 %collective-permute-start.2 = (f32[3,1,2048]{2,1,0:T(1,128)S(1)}, f32[3,1,2048]{2,1,0:T(1,128)S(1)}, u32[]{:S(2)}, u32[]{:S(2)}) collective-permute-start(f32[3,1,2048]{2,1,0:T(1,128)S(1)} %get-tuple-element.52), channel_id=1, source_target_pairs={{0,4},{4,0},{8,12},{12,8},{16,20},{20,16},{24,28},{28,24},{1,5},{5... | collective-permute-start | bytes 73736 | tf_op jit(solution)/shard_map/ppermute | solution.py:482
  42.4 0.7 collective-permute-start.3
  43.1 2.4 %collective-permute-done.2.refs_2_ = f32[3,1,2048]{2,1,0:T(1,128)S(1)} collective-permute-done((f32[3,1,2048]{2,1,0:T(1,128)S(1)}, f32[3,1,2048]{2,1,0:T(1,128)S(1)}, u32[]{:S(2)}, u32[]{:S(2)}) %collective-permute-start.2) | collective-permute-done | bytes 24608 | tf_op jit(solution)/shard_map/ppermute | solution.py:482
  45.5 0.0 collective-permute-done.3.refs_3_
  45.5 0.9 %shard_map.144 = (f32[3,3,16,2048]{3,2,1,0:T(8,128)S(1)}, f32[3,3,1,2048]{3,2,1,0:T(1,128)S(1)}, f32[3,3,1,2048]{3,2,1,0:T(1,128)S(1)}, f32[3,16,2048]{2,1,0:T(8,128)S(1)}, f32[3,16,2048]{2,1,0:T(8,128)S(1)}) custom-call(f32[3,16,2048]{2,1,0:T(8,128)S(1)} %get-tuple-element.50.refs_0_, f32[3,16,2048]{2,1,0:T(8,128)S(1)} %get-tuple-element.51.refs_1_, ...), custom_call_target="tpu_custom_call" | custom-call | tf_op jit(solution)/shard_map/pallas_call | solution.py:49
  46.4 0.1 collective-permute-start.6
  46.5 0.7 collective-permute-start.7
  47.2 4.9 %collective-permute-start.4 = (f32[3,3,1,2048]{3,2,1,0:T(1,128)S(1)}, f32[3,3,1,2048]{3,2,1,0:T(1,128)S(1)}, u32[]{:S(2)}, u32[]{:S(2)}) collective-permute-start(f32[3,3,1,2048]{3,2,1,0:T(1,128)S(1)} %get-tuple-element.60), channel_id=1, source_target_pairs={{0,4},{4,0},{8,12},{12,8},{16,20},{20,16},{24,28},{28,24},{1,5},{5... | collective-permute-start | bytes 221192 | tf_op jit(solution)/shard_map/ppermute | solution.py:482
  52.0 0.7 collective-permute-start.5
  52.7 1.2 %shard_map.145.refs_0_ = f32[3,3,16,2048]{3,2,1,0:T(8,128)S(1)} custom-call(f32[3,3,16,2048]{3,2,1,0:T(8,128)S(1)} %get-tuple-element.59.refs_0_.refs_1_, f32[3,3,3,16,2048]{4,3,2,1,0:T(8,128)S(1)} %get-tuple-element.57.refs_8_.refs_1_, f32[3,16,2048]{2,1,0:T(8,128)S(1)} %get-tuple-element.47.refs_2_.refs_6_, ...), custom_call_target="tpu_custom_call" | custom-call | tf_op jit(solution)/shard_map/pallas_call | solution.py:49
  53.9 0.5 collective-permute-done.4.refs_1_
  54.4 1.2 %shard_map.146 = (f32[3,3,16,2048]{3,2,1,0:T(8,128)S(1)}, f32[32,1,128]{2,1,0:T(1,128)S(1)}) custom-call(f32[3,3,16,2048]{3,2,1,0:T(8,128)S(1)} %shard_map.145.refs_0_, f32[3,3,1,2048]{3,2,1,0:T(1,128)S(1)} %collective-permute-done.4.refs_1_, f32[3,3,1,2048]{3,2,1,0:T(1,128)S(1)} %collective-permute-done.5.refs_2_, ...), custom_call_target="tpu_custom_call" | custom-call | tf_op jit(solution)/shard_map/pallas_call | solution.py:49
  55.6 15.9 %all_to_all.16.refs_0_ = f32[32,1,128]{2,1,0:T(1,128)S(1)} all-to-all(f32[32,1,128]{2,1,0:T(1,128)S(1)} %get-tuple-element.64), channel_id=1, replica_groups=mesh['tile'=8,'layer'=4] {'tile','layer'}, dimensions={0} | all-to-all | bytes 32768 | tf_op jit(solution)/shard_map/all_to_all | solution.py:491
  71.4 1.7 %shard_map.147 = (f32[3,3,16,2048]{3,2,1,0:T(8,128)}, f32[3,3,16,2048]{3,2,1,0:T(8,128)}, f32[1,1]{1,0:T(1,128)}) custom-call(f32[32,1,128]{2,1,0:T(1,128)S(1)} %all_to_all.16.refs_0_, f32[3,3,16,2048]{3,2,1,0:T(8,128)S(1)} %get-tuple-element.59.refs_0_.refs_1_, f32[3,3,16,2048]{3,2,1,0:T(8,128)S(1)} %get-tuple-element.65.refs_2_, ...), custom_call_target="tpu_custom_call" | custom-call | tf_op jit(solution)/shard_map/pallas_call | solution.py:49
  (9 shorter events, 0.0 us)
Async XLA Ops:
  4.8 0.8 %copy-start = (f32[3,16,2048]{2,1,0:T(8,128)}, f32[3,16,2048]{2,1,0:T(8,128)S(1)}, u32[]{:S(2)}) copy-start(f32[3,16,2048]{2,1,0:T(8,128)S(1)} %get-tuple-element.48.refs_3_) | copy-start | bytes 1179652
  5.5 7.4 %collective-permute-start = (f32[6,16,2048]{2,1,0:T(8,128)S(1)}, f32[6,16,2048]{2,1,0:T(8,128)S(1)}, u32[]{:S(2)}, u32[]{:S(2)}) collective-permute-start(f32[6,16,2048]{2,1,0:T(8,128)S(1)} %get-tuple-element.42.refs_0_), channel_id=1, source_target_pairs={{0,1},{1,0},{2,3},{3,2},{4,5},{5,4},{6,7},{7,6},{8,9},{9,8},{10,11... | collective-permute-start | bytes 2359304 | tf_op jit(solution)/shard_map/ppermute | solution.py:482
  6.0 14.8 %all-to-all-start = ((f32[32,1,768]{2,1,0:T(1,128)}), f32[32,1,768]{2,1,0:T(1,128)S(1)}, u32[]{:S(2)}, u32[]{:S(2)}) async-start(f32[32,1,768]{2,1,0:T(1,128)} %get-tuple-element.36), calls=%async_computation | async-start | bytes 196608 | tf_op jit(solution)/shard_map/all_to_all | solution.py:491
  13.0 7.8 %copy-start.4 = (s32[256]{0:T(256)S(1)}, s32[256]{0:T(256)}, u32[]{:S(2)}) copy-start(s32[256]{0:T(256)} %param.20) | copy-start | bytes 3076
  13.0 7.8 %copy-start.5 = (f32[256]{0:T(256)S(1)}, f32[256]{0:T(256)}, u32[]{:S(2)}) copy-start(f32[256]{0:T(256)} %param.22) | copy-start | bytes 3076
  14.4 0.7 %copy-start.2 = (f32[3,16,2048]{2,1,0:T(8,128)}, f32[3,16,2048]{2,1,0:T(8,128)S(1)}, u32[]{:S(2)}) copy-start(f32[3,16,2048]{2,1,0:T(8,128)S(1)} %get-tuple-element.46.tables_1_) | copy-start | bytes 1179652
  15.2 21.9 %collective-permute-start.1 = (f32[3,16,2048]{2,1,0:T(8,128)}, f32[3,16,2048]{2,1,0:T(8,128)S(1)}, u32[]{:S(2)}, u32[]{:S(2)}) collective-permute-start(f32[3,16,2048]{2,1,0:T(8,128)} %get-tuple-element.49), channel_id=1, source_target_pairs={{0,2},{1,3},{2,0},{3,1},{4,6},{5,7},{6,4},{7,5},{8,10},{9,11},{10,... | collective-permute-start | bytes 1179656 | tf_op jit(solution)/shard_map/ppermute | solution.py:482
  20.8 1.0 %copy-start.3 = (f32[3,16,2048]{2,1,0:T(8,128)S(1)}, f32[3,16,2048]{2,1,0:T(8,128)}, u32[]{:S(2)}) copy-start(f32[3,16,2048]{2,1,0:T(8,128)} %copy-done.2) | copy-start | bytes 1179652
  21.8 15.3 %copy-start.1 = (f32[3,16,2048]{2,1,0:T(8,128)S(1)}, f32[3,16,2048]{2,1,0:T(8,128)}, u32[]{:S(2)}) copy-start(f32[3,16,2048]{2,1,0:T(8,128)} %copy-done) | copy-start | bytes 1179652
  41.6 3.9 %collective-permute-start.2 = (f32[3,1,2048]{2,1,0:T(1,128)S(1)}, f32[3,1,2048]{2,1,0:T(1,128)S(1)}, u32[]{:S(2)}, u32[]{:S(2)}) collective-permute-start(f32[3,1,2048]{2,1,0:T(1,128)S(1)} %get-tuple-element.52), channel_id=1, source_target_pairs={{0,4},{4,0},{8,12},{12,8},{16,20},{20,16},{24,28},{28,24},{1,5},{5... | collective-permute-start | bytes 73736 | tf_op jit(solution)/shard_map/ppermute | solution.py:482
  42.4 3.1 %collective-permute-start.3 = (f32[3,1,2048]{2,1,0:T(1,128)S(1)}, f32[3,1,2048]{2,1,0:T(1,128)S(1)}, u32[]{:S(2)}, u32[]{:S(2)}) collective-permute-start(f32[3,1,2048]{2,1,0:T(1,128)S(1)} %get-tuple-element.53), channel_id=1, source_target_pairs={{4,8},{12,16},{20,24},{8,4},{16,12},{24,20},{5,9},{13,17},{21,25},... | collective-permute-start | bytes 73736 | tf_op jit(solution)/shard_map/ppermute | solution.py:487
  46.4 8.0 %collective-permute-start.6 = (f32[3,16,2048]{2,1,0:T(8,128)S(1)}, f32[3,16,2048]{2,1,0:T(8,128)S(1)}, u32[]{:S(2)}, u32[]{:S(2)}) collective-permute-start(f32[3,16,2048]{2,1,0:T(8,128)S(1)} %get-tuple-element.62), channel_id=1, source_target_pairs={{0,1},{1,0},{2,3},{3,2},{4,5},{5,4},{6,7},{7,6},{8,9},{9,8},{10,11... | collective-permute-start | bytes 1179656 | tf_op jit(solution)/shard_map/ppermute | solution.py:482
  46.5 7.9 %collective-permute-start.7 = (f32[3,16,2048]{2,1,0:T(8,128)S(1)}, f32[3,16,2048]{2,1,0:T(8,128)S(1)}, u32[]{:S(2)}, u32[]{:S(2)}) collective-permute-start(f32[3,16,2048]{2,1,0:T(8,128)S(1)} %get-tuple-element.63), channel_id=1, source_target_pairs={{1,2},{2,1},{5,6},{6,5},{9,10},{10,9},{13,14},{14,13},{17,18},{18,... | collective-permute-start | bytes 1179656 | tf_op jit(solution)/shard_map/ppermute | solution.py:487
  47.2 7.2 %collective-permute-start.4 = (f32[3,3,1,2048]{3,2,1,0:T(1,128)S(1)}, f32[3,3,1,2048]{3,2,1,0:T(1,128)S(1)}, u32[]{:S(2)}, u32[]{:S(2)}) collective-permute-start(f32[3,3,1,2048]{3,2,1,0:T(1,128)S(1)} %get-tuple-element.60), channel_id=1, source_target_pairs={{0,4},{4,0},{8,12},{12,8},{16,20},{20,16},{24,28},{28,24},{1,5},{5... | collective-permute-start | bytes 221192 | tf_op jit(solution)/shard_map/ppermute | solution.py:482
  52.0 2.3 %collective-permute-start.5 = (f32[3,3,1,2048]{3,2,1,0:T(1,128)S(1)}, f32[3,3,1,2048]{3,2,1,0:T(1,128)S(1)}, u32[]{:S(2)}, u32[]{:S(2)}) collective-permute-start(f32[3,3,1,2048]{3,2,1,0:T(1,128)S(1)} %get-tuple-element.61), channel_id=1, source_target_pairs={{4,8},{12,16},{20,24},{8,4},{16,12},{24,20},{5,9},{13,17},{21,25},... | collective-permute-start | bytes 221192 | tf_op jit(solution)/shard_map/ppermute | solution.py:487

commit v6 on v5

--- a/solution.py
+++ b/solution.py
@@ -12,6 +12,7 @@
 BOTH = ("tile", "layer")
 VM = pl.BlockSpec(memory_space=pltpu.VMEM)
 LIMIT = 16 << 20
+PARTS = 2
 
 
 def hbm(shape):
@@ -61,6 +62,15 @@
     )(*[pltpu.with_memory_space_constraint(a, s) for a, s in zip(args, spaces)])
 
 
+def nothing(*refs):
+    pass
+
+
+def load(*args):
+    every = range(len(args))
+    return call(nothing, (), args, far=every, keep=every, limit=1 << 20)
+
+
 def iota(shape, dim):
     return lax.broadcasted_iota(I32, shape, dim)
 
@@ -73,9 +83,12 @@
     return [one, two, three]
 
 
-def fold(x):
-    n = x.shape[0] // 3
-    return x[:n] + (x[n : 2 * n] + x[2 * n :])
+def fold(x, parts=3):
+    n = x.shape[0] // parts
+    total = x[(parts - 1) * n :]
+    for i in range(parts - 2, -1, -1):
+        total = x[i * n : (i + 1) * n] + total
+    return total
 
 
 def onehot(index, size):
@@ -90,27 +103,38 @@
     return lax.dot_general(a, b, (((1,), (1,)), ((), ())), preferred_element_type=F32)
 
 
-def pick(table, hi, lo):
-    rows, cols = table.shape
-    parts = jnp.concatenate(split(table), 0)
-    got = fold(dot(parts, onehot(lo, cols).astype(BF16)))
-    return jnp.sum(got * onehot(hi, rows), axis=0, keepdims=True)
-
-
-def spread(value, hi, lo, rows, cols):
-    parts = [jnp.where(iota((rows, hi.shape[1]), 0) == hi, v.astype(F32), 0.0).astype(BF16) for v in split(value)]
-    return fold(dot_nt(jnp.concatenate(parts, 0), onehot(lo, cols).astype(BF16)))
-
-
-def pres_kernel(rhs, wts, cell, front, prod, pres, send):
+def pick(tables, hi, hot):
+    rows = tables[0].shape[0]
+    parts = jnp.concatenate([p for table in tables for p in split(table)[:PARTS]], 0)
+    got = dot(parts, hot)
+    mask = onehot(hi, rows)
+    n = PARTS * rows
+    return [jnp.sum(fold(got[i * n : (i + 1) * n], PARTS) * mask, axis=0, keepdims=True) for i in range(len(tables))]
+
+
+def pres_kernel(cell_in, front_in, prod_in, rhs_in, wts_in, tz_in, store_in, pres, send, ends, *scratch):
+    (cell, front, prod, rhs, wts, tz, store), sems = scratch[:-1], scratch[-1]
+    pairs = ((cell_in, cell), (front_in, front), (prod_in, prod), (rhs_in, rhs), (wts_in, wts), (tz_in, tz), (store_in, store))
+    copies = [pltpu.make_async_copy(a, b, sems.at[i]) for i, (a, b) in enumerate(pairs)]
+    for copy in copies:
+        copy.start()
+    for copy in copies[:3]:
+        copy.wait()
     depth, width, long = pres.shape
+    where = cell[...]
+    hot = onehot(lax.rem(where, long), long).astype(BF16)
+    for copy in copies[3:]:
+        copy.wait()
     for z in range(depth):
         pres[z] = wts[0, z] * rhs[0, z] + wts[1, z] * rhs[1, z] + wts[2, z] * rhs[2, z]
-    where = cell[...]
-    table = pres[...].reshape(depth * width, long)
-    value = prod[...] * pick(table, lax.div(where, long), lax.rem(where, long))
-    both = jnp.concatenate([value, front[...].astype(F32), where.astype(F32)], 1)
+    (found,) = pick([pres[...].reshape(depth * width, long)], lax.div(where, long), hot)
+    both = jnp.concatenate([prod[...] * found, front[...].astype(F32), where.astype(F32)], 1)
     send[...] = jnp.broadcast_to(both[:, None], send.shape)
+    tzs = [tz[z] for z in range(depth)]
+    gs, invs, _, _, coefs = factors(tzs, [store[z] for z in range(depth)])
+    y = local_solve([pres[z] for z in range(depth)], gs, invs, tzs)
+    for i, value in enumerate((*coefs, y[0], y[-1], tzs[-1])):
+        ends[i] = value
 
 
 def is_right(level, axis="layer"):
@@ -151,18 +175,6 @@
     return gs, invs, first, final, (first[0], first[-1], final[-1] + 1.0 / jnp.maximum(tz[-1], 1e-30))
 
 
-def coef_kernel(tz, store, pres, answers, ends):
-    depth = pres.shape[0]
-    tzs = [tz[z] for z in range(depth)]
-    gs, invs, first, final, coefs = factors(tzs, [store[z] for z in range(depth)])
-    for z in range(depth):
-        answers[z] = first[z]
-        answers[depth + z] = final[z]
-    y = local_solve([pres[z] for z in range(depth)], gs, invs, tzs)
-    for i, value in enumerate((*coefs, y[0], y[-1], tzs[-1])):
-        ends[i] = value
-
-
 def pair(level, own, sib):
     af, af_ = choose(level, own[0], sib[0])
     c, c_ = choose(level, own[1], sib[1])
@@ -181,6 +193,15 @@
     yl, yl_ = choose(level, mine[1], other[1])
     flux = g * (yl - yf_)
     return (yf - c * flux, yl_ + c_ * flux)
+
+
+def first_join_kernel(own, sib, tz, store, out, face, more, one, answers):
+    depth = tz.shape[0]
+    _, _, first, final, _ = factors([tz[z] for z in range(depth)], [store[z] for z in range(depth)])
+    for z in range(depth):
+        answers[z] = first[z]
+        answers[depth + z] = final[z]
+    join_kernel(0, own, sib, answers, out, face, more, one)
 
 
 def join_kernel(level, own, sib, answers, out, face, more, one):
@@ -234,11 +255,7 @@
     depth, width, long = tables[-1].shape
     hi, lo = lax.div(where, long), lax.rem(where, long)
     stack = [t[k * depth : (k + 1) * depth].reshape(depth * width, long) for t in tables for k in range(t.shape[0] // depth)]
-    parts = jnp.concatenate([p for table in stack for p in split(table)], 0)
-    got = dot(parts, onehot(lo, long).astype(BF16))
-    mask = onehot(hi, depth * width)
-    n = 3 * depth * width
-    found = [value * jnp.sum(fold(got[i * n : (i + 1) * n]) * mask, axis=0, keepdims=True) for i in range(len(stack))]
+    found = [value * f for f in pick(stack, hi, onehot(lo, long).astype(BF16))]
     total = jnp.zeros((length // lanes, lanes), F32)
     group = 8
     for first in range(0, devices, group):
@@ -292,15 +309,15 @@
 
 
 def pressure_kernel(levels, *refs):
-    (recv, terms, tz, store, pres), refs = (refs[:5], refs[5:])
+    (recv, terms, pres), refs = (refs[:3], refs[3:])
     sib, refs = (refs[:levels], refs[levels:])
-    far, refs = (refs[:5], refs[5:])
-    (p, coupled_z, one, two), near_by, refs = (refs[:4], refs[4:9], refs[9:])
+    far, refs = (refs[:3], refs[3:])
+    (p, coupled_z, one, two), near_by, refs = (refs[:4], refs[4:7], refs[7:])
     rows_hot, lanes_hot, sol_hot, sol_row, sems = refs
     copies = [pltpu.make_async_copy(a, b, sems.at[i]) for i, (a, b) in enumerate(zip(far, near_by))]
     for copy in copies:
         copy.start()
-    tx = near_by[0]
+    tz, store, tx = near_by
     depth, width, long = pres.shape
     rows = sol_hot.shape[0]
     count = terms.shape[2] // 3
@@ -330,12 +347,14 @@
         at = rows + column * count
         return jnp.concatenate([recv[device][:, at : at + count] for device in group], 1)
 
+    for copy in copies:
+        copy.wait()
     tzs = [tz[z] for z in range(depth)]
     gs, invs, first, final, coefs = factors(tzs, [store[z] for z in range(depth)])
     own = [coefs]
     value = listed(groups[0], 0) * sol[:, :count]
     values = [jnp.where(layer == z, value, 0.0) for z in range(depth)]
-    change = gathered(values, rows_hot, lanes_hot, 0, count, width, 3)
+    change = gathered(values, rows_hot, lanes_hot, 0, count, width, PARTS)
     y = local_solve([pres[z] - change[z] for z in range(depth)], gs, invs, tzs)
     mine = (y[0], y[-1])
     steps = []
@@ -345,7 +364,7 @@
         top = level == levels - 1
         columns = [1 + 2 * level] if top else [1 + 2 * level, 2 + 2 * level]
         values = [listed(groups[level + 1], c) * sol[:, start : start + size] for c in columns]
-        change = gathered(values, rows_hot, lanes_hot, start, size, width, 3)
+        change = gathered(values, rows_hot, lanes_hot, start, size, width, PARTS)
         start += size
         if top:
             other = sib[level][1] - change[0]
@@ -385,8 +404,6 @@
             coupled_z[z] = total + jnp.where(is_last, 0.0, below + tzs[z] * values[z])
         else:
             coupled_z[z] = total + tzs[z] * values[z + 1]
-    for copy in copies:
-        copy.wait()
     for z in range(depth):
         tile_rows(values[z][0:1], (tx[z] * values[z])[width - 1 :], one.at[z], two.at[z])
 
@@ -505,26 +522,32 @@
     def planes(n):
         return vmem((n, width, long))
 
-    pres, send = call(
-        pres_kernel, (field, vmem((devices, 1, 3 * count))), (rhs, weights, cell, front, prod), far=range(5)
-    )
+    hbm_spec = pl.BlockSpec(memory_space=pltpu.HBM)
+    given = (cell, front, prod, rhs, weights, tz, store)
+    pres, send, ends = pl.pallas_call(
+        pres_kernel,
+        out_shape=(field, vmem((devices, 1, 3 * count)), planes(6)),
+        in_specs=[hbm_spec] * len(given),
+        out_specs=(VM,) * 3,
+        scratch_shapes=[vmem(a.shape, a.dtype) for a in given] + [pltpu.SemaphoreType.DMA((len(given),))],
+        compiler_params=pltpu.CompilerParams(vmem_limit_bytes=LIMIT),
+    )(*[pltpu.with_memory_space_constraint(a, pltpu.HBM) for a in given])
     terms = everywhere(send)
-    pres, tz, store = lax.optimization_barrier((pres, tz, store))
-    answers, ends, tz_v, store_v = call(
-        coef_kernel, (planes(2 * depth), planes(6)), (tz, store, pres), far=(0, 1), keep=(0, 1)
-    )
     sib, tables = ([], [])
-    last = answers
     for level in range(levels - 1):
+        sib.append(flip(ends, level))
+        outs = (planes(6), planes(3), planes(2 * depth), field)
+        if level == 0:
+            ends, face, more, last, answers = call(
+                first_join_kernel, (*outs, planes(2 * depth)), (ends, sib[-1], tz, store), far=(2, 3)
+            )
+        else:
+            ends, face, more, last = call(functools.partial(join_kernel, level), outs, (ends, sib[-1], answers))
         tables.append(answers)
-        sib.append(flip(ends, level))
-        ends, face, answers, last = call(
-            functools.partial(join_kernel, level), (planes(6), planes(3), planes(2 * depth), field), (ends, sib[-1], answers)
-        )
+        answers = more
     tables.append(last)
     sib.append(flip(face, levels - 1))
     chunks = 8
-    hbm_spec = pl.BlockSpec(memory_space=pltpu.HBM)
     terms, *tables = lax.optimization_barrier((terms, *tables))
     send = pl.pallas_call(
         front_kernel,
@@ -535,14 +558,14 @@
         compiler_params=pltpu.CompilerParams(vmem_limit_bytes=LIMIT),
     )(terms, cell, prod, tables, pltpu.with_memory_space_constraint(inverse, pltpu.HBM))
     sol = everywhere(send)
-    far = (tx, ty, rhs, block_diag, block_inv)
-    args = (sol, terms, tz_v, store_v, pres, *sib)
+    far = (tz, store, tx)
+    args = (sol, terms, pres, *sib)
     row3 = vmem((depth, 1, long))
-    p, coupled_z, one, two, tx, ty, rhs, diag, binv = pl.pallas_call(
+    p, coupled_z, one, two, tz, _, tx = pl.pallas_call(
         functools.partial(pressure_kernel, levels),
         out_shape=(field, field, row3, row3) + tuple(vmem(a.shape) for a in far),
         in_specs=[VM] * len(args) + [hbm_spec] * len(far),
-        out_specs=(VM,) * 9,
+        out_specs=(VM,) * 7,
         scratch_shapes=[
             vmem((width * long // 128, lists), BF16),
             vmem((128, lists), BF16),
@@ -555,21 +578,22 @@
         *[pltpu.with_memory_space_constraint(a, pltpu.VMEM) for a in args],
         *[pltpu.with_memory_space_constraint(a, pltpu.HBM) for a in far],
     )
+    ty, rhs, diag, binv = load(ty, rhs, block_diag, block_inv)
     one, two = (flip(one, 0, "tile"), neighbour(two, "tile"))
     row9 = vmem((3, depth, 1, long))
     plane3 = planes(3)
     s, row_one, row_two, inner, outer = call(
         search_kernel,
         (vmem(rhs.shape), row9, row9, plane3, plane3),
-        (p, coupled_z, one, two, tx, ty, tz_v, rhs, diag, binv),
+        (p, coupled_z, one, two, tx, ty, tz, rhs, diag, binv),
     )
-    inner, outer = (flip(inner, 0), neighbour(outer))
+    outer, inner = (neighbour(outer), flip(inner, 0))
     row_one, row_two = (flip(row_one, 0, "tile"), neighbour(row_two, "tile"))
-    (part,) = call(inner_kernel, (vmem(rhs.shape),), (s, diag, tz_v, tx, ty))
+    (part,) = call(inner_kernel, (vmem(rhs.shape),), (s, diag, tz, tx, ty))
     image, send = call(
         image_kernel,
         (vmem(rhs.shape), vmem((devices, 1, 128))),
-        (part, row_one, row_two, inner, outer, rhs, tz_v, tx),
+        (part, row_one, row_two, inner, outer, rhs, tz, tx),
     )
     sums = everywhere(send)
     update, lin_res, ratio = call(

time: 73.4 us -> 69.9 us (0.952)
  waiting for transfers between devices: 6.7 us -> 3.72 us
  local copies, waits for them, and re-layouts: 2.5 us -> 0.01 us
  Pallas kernels: 20 us -> 22 us
  blocking collectives: 26.1 us -> 27.2 us
  starting transfers between devices: 16.9 us -> 15.9 us
    pallas_call x0 -> x1, Pallas kernels: none -> 3.13 us  [shards(): pl.pallas_call(pres_kernel, out_shape=(field, vmem((devices, 1, 3 * count...]
    unnamed x12 -> x4, local copies, waits for them, and re-layouts: 2.5 us -> 0.01 us
    ppermute x5, waiting for transfers between devices: 2.89 us -> 0.47 us  [flip(): lax.ppermute(x, axis, [(i, i ^ 1 << level) for i in range(lax.axis_size(a...]
    pallas_call x1, Pallas kernels: 4.42 us -> 2.72 us  [shards(): pl.pallas_call(functools.partial(pressure_kernel, levels), out_shape=(fie...]
    ppermute x5, starting transfers between devices: 8 us -> 6.92 us  [flip(): lax.ppermute(x, axis, [(i, i ^ 1 << level) for i in range(lax.axis_size(a...]
    all_to_all x2, blocking collectives: 26.1 us -> 27.2 us  [everywhere(): return lax.all_to_all(x, BOTH, split_axis=0, concat_axis=0, tiled=True)]
    pallas_call x7 -> x6, Pallas kernels: 10.5 us -> 11.3 us  [call(): pl.pallas_call(functools.partial(staged, kernel, where, len(outs), tuple(...]
  transfers between devices with their start and end apart: 9 -> 9, of which waited for: 3 -> 2; matrix products, arithmetic and copies ran while one was open for 0% -> 0% of each run, Pallas kernels for 11% -> 18%
where the time goes in v6:
time: 69.9 us; the launch traced here: 69.6 us
  blocking collectives  27.2 us (39%)
  Pallas kernels  22 us (31%)
  starting transfers between devices  15.9 us (23%)
  waiting for transfers between devices  3.72 us (5%)
  between operations  0.78 us (1%)
    all_to_all x2, blocking collectives, everywhere(): return lax.all_to_all(x, BOTH, split_axis=0, concat_axis=0, tiled=True)  27.2 us
    pallas_call x6, Pallas kernels, call(): pl.pallas_call(functools.partial(staged, kernel, where, len(outs), tuple(...  11.3 us
    all_to_all x1, starting transfers between devices, everywhere(): return lax.all_to_all(x, BOTH, split_axis=0, concat_axis=0, tiled=True)  6.96 us
    ppermute x5, starting transfers between devices, flip(): lax.ppermute(x, axis, [(i, i ^ 1 << level) for i in range(lax.axis_size(a...  6.92 us
    pallas_call x1, Pallas kernels, shards(): pl.pallas_call(front_kernel, out_shape=vmem((devices, 1, rows + 2 * level...  4.91 us
    all_to_all x1, waiting for transfers between devices, everywhere(): return lax.all_to_all(x, BOTH, split_axis=0, concat_axis=0, tiled=True)  3.24 us
    pallas_call x1, Pallas kernels, shards(): pl.pallas_call(pres_kernel, out_shape=(field, vmem((devices, 1, 3 * count...  3.13 us
    pallas_call x1, Pallas kernels, shards(): pl.pallas_call(functools.partial(pressure_kernel, levels), out_shape=(fie...  2.72 us
  transfers between devices with their start and end apart: 9, of which 2 were waited for; matrix products, arithmetic and copies ran while one was open for 0% of the time, Pallas kernels for 18%

profile of v6, /device:TPU:0, one launch (start us, length us, event | category | flops | bytes accessed | tf_op | source)
XLA Modules:
  0.0 69.6 jit_solution(17636698745640285313)
XLA Ops:
  0.6 3.1 %shard_map.139 = (f32[3,16,2048]{2,1,0:T(8,128)S(1)}, f32[32,1,768]{2,1,0:T(1,128)}, f32[6,16,2048]{2,1,0:T(8,128)S(1)}) custom-call(s32[1,256]{1,0:T(1,128)} %bitcast.4, s32[1,256]{1,0:T(1,128)} %bitcast.8, f32[1,256]{1,0:T(1,128)} %bitcast.6, f32[3,3,16,2048]{3,2,1,0:T(8,128)} %refs_1_.1, f32[3,3,16,2048]{3,2,1,0:T(8,128)} %wts_in.1, ...), custom_call_target="tpu_custom_call" | custom-call | tf_op jit(solution)/shard_map/pallas_call | solution.py:527
  3.8 0.5 collective-permute-start
  4.3 7.0 %all-to-all-start = ((f32[32,1,768]{2,1,0:T(1,128)}), f32[32,1,768]{2,1,0:T(1,128)S(1)}, u32[]{:S(2)}, u32[]{:S(2)}) async-start(f32[32,1,768]{2,1,0:T(1,128)} %get-tuple-element.32), calls=%async_computation | async-start | bytes 196608 | tf_op jit(solution)/shard_map/all_to_all | solution.py:508
  11.3 0.0 copy-start
  11.3 0.0 copy-start.1
  11.3 0.0 collective-permute-done.refs_1_.refs_3_
  11.3 2.7 %shard_map.140 = (f32[6,16,2048]{2,1,0:T(8,128)}, f32[3,16,2048]{2,1,0:T(8,128)}, f32[6,16,2048]{2,1,0:T(8,128)}, f32[3,16,2048]{2,1,0:T(8,128)S(1)}, f32[6,16,2048]{2,1,0:T(8,128)S(1)}) custom-call(f32[6,16,2048]{2,1,0:T(8,128)S(1)} %get-tuple-element.33.refs_0_, f32[6,16,2048]{2,1,0:T(8,128)S(1)} %collective-permute-done.refs_1_.refs_3_, ...), custom_call_target="tpu_custom_call" | custom-call | tf_op jit(solution)/shard_map/pallas_call | solution.py:50
  14.0 1.8 %collective-permute-start.1 = (f32[3,16,2048]{2,1,0:T(8,128)}, f32[3,16,2048]{2,1,0:T(8,128)S(1)}, u32[]{:S(2)}, u32[]{:S(2)}) collective-permute-start(f32[3,16,2048]{2,1,0:T(8,128)} %get-tuple-element.40), channel_id=1, source_target_pairs={{0,2},{1,3},{2,0},{3,1},{4,6},{5,7},{6,4},{7,5},{8,10},{9,11},{10,... | collective-permute-start | bytes 1179656 | tf_op jit(solution)/shard_map/ppermute | solution.py:499
  15.8 3.2 %all-to-all-done.recv.refs_1_ = f32[32,1,768]{2,1,0:T(1,128)S(1)} async-done(((f32[32,1,768]{2,1,0:T(1,128)}), f32[32,1,768]{2,1,0:T(1,128)S(1)}, u32[]{:S(2)}, u32[]{:S(2)}) %all-to-all-start) | async-done | bytes 98336 | tf_op jit(solution)/shard_map/all_to_all | solution.py:508
  19.1 0.0 copy-done
  19.1 4.9 %shard_map.141 = f32[32,1,1280]{2,1,0:T(1,128)S(1)} custom-call(f32[32,1,768]{2,1,0:T(1,128)S(1)} %all-to-all-done.recv.refs_1_, s32[1,256]{1,0:T(1,128)S(1)} %bitcast.5, f32[1,256]{1,0:T(1,128)S(1)} %bitcast.7, f32[6,16,2048]{2,1,0:T(8,128)S(1)} %get-tuple-element.37.tables_0_, f32[3,16,2048]{2,1,0:T(8,128)S(1)} %get-tuple-element.38.tables_1_, ...), custom_call_target="tpu_custom_call" | custom-call | tf_op jit(solution)/shard_map/pallas_call | solution.py:552
  24.0 10.3 %all_to_all.15.refs_0_ = f32[32,1,1280]{2,1,0:T(1,128)S(1)} all-to-all(f32[32,1,1280]{2,1,0:T(1,128)S(1)} %shard_map.141), channel_id=1, replica_groups=mesh['tile'=8,'layer'=4] {'tile','layer'}, dimensions={0} | all-to-all | bytes 327680 | tf_op jit(solution)/shard_map/all_to_all | solution.py:508
  34.3 0.0 collective-permute-done.1.refs_4_
  34.3 2.7 %shard_map.142 = (f32[3,16,2048]{2,1,0:T(8,128)S(1)}, f32[3,16,2048]{2,1,0:T(8,128)S(1)}, f32[3,1,2048]{2,1,0:T(1,128)S(1)}, f32[3,1,2048]{2,1,0:T(1,128)S(1)}, ...) custom-call(f32[32,1,1280]{2,1,0:T(1,128)S(1)} %all_to_all.15.refs_0_, ...), custom_call_target="tpu_custom_call" | custom-call | tf_op jit(solution)/shard_map/pallas_call | solution.py:564
  37.0 0.8 %collective-permute-start.2 = (f32[3,1,2048]{2,1,0:T(1,128)S(1)}, f32[3,1,2048]{2,1,0:T(1,128)S(1)}, u32[]{:S(2)}, u32[]{:S(2)}) collective-permute-start(f32[3,1,2048]{2,1,0:T(1,128)S(1)} %get-tuple-element.43), channel_id=1, source_target_pairs={{0,4},{4,0},{8,12},{12,8},{16,20},{20,16},{24,28},{28,24},{1,5},{5... | collective-permute-start | bytes 73736 | tf_op jit(solution)/shard_map/ppermute | solution.py:499
  37.8 0.7 collective-permute-start.3
  38.5 3.6 %shard_map.143 = (f32[3,16,2048]{2,1,0:T(8,128)S(1)}, f32[3,3,16,2048]{3,2,1,0:T(8,128)S(1)}, f32[3,3,3,16,2048]{4,3,2,1,0:T(8,128)S(1)}, f32[3,3,3,16,2048]{4,3,2,1,0:T(8,128)S(1)}) custom-call(f32[3,16,2048]{2,1,0:T(8,128)} %refs_0_.1, f32[3,3,16,2048]{3,2,1,0:T(8,128)} %refs_1_.1, f32[3,3,3,16,2048]{4,3,2,1,0:T(8,128)} %refs_2_.3, ...), custom_call_target="tpu_custom_call" | custom-call | tf_op jit(solution)/shard_map/pallas_call | solution.py:50
  42.1 0.0 collective-permute-done.2.refs_2_
  42.1 0.0 collective-permute-done.3.refs_3_
  42.1 0.9 %shard_map.144 = (f32[3,3,16,2048]{3,2,1,0:T(8,128)S(1)}, f32[3,3,1,2048]{3,2,1,0:T(1,128)S(1)}, f32[3,3,1,2048]{3,2,1,0:T(1,128)S(1)}, f32[3,16,2048]{2,1,0:T(8,128)S(1)}, f32[3,16,2048]{2,1,0:T(8,128)S(1)}) custom-call(f32[3,16,2048]{2,1,0:T(8,128)S(1)} %get-tuple-element.41.refs_0_, f32[3,16,2048]{2,1,0:T(8,128)S(1)} %get-tuple-element.42.refs_1_, ...), custom_call_target="tpu_custom_call" | custom-call | tf_op jit(solution)/shard_map/pallas_call | solution.py:50
  43.0 0.1 collective-permute-start.6
  43.1 0.7 collective-permute-start.7
  43.8 3.7 %collective-permute-start.4 = (f32[3,3,1,2048]{3,2,1,0:T(1,128)S(1)}, f32[3,3,1,2048]{3,2,1,0:T(1,128)S(1)}, u32[]{:S(2)}, u32[]{:S(2)}) collective-permute-start(f32[3,3,1,2048]{3,2,1,0:T(1,128)S(1)} %get-tuple-element.52), channel_id=1, source_target_pairs={{0,4},{4,0},{8,12},{12,8},{16,20},{20,16},{24,28},{28,24},{1,5},{5... | collective-permute-start | bytes 221192 | tf_op jit(solution)/shard_map/ppermute | solution.py:499
  47.5 0.7 collective-permute-start.5
  48.1 1.2 %shard_map.145.refs_0_ = f32[3,3,16,2048]{3,2,1,0:T(8,128)S(1)} custom-call(f32[3,3,16,2048]{3,2,1,0:T(8,128)S(1)} %get-tuple-element.51.refs_0_.refs_1_, f32[3,3,3,16,2048]{4,3,2,1,0:T(8,128)S(1)} %get-tuple-element.49.refs_8_.refs_1_, f32[3,16,2048]{2,1,0:T(8,128)S(1)} %get-tuple-element.47.refs_6_.refs_2_, ...), custom_call_target="tpu_custom_call" | custom-call | tf_op jit(solution)/shard_map/pallas_call | solution.py:50
  49.4 0.5 collective-permute-done.4.refs_1_
  49.8 0.0 collective-permute-done.5.refs_2_
  49.8 0.0 collective-permute-done.6.refs_3_
  49.8 0.0 collective-permute-done.7.refs_4_
  49.8 1.2 %shard_map.146 = (f32[3,3,16,2048]{3,2,1,0:T(8,128)S(1)}, f32[32,1,128]{2,1,0:T(1,128)S(1)}) custom-call(f32[3,3,16,2048]{3,2,1,0:T(8,128)S(1)} %shard_map.145.refs_0_, f32[3,3,1,2048]{3,2,1,0:T(1,128)S(1)} %collective-permute-done.4.refs_1_, f32[3,3,1,2048]{3,2,1,0:T(1,128)S(1)} %collective-permute-done.5.refs_2_, ...), custom_call_target="tpu_custom_call" | custom-call | tf_op jit(solution)/shard_map/pallas_call | solution.py:50
  51.0 16.9 %all_to_all.16.refs_0_ = f32[32,1,128]{2,1,0:T(1,128)S(1)} all-to-all(f32[32,1,128]{2,1,0:T(1,128)S(1)} %get-tuple-element.56), channel_id=1, replica_groups=mesh['tile'=8,'layer'=4] {'tile','layer'}, dimensions={0} | all-to-all | bytes 32768 | tf_op jit(solution)/shard_map/all_to_all | solution.py:508
  67.9 1.7 %shard_map.147 = (f32[3,3,16,2048]{3,2,1,0:T(8,128)}, f32[3,3,16,2048]{3,2,1,0:T(8,128)}, f32[1,1]{1,0:T(1,128)}) custom-call(f32[32,1,128]{2,1,0:T(1,128)S(1)} %all_to_all.16.refs_0_, f32[3,3,16,2048]{3,2,1,0:T(8,128)S(1)} %get-tuple-element.51.refs_0_.refs_1_, f32[3,3,16,2048]{3,2,1,0:T(8,128)S(1)} %get-tuple-element.57.refs_2_, ...), custom_call_target="tpu_custom_call" | custom-call | tf_op jit(solution)/shard_map/pallas_call | solution.py:50
  (1 shorter events, 0.0 us)
Async XLA Ops:
  3.8 7.5 %collective-permute-start = (f32[6,16,2048]{2,1,0:T(8,128)S(1)}, f32[6,16,2048]{2,1,0:T(8,128)S(1)}, u32[]{:S(2)}, u32[]{:S(2)}) collective-permute-start(f32[6,16,2048]{2,1,0:T(8,128)S(1)} %get-tuple-element.33.refs_0_), channel_id=1, source_target_pairs={{0,1},{1,0},{2,3},{3,2},{4,5},{5,4},{6,7},{7,6},{8,9},{9,8},{10,11... | collective-permute-start | bytes 2359304 | tf_op jit(solution)/shard_map/ppermute | solution.py:499
  4.3 14.8 %all-to-all-start = ((f32[32,1,768]{2,1,0:T(1,128)}), f32[32,1,768]{2,1,0:T(1,128)S(1)}, u32[]{:S(2)}, u32[]{:S(2)}) async-start(f32[32,1,768]{2,1,0:T(1,128)} %get-tuple-element.32), calls=%async_computation | async-start | bytes 196608 | tf_op jit(solution)/shard_map/all_to_all | solution.py:508
  11.3 7.8 %copy-start = (s32[256]{0:T(256)S(1)}, s32[256]{0:T(256)}, u32[]{:S(2)}) copy-start(s32[256]{0:T(256)} %param.20) | copy-start | bytes 3076
  11.3 7.8 %copy-start.1 = (f32[256]{0:T(256)S(1)}, f32[256]{0:T(256)}, u32[]{:S(2)}) copy-start(f32[256]{0:T(256)} %param.22) | copy-start | bytes 3076
  14.0 20.3 %collective-permute-start.1 = (f32[3,16,2048]{2,1,0:T(8,128)}, f32[3,16,2048]{2,1,0:T(8,128)S(1)}, u32[]{:S(2)}, u32[]{:S(2)}) collective-permute-start(f32[3,16,2048]{2,1,0:T(8,128)} %get-tuple-element.40), channel_id=1, source_target_pairs={{0,2},{1,3},{2,0},{3,1},{4,6},{5,7},{6,4},{7,5},{8,10},{9,11},{10,... | collective-permute-start | bytes 1179656 | tf_op jit(solution)/shard_map/ppermute | solution.py:499
  37.0 5.1 %collective-permute-start.2 = (f32[3,1,2048]{2,1,0:T(1,128)S(1)}, f32[3,1,2048]{2,1,0:T(1,128)S(1)}, u32[]{:S(2)}, u32[]{:S(2)}) collective-permute-start(f32[3,1,2048]{2,1,0:T(1,128)S(1)} %get-tuple-element.43), channel_id=1, source_target_pairs={{0,4},{4,0},{8,12},{12,8},{16,20},{20,16},{24,28},{28,24},{1,5},{5... | collective-permute-start | bytes 73736 | tf_op jit(solution)/shard_map/ppermute | solution.py:499
  37.8 4.3 %collective-permute-start.3 = (f32[3,1,2048]{2,1,0:T(1,128)S(1)}, f32[3,1,2048]{2,1,0:T(1,128)S(1)}, u32[]{:S(2)}, u32[]{:S(2)}) collective-permute-start(f32[3,1,2048]{2,1,0:T(1,128)S(1)} %get-tuple-element.44), channel_id=1, source_target_pairs={{4,8},{12,16},{20,24},{8,4},{16,12},{24,20},{5,9},{13,17},{21,25},... | collective-permute-start | bytes 73736 | tf_op jit(solution)/shard_map/ppermute | solution.py:504
  43.0 6.8 %collective-permute-start.6 = (f32[3,16,2048]{2,1,0:T(8,128)S(1)}, f32[3,16,2048]{2,1,0:T(8,128)S(1)}, u32[]{:S(2)}, u32[]{:S(2)}) collective-permute-start(f32[3,16,2048]{2,1,0:T(8,128)S(1)} %get-tuple-element.54), channel_id=1, source_target_pairs={{0,1},{1,0},{2,3},{3,2},{4,5},{5,4},{6,7},{7,6},{8,9},{9,8},{10,11... | collective-permute-start | bytes 1179656 | tf_op jit(solution)/shard_map/ppermute | solution.py:499
  43.1 6.7 %collective-permute-start.7 = (f32[3,16,2048]{2,1,0:T(8,128)S(1)}, f32[3,16,2048]{2,1,0:T(8,128)S(1)}, u32[]{:S(2)}, u32[]{:S(2)}) collective-permute-start(f32[3,16,2048]{2,1,0:T(8,128)S(1)} %get-tuple-element.55), channel_id=1, source_target_pairs={{1,2},{2,1},{5,6},{6,5},{9,10},{10,9},{13,14},{14,13},{17,18},{18,... | collective-permute-start | bytes 1179656 | tf_op jit(solution)/shard_map/ppermute | solution.py:504
  43.8 6.0 %collective-permute-start.4 = (f32[3,3,1,2048]{3,2,1,0:T(1,128)S(1)}, f32[3,3,1,2048]{3,2,1,0:T(1,128)S(1)}, u32[]{:S(2)}, u32[]{:S(2)}) collective-permute-start(f32[3,3,1,2048]{3,2,1,0:T(1,128)S(1)} %get-tuple-element.52), channel_id=1, source_target_pairs={{0,4},{4,0},{8,12},{12,8},{16,20},{20,16},{24,28},{28,24},{1,5},{5... | collective-permute-start | bytes 221192 | tf_op jit(solution)/shard_map/ppermute | solution.py:499
  47.5 2.3 %collective-permute-start.5 = (f32[3,3,1,2048]{3,2,1,0:T(1,128)S(1)}, f32[3,3,1,2048]{3,2,1,0:T(1,128)S(1)}, u32[]{:S(2)}, u32[]{:S(2)}) collective-permute-start(f32[3,3,1,2048]{3,2,1,0:T(1,128)S(1)} %get-tuple-element.53), channel_id=1, source_target_pairs={{4,8},{12,16},{20,24},{8,4},{16,12},{24,20},{5,9},{13,17},{21,25},... | collective-permute-start | bytes 221192 | tf_op jit(solution)/shard_map/ppermute | solution.py:504

commit v7 on v6

--- a/solution.py
+++ b/solution.py
@@ -26,6 +26,8 @@
 def staged(kernel, where, outs, kept, column, *refs):
     count, sems = (len(where), refs[-1])
     held = list(refs[count + outs + len(kept) : -1])
+    target_count = sum(where) - len(kept)
+    held, extra = (held[:target_count], held[target_count:])
     target = dict(zip(kept, refs[count + outs : count + outs + len(kept)]))
     operands, copies = ([], [])
     for i, far in enumerate(where):
@@ -40,10 +42,10 @@
         copy.start()
     for copy in copies:
         copy.wait()
-    kernel(*operands, *refs[count : count + outs])
-
-
-def call(kernel, outs, args, far=(), keep=(), column=(), limit=LIMIT):
+    kernel(*operands, *refs[count : count + outs], *extra)
+
+
+def call(kernel, outs, args, far=(), keep=(), column=(), scratch=(), limit=LIMIT):
     where = [i in far for i in range(len(args))]
     spaces = [pltpu.HBM if w else pltpu.VMEM for w in where]
     every = (*outs, *(vmem(args[i].shape, args[i].dtype) for i in keep))
@@ -57,18 +59,9 @@
             for i, a in enumerate(args)
             if where[i] and i not in keep
         ]
-        + [pltpu.SemaphoreType.DMA((max(1, sum(where)),))],
+        + [*scratch, pltpu.SemaphoreType.DMA((max(1, sum(where)),))],
         compiler_params=pltpu.CompilerParams(vmem_limit_bytes=limit),
     )(*[pltpu.with_memory_space_constraint(a, s) for a, s in zip(args, spaces)])
-
-
-def nothing(*refs):
-    pass
-
-
-def load(*args):
-    every = range(len(args))
-    return call(nothing, (), args, far=every, keep=every, limit=1 << 20)
 
 
 def iota(shape, dim):
@@ -256,18 +249,18 @@
     hi, lo = lax.div(where, long), lax.rem(where, long)
     stack = [t[k * depth : (k + 1) * depth].reshape(depth * width, long) for t in tables for k in range(t.shape[0] // depth)]
     found = [value * f for f in pick(stack, hi, onehot(lo, long).astype(BF16))]
+    terms, index = (recv[:, 0, :count], recv[:, 0, count : 2 * count])
+    high = jnp.floor(index * (1.0 / lanes))
+    low = index - high * lanes
+    parts = [p.astype(F32) for p in split(terms)[:PARTS]]
+    row_of = iota((length // lanes, count), 0).astype(F32)
+    lane_of = iota((lanes, count), 0).astype(F32)
     total = jnp.zeros((length // lanes, lanes), F32)
-    group = 8
-    for first in range(0, devices, group):
-        lefts, rights = ([], [])
-        for d in range(first, first + group):
-            term = recv[d, :, :count]
-            index = recv[d, :, count : 2 * count].astype(I32)
-            hi, lo = lax.div(index, lanes), lax.rem(index, lanes)
-            hit = iota((length // lanes, count), 0) == hi
-            lefts.append(jnp.concatenate([jnp.where(hit, v.astype(F32), 0.0).astype(BF16) for v in split(term)], 0))
-            rights.append(onehot(lo, lanes).astype(BF16))
-        total = total + fold(dot_nt(jnp.concatenate(lefts, 1), jnp.concatenate(rights, 1)))
+    for d in range(devices):
+        hit = row_of == high[d : d + 1]
+        left = jnp.concatenate([jnp.where(hit, p[d : d + 1], 0.0).astype(BF16) for p in parts], 0)
+        right = jnp.where(lane_of == low[d : d + 1], 1.0, 0.0).astype(BF16)
+        total = total + fold(dot_nt(left, right), PARTS)
     acc = jnp.zeros((rows, lanes), F32)
     for i in range(chunks):
         copies[i].wait()
@@ -308,24 +301,13 @@
     two[...] = jnp.where(odd, last, first)
 
 
-def pressure_kernel(levels, *refs):
-    (recv, terms, pres), refs = (refs[:3], refs[3:])
-    sib, refs = (refs[:levels], refs[levels:])
-    far, refs = (refs[:3], refs[3:])
-    (p, coupled_z, one, two), near_by, refs = (refs[:4], refs[4:7], refs[7:])
-    rows_hot, lanes_hot, sol_hot, sol_row, sems = refs
-    copies = [pltpu.make_async_copy(a, b, sems.at[i]) for i, (a, b) in enumerate(zip(far, near_by))]
-    for copy in copies:
-        copy.start()
-    tz, store, tx = near_by
-    depth, width, long = pres.shape
+def table_kernel(levels, shape, terms, rows_hot, lanes_hot, sol_hot, sol_row, layer):
+    _, width, long = shape
+    lanes = 128
     rows = sol_hot.shape[0]
     count = terms.shape[2] // 3
-    lanes = 128
-    groups = groups_of(levels)
     at = 0
-    layer = None
-    for members in groups:
+    for members in groups_of(levels):
         for device in members:
             entry = terms[device]
             index = entry[:, count : 2 * count].astype(I32)
@@ -336,9 +318,18 @@
             lanes_hot[:, here] = onehot(lax.rem(y, lanes), lanes).astype(BF16)
             sol_hot[:, here] = onehot(lax.rem(index, rows), rows).astype(BF16)
             sol_row[:, here] = lax.div(index, rows)
-            if layer is None:
-                layer = lax.div(cell, long * width)
+            if at == 0:
+                layer[...] = lax.div(cell, long * width)
             at += count
+
+
+def pressure_kernel(levels, recv, terms, pres, *refs):
+    sib, (tz, store, tx, p, coupled_z, one, two, rows_hot, lanes_hot, sol_hot, sol_row, layer) = (refs[:levels], refs[levels:])
+    depth, width, long = pres.shape
+    table_kernel(levels, pres.shape, terms, rows_hot, lanes_hot, sol_hot, sol_row, layer)
+    rows, count = (sol_hot.shape[0], layer.shape[1])
+    groups = groups_of(levels)
+    layer = layer[...]
     table = jnp.concatenate(split(recv[...].reshape(recv.shape[0], recv.shape[2])[:, :rows]), 0)
     sol = fold(dot(table, sol_hot[...]))
     sol = jnp.sum(jnp.where(iota(sol.shape, 0) == sol_row[...], sol, 0.0), axis=0, keepdims=True)
@@ -347,8 +338,6 @@
         at = rows + column * count
         return jnp.concatenate([recv[device][:, at : at + count] for device in group], 1)
 
-    for copy in copies:
-        copy.wait()
     tzs = [tz[z] for z in range(depth)]
     gs, invs, first, final, coefs = factors(tzs, [store[z] for z in range(depth)])
     own = [coefs]
@@ -482,17 +471,23 @@
     send[...] = jnp.broadcast_to(out[:, None], send.shape)
 
 
-def finish_kernel(recv, s, image, rhs, update, lin_res, ratio):
+def finish_kernel(recv, s, image, rhs, update, lin_res, ratio, held_update, held_res, sems):
     sums = recv[...].reshape(recv.shape[0], recv.shape[2])
     whole = jnp.sum(sums, axis=0, keepdims=True)
     omega = whole[:, 0:1] / whole[:, 1:2]
+    copies = []
+    for c in range(3):
+        for z in range(s.shape[1]):
+            held_update[c, z] = omega * s[c, z]
+            held_res[c, z] = rhs[c, z] - omega * image[c, z]
+        for held, out in ((held_update, update), (held_res, lin_res)):
+            copies.append(pltpu.make_async_copy(held.at[c], out.at[c], sems.at[len(copies)]))
+            copies[-1].start()
     shift = sums[:, 5:6] - omega
     square = sums[:, 3:4] + 2.0 * shift * sums[:, 4:5] + shift * shift * sums[:, 1:2]
     ratio[...] = jnp.sqrt(jnp.sum(square, axis=0, keepdims=True) / whole[:, 2:3])
-    for c in range(3):
-        for z in range(s.shape[1]):
-            update[c, z] = omega * s[c, z]
-            lin_res[c, z] = rhs[c, z] - omega * image[c, z]
+    for copy in copies:
+        copy.wait()
 
 
 def flip(x, level, axis="layer"):
@@ -558,47 +553,47 @@
         compiler_params=pltpu.CompilerParams(vmem_limit_bytes=LIMIT),
     )(terms, cell, prod, tables, pltpu.with_memory_space_constraint(inverse, pltpu.HBM))
     sol = everywhere(send)
-    far = (tz, store, tx)
-    args = (sol, terms, pres, *sib)
     row3 = vmem((depth, 1, long))
-    p, coupled_z, one, two, tz, _, tx = pl.pallas_call(
+    at = 3 + levels
+    p, coupled_z, one, two, tz, _, tx = call(
         functools.partial(pressure_kernel, levels),
-        out_shape=(field, field, row3, row3) + tuple(vmem(a.shape) for a in far),
-        in_specs=[VM] * len(args) + [hbm_spec] * len(far),
-        out_specs=(VM,) * 7,
-        scratch_shapes=[
+        (field, field, row3, row3),
+        (sol, terms, pres, *sib, tz, store, tx),
+        far=(at, at + 1, at + 2),
+        keep=(at, at + 1, at + 2),
+        scratch=(
             vmem((width * long // 128, lists), BF16),
             vmem((128, lists), BF16),
             vmem((rows, lists), BF16),
             vmem((1, lists), I32),
-            pltpu.SemaphoreType.DMA((len(far),)),
-        ],
-        compiler_params=pltpu.CompilerParams(vmem_limit_bytes=LIMIT),
-    )(
-        *[pltpu.with_memory_space_constraint(a, pltpu.VMEM) for a in args],
-        *[pltpu.with_memory_space_constraint(a, pltpu.HBM) for a in far],
+            vmem((1, count), I32),
+        ),
     )
-    ty, rhs, diag, binv = load(ty, rhs, block_diag, block_inv)
     one, two = (flip(one, 0, "tile"), neighbour(two, "tile"))
     row9 = vmem((3, depth, 1, long))
     plane3 = planes(3)
     s, row_one, row_two, inner, outer = call(
         search_kernel,
         (vmem(rhs.shape), row9, row9, plane3, plane3),
-        (p, coupled_z, one, two, tx, ty, tz, rhs, diag, binv),
+        (p, coupled_z, one, two, tx, ty, tz, rhs, block_diag, block_inv),
     )
     outer, inner = (neighbour(outer), flip(inner, 0))
     row_one, row_two = (flip(row_one, 0, "tile"), neighbour(row_two, "tile"))
-    (part,) = call(inner_kernel, (vmem(rhs.shape),), (s, diag, tz, tx, ty))
+    (part,) = call(inner_kernel, (vmem(rhs.shape),), (s, block_diag, tz, tx, ty))
     image, send = call(
         image_kernel,
         (vmem(rhs.shape), vmem((devices, 1, 128))),
         (part, row_one, row_two, inner, outer, rhs, tz, tx),
     )
     sums = everywhere(send)
-    update, lin_res, ratio = call(
-        finish_kernel, (hbm(rhs.shape), hbm(rhs.shape), hbm((1, 1))), (sums, s, image, rhs)
-    )
+    update, lin_res, ratio = pl.pallas_call(
+        finish_kernel,
+        out_shape=(hbm(rhs.shape), hbm(rhs.shape), hbm((1, 1))),
+        in_specs=[VM] * 4,
+        out_specs=(hbm_spec, hbm_spec, VM),
+        scratch_shapes=[vmem(rhs.shape), vmem(rhs.shape), pltpu.SemaphoreType.DMA((6,))],
+        compiler_params=pltpu.CompilerParams(vmem_limit_bytes=LIMIT),
+    )(*[pltpu.with_memory_space_constraint(a, pltpu.VMEM) for a in (sums, s, image, rhs)])
     return (update, lin_res, ratio.reshape(()))
 
 

time: 69.9 us -> 69.3 us (level)
  Pallas kernels: 22 us -> 18.9 us
  waiting for transfers between devices: 3.72 us -> 6.14 us
  starting transfers between devices: 15.9 us -> 17.1 us
  blocking collectives: 27.2 us -> 26.1 us
    pallas_call x6 -> x5, Pallas kernels: 11.3 us -> 8.61 us  [call(): pl.pallas_call(functools.partial(staged, kernel, where, len(outs), tuple(...]
    ppermute x5, waiting for transfers between devices: 0.47 us -> 2.89 us  [flip(): lax.ppermute(x, axis, [(i, i ^ 1 << level) for i in range(lax.axis_size(a...]
    ppermute x5, starting transfers between devices: 6.92 us -> 8.12 us  [flip(): lax.ppermute(x, axis, [(i, i ^ 1 << level) for i in range(lax.axis_size(a...]
    all_to_all x2, blocking collectives: 27.2 us -> 26.1 us  [everywhere(): return lax.all_to_all(x, BOTH, split_axis=0, concat_axis=0, tiled=True)]
  transfers between devices with their start and end apart: 9 -> 9, of which waited for: 2 -> 3; matrix products, arithmetic and copies ran while one was open for 0% -> 0% of each run, Pallas kernels for 18% -> 13%
where the time goes in v7:
time: 69.3 us; the launch traced here: 69.1 us
  blocking collectives  26.1 us (38%)
  Pallas kernels  18.9 us (27%)
  starting transfers between devices  17.1 us (25%)
  waiting for transfers between devices  6.14 us (9%)
  between operations  0.79 us (1%)
    all_to_all x2, blocking collectives, everywhere(): return lax.all_to_all(x, BOTH, split_axis=0, concat_axis=0, tiled=True)  26.1 us
    pallas_call x5, Pallas kernels, call(): pl.pallas_call(functools.partial(staged, kernel, where, len(outs), tuple(...  8.61 us
    ppermute x5, starting transfers between devices, flip(): lax.ppermute(x, axis, [(i, i ^ 1 << level) for i in range(lax.axis_size(a...  8.12 us
    all_to_all x1, starting transfers between devices, everywhere(): return lax.all_to_all(x, BOTH, split_axis=0, concat_axis=0, tiled=True)  6.96 us
    pallas_call x1, Pallas kernels, shards(): pl.pallas_call(front_kernel, out_shape=vmem((devices, 1, rows + 2 * level...  5.06 us
    all_to_all x1, waiting for transfers between devices, everywhere(): return lax.all_to_all(x, BOTH, split_axis=0, concat_axis=0, tiled=True)  3.24 us
    pallas_call x1, Pallas kernels, shards(): pl.pallas_call(pres_kernel, out_shape=(field, vmem((devices, 1, 3 * count...  3.12 us
    ppermute x5, waiting for transfers between devices, flip(): lax.ppermute(x, axis, [(i, i ^ 1 << level) for i in range(lax.axis_size(a...  2.89 us
  transfers between devices with their start and end apart: 9, of which 3 were waited for; matrix products, arithmetic and copies ran while one was open for 0% of the time, Pallas kernels for 13%

profile of v7, /device:TPU:0, one launch (start us, length us, event | category | flops | bytes accessed | tf_op | source)
XLA Modules:
  0.0 69.1 jit_solution(11102252897317297377)
XLA Ops:
  0.6 3.1 %shard_map.139 = (f32[3,16,2048]{2,1,0:T(8,128)S(1)}, f32[32,1,768]{2,1,0:T(1,128)}, f32[6,16,2048]{2,1,0:T(8,128)S(1)}) custom-call(s32[1,256]{1,0:T(1,128)} %bitcast.4, s32[1,256]{1,0:T(1,128)} %bitcast.8, f32[1,256]{1,0:T(1,128)} %bitcast.6, f32[3,3,16,2048]{3,2,1,0:T(8,128)} %rhs.1, f32[3,3,16,2048]{3,2,1,0:T(8,128)} %wts_in.1, f32[3,16,2048]{2,1,0:T(8,128)} %refs_5_.3, ...), custom_call_target="tpu_custom_call" | custom-call | tf_op jit(solution)/shard_map/pallas_call | solution.py:522
  3.8 0.5 collective-permute-start
  4.3 7.0 %all-to-all-start = ((f32[32,1,768]{2,1,0:T(1,128)}), f32[32,1,768]{2,1,0:T(1,128)S(1)}, u32[]{:S(2)}, u32[]{:S(2)}) async-start(f32[32,1,768]{2,1,0:T(1,128)} %get-tuple-element.28), calls=%async_computation | async-start | bytes 196608 | tf_op jit(solution)/shard_map/all_to_all | solution.py:503
  11.2 0.0 copy-start.4
  11.3 0.0 copy-start.5
  11.3 0.0 collective-permute-done.refs_1_.refs_3_
  11.3 2.7 %shard_map.140 = (f32[6,16,2048]{2,1,0:T(8,128)}, f32[3,16,2048]{2,1,0:T(8,128)}, f32[6,16,2048]{2,1,0:T(8,128)}, f32[3,16,2048]{2,1,0:T(8,128)S(1)}, f32[6,16,2048]{2,1,0:T(8,128)S(1)}) custom-call(f32[6,16,2048]{2,1,0:T(8,128)S(1)} %get-tuple-element.29.refs_0_, f32[6,16,2048]{2,1,0:T(8,128)S(1)} %collective-permute-done.refs_1_.refs_3_, ...), custom_call_target="tpu_custom_call" | custom-call | tf_op jit(solution)/shard_map/pallas_call | solution.py:52
  14.0 1.8 %collective-permute-start.1 = (f32[3,16,2048]{2,1,0:T(8,128)}, f32[3,16,2048]{2,1,0:T(8,128)S(1)}, u32[]{:S(2)}, u32[]{:S(2)}) collective-permute-start(f32[3,16,2048]{2,1,0:T(8,128)} %get-tuple-element.36), channel_id=1, source_target_pairs={{0,2},{1,3},{2,0},{3,1},{4,6},{5,7},{6,4},{7,5},{8,10},{9,11},{10,... | collective-permute-start | bytes 1179656 | tf_op jit(solution)/shard_map/ppermute | solution.py:494
  15.8 3.2 %all-to-all-done.recv.refs_1_ = f32[32,1,768]{2,1,0:T(1,128)S(1)} async-done(((f32[32,1,768]{2,1,0:T(1,128)}), f32[32,1,768]{2,1,0:T(1,128)S(1)}, u32[]{:S(2)}, u32[]{:S(2)}) %all-to-all-start) | async-done | bytes 98336 | tf_op jit(solution)/shard_map/all_to_all | solution.py:503
  19.1 0.0 copy-done.5
  19.1 5.1 %shard_map.141 = f32[32,1,1280]{2,1,0:T(1,128)S(1)} custom-call(f32[32,1,768]{2,1,0:T(1,128)S(1)} %all-to-all-done.recv.refs_1_, s32[1,256]{1,0:T(1,128)S(1)} %bitcast.5, f32[1,256]{1,0:T(1,128)S(1)} %bitcast.7, f32[6,16,2048]{2,1,0:T(8,128)S(1)} %get-tuple-element.33.tables_0_, f32[3,16,2048]{2,1,0:T(8,128)S(1)} %get-tuple-element.34.tables_1_, ...), custom_call_target="tpu_custom_call" | custom-call | tf_op jit(solution)/shard_map/pallas_call | solution.py:547
  24.1 10.3 %all_to_all.15.refs_0_ = f32[32,1,1280]{2,1,0:T(1,128)S(1)} all-to-all(f32[32,1,1280]{2,1,0:T(1,128)S(1)} %shard_map.141), channel_id=1, replica_groups=mesh['tile'=8,'layer'=4] {'tile','layer'}, dimensions={0} | all-to-all | bytes 327680 | tf_op jit(solution)/shard_map/all_to_all | solution.py:503
  34.4 0.0 collective-permute-done.1.refs_4_
  34.4 2.6 %shard_map.142 = (f32[3,16,2048]{2,1,0:T(8,128)S(1)}, f32[3,16,2048]{2,1,0:T(8,128)S(1)}, f32[3,1,2048]{2,1,0:T(1,128)S(1)}, f32[3,1,2048]{2,1,0:T(1,128)S(1)}, ...) custom-call(f32[32,1,1280]{2,1,0:T(1,128)S(1)} %all_to_all.15.refs_0_, ...), custom_call_target="tpu_custom_call" | custom-call | tf_op jit(solution)/shard_map/pallas_call | solution.py:52
  37.0 0.8 %collective-permute-start.2 = (f32[3,1,2048]{2,1,0:T(1,128)S(1)}, f32[3,1,2048]{2,1,0:T(1,128)S(1)}, u32[]{:S(2)}, u32[]{:S(2)}) collective-permute-start(f32[3,1,2048]{2,1,0:T(1,128)S(1)} %get-tuple-element.39), channel_id=1, source_target_pairs={{0,4},{4,0},{8,12},{12,8},{16,20},{20,16},{24,28},{28,24},{1,5},{5... | collective-permute-start | bytes 73736 | tf_op jit(solution)/shard_map/ppermute | solution.py:494
  37.9 0.7 collective-permute-start.3
  38.5 2.4 %collective-permute-done.2.refs_2_ = f32[3,1,2048]{2,1,0:T(1,128)S(1)} collective-permute-done((f32[3,1,2048]{2,1,0:T(1,128)S(1)}, f32[3,1,2048]{2,1,0:T(1,128)S(1)}, u32[]{:S(2)}, u32[]{:S(2)}) %collective-permute-start.2) | collective-permute-done | bytes 24608 | tf_op jit(solution)/shard_map/ppermute | solution.py:494
  41.0 0.0 collective-permute-done.3.refs_3_
  41.0 0.0 copy-done.1
  41.0 0.9 %shard_map.143 = (f32[3,3,16,2048]{3,2,1,0:T(8,128)S(1)}, f32[3,3,1,2048]{3,2,1,0:T(1,128)S(1)}, f32[3,3,1,2048]{3,2,1,0:T(1,128)S(1)}, f32[3,16,2048]{2,1,0:T(8,128)S(1)}, f32[3,16,2048]{2,1,0:T(8,128)S(1)}) custom-call(f32[3,16,2048]{2,1,0:T(8,128)S(1)} %get-tuple-element.37.refs_0_, f32[3,16,2048]{2,1,0:T(8,128)S(1)} %get-tuple-element.38.refs_1_, ...), custom_call_target="tpu_custom_call" | custom-call | tf_op jit(solution)/shard_map/pallas_call | solution.py:52
  41.9 0.1 collective-permute-start.6
  42.0 0.7 collective-permute-start.7
  42.7 4.9 %collective-permute-start.4 = (f32[3,3,1,2048]{3,2,1,0:T(1,128)S(1)}, f32[3,3,1,2048]{3,2,1,0:T(1,128)S(1)}, u32[]{:S(2)}, u32[]{:S(2)}) collective-permute-start(f32[3,3,1,2048]{3,2,1,0:T(1,128)S(1)} %get-tuple-element.44), channel_id=1, source_target_pairs={{0,4},{4,0},{8,12},{12,8},{16,20},{20,16},{24,28},{28,24},{1,5},{5... | collective-permute-start | bytes 221192 | tf_op jit(solution)/shard_map/ppermute | solution.py:494
  47.5 0.7 collective-permute-start.5
  48.2 1.2 %shard_map.144.refs_0_ = f32[3,3,16,2048]{3,2,1,0:T(8,128)S(1)} custom-call(f32[3,3,16,2048]{3,2,1,0:T(8,128)S(1)} %get-tuple-element.43.refs_0_.s, f32[3,3,3,16,2048]{4,3,2,1,0:T(8,128)S(1)} %copy-done.1, f32[3,16,2048]{2,1,0:T(8,128)S(1)} %get-tuple-element.42.refs_6_.refs_2_, f32[3,16,2048]{2,1,0:T(8,128)S(1)} %get-tuple-element.41.refs_4_.refs_3_.refs_7_, ...), custom_call_target="tpu_custom_call" | custom-call | tf_op jit(solution)/shard_map/pallas_call | solution.py:52
  49.4 0.5 collective-permute-done.4.refs_1_
  49.9 0.0 collective-permute-done.5.refs_2_
  49.9 0.0 collective-permute-done.6.refs_3_
  49.9 0.0 collective-permute-done.7.refs_4_
  49.9 1.2 %shard_map.145 = (f32[3,3,16,2048]{3,2,1,0:T(8,128)S(1)}, f32[32,1,128]{2,1,0:T(1,128)S(1)}) custom-call(f32[3,3,16,2048]{3,2,1,0:T(8,128)S(1)} %shard_map.144.refs_0_, f32[3,3,1,2048]{3,2,1,0:T(1,128)S(1)} %collective-permute-done.4.refs_1_, f32[3,3,1,2048]{3,2,1,0:T(1,128)S(1)} %collective-permute-done.5.refs_2_, ...), custom_call_target="tpu_custom_call" | custom-call | tf_op jit(solution)/shard_map/pallas_call | solution.py:52
  51.1 15.9 %all_to_all.16.recv = f32[32,1,128]{2,1,0:T(1,128)S(1)} all-to-all(f32[32,1,128]{2,1,0:T(1,128)S(1)} %get-tuple-element.48), channel_id=1, replica_groups=mesh['tile'=8,'layer'=4] {'tile','layer'}, dimensions={0} | all-to-all | bytes 32768 | tf_op jit(solution)/shard_map/all_to_all | solution.py:503
  66.9 2.1 %shard_map.146 = (f32[3,3,16,2048]{3,2,1,0:T(8,128)}, f32[3,3,16,2048]{3,2,1,0:T(8,128)}, f32[1,1]{1,0:T(1,128)}) custom-call(f32[32,1,128]{2,1,0:T(1,128)S(1)} %all_to_all.16.recv, f32[3,3,16,2048]{3,2,1,0:T(8,128)S(1)} %get-tuple-element.43.refs_0_.s, f32[3,3,16,2048]{3,2,1,0:T(8,128)S(1)} %get-tuple-element.49.image, f32[3,3,16,2048]{3,2,1,0:T(8,128)S(1)} %copy-done), custom_call_target="tpu_custom_call" | custom-call | tf_op jit(solution)/shard_map/pallas_call | solution.py:589
  (8 shorter events, 0.0 us)
Async XLA Ops:
  3.8 7.5 %collective-permute-start = (f32[6,16,2048]{2,1,0:T(8,128)S(1)}, f32[6,16,2048]{2,1,0:T(8,128)S(1)}, u32[]{:S(2)}, u32[]{:S(2)}) collective-permute-start(f32[6,16,2048]{2,1,0:T(8,128)S(1)} %get-tuple-element.29.refs_0_), channel_id=1, source_target_pairs={{0,1},{1,0},{2,3},{3,2},{4,5},{5,4},{6,7},{7,6},{8,9},{9,8},{10,11... | collective-permute-start | bytes 2359304 | tf_op jit(solution)/shard_map/ppermute | solution.py:494
  4.3 14.8 %all-to-all-start = ((f32[32,1,768]{2,1,0:T(1,128)}), f32[32,1,768]{2,1,0:T(1,128)S(1)}, u32[]{:S(2)}, u32[]{:S(2)}) async-start(f32[32,1,768]{2,1,0:T(1,128)} %get-tuple-element.28), calls=%async_computation | async-start | bytes 196608 | tf_op jit(solution)/shard_map/all_to_all | solution.py:503
  11.2 7.8 %copy-start.4 = (s32[256]{0:T(256)S(1)}, s32[256]{0:T(256)}, u32[]{:S(2)}) copy-start(s32[256]{0:T(256)} %param.20) | copy-start | bytes 3076
  11.3 7.8 %copy-start.5 = (f32[256]{0:T(256)S(1)}, f32[256]{0:T(256)}, u32[]{:S(2)}) copy-start(f32[256]{0:T(256)} %param.22) | copy-start | bytes 3076
  14.0 20.4 %collective-permute-start.1 = (f32[3,16,2048]{2,1,0:T(8,128)}, f32[3,16,2048]{2,1,0:T(8,128)S(1)}, u32[]{:S(2)}, u32[]{:S(2)}) collective-permute-start(f32[3,16,2048]{2,1,0:T(8,128)} %get-tuple-element.36), channel_id=1, source_target_pairs={{0,2},{1,3},{2,0},{3,1},{4,6},{5,7},{6,4},{7,5},{8,10},{9,11},{10,... | collective-permute-start | bytes 1179656 | tf_op jit(solution)/shard_map/ppermute | solution.py:494
  19.1 21.9 %copy-start.1 = (f32[3,3,3,16,2048]{4,3,2,1,0:T(8,128)S(1)}, f32[3,3,3,16,2048]{4,3,2,1,0:T(8,128)}, u32[]{:S(2)}) copy-start(f32[3,3,3,16,2048]{4,3,2,1,0:T(8,128)} %refs_1_.1) | copy-start | bytes 10616836
  19.1 21.9 %copy-start.2 = (f32[3,3,3,16,2048]{4,3,2,1,0:T(8,128)S(1)}, f32[3,3,3,16,2048]{4,3,2,1,0:T(8,128)}, u32[]{:S(2)}) copy-start(f32[3,3,3,16,2048]{4,3,2,1,0:T(8,128)} %refs_9_.1) | copy-start | bytes 10616836
  34.4 6.6 %copy-start = (f32[3,3,16,2048]{3,2,1,0:T(8,128)S(1)}, f32[3,3,16,2048]{3,2,1,0:T(8,128)}, u32[]{:S(2)}) copy-start(f32[3,3,16,2048]{3,2,1,0:T(8,128)} %rhs.1) | copy-start | bytes 3538948
  34.4 6.6 %copy-start.3 = (f32[3,16,2048]{2,1,0:T(8,128)S(1)}, f32[3,16,2048]{2,1,0:T(8,128)}, u32[]{:S(2)}) copy-start(f32[3,16,2048]{2,1,0:T(8,128)} %refs_4_.1) | copy-start | bytes 1179652
  37.0 3.9 %collective-permute-start.2 = (f32[3,1,2048]{2,1,0:T(1,128)S(1)}, f32[3,1,2048]{2,1,0:T(1,128)S(1)}, u32[]{:S(2)}, u32[]{:S(2)}) collective-permute-start(f32[3,1,2048]{2,1,0:T(1,128)S(1)} %get-tuple-element.39), channel_id=1, source_target_pairs={{0,4},{4,0},{8,12},{12,8},{16,20},{20,16},{24,28},{28,24},{1,5},{5... | collective-permute-start | bytes 73736 | tf_op jit(solution)/shard_map/ppermute | solution.py:494
  37.9 3.1 %collective-permute-start.3 = (f32[3,1,2048]{2,1,0:T(1,128)S(1)}, f32[3,1,2048]{2,1,0:T(1,128)S(1)}, u32[]{:S(2)}, u32[]{:S(2)}) collective-permute-start(f32[3,1,2048]{2,1,0:T(1,128)S(1)} %get-tuple-element.40), channel_id=1, source_target_pairs={{4,8},{12,16},{20,24},{8,4},{16,12},{24,20},{5,9},{13,17},{21,25},... | collective-permute-start | bytes 73736 | tf_op jit(solution)/shard_map/ppermute | solution.py:499
  41.9 8.0 %collective-permute-start.6 = (f32[3,16,2048]{2,1,0:T(8,128)S(1)}, f32[3,16,2048]{2,1,0:T(8,128)S(1)}, u32[]{:S(2)}, u32[]{:S(2)}) collective-permute-start(f32[3,16,2048]{2,1,0:T(8,128)S(1)} %get-tuple-element.46), channel_id=1, source_target_pairs={{0,1},{1,0},{2,3},{3,2},{4,5},{5,4},{6,7},{7,6},{8,9},{9,8},{10,11... | collective-permute-start | bytes 1179656 | tf_op jit(solution)/shard_map/ppermute | solution.py:494
  42.0 7.9 %collective-permute-start.7 = (f32[3,16,2048]{2,1,0:T(8,128)S(1)}, f32[3,16,2048]{2,1,0:T(8,128)S(1)}, u32[]{:S(2)}, u32[]{:S(2)}) collective-permute-start(f32[3,16,2048]{2,1,0:T(8,128)S(1)} %get-tuple-element.47), channel_id=1, source_target_pairs={{1,2},{2,1},{5,6},{6,5},{9,10},{10,9},{13,14},{14,13},{17,18},{18,... | collective-permute-start | bytes 1179656 | tf_op jit(solution)/shard_map/ppermute | solution.py:499
  42.7 7.2 %collective-permute-start.4 = (f32[3,3,1,2048]{3,2,1,0:T(1,128)S(1)}, f32[3,3,1,2048]{3,2,1,0:T(1,128)S(1)}, u32[]{:S(2)}, u32[]{:S(2)}) collective-permute-start(f32[3,3,1,2048]{3,2,1,0:T(1,128)S(1)} %get-tuple-element.44), channel_id=1, source_target_pairs={{0,4},{4,0},{8,12},{12,8},{16,20},{20,16},{24,28},{28,24},{1,5},{5... | collective-permute-start | bytes 221192 | tf_op jit(solution)/shard_map/ppermute | solution.py:494
  47.5 2.3 %collective-permute-start.5 = (f32[3,3,1,2048]{3,2,1,0:T(1,128)S(1)}, f32[3,3,1,2048]{3,2,1,0:T(1,128)S(1)}, u32[]{:S(2)}, u32[]{:S(2)}) collective-permute-start(f32[3,3,1,2048]{3,2,1,0:T(1,128)S(1)} %get-tuple-element.45), channel_id=1, source_target_pairs={{4,8},{12,16},{20,24},{8,4},{16,12},{24,20},{5,9},{13,17},{21,25},... | collective-permute-start | bytes 221192 | tf_op jit(solution)/shard_map/ppermute | solution.py:499

commit v8 on v7

--- a/solution.py
+++ b/solution.py
@@ -324,7 +324,7 @@
 
 
 def pressure_kernel(levels, recv, terms, pres, *refs):
-    sib, (tz, store, tx, p, coupled_z, one, two, rows_hot, lanes_hot, sol_hot, sol_row, layer) = (refs[:levels], refs[levels:])
+    sib, (tz, store, tx, p, coupled_z, two, one, rows_hot, lanes_hot, sol_hot, sol_row, layer) = (refs[:levels], refs[levels:])
     depth, width, long = pres.shape
     table_kernel(levels, pres.shape, terms, rows_hot, lanes_hot, sol_hot, sol_row, layer)
     rows, count = (sol_hot.shape[0], layer.shape[1])
@@ -397,7 +397,7 @@
         tile_rows(values[z][0:1], (tx[z] * values[z])[width - 1 :], one.at[z], two.at[z])
 
 
-def search_kernel(p, coupled_z, one, two, tx, ty, tz, rhs, diag, binv, s, row_one, row_two, inner, outer):
+def search_kernel(p, coupled_z, two, one, tx, ty, tz, rhs, diag, binv, s, outer, row_two, row_one, inner):
     depth, width, _ = p.shape
     odd = is_right(0, "tile")
     right = is_right(0)
@@ -435,7 +435,7 @@
             image[c, z] = total
 
 
-def image_kernel(part, row_one, row_two, inner, outer, rhs, tz, tx, image, send):
+def image_kernel(part, outer, row_two, row_one, inner, rhs, tz, tx, image, send):
     depth, width = part.shape[1:3]
     right, odd = (is_right(0), is_right(0, "tile"))
     row = iota(part.shape[2:], 0)
@@ -471,23 +471,17 @@
     send[...] = jnp.broadcast_to(out[:, None], send.shape)
 
 
-def finish_kernel(recv, s, image, rhs, update, lin_res, ratio, held_update, held_res, sems):
+def finish_kernel(recv, s, image, rhs, update, lin_res, ratio):
     sums = recv[...].reshape(recv.shape[0], recv.shape[2])
     whole = jnp.sum(sums, axis=0, keepdims=True)
     omega = whole[:, 0:1] / whole[:, 1:2]
-    copies = []
-    for c in range(3):
-        for z in range(s.shape[1]):
-            held_update[c, z] = omega * s[c, z]
-            held_res[c, z] = rhs[c, z] - omega * image[c, z]
-        for held, out in ((held_update, update), (held_res, lin_res)):
-            copies.append(pltpu.make_async_copy(held.at[c], out.at[c], sems.at[len(copies)]))
-            copies[-1].start()
     shift = sums[:, 5:6] - omega
     square = sums[:, 3:4] + 2.0 * shift * sums[:, 4:5] + shift * shift * sums[:, 1:2]
     ratio[...] = jnp.sqrt(jnp.sum(square, axis=0, keepdims=True) / whole[:, 2:3])
-    for copy in copies:
-        copy.wait()
+    for c in range(3):
+        for z in range(s.shape[1]):
+            update[c, z] = omega * s[c, z]
+            lin_res[c, z] = rhs[c, z] - omega * image[c, z]
 
 
 def flip(x, level, axis="layer"):
@@ -555,7 +549,7 @@
     sol = everywhere(send)
     row3 = vmem((depth, 1, long))
     at = 3 + levels
-    p, coupled_z, one, two, tz, _, tx = call(
+    p, coupled_z, two, one, tz, _, tx = call(
         functools.partial(pressure_kernel, levels),
         (field, field, row3, row3),
         (sol, terms, pres, *sib, tz, store, tx),
@@ -569,31 +563,26 @@
             vmem((1, count), I32),
         ),
     )
-    one, two = (flip(one, 0, "tile"), neighbour(two, "tile"))
+    two, one = (neighbour(two, "tile"), flip(one, 0, "tile"))
     row9 = vmem((3, depth, 1, long))
     plane3 = planes(3)
-    s, row_one, row_two, inner, outer = call(
+    s, outer, row_two, row_one, inner = call(
         search_kernel,
-        (vmem(rhs.shape), row9, row9, plane3, plane3),
-        (p, coupled_z, one, two, tx, ty, tz, rhs, block_diag, block_inv),
+        (vmem(rhs.shape), plane3, row9, row9, plane3),
+        (p, coupled_z, two, one, tx, ty, tz, rhs, block_diag, block_inv),
     )
-    outer, inner = (neighbour(outer), flip(inner, 0))
-    row_one, row_two = (flip(row_one, 0, "tile"), neighbour(row_two, "tile"))
+    outer, row_two = (neighbour(outer), neighbour(row_two, "tile"))
+    row_one, inner = (flip(row_one, 0, "tile"), flip(inner, 0))
     (part,) = call(inner_kernel, (vmem(rhs.shape),), (s, block_diag, tz, tx, ty))
     image, send = call(
         image_kernel,
         (vmem(rhs.shape), vmem((devices, 1, 128))),
-        (part, row_one, row_two, inner, outer, rhs, tz, tx),
+        (part, outer, row_two, row_one, inner, rhs, tz, tx),
     )
     sums = everywhere(send)
-    update, lin_res, ratio = pl.pallas_call(
-        finish_kernel,
-        out_shape=(hbm(rhs.shape), hbm(rhs.shape), hbm((1, 1))),
-        in_specs=[VM] * 4,
-        out_specs=(hbm_spec, hbm_spec, VM),
-        scratch_shapes=[vmem(rhs.shape), vmem(rhs.shape), pltpu.SemaphoreType.DMA((6,))],
-        compiler_params=pltpu.CompilerParams(vmem_limit_bytes=LIMIT),
-    )(*[pltpu.with_memory_space_constraint(a, pltpu.VMEM) for a in (sums, s, image, rhs)])
+    update, lin_res, ratio = call(
+        finish_kernel, (hbm(rhs.shape), hbm(rhs.shape), hbm((1, 1))), (sums, s, image, rhs)
+    )
     return (update, lin_res, ratio.reshape(()))
 
 

time: 69.3 us -> 68.2 us (0.984)
  blocking collectives: 26.1 us -> 20.7 us
  starting transfers between devices: 17.1 us -> 21.9 us
    all_to_all x2, blocking collectives: 26.1 us -> 20.7 us  [everywhere(): return lax.all_to_all(x, BOTH, split_axis=0, concat_axis=0, tiled=True)]
    ppermute x5, starting transfers between devices: 8.12 us -> 12.9 us  [flip(): lax.ppermute(x, axis, [(i, i ^ 1 << level) for i in range(lax.axis_size(a...]
    pallas_call x1 -> x0, Pallas kernels: 2.11 us -> none  [shards(): pl.pallas_call(finish_kernel, out_shape=(hbm(rhs.shape), hbm(rhs.shape),...]
    pallas_call x5 -> x6, Pallas kernels: 8.61 us -> 10.3 us  [call(): pl.pallas_call(functools.partial(staged, kernel, where, len(outs), tuple(...]
where the time goes in v8:
time: 68.2 us; the launch traced here: 68 us
  starting transfers between devices  21.9 us (32%)
  blocking collectives  20.7 us (30%)
  Pallas kernels  18.4 us (27%)
  waiting for transfers between devices  6.17 us (9%)
  between operations  0.78 us (1%)
    all_to_all x2, blocking collectives, everywhere(): return lax.all_to_all(x, BOTH, split_axis=0, concat_axis=0, tiled=True)  20.7 us
    ppermute x5, starting transfers between devices, flip(): lax.ppermute(x, axis, [(i, i ^ 1 << level) for i in range(lax.axis_size(a...  12.9 us
    pallas_call x6, Pallas kernels, call(): pl.pallas_call(functools.partial(staged, kernel, where, len(outs), tuple(...  10.3 us
    all_to_all x1, starting transfers between devices, everywhere(): return lax.all_to_all(x, BOTH, split_axis=0, concat_axis=0, tiled=True)  6.96 us
    pallas_call x1, Pallas kernels, shards(): pl.pallas_call(front_kernel, out_shape=vmem((devices, 1, rows + 2 * level...  5.06 us
    all_to_all x1, waiting for transfers between devices, everywhere(): return lax.all_to_all(x, BOTH, split_axis=0, concat_axis=0, tiled=True)  3.24 us
    pallas_call x1, Pallas kernels, shards(): pl.pallas_call(pres_kernel, out_shape=(field, vmem((devices, 1, 3 * count...  3.12 us
    ppermute x5, waiting for transfers between devices, flip(): lax.ppermute(x, axis, [(i, i ^ 1 << level) for i in range(lax.axis_size(a...  2.92 us
  transfers between devices with their start and end apart: 9, of which 3 were waited for; matrix products, arithmetic and copies ran while one was open for 0% of the time, Pallas kernels for 13%

profile of v8, /device:TPU:0, one launch (start us, length us, event | category | flops | bytes accessed | tf_op | source)
XLA Modules:
  0.0 68.0 jit_solution(11586442436850919223)
XLA Ops:
  0.6 3.1 %shard_map.139 = (f32[3,16,2048]{2,1,0:T(8,128)S(1)}, f32[32,1,768]{2,1,0:T(1,128)}, f32[6,16,2048]{2,1,0:T(8,128)S(1)}) custom-call(s32[1,256]{1,0:T(1,128)} %bitcast.4, s32[1,256]{1,0:T(1,128)} %bitcast.8, f32[1,256]{1,0:T(1,128)} %bitcast.6, f32[3,3,16,2048]{3,2,1,0:T(8,128)} %refs_3_.3, f32[3,3,16,2048]{3,2,1,0:T(8,128)} %wts_in.1, ...), custom_call_target="tpu_custom_call" | custom-call | tf_op jit(solution)/shard_map/pallas_call | solution.py:516
  3.8 0.5 collective-permute-start
  4.3 7.0 %all-to-all-start = ((f32[32,1,768]{2,1,0:T(1,128)}), f32[32,1,768]{2,1,0:T(1,128)S(1)}, u32[]{:S(2)}, u32[]{:S(2)}) async-start(f32[32,1,768]{2,1,0:T(1,128)} %get-tuple-element.28), calls=%async_computation | async-start | bytes 196608 | tf_op jit(solution)/shard_map/all_to_all | solution.py:497
  11.2 0.0 copy-start.4
  11.3 0.0 copy-start.5
  11.3 0.0 collective-permute-done.refs_1_.refs_3_
  11.3 2.7 %shard_map.140 = (f32[6,16,2048]{2,1,0:T(8,128)}, f32[3,16,2048]{2,1,0:T(8,128)}, f32[6,16,2048]{2,1,0:T(8,128)}, f32[3,16,2048]{2,1,0:T(8,128)S(1)}, f32[6,16,2048]{2,1,0:T(8,128)S(1)}) custom-call(f32[6,16,2048]{2,1,0:T(8,128)S(1)} %get-tuple-element.29.refs_0_, f32[6,16,2048]{2,1,0:T(8,128)S(1)} %collective-permute-done.refs_1_.refs_3_, ...), custom_call_target="tpu_custom_call" | custom-call | tf_op jit(solution)/shard_map/pallas_call | solution.py:52
  14.0 1.8 %collective-permute-start.1 = (f32[3,16,2048]{2,1,0:T(8,128)}, f32[3,16,2048]{2,1,0:T(8,128)S(1)}, u32[]{:S(2)}, u32[]{:S(2)}) collective-permute-start(f32[3,16,2048]{2,1,0:T(8,128)} %get-tuple-element.36), channel_id=1, source_target_pairs={{0,2},{1,3},{2,0},{3,1},{4,6},{5,7},{6,4},{7,5},{8,10},{9,11},{10,... | collective-permute-start | bytes 1179656 | tf_op jit(solution)/shard_map/ppermute | solution.py:488
  15.8 3.2 %all-to-all-done.recv.refs_1_ = f32[32,1,768]{2,1,0:T(1,128)S(1)} async-done(((f32[32,1,768]{2,1,0:T(1,128)}), f32[32,1,768]{2,1,0:T(1,128)S(1)}, u32[]{:S(2)}, u32[]{:S(2)}) %all-to-all-start) | async-done | bytes 98336 | tf_op jit(solution)/shard_map/all_to_all | solution.py:497
  19.1 0.0 copy-done.5
  19.1 5.1 %shard_map.141 = f32[32,1,1280]{2,1,0:T(1,128)S(1)} custom-call(f32[32,1,768]{2,1,0:T(1,128)S(1)} %all-to-all-done.recv.refs_1_, s32[1,256]{1,0:T(1,128)S(1)} %bitcast.5, f32[1,256]{1,0:T(1,128)S(1)} %bitcast.7, f32[6,16,2048]{2,1,0:T(8,128)S(1)} %get-tuple-element.33.tables_0_, f32[3,16,2048]{2,1,0:T(8,128)S(1)} %get-tuple-element.34.tables_1_, ...), custom_call_target="tpu_custom_call" | custom-call | tf_op jit(solution)/shard_map/pallas_call | solution.py:541
  24.1 10.3 %all_to_all.15.refs_0_ = f32[32,1,1280]{2,1,0:T(1,128)S(1)} all-to-all(f32[32,1,1280]{2,1,0:T(1,128)S(1)} %shard_map.141), channel_id=1, replica_groups=mesh['tile'=8,'layer'=4] {'tile','layer'}, dimensions={0} | all-to-all | bytes 327680 | tf_op jit(solution)/shard_map/all_to_all | solution.py:497
  34.4 0.0 collective-permute-done.1.refs_4_
  34.4 2.6 %shard_map.142 = (f32[3,16,2048]{2,1,0:T(8,128)S(1)}, f32[3,16,2048]{2,1,0:T(8,128)S(1)}, f32[3,1,2048]{2,1,0:T(1,128)S(1)}, f32[3,1,2048]{2,1,0:T(1,128)S(1)}, ...) custom-call(f32[32,1,1280]{2,1,0:T(1,128)S(1)} %all_to_all.15.refs_0_, ...), custom_call_target="tpu_custom_call" | custom-call | tf_op jit(solution)/shard_map/pallas_call | solution.py:52
  37.0 0.7 collective-permute-start.2
  37.7 3.5 %collective-permute-start.3 = (f32[3,1,2048]{2,1,0:T(1,128)S(1)}, f32[3,1,2048]{2,1,0:T(1,128)S(1)}, u32[]{:S(2)}, u32[]{:S(2)}) collective-permute-start(f32[3,1,2048]{2,1,0:T(1,128)S(1)} %get-tuple-element.40), channel_id=1, source_target_pairs={{0,4},{4,0},{8,12},{12,8},{16,20},{20,16},{24,28},{28,24},{1,5},{5... | collective-permute-start | bytes 73736 | tf_op jit(solution)/shard_map/ppermute | solution.py:488
  41.2 0.0 collective-permute-done.2.refs_2_
  41.2 1.8 %collective-permute-done.3.refs_3_ = f32[3,1,2048]{2,1,0:T(1,128)S(1)} collective-permute-done((f32[3,1,2048]{2,1,0:T(1,128)S(1)}, f32[3,1,2048]{2,1,0:T(1,128)S(1)}, u32[]{:S(2)}, u32[]{:S(2)}) %collective-permute-start.3) | collective-permute-done | bytes 24608 | tf_op jit(solution)/shard_map/ppermute | solution.py:488
  43.1 0.0 copy-done.3
  43.1 0.9 %shard_map.143 = (f32[3,3,16,2048]{3,2,1,0:T(8,128)S(1)}, f32[3,16,2048]{2,1,0:T(8,128)S(1)}, f32[3,3,1,2048]{3,2,1,0:T(1,128)S(1)}, f32[3,3,1,2048]{3,2,1,0:T(1,128)S(1)}, f32[3,16,2048]{2,1,0:T(8,128)S(1)}) custom-call(f32[3,16,2048]{2,1,0:T(8,128)S(1)} %get-tuple-element.37.refs_0_, f32[3,16,2048]{2,1,0:T(8,128)S(1)} %get-tuple-element.38.refs_1_, ...), custom_call_target="tpu_custom_call" | custom-call | tf_op jit(solution)/shard_map/pallas_call | solution.py:52
  44.0 0.7 %collective-permute-start.4 = (f32[3,16,2048]{2,1,0:T(8,128)S(1)}, f32[3,16,2048]{2,1,0:T(8,128)S(1)}, u32[]{:S(2)}, u32[]{:S(2)}) collective-permute-start(f32[3,16,2048]{2,1,0:T(8,128)S(1)} %get-tuple-element.44), channel_id=1, source_target_pairs={{1,2},{2,1},{5,6},{6,5},{9,10},{10,9},{13,14},{14,13},{17,18},{18,... | collective-permute-start | bytes 1179656 | tf_op jit(solution)/shard_map/ppermute | solution.py:493
  44.7 1.5 %collective-permute-start.7 = (f32[3,16,2048]{2,1,0:T(8,128)S(1)}, f32[3,16,2048]{2,1,0:T(8,128)S(1)}, u32[]{:S(2)}, u32[]{:S(2)}) collective-permute-start(f32[3,16,2048]{2,1,0:T(8,128)S(1)} %get-tuple-element.47), channel_id=1, source_target_pairs={{0,1},{1,0},{2,3},{3,2},{4,5},{5,4},{6,7},{7,6},{8,9},{9,8},{10,11... | collective-permute-start | bytes 1179656 | tf_op jit(solution)/shard_map/ppermute | solution.py:488
  46.2 0.7 collective-permute-start.5
  46.8 5.6 %collective-permute-start.6 = (f32[3,3,1,2048]{3,2,1,0:T(1,128)S(1)}, f32[3,3,1,2048]{3,2,1,0:T(1,128)S(1)}, u32[]{:S(2)}, u32[]{:S(2)}) collective-permute-start(f32[3,3,1,2048]{3,2,1,0:T(1,128)S(1)} %get-tuple-element.46), channel_id=1, source_target_pairs={{0,4},{4,0},{8,12},{12,8},{16,20},{20,16},{24,28},{28,24},{1,5},{5... | collective-permute-start | bytes 221192 | tf_op jit(solution)/shard_map/ppermute | solution.py:488
  52.4 1.2 %shard_map.144.refs_0_ = f32[3,3,16,2048]{3,2,1,0:T(8,128)S(1)} custom-call(f32[3,3,16,2048]{3,2,1,0:T(8,128)S(1)} %get-tuple-element.43.refs_0_.refs_1_, f32[3,3,3,16,2048]{4,3,2,1,0:T(8,128)S(1)} %copy-done.1, f32[3,16,2048]{2,1,0:T(8,128)S(1)} %get-tuple-element.42.refs_6_.refs_2_, f32[3,16,2048]{2,1,0:T(8,128)S(1)} %get-tuple-element.41.refs_4_.refs_3_.refs_7_, ...), custom_call_target="tpu_custom_call" | custom-call | tf_op jit(solution)/shard_map/pallas_call | solution.py:52
  53.6 0.0 collective-permute-done.5.refs_2_
  53.6 1.1 %collective-permute-done.6.refs_3_ = f32[3,3,1,2048]{3,2,1,0:T(1,128)S(1)} collective-permute-done((f32[3,3,1,2048]{3,2,1,0:T(1,128)S(1)}, f32[3,3,1,2048]{3,2,1,0:T(1,128)S(1)}, u32[]{:S(2)}, u32[]{:S(2)}) %collective-permute-start.6) | collective-permute-done | bytes 73760 | tf_op jit(solution)/shard_map/ppermute | solution.py:488
  54.7 0.0 collective-permute-done.4.refs_1_
  54.7 0.0 collective-permute-done.7.refs_4_
  54.7 1.2 %shard_map.145 = (f32[3,3,16,2048]{3,2,1,0:T(8,128)S(1)}, f32[32,1,128]{2,1,0:T(1,128)S(1)}) custom-call(f32[3,3,16,2048]{3,2,1,0:T(8,128)S(1)} %shard_map.144.refs_0_, f32[3,16,2048]{2,1,0:T(8,128)S(1)} %collective-permute-done.4.refs_1_, f32[3,3,1,2048]{3,2,1,0:T(1,128)S(1)} %collective-permute-done.5.refs_2_, ...), custom_call_target="tpu_custom_call" | custom-call | tf_op jit(solution)/shard_map/pallas_call | solution.py:52
  55.9 10.4 %all_to_all.16.refs_0_ = f32[32,1,128]{2,1,0:T(1,128)S(1)} all-to-all(f32[32,1,128]{2,1,0:T(1,128)S(1)} %get-tuple-element.48), channel_id=1, replica_groups=mesh['tile'=8,'layer'=4] {'tile','layer'}, dimensions={0} | all-to-all | bytes 32768 | tf_op jit(solution)/shard_map/all_to_all | solution.py:497
  66.3 1.7 %shard_map.146 = (f32[3,3,16,2048]{3,2,1,0:T(8,128)}, f32[3,3,16,2048]{3,2,1,0:T(8,128)}, f32[1,1]{1,0:T(1,128)}) custom-call(f32[32,1,128]{2,1,0:T(1,128)S(1)} %all_to_all.16.refs_0_, f32[3,3,16,2048]{3,2,1,0:T(8,128)S(1)} %get-tuple-element.43.refs_0_.refs_1_, f32[3,3,16,2048]{3,2,1,0:T(8,128)S(1)} %get-tuple-element.49.refs_2_, f32[3,3,16,2048]{3,2,1,0:T(8,128)S(1)} %copy-done), custom_call_target="tpu_custom_call" | custom-call | tf_op jit(solution)/shard_map/pallas_call | solution.py:52
  (8 shorter events, 0.0 us)
Async XLA Ops:
  3.8 7.5 %collective-permute-start = (f32[6,16,2048]{2,1,0:T(8,128)S(1)}, f32[6,16,2048]{2,1,0:T(8,128)S(1)}, u32[]{:S(2)}, u32[]{:S(2)}) collective-permute-start(f32[6,16,2048]{2,1,0:T(8,128)S(1)} %get-tuple-element.29.refs_0_), channel_id=1, source_target_pairs={{0,1},{1,0},{2,3},{3,2},{4,5},{5,4},{6,7},{7,6},{8,9},{9,8},{10,11... | collective-permute-start | bytes 2359304 | tf_op jit(solution)/shard_map/ppermute | solution.py:488
  4.3 14.8 %all-to-all-start = ((f32[32,1,768]{2,1,0:T(1,128)}), f32[32,1,768]{2,1,0:T(1,128)S(1)}, u32[]{:S(2)}, u32[]{:S(2)}) async-start(f32[32,1,768]{2,1,0:T(1,128)} %get-tuple-element.28), calls=%async_computation | async-start | bytes 196608 | tf_op jit(solution)/shard_map/all_to_all | solution.py:497
  11.2 7.8 %copy-start.4 = (s32[256]{0:T(256)S(1)}, s32[256]{0:T(256)}, u32[]{:S(2)}) copy-start(s32[256]{0:T(256)} %param.20) | copy-start | bytes 3076
  11.3 7.8 %copy-start.5 = (f32[256]{0:T(256)S(1)}, f32[256]{0:T(256)}, u32[]{:S(2)}) copy-start(f32[256]{0:T(256)} %param.22) | copy-start | bytes 3076
  14.0 20.4 %collective-permute-start.1 = (f32[3,16,2048]{2,1,0:T(8,128)}, f32[3,16,2048]{2,1,0:T(8,128)S(1)}, u32[]{:S(2)}, u32[]{:S(2)}) collective-permute-start(f32[3,16,2048]{2,1,0:T(8,128)} %get-tuple-element.36), channel_id=1, source_target_pairs={{0,2},{1,3},{2,0},{3,1},{4,6},{5,7},{6,4},{7,5},{8,10},{9,11},{10,... | collective-permute-start | bytes 1179656 | tf_op jit(solution)/shard_map/ppermute | solution.py:488
  19.1 24.0 %copy-start.1 = (f32[3,3,3,16,2048]{4,3,2,1,0:T(8,128)S(1)}, f32[3,3,3,16,2048]{4,3,2,1,0:T(8,128)}, u32[]{:S(2)}) copy-start(f32[3,3,3,16,2048]{4,3,2,1,0:T(8,128)} %refs_1_.1) | copy-start | bytes 10616836
  19.1 24.0 %copy-start.2 = (f32[3,3,3,16,2048]{4,3,2,1,0:T(8,128)S(1)}, f32[3,3,3,16,2048]{4,3,2,1,0:T(8,128)}, u32[]{:S(2)}) copy-start(f32[3,3,3,16,2048]{4,3,2,1,0:T(8,128)} %refs_9_.1) | copy-start | bytes 10616836
  34.4 8.6 %copy-start = (f32[3,3,16,2048]{3,2,1,0:T(8,128)S(1)}, f32[3,3,16,2048]{3,2,1,0:T(8,128)}, u32[]{:S(2)}) copy-start(f32[3,3,16,2048]{3,2,1,0:T(8,128)} %refs_3_.3) | copy-start | bytes 3538948
  34.4 8.6 %copy-start.3 = (f32[3,16,2048]{2,1,0:T(8,128)S(1)}, f32[3,16,2048]{2,1,0:T(8,128)}, u32[]{:S(2)}) copy-start(f32[3,16,2048]{2,1,0:T(8,128)} %refs_4_.1) | copy-start | bytes 1179652
  37.0 4.2 %collective-permute-start.2 = (f32[3,1,2048]{2,1,0:T(1,128)S(1)}, f32[3,1,2048]{2,1,0:T(1,128)S(1)}, u32[]{:S(2)}, u32[]{:S(2)}) collective-permute-start(f32[3,1,2048]{2,1,0:T(1,128)S(1)} %get-tuple-element.39), channel_id=1, source_target_pairs={{4,8},{12,16},{20,24},{8,4},{16,12},{24,20},{5,9},{13,17},{21,25},... | collective-permute-start | bytes 73736 | tf_op jit(solution)/shard_map/ppermute | solution.py:493
  37.7 5.3 %collective-permute-start.3 = (f32[3,1,2048]{2,1,0:T(1,128)S(1)}, f32[3,1,2048]{2,1,0:T(1,128)S(1)}, u32[]{:S(2)}, u32[]{:S(2)}) collective-permute-start(f32[3,1,2048]{2,1,0:T(1,128)S(1)} %get-tuple-element.40), channel_id=1, source_target_pairs={{0,4},{4,0},{8,12},{12,8},{16,20},{20,16},{24,28},{28,24},{1,5},{5... | collective-permute-start | bytes 73736 | tf_op jit(solution)/shard_map/ppermute | solution.py:488
  44.0 10.7 %collective-permute-start.4 = (f32[3,16,2048]{2,1,0:T(8,128)S(1)}, f32[3,16,2048]{2,1,0:T(8,128)S(1)}, u32[]{:S(2)}, u32[]{:S(2)}) collective-permute-start(f32[3,16,2048]{2,1,0:T(8,128)S(1)} %get-tuple-element.44), channel_id=1, source_target_pairs={{1,2},{2,1},{5,6},{6,5},{9,10},{10,9},{13,14},{14,13},{17,18},{18,... | collective-permute-start | bytes 1179656 | tf_op jit(solution)/shard_map/ppermute | solution.py:493
  44.7 10.0 %collective-permute-start.7 = (f32[3,16,2048]{2,1,0:T(8,128)S(1)}, f32[3,16,2048]{2,1,0:T(8,128)S(1)}, u32[]{:S(2)}, u32[]{:S(2)}) collective-permute-start(f32[3,16,2048]{2,1,0:T(8,128)S(1)} %get-tuple-element.47), channel_id=1, source_target_pairs={{0,1},{1,0},{2,3},{3,2},{4,5},{5,4},{6,7},{7,6},{8,9},{9,8},{10,11... | collective-permute-start | bytes 1179656 | tf_op jit(solution)/shard_map/ppermute | solution.py:488
  46.2 7.4 %collective-permute-start.5 = (f32[3,3,1,2048]{3,2,1,0:T(1,128)S(1)}, f32[3,3,1,2048]{3,2,1,0:T(1,128)S(1)}, u32[]{:S(2)}, u32[]{:S(2)}) collective-permute-start(f32[3,3,1,2048]{3,2,1,0:T(1,128)S(1)} %get-tuple-element.45), channel_id=1, source_target_pairs={{4,8},{12,16},{20,24},{8,4},{16,12},{24,20},{5,9},{13,17},{21,25},... | collective-permute-start | bytes 221192 | tf_op jit(solution)/shard_map/ppermute | solution.py:493
  46.8 7.9 %collective-permute-start.6 = (f32[3,3,1,2048]{3,2,1,0:T(1,128)S(1)}, f32[3,3,1,2048]{3,2,1,0:T(1,128)S(1)}, u32[]{:S(2)}, u32[]{:S(2)}) collective-permute-start(f32[3,3,1,2048]{3,2,1,0:T(1,128)S(1)} %get-tuple-element.46), channel_id=1, source_target_pairs={{0,4},{4,0},{8,12},{12,8},{16,20},{20,16},{24,28},{28,24},{1,5},{5... | collective-permute-start | bytes 221192 | tf_op jit(solution)/shard_map/ppermute | solution.py:488

commit v9 on v8

--- a/solution.py
+++ b/solution.py
@@ -435,7 +435,7 @@
             image[c, z] = total
 
 
-def image_kernel(part, outer, row_two, row_one, inner, rhs, tz, tx, image, send):
+def image_kernel(part, outer, row_one, row_two, inner, rhs, tz, tx, image, send):
     depth, width = part.shape[1:3]
     right, odd = (is_right(0), is_right(0, "tile"))
     row = iota(part.shape[2:], 0)
@@ -577,7 +577,7 @@
     image, send = call(
         image_kernel,
         (vmem(rhs.shape), vmem((devices, 1, 128))),
-        (part, outer, row_two, row_one, inner, rhs, tz, tx),
+        (part, outer, row_one, row_two, inner, rhs, tz, tx),
     )
     sums = everywhere(send)
     update, lin_res, ratio = call(

time: 68.2 us -> 68.2 us (level)
  blocking collectives: 20.7 us -> 24.4 us
  starting transfers between devices: 21.9 us -> 18.6 us
    all_to_all x2, blocking collectives: 20.7 us -> 24.4 us  [everywhere(): return lax.all_to_all(x, BOTH, split_axis=0, concat_axis=0, tiled=True)]
    ppermute x5, starting transfers between devices: 12.9 us -> 9.63 us  [flip(): lax.ppermute(x, axis, [(i, i ^ 1 << level) for i in range(lax.axis_size(a...]
where the time goes in v9:
time: 68.2 us; the launch traced here: 67.9 us
  blocking collectives  24.4 us (36%)
  starting transfers between devices  18.6 us (27%)
  Pallas kernels  18.4 us (27%)
  waiting for transfers between devices  5.7 us (8%)
  between operations  0.77 us (1%)
    all_to_all x2, blocking collectives, everywhere(): return lax.all_to_all(x, BOTH, split_axis=0, concat_axis=0, tiled=True)  24.4 us
    pallas_call x6, Pallas kernels, call(): pl.pallas_call(functools.partial(staged, kernel, where, len(outs), tuple(...  10.3 us
    ppermute x5, starting transfers between devices, flip(): lax.ppermute(x, axis, [(i, i ^ 1 << level) for i in range(lax.axis_size(a...  9.63 us
    all_to_all x1, starting transfers between devices, everywhere(): return lax.all_to_all(x, BOTH, split_axis=0, concat_axis=0, tiled=True)  6.96 us
    pallas_call x1, Pallas kernels, shards(): pl.pallas_call(front_kernel, out_shape=vmem((devices, 1, rows + 2 * level...  5.06 us
    all_to_all x1, waiting for transfers between devices, everywhere(): return lax.all_to_all(x, BOTH, split_axis=0, concat_axis=0, tiled=True)  3.24 us
    pallas_call x1, Pallas kernels, shards(): pl.pallas_call(pres_kernel, out_shape=(field, vmem((devices, 1, 3 * count...  3.12 us
    ppermute x5, waiting for transfers between devices, flip(): lax.ppermute(x, axis, [(i, i ^ 1 << level) for i in range(lax.axis_size(a...  2.45 us
  transfers between devices with their start and end apart: 9, of which 3 were waited for; matrix products, arithmetic and copies ran while one was open for 0% of the time, Pallas kernels for 13%

profile of v9, /device:TPU:0, one launch (start us, length us, event | category | flops | bytes accessed | tf_op | source)
XLA Modules:
  0.0 67.9 jit_solution(4049044015902032638)
XLA Ops:
  0.6 3.1 %shard_map.139 = (f32[3,16,2048]{2,1,0:T(8,128)S(1)}, f32[32,1,768]{2,1,0:T(1,128)}, f32[6,16,2048]{2,1,0:T(8,128)S(1)}) custom-call(s32[1,256]{1,0:T(1,128)} %bitcast.4, s32[1,256]{1,0:T(1,128)} %bitcast.8, f32[1,256]{1,0:T(1,128)} %bitcast.6, f32[3,3,16,2048]{3,2,1,0:T(8,128)} %refs_3_.3, f32[3,3,16,2048]{3,2,1,0:T(8,128)} %wts_in.1, ...), custom_call_target="tpu_custom_call" | custom-call | tf_op jit(solution)/shard_map/pallas_call | solution.py:516
  3.8 0.5 collective-permute-start
  4.3 7.0 %all-to-all-start = ((f32[32,1,768]{2,1,0:T(1,128)}), f32[32,1,768]{2,1,0:T(1,128)S(1)}, u32[]{:S(2)}, u32[]{:S(2)}) async-start(f32[32,1,768]{2,1,0:T(1,128)} %get-tuple-element.28), calls=%async_computation | async-start | bytes 196608 | tf_op jit(solution)/shard_map/all_to_all | solution.py:497
  11.2 0.0 copy-start.4
  11.3 0.0 copy-start.5
  11.3 0.0 collective-permute-done.refs_1_.refs_3_
  11.3 2.7 %shard_map.140 = (f32[6,16,2048]{2,1,0:T(8,128)}, f32[3,16,2048]{2,1,0:T(8,128)}, f32[6,16,2048]{2,1,0:T(8,128)}, f32[3,16,2048]{2,1,0:T(8,128)S(1)}, f32[6,16,2048]{2,1,0:T(8,128)S(1)}) custom-call(f32[6,16,2048]{2,1,0:T(8,128)S(1)} %get-tuple-element.29.refs_0_, f32[6,16,2048]{2,1,0:T(8,128)S(1)} %collective-permute-done.refs_1_.refs_3_, ...), custom_call_target="tpu_custom_call" | custom-call | tf_op jit(solution)/shard_map/pallas_call | solution.py:52
  14.0 1.8 %collective-permute-start.1 = (f32[3,16,2048]{2,1,0:T(8,128)}, f32[3,16,2048]{2,1,0:T(8,128)S(1)}, u32[]{:S(2)}, u32[]{:S(2)}) collective-permute-start(f32[3,16,2048]{2,1,0:T(8,128)} %get-tuple-element.36), channel_id=1, source_target_pairs={{0,2},{1,3},{2,0},{3,1},{4,6},{5,7},{6,4},{7,5},{8,10},{9,11},{10,... | collective-permute-start | bytes 1179656 | tf_op jit(solution)/shard_map/ppermute | solution.py:488
  15.8 3.2 %all-to-all-done.recv.refs_1_ = f32[32,1,768]{2,1,0:T(1,128)S(1)} async-done(((f32[32,1,768]{2,1,0:T(1,128)}), f32[32,1,768]{2,1,0:T(1,128)S(1)}, u32[]{:S(2)}, u32[]{:S(2)}) %all-to-all-start) | async-done | bytes 98336 | tf_op jit(solution)/shard_map/all_to_all | solution.py:497
  19.1 0.0 copy-done.5
  19.1 5.1 %shard_map.141 = f32[32,1,1280]{2,1,0:T(1,128)S(1)} custom-call(f32[32,1,768]{2,1,0:T(1,128)S(1)} %all-to-all-done.recv.refs_1_, s32[1,256]{1,0:T(1,128)S(1)} %bitcast.5, f32[1,256]{1,0:T(1,128)S(1)} %bitcast.7, f32[6,16,2048]{2,1,0:T(8,128)S(1)} %get-tuple-element.33.tables_0_, f32[3,16,2048]{2,1,0:T(8,128)S(1)} %get-tuple-element.34.tables_1_, ...), custom_call_target="tpu_custom_call" | custom-call | tf_op jit(solution)/shard_map/pallas_call | solution.py:541
  24.1 10.3 %all_to_all.15.refs_0_ = f32[32,1,1280]{2,1,0:T(1,128)S(1)} all-to-all(f32[32,1,1280]{2,1,0:T(1,128)S(1)} %shard_map.141), channel_id=1, replica_groups=mesh['tile'=8,'layer'=4] {'tile','layer'}, dimensions={0} | all-to-all | bytes 327680 | tf_op jit(solution)/shard_map/all_to_all | solution.py:497
  34.4 0.0 collective-permute-done.1.refs_4_
  34.4 2.6 %shard_map.142 = (f32[3,16,2048]{2,1,0:T(8,128)S(1)}, f32[3,16,2048]{2,1,0:T(8,128)S(1)}, f32[3,1,2048]{2,1,0:T(1,128)S(1)}, f32[3,1,2048]{2,1,0:T(1,128)S(1)}, ...) custom-call(f32[32,1,1280]{2,1,0:T(1,128)S(1)} %all_to_all.15.refs_0_, ...), custom_call_target="tpu_custom_call" | custom-call | tf_op jit(solution)/shard_map/pallas_call | solution.py:52
  37.0 0.7 collective-permute-start.2
  37.7 3.5 %collective-permute-start.3 = (f32[3,1,2048]{2,1,0:T(1,128)S(1)}, f32[3,1,2048]{2,1,0:T(1,128)S(1)}, u32[]{:S(2)}, u32[]{:S(2)}) collective-permute-start(f32[3,1,2048]{2,1,0:T(1,128)S(1)} %get-tuple-element.40), channel_id=1, source_target_pairs={{0,4},{4,0},{8,12},{12,8},{16,20},{20,16},{24,28},{28,24},{1,5},{5... | collective-permute-start | bytes 73736 | tf_op jit(solution)/shard_map/ppermute | solution.py:488
  41.2 0.0 collective-permute-done.2.refs_2_
  41.2 1.8 %collective-permute-done.3.refs_3_ = f32[3,1,2048]{2,1,0:T(1,128)S(1)} collective-permute-done((f32[3,1,2048]{2,1,0:T(1,128)S(1)}, f32[3,1,2048]{2,1,0:T(1,128)S(1)}, u32[]{:S(2)}, u32[]{:S(2)}) %collective-permute-start.3) | collective-permute-done | bytes 24608 | tf_op jit(solution)/shard_map/ppermute | solution.py:488
  43.1 0.0 copy-done.3
  43.1 0.9 %shard_map.143 = (f32[3,3,16,2048]{3,2,1,0:T(8,128)S(1)}, f32[3,16,2048]{2,1,0:T(8,128)S(1)}, f32[3,3,1,2048]{3,2,1,0:T(1,128)S(1)}, f32[3,3,1,2048]{3,2,1,0:T(1,128)S(1)}, f32[3,16,2048]{2,1,0:T(8,128)S(1)}) custom-call(f32[3,16,2048]{2,1,0:T(8,128)S(1)} %get-tuple-element.37.refs_0_, f32[3,16,2048]{2,1,0:T(8,128)S(1)} %get-tuple-element.38.refs_1_, ...), custom_call_target="tpu_custom_call" | custom-call | tf_op jit(solution)/shard_map/pallas_call | solution.py:52
  44.0 0.7 %collective-permute-start.4 = (f32[3,16,2048]{2,1,0:T(8,128)S(1)}, f32[3,16,2048]{2,1,0:T(8,128)S(1)}, u32[]{:S(2)}, u32[]{:S(2)}) collective-permute-start(f32[3,16,2048]{2,1,0:T(8,128)S(1)} %get-tuple-element.44), channel_id=1, source_target_pairs={{1,2},{2,1},{5,6},{6,5},{9,10},{10,9},{13,14},{14,13},{17,18},{18,... | collective-permute-start | bytes 1179656 | tf_op jit(solution)/shard_map/ppermute | solution.py:493
  44.7 1.5 %collective-permute-start.7 = (f32[3,16,2048]{2,1,0:T(8,128)S(1)}, f32[3,16,2048]{2,1,0:T(8,128)S(1)}, u32[]{:S(2)}, u32[]{:S(2)}) collective-permute-start(f32[3,16,2048]{2,1,0:T(8,128)S(1)} %get-tuple-element.47), channel_id=1, source_target_pairs={{0,1},{1,0},{2,3},{3,2},{4,5},{5,4},{6,7},{7,6},{8,9},{9,8},{10,11... | collective-permute-start | bytes 1179656 | tf_op jit(solution)/shard_map/ppermute | solution.py:488
  46.2 2.3 %collective-permute-start.5 = (f32[3,3,1,2048]{3,2,1,0:T(1,128)S(1)}, f32[3,3,1,2048]{3,2,1,0:T(1,128)S(1)}, u32[]{:S(2)}, u32[]{:S(2)}) collective-permute-start(f32[3,3,1,2048]{3,2,1,0:T(1,128)S(1)} %get-tuple-element.45), channel_id=1, source_target_pairs={{0,4},{4,0},{8,12},{12,8},{16,20},{20,16},{24,28},{28,24},{1,5},{5... | collective-permute-start | bytes 221192 | tf_op jit(solution)/shard_map/ppermute | solution.py:488
  48.4 0.7 collective-permute-start.6
  49.1 1.2 %shard_map.144.refs_0_ = f32[3,3,16,2048]{3,2,1,0:T(8,128)S(1)} custom-call(f32[3,3,16,2048]{3,2,1,0:T(8,128)S(1)} %get-tuple-element.43.refs_0_.refs_1_, f32[3,3,3,16,2048]{4,3,2,1,0:T(8,128)S(1)} %copy-done.1, f32[3,16,2048]{2,1,0:T(8,128)S(1)} %get-tuple-element.42.refs_6_.refs_2_, f32[3,16,2048]{2,1,0:T(8,128)S(1)} %get-tuple-element.41.refs_4_.refs_3_.refs_7_, ...), custom_call_target="tpu_custom_call" | custom-call | tf_op jit(solution)/shard_map/pallas_call | solution.py:52
  50.3 0.6 collective-permute-done.5.refs_2_
  50.9 0.0 collective-permute-done.6.refs_3_
  51.0 0.0 collective-permute-done.4.refs_1_
  51.0 0.0 collective-permute-done.7.refs_4_
  51.0 1.2 %shard_map.145 = (f32[3,3,16,2048]{3,2,1,0:T(8,128)S(1)}, f32[32,1,128]{2,1,0:T(1,128)S(1)}) custom-call(f32[3,3,16,2048]{3,2,1,0:T(8,128)S(1)} %shard_map.144.refs_0_, f32[3,16,2048]{2,1,0:T(8,128)S(1)} %collective-permute-done.4.refs_1_, f32[3,3,1,2048]{3,2,1,0:T(1,128)S(1)} %collective-permute-done.5.refs_2_, ...), custom_call_target="tpu_custom_call" | custom-call | tf_op jit(solution)/shard_map/pallas_call | solution.py:52
  52.2 14.1 %all_to_all.16.refs_0_ = f32[32,1,128]{2,1,0:T(1,128)S(1)} all-to-all(f32[32,1,128]{2,1,0:T(1,128)S(1)} %get-tuple-element.48), channel_id=1, replica_groups=mesh['tile'=8,'layer'=4] {'tile','layer'}, dimensions={0} | all-to-all | bytes 32768 | tf_op jit(solution)/shard_map/all_to_all | solution.py:497
  66.2 1.7 %shard_map.146 = (f32[3,3,16,2048]{3,2,1,0:T(8,128)}, f32[3,3,16,2048]{3,2,1,0:T(8,128)}, f32[1,1]{1,0:T(1,128)}) custom-call(f32[32,1,128]{2,1,0:T(1,128)S(1)} %all_to_all.16.refs_0_, f32[3,3,16,2048]{3,2,1,0:T(8,128)S(1)} %get-tuple-element.43.refs_0_.refs_1_, f32[3,3,16,2048]{3,2,1,0:T(8,128)S(1)} %get-tuple-element.49.refs_2_, f32[3,3,16,2048]{3,2,1,0:T(8,128)S(1)} %copy-done), custom_call_target="tpu_custom_call" | custom-call | tf_op jit(solution)/shard_map/pallas_call | solution.py:52
  (8 shorter events, 0.0 us)
Async XLA Ops:
  3.8 7.5 %collective-permute-start = (f32[6,16,2048]{2,1,0:T(8,128)S(1)}, f32[6,16,2048]{2,1,0:T(8,128)S(1)}, u32[]{:S(2)}, u32[]{:S(2)}) collective-permute-start(f32[6,16,2048]{2,1,0:T(8,128)S(1)} %get-tuple-element.29.refs_0_), channel_id=1, source_target_pairs={{0,1},{1,0},{2,3},{3,2},{4,5},{5,4},{6,7},{7,6},{8,9},{9,8},{10,11... | collective-permute-start | bytes 2359304 | tf_op jit(solution)/shard_map/ppermute | solution.py:488
  4.3 14.8 %all-to-all-start = ((f32[32,1,768]{2,1,0:T(1,128)}), f32[32,1,768]{2,1,0:T(1,128)S(1)}, u32[]{:S(2)}, u32[]{:S(2)}) async-start(f32[32,1,768]{2,1,0:T(1,128)} %get-tuple-element.28), calls=%async_computation | async-start | bytes 196608 | tf_op jit(solution)/shard_map/all_to_all | solution.py:497
  11.2 7.8 %copy-start.4 = (s32[256]{0:T(256)S(1)}, s32[256]{0:T(256)}, u32[]{:S(2)}) copy-start(s32[256]{0:T(256)} %param.20) | copy-start | bytes 3076
  11.3 7.8 %copy-start.5 = (f32[256]{0:T(256)S(1)}, f32[256]{0:T(256)}, u32[]{:S(2)}) copy-start(f32[256]{0:T(256)} %param.22) | copy-start | bytes 3076
  14.0 20.4 %collective-permute-start.1 = (f32[3,16,2048]{2,1,0:T(8,128)}, f32[3,16,2048]{2,1,0:T(8,128)S(1)}, u32[]{:S(2)}, u32[]{:S(2)}) collective-permute-start(f32[3,16,2048]{2,1,0:T(8,128)} %get-tuple-element.36), channel_id=1, source_target_pairs={{0,2},{1,3},{2,0},{3,1},{4,6},{5,7},{6,4},{7,5},{8,10},{9,11},{10,... | collective-permute-start | bytes 1179656 | tf_op jit(solution)/shard_map/ppermute | solution.py:488
  19.1 24.0 %copy-start.1 = (f32[3,3,3,16,2048]{4,3,2,1,0:T(8,128)S(1)}, f32[3,3,3,16,2048]{4,3,2,1,0:T(8,128)}, u32[]{:S(2)}) copy-start(f32[3,3,3,16,2048]{4,3,2,1,0:T(8,128)} %refs_1_.1) | copy-start | bytes 10616836
  19.1 24.0 %copy-start.2 = (f32[3,3,3,16,2048]{4,3,2,1,0:T(8,128)S(1)}, f32[3,3,3,16,2048]{4,3,2,1,0:T(8,128)}, u32[]{:S(2)}) copy-start(f32[3,3,3,16,2048]{4,3,2,1,0:T(8,128)} %refs_9_.1) | copy-start | bytes 10616836
  34.4 8.6 %copy-start = (f32[3,3,16,2048]{3,2,1,0:T(8,128)S(1)}, f32[3,3,16,2048]{3,2,1,0:T(8,128)}, u32[]{:S(2)}) copy-start(f32[3,3,16,2048]{3,2,1,0:T(8,128)} %refs_3_.3) | copy-start | bytes 3538948
  34.4 8.6 %copy-start.3 = (f32[3,16,2048]{2,1,0:T(8,128)S(1)}, f32[3,16,2048]{2,1,0:T(8,128)}, u32[]{:S(2)}) copy-start(f32[3,16,2048]{2,1,0:T(8,128)} %refs_4_.1) | copy-start | bytes 1179652
  37.0 4.2 %collective-permute-start.2 = (f32[3,1,2048]{2,1,0:T(1,128)S(1)}, f32[3,1,2048]{2,1,0:T(1,128)S(1)}, u32[]{:S(2)}, u32[]{:S(2)}) collective-permute-start(f32[3,1,2048]{2,1,0:T(1,128)S(1)} %get-tuple-element.39), channel_id=1, source_target_pairs={{4,8},{12,16},{20,24},{8,4},{16,12},{24,20},{5,9},{13,17},{21,25},... | collective-permute-start | bytes 73736 | tf_op jit(solution)/shard_map/ppermute | solution.py:493
  37.7 5.3 %collective-permute-start.3 = (f32[3,1,2048]{2,1,0:T(1,128)S(1)}, f32[3,1,2048]{2,1,0:T(1,128)S(1)}, u32[]{:S(2)}, u32[]{:S(2)}) collective-permute-start(f32[3,1,2048]{2,1,0:T(1,128)S(1)} %get-tuple-element.40), channel_id=1, source_target_pairs={{0,4},{4,0},{8,12},{12,8},{16,20},{20,16},{24,28},{28,24},{1,5},{5... | collective-permute-start | bytes 73736 | tf_op jit(solution)/shard_map/ppermute | solution.py:488
  44.0 7.0 %collective-permute-start.4 = (f32[3,16,2048]{2,1,0:T(8,128)S(1)}, f32[3,16,2048]{2,1,0:T(8,128)S(1)}, u32[]{:S(2)}, u32[]{:S(2)}) collective-permute-start(f32[3,16,2048]{2,1,0:T(8,128)S(1)} %get-tuple-element.44), channel_id=1, source_target_pairs={{1,2},{2,1},{5,6},{6,5},{9,10},{10,9},{13,14},{14,13},{17,18},{18,... | collective-permute-start | bytes 1179656 | tf_op jit(solution)/shard_map/ppermute | solution.py:493
  44.7 6.3 %collective-permute-start.7 = (f32[3,16,2048]{2,1,0:T(8,128)S(1)}, f32[3,16,2048]{2,1,0:T(8,128)S(1)}, u32[]{:S(2)}, u32[]{:S(2)}) collective-permute-start(f32[3,16,2048]{2,1,0:T(8,128)S(1)} %get-tuple-element.47), channel_id=1, source_target_pairs={{0,1},{1,0},{2,3},{3,2},{4,5},{5,4},{6,7},{7,6},{8,9},{9,8},{10,11... | collective-permute-start | bytes 1179656 | tf_op jit(solution)/shard_map/ppermute | solution.py:488
  46.2 4.8 %collective-permute-start.5 = (f32[3,3,1,2048]{3,2,1,0:T(1,128)S(1)}, f32[3,3,1,2048]{3,2,1,0:T(1,128)S(1)}, u32[]{:S(2)}, u32[]{:S(2)}) collective-permute-start(f32[3,3,1,2048]{3,2,1,0:T(1,128)S(1)} %get-tuple-element.45), channel_id=1, source_target_pairs={{0,4},{4,0},{8,12},{12,8},{16,20},{20,16},{24,28},{28,24},{1,5},{5... | collective-permute-start | bytes 221192 | tf_op jit(solution)/shard_map/ppermute | solution.py:488
  48.4 2.5 %collective-permute-start.6 = (f32[3,3,1,2048]{3,2,1,0:T(1,128)S(1)}, f32[3,3,1,2048]{3,2,1,0:T(1,128)S(1)}, u32[]{:S(2)}, u32[]{:S(2)}) collective-permute-start(f32[3,3,1,2048]{3,2,1,0:T(1,128)S(1)} %get-tuple-element.46), channel_id=1, source_target_pairs={{4,8},{12,16},{20,24},{8,4},{16,12},{24,20},{5,9},{13,17},{21,25},... | collective-permute-start | bytes 221192 | tf_op jit(solution)/shard_map/ppermute | solution.py:493

commit v10 on v8

--- a/solution.py
+++ b/solution.py
@@ -23,7 +23,7 @@
     return pltpu.VMEM(shape, dtype)
 
 
-def staged(kernel, where, outs, kept, column, *refs):
+def staged(kernel, where, outs, kept, column, late, *refs):
     count, sems = (len(where), refs[-1])
     held = list(refs[count + outs + len(kept) : -1])
     target_count = sum(where) - len(kept)
@@ -40,17 +40,21 @@
             operands.append(refs[i])
     for copy in copies:
         copy.start()
-    for copy in copies:
-        copy.wait()
-    kernel(*operands, *refs[count : count + outs], *extra)
-
-
-def call(kernel, outs, args, far=(), keep=(), column=(), scratch=(), limit=LIMIT):
+    places = [i for i, far in enumerate(where) if far]
+    rest = [copy for i, copy in zip(places, copies) if i in late]
+    for i, copy in zip(places, copies):
+        if i not in late:
+            copy.wait()
+    more = (lambda: [copy.wait() for copy in rest],) if late else ()
+    kernel(*more, *operands, *refs[count : count + outs], *extra)
+
+
+def call(kernel, outs, args, far=(), keep=(), column=(), late=(), scratch=(), limit=LIMIT):
     where = [i in far for i in range(len(args))]
     spaces = [pltpu.HBM if w else pltpu.VMEM for w in where]
     every = (*outs, *(vmem(args[i].shape, args[i].dtype) for i in keep))
     return pl.pallas_call(
-        functools.partial(staged, kernel, where, len(outs), tuple(keep), tuple(column)),
+        functools.partial(staged, kernel, where, len(outs), tuple(keep), tuple(column), tuple(late)),
         out_shape=every,
         in_specs=[pl.BlockSpec(memory_space=s) for s in spaces],
         out_specs=(VM,) * len(every),
@@ -188,36 +192,51 @@
     return (yf - c * flux, yl_ + c_ * flux)
 
 
-def first_join_kernel(own, sib, tz, store, out, face, more, one, answers):
-    depth = tz.shape[0]
-    _, _, first, final, _ = factors([tz[z] for z in range(depth)], [store[z] for z in range(depth)])
-    for z in range(depth):
-        answers[z] = first[z]
-        answers[depth + z] = final[z]
-    join_kernel(0, own, sib, answers, out, face, more, one)
-
-
-def join_kernel(level, own, sib, answers, out, face, more, one):
-    depth, width, _ = more.shape
-    depth = depth // 2
+def first_join_kernel(final, own, sib, pres, tz, store, tx, cell, prod, low, high, *outs):
+    depth, width, _ = tz.shape
+    for k, ref in enumerate((tz, store, pres, tx)):
+        for z in range(depth):
+            low[k * depth + z] = ref[z, 0:1]
+            high[k * depth + z] = ref[z, width - 1 : width]
+    _, _, first, last, _ = factors([tz[z] for z in range(depth)], [store[z] for z in range(depth)])
+    join(0, final, own, sib, first + last, cell, prod, *outs)
+
+
+def join_kernel(level, final, own, sib, answers, cell, prod, *outs):
+    join(level, final, own, sib, [answers[i] for i in range(answers.shape[0])], cell, prod, *outs)
+
+
+def join(level, final, own, sib, answers, cell, prod, found, *outs):
+    depth = len(answers) // 2
+    width, long = answers[0].shape
     _, c, _, _, c_, _, g = pair(level, own, sib)
     first, both, last = join_coefs(level, own, sib)
     yf, yl = join_ends(level, own, sib, (own[3], own[4]), (sib[3], sib[4]))
-    out[0], out[1], out[2] = (first, both, last)
-    out[3], out[4] = (yf, yl)
     lower = choose(level, own[5], sib[5])[1]
-    out[5] = lower
-    face[2] = lower
     right, later = (is_right(level), is_right(level + 1))
-    face[0], face[1] = (jnp.where(later, first, last), jnp.where(later, yf, yl))
     cg, cg_ = (c * g, c_ * g)
+    tops, bottoms = ([], [])
     for z in range(depth):
         kf, kl = (answers[z], answers[depth + z])
-        top = jnp.where(right, cg * kf, kf - cg * kl)
-        bottom = jnp.where(right, kl - cg_ * kf, cg_ * kl)
-        more[z] = top
-        more[depth + z] = bottom
-        one[z] = jnp.where(later, top, bottom)
+        tops.append(jnp.where(right, cg * kf, kf - cg * kl))
+        bottoms.append(jnp.where(right, kl - cg_ * kf, cg_ * kl))
+    tables = [answers[:depth], answers[depth:]]
+    if final:
+        (face,) = outs
+        face[0], face[1] = (jnp.where(later, first, last), jnp.where(later, yf, yl))
+        face[2] = lower
+        tables.append([jnp.where(later, tops[z], bottoms[z]) for z in range(depth)])
+    else:
+        out, more = outs
+        for i, value in enumerate((first, both, last, yf, yl, lower)):
+            out[i] = value
+        for i, value in enumerate(tops + bottoms):
+            more[i] = value
+    where = cell[...]
+    hot = onehot(lax.rem(where, long), long).astype(BF16)
+    stack = [jnp.concatenate(t, 0) for t in tables]
+    got = pick(stack, lax.div(where, long), hot)
+    found[...] = jnp.concatenate([prod[...] * value for value in got], 1)
 
 
 def groups_of(levels):
@@ -230,25 +249,20 @@
     return out
 
 
-def front_kernel(recv, cell, prod, tables, inverse, send, held, sems):
+def front_kernel(recv, found, inverse, send, held, sems):
     devices = recv.shape[0]
     count = recv.shape[2] // 3
     rows, length = inverse.shape
     lanes = 128
     chunks = sems.shape[0]
     wide = length // chunks
-    cell, prod = (cell[...], prod[...])
+    found = found[...]
     copies = [
         pltpu.make_async_copy(inverse.at[:, pl.ds(i * wide, wide)], held.at[:, pl.ds(i * wide, wide)], sems.at[i])
         for i in range(chunks)
     ]
     for copy in copies:
         copy.start()
-    where, value = (cell, prod)
-    depth, width, long = tables[-1].shape
-    hi, lo = lax.div(where, long), lax.rem(where, long)
-    stack = [t[k * depth : (k + 1) * depth].reshape(depth * width, long) for t in tables for k in range(t.shape[0] // depth)]
-    found = [value * f for f in pick(stack, hi, onehot(lo, long).astype(BF16))]
     terms, index = (recv[:, 0, :count], recv[:, 0, count : 2 * count])
     high = jnp.floor(index * (1.0 / lanes))
     low = index - high * lanes
@@ -268,7 +282,7 @@
             acc = acc + held[:, r * lanes : (r + 1) * lanes] * total[r : r + 1]
     parts = jnp.concatenate(split(acc), 1)
     out = dot_nt(jnp.ones((8, parts.shape[1]), BF16), parts)
-    send[...] = jnp.broadcast_to(jnp.concatenate([out[0:1], value, *found], 1)[:, None], send.shape)
+    send[...] = jnp.broadcast_to(jnp.concatenate([out[0:1], found], 1)[:, None], send.shape)
 
 
 def gathered(values, rows_hot, lanes_hot, start, size, ext, parts):
@@ -301,59 +315,65 @@
     two[...] = jnp.where(odd, last, first)
 
 
-def table_kernel(levels, shape, terms, rows_hot, lanes_hot, sol_hot, sol_row, layer):
+def table_kernel(lists, shape, terms, hots, side=False):
     _, width, long = shape
+    rows_hot, lanes_hot, sol_hot, sol_row, layer = hots
     lanes = 128
     rows = sol_hot.shape[0]
     count = terms.shape[2] // 3
     at = 0
-    for members in groups_of(levels):
-        for device in members:
+    for members in lists:
+        for k, device in enumerate(members):
             entry = terms[device]
             index = entry[:, count : 2 * count].astype(I32)
             cell = entry[:, 2 * count :].astype(I32)
             y, x = lax.rem(cell, long), lax.rem(lax.div(cell, long), width)
+            if not side:
+                row = lax.div(y, lanes) * width + x
+            elif k % 2 == 0:
+                row = jnp.where(x == 0, lax.div(y, lanes) * 8, -1)
+            else:
+                row = jnp.where(x == width - 1, lax.div(y, lanes) * 8 + 7, -1)
             here = pl.ds(at, count)
-            rows_hot[:, here] = onehot(lax.div(y, lanes) * width + x, rows_hot.shape[0]).astype(BF16)
+            rows_hot[:, here] = onehot(row, rows_hot.shape[0]).astype(BF16)
             lanes_hot[:, here] = onehot(lax.rem(y, lanes), lanes).astype(BF16)
             sol_hot[:, here] = onehot(lax.rem(index, rows), rows).astype(BF16)
             sol_row[:, here] = lax.div(index, rows)
-            if at == 0:
-                layer[...] = lax.div(cell, long * width)
+            if at < layer.shape[1]:
+                layer[:, here] = lax.div(cell, long * width)
             at += count
 
 
-def pressure_kernel(levels, recv, terms, pres, *refs):
-    sib, (tz, store, tx, p, coupled_z, two, one, rows_hot, lanes_hot, sol_hot, sol_row, layer) = (refs[:levels], refs[levels:])
-    depth, width, long = pres.shape
-    table_kernel(levels, pres.shape, terms, rows_hot, lanes_hot, sol_hot, sol_row, layer)
-    rows, count = (sol_hot.shape[0], layer.shape[1])
-    groups = groups_of(levels)
-    layer = layer[...]
+def column_solve(levels, recv, lists, hots, tz, store, pres, sib):
+    rows_hot, lanes_hot, sol_hot, sol_row, layer = hots
+    depth = len(tz)
+    high = tz[0].shape[0]
+    rows, count = (sol_hot.shape[0], recv.shape[2])
+    count = (count - rows) // (2 * levels)
     table = jnp.concatenate(split(recv[...].reshape(recv.shape[0], recv.shape[2])[:, :rows]), 0)
     sol = fold(dot(table, sol_hot[...]))
     sol = jnp.sum(jnp.where(iota(sol.shape, 0) == sol_row[...], sol, 0.0), axis=0, keepdims=True)
+    layer = layer[...]
 
     def listed(group, column):
         at = rows + column * count
         return jnp.concatenate([recv[device][:, at : at + count] for device in group], 1)
 
-    tzs = [tz[z] for z in range(depth)]
-    gs, invs, first, final, coefs = factors(tzs, [store[z] for z in range(depth)])
+    gs, invs, first, final, coefs = factors(tz, store)
     own = [coefs]
-    value = listed(groups[0], 0) * sol[:, :count]
+    start = layer.shape[1]
+    value = listed(lists[0], 0) * sol[:, :start]
     values = [jnp.where(layer == z, value, 0.0) for z in range(depth)]
-    change = gathered(values, rows_hot, lanes_hot, 0, count, width, PARTS)
-    y = local_solve([pres[z] - change[z] for z in range(depth)], gs, invs, tzs)
+    change = gathered(values, rows_hot, lanes_hot, 0, start, high, PARTS)
+    y = local_solve([pres[z] - change[z] for z in range(depth)], gs, invs, tz)
     mine = (y[0], y[-1])
     steps = []
-    start = count
     for level in range(levels):
-        size = len(groups[level + 1]) * count
+        size = len(lists[level + 1]) * count
         top = level == levels - 1
         columns = [1 + 2 * level] if top else [1 + 2 * level, 2 + 2 * level]
-        values = [listed(groups[level + 1], c) * sol[:, start : start + size] for c in columns]
-        change = gathered(values, rows_hot, lanes_hot, start, size, width, PARTS)
+        values = [listed(lists[level + 1], c) * sol[:, start : start + size] for c in columns]
+        change = gathered(values, rows_hot, lanes_hot, start, size, high, PARTS)
         start += size
         if top:
             other = sib[level][1] - change[0]
@@ -363,8 +383,7 @@
             steps.append((mine, other))
             mine = join_ends(level, own[level], sib[level], mine, other)
             own.append(join_coefs(level, own[level], sib[level]))
-    above = below = jnp.zeros((width, long), F32)
-    tzp = jnp.zeros((width, long), F32)
+    above = below = tzp = jnp.zeros(tz[0].shape, F32)
     place = lax.axis_index("layer")
     for level in range(levels - 1, -1, -1):
         mine, other = steps[level]
@@ -384,8 +403,19 @@
         flux = g * flux
         right = is_right(level)
         above, below = (jnp.where(right, flux, above), jnp.where(right, below, -flux))
-    values = [y[z] + first[z] * above + final[z] * below for z in range(depth)]
-    is_last = place == (1 << levels) - 1
+    return [y[z] + first[z] * above + final[z] * below for z in range(depth)], above, below, tzp
+
+
+def pressure_kernel(levels, recv, terms, pres, *refs):
+    sib, (tz, store, tx, binv, p, coupled_z, *hots) = (refs[:levels], refs[levels:])
+    depth = pres.shape[0]
+    lists = groups_of(levels)
+    table_kernel(lists, pres.shape, terms, hots)
+    tzs = [tz[z] for z in range(depth)]
+    values, above, below, tzp = column_solve(
+        levels, recv, lists, hots, tzs, [store[z] for z in range(depth)], [pres[z] for z in range(depth)], sib
+    )
+    is_last = lax.axis_index("layer") == (1 << levels) - 1
     for z in range(depth):
         p[z] = values[z]
         total = above + tzp * values[z] if z == 0 else tzs[z - 1] * values[z - 1]
@@ -393,19 +423,61 @@
             coupled_z[z] = total + jnp.where(is_last, 0.0, below + tzs[z] * values[z])
         else:
             coupled_z[z] = total + tzs[z] * values[z + 1]
-    for z in range(depth):
-        tile_rows(values[z][0:1], (tx[z] * values[z])[width - 1 :], one.at[z], two.at[z])
-
-
-def search_kernel(p, coupled_z, two, one, tx, ty, tz, rhs, diag, binv, s, outer, row_two, row_one, inner):
-    depth, width, _ = p.shape
-    odd = is_right(0, "tile")
-    right = is_right(0)
+
+
+def edge_kernel(levels, low, high, *refs):
+    sib, (one, two) = (refs[:levels], refs[levels:])
+    for ref in (one, two):
+        ref[...] = jnp.zeros(ref.shape, F32)
+    n = low.shape[0]
+    tile_rows(low[...], high[...], one.at[pl.ds(0, n)], two.at[pl.ds(0, n)])
+    at = n
+    for block in sib:
+        width = block.shape[1]
+        for i in range(block.shape[0]):
+            tile_rows(block[i, 0:1], block[i, width - 1 : width], one.at[at], two.at[at])
+            at += 1
+
+
+def search_kernel(levels, shapes, ready, recv, terms, two, one, p, coupled_z, tx, tz, binv, rhs, diag, ty, *refs):
+    (s, outer, row_two, row_one, inner), (planes, *hots) = (refs[:5], refs[5:])
+    depth, width, long = p.shape
+    tiles, layers = (lax.axis_size("tile"), lax.axis_size("layer"))
+    tile = lax.axis_index("tile")
+    odd, right = (is_right(0, "tile"), is_right(0))
     row = iota(p.shape[1:], 0)
+    planes[...] = jnp.zeros(planes.shape, F32)
+    for i in range(planes.shape[0]):
+        planes[i, 0:1] = jnp.where(odd, two[i], one[i])
+        planes[i, 7:8] = jnp.where(odd, one[i], two[i])
+    lists = [
+        [jnp.clip(device + step, 0, tiles * layers - 1) for device in members for step in (layers, -layers)]
+        for members in groups_of(levels)
+    ]
+    table_kernel(lists, p.shape, terms, hots, side=True)
+    has_next, has_last = ((tile < tiles - 1).astype(F32), (tile > 0).astype(F32))
+    real = jnp.where(iota((8, long), 0) < 4, has_next, has_last)
+    blocks = []
+    at = 4 * depth
+    for size in shapes:
+        blocks.append([planes[at + i] for i in range(size)])
+        at += size
+    beyond, _, _, _ = column_solve(
+        levels,
+        recv,
+        lists,
+        hots,
+        [planes[z] for z in range(depth)],
+        [jnp.where(planes[depth + z] == 0.0, 1.0, planes[depth + z]) for z in range(depth)],
+        [planes[2 * depth + z] for z in range(depth)],
+        blocks,
+    )
+    ready()
     for z in range(depth):
         centre = p[z]
-        after = jnp.where(odd, two[z], one[z])
-        before = jnp.where(odd, one[z], two[z])
+        far = jnp.where(real > 0.0, beyond[z], 0.0)
+        after = far[0:1]
+        before = (planes[3 * depth + z] * far)[7:8]
         coupled = coupled_z[z] + beside(centre, tx[z], ty[z])
         coupled = coupled + jnp.where(row == 0, before, 0.0) + jnp.where(row == width - 1, tx[z] * after, 0.0)
         remain = [rhs[c, z] - diag[c, 0, z] * centre for c in range(3)]
@@ -522,54 +594,76 @@
         compiler_params=pltpu.CompilerParams(vmem_limit_bytes=LIMIT),
     )(*[pltpu.with_memory_space_constraint(a, pltpu.HBM) for a in given])
     terms = everywhere(send)
-    sib, tables = ([], [])
+    sib, found = ([], [prod])
     for level in range(levels - 1):
         sib.append(flip(ends, level))
-        outs = (planes(6), planes(3), planes(2 * depth), field)
+        final = level == levels - 2
+        outs = (vmem((1, (3 if final else 2) * count)), *((planes(3),) if final else (planes(6), planes(2 * depth))))
         if level == 0:
-            ends, face, more, last, answers = call(
-                first_join_kernel, (*outs, planes(2 * depth)), (ends, sib[-1], tz, store), far=(2, 3)
+            rim = vmem((4 * depth, 1, long))
+            low, high, *got = call(
+                functools.partial(first_join_kernel, final),
+                (rim, rim, *outs),
+                (ends, sib[-1], pres, tz, store, tx, cell, prod),
+                far=range(3, 8),
             )
         else:
-            ends, face, more, last = call(functools.partial(join_kernel, level), outs, (ends, sib[-1], answers))
-        tables.append(answers)
-        answers = more
-    tables.append(last)
+            got = call(
+                functools.partial(join_kernel, level, final), outs, (ends, sib[-1], answers, cell, prod), far=(3, 4)
+            )
+        found.append(got[0])
+        if final:
+            face = got[1]
+        else:
+            ends, answers = got[1:]
+    found = jnp.concatenate(found, 1)
+    terms, face, found = lax.optimization_barrier((terms, face, found))
     sib.append(flip(face, levels - 1))
     chunks = 8
-    terms, *tables = lax.optimization_barrier((terms, *tables))
     send = pl.pallas_call(
         front_kernel,
         out_shape=vmem((devices, 1, rows + 2 * levels * count)),
-        in_specs=[VM, VM, VM, [VM] * len(tables), hbm_spec],
+        in_specs=[VM, VM, hbm_spec],
         out_specs=VM,
         scratch_shapes=[vmem(inverse.shape), pltpu.SemaphoreType.DMA((chunks,))],
         compiler_params=pltpu.CompilerParams(vmem_limit_bytes=LIMIT),
-    )(terms, cell, prod, tables, pltpu.with_memory_space_constraint(inverse, pltpu.HBM))
+    )(terms, found, pltpu.with_memory_space_constraint(inverse, pltpu.HBM))
+    sizes = [block.shape[0] for block in sib]
+    rim = vmem((4 * depth + sum(sizes), 1, long))
+    send, low, high = lax.optimization_barrier((send, low, high))
+    one, two = call(functools.partial(edge_kernel, levels), (rim, rim), (low, high, *sib))
     sol = everywhere(send)
-    row3 = vmem((depth, 1, long))
+    two, one = (neighbour(two, "tile"), flip(one, 0, "tile"))
+
+    def hots(high, long_list, short_list):
+        return (
+            vmem((high * long // 128, long_list), BF16),
+            vmem((128, long_list), BF16),
+            vmem((rows, long_list), BF16),
+            vmem((1, long_list), I32),
+            vmem((1, short_list), I32),
+        )
+
     at = 3 + levels
-    p, coupled_z, two, one, tz, _, tx = call(
+    p, coupled_z, tz, _, tx, block_inv = call(
         functools.partial(pressure_kernel, levels),
-        (field, field, row3, row3),
-        (sol, terms, pres, *sib, tz, store, tx),
-        far=(at, at + 1, at + 2),
-        keep=(at, at + 1, at + 2),
-        scratch=(
-            vmem((width * long // 128, lists), BF16),
-            vmem((128, lists), BF16),
-            vmem((rows, lists), BF16),
-            vmem((1, lists), I32),
-            vmem((1, count), I32),
-        ),
+        (field, field),
+        (sol, terms, pres, *sib, tz, store, tx, block_inv),
+        far=range(at, at + 4),
+        keep=range(at, at + 4),
+        late=(),
+        scratch=hots(width, lists, count),
     )
-    two, one = (neighbour(two, "tile"), flip(one, 0, "tile"))
     row9 = vmem((3, depth, 1, long))
     plane3 = planes(3)
-    s, outer, row_two, row_one, inner = call(
-        search_kernel,
+    s, outer, row_two, row_one, inner, rhs, block_diag, ty = call(
+        functools.partial(search_kernel, levels, sizes),
         (vmem(rhs.shape), plane3, row9, row9, plane3),
-        (p, coupled_z, two, one, tx, ty, tz, rhs, block_diag, block_inv),
+        (sol, terms, two, one, p, coupled_z, tx, tz, block_inv, rhs, block_diag, ty),
+        far=(9, 10, 11),
+        keep=(9, 10, 11),
+        late=(9, 10, 11),
+        scratch=(vmem((4 * depth + sum(sizes), 8, long)), *hots(8, 2 * lists, 2 * count)),
     )
     outer, row_two = (neighbour(outer), neighbour(row_two, "tile"))
     row_one, inner = (flip(row_one, 0, "tile"), flip(inner, 0))

time: 68.2 us -> 70.9 us (1.040)
  blocking collectives: 20.7 us -> 11.5 us
  waiting for transfers between devices: 6.17 us -> 13 us
  Pallas kernels: 18.4 us -> 22.8 us
    all_to_all x2 -> x1, blocking collectives: 20.7 us -> 11.5 us  [everywhere(): return lax.all_to_all(x, BOTH, split_axis=0, concat_axis=0, tiled=True)]
    all_to_all x1 -> x2, waiting for transfers between devices: 3.24 us -> 7.87 us  [everywhere(): return lax.all_to_all(x, BOTH, split_axis=0, concat_axis=0, tiled=True)]
    pallas_call x6 -> x7, Pallas kernels: 10.3 us -> 14.7 us  [call(): pl.pallas_call(functools.partial(staged, kernel, where, len(outs), tuple(...]
    all_to_all x1 -> x2, starting transfers between devices: 6.96 us -> 9.63 us  [everywhere(): return lax.all_to_all(x, BOTH, split_axis=0, concat_axis=0, tiled=True)]
    ppermute x5, waiting for transfers between devices: 2.92 us -> 5.09 us  [flip(): lax.ppermute(x, axis, [(i, i ^ 1 << level) for i in range(lax.axis_size(a...]
    ppermute x5, starting transfers between devices: 12.9 us -> 10.9 us  [flip(): lax.ppermute(x, axis, [(i, i ^ 1 << level) for i in range(lax.axis_size(a...]
  transfers between devices with their start and end apart: 9 -> 10, of which waited for: 3 -> 5; matrix products, arithmetic and copies ran while one was open for 0% -> 0% of each run, Pallas kernels for 13% -> 18%
where the time goes in v10:
time: 70.9 us; the launch traced here: 70.6 us
  Pallas kernels  22.8 us (32%)
  starting transfers between devices  22.5 us (32%)
  waiting for transfers between devices  13 us (18%)
  blocking collectives  11.5 us (16%)
  between operations  0.79 us (1%)
    pallas_call x7, Pallas kernels, call(): pl.pallas_call(functools.partial(staged, kernel, where, len(outs), tuple(...  14.7 us
    all_to_all x1, blocking collectives, everywhere(): return lax.all_to_all(x, BOTH, split_axis=0, concat_axis=0, tiled=True)  11.5 us
    ppermute x5, starting transfers between devices, flip(): lax.ppermute(x, axis, [(i, i ^ 1 << level) for i in range(lax.axis_size(a...  10.9 us
    all_to_all x2, starting transfers between devices, everywhere(): return lax.all_to_all(x, BOTH, split_axis=0, concat_axis=0, tiled=True)  9.63 us
    all_to_all x2, waiting for transfers between devices, everywhere(): return lax.all_to_all(x, BOTH, split_axis=0, concat_axis=0, tiled=True)  7.87 us
    ppermute x5, waiting for transfers between devices, flip(): lax.ppermute(x, axis, [(i, i ^ 1 << level) for i in range(lax.axis_size(a...  5.09 us
    pallas_call x1, Pallas kernels, shards(): pl.pallas_call(front_kernel, out_shape=vmem((devices, 1, rows + 2 * level...  5 us
    pallas_call x1, Pallas kernels, shards(): pl.pallas_call(pres_kernel, out_shape=(field, vmem((devices, 1, 3 * count...  3.13 us
  transfers between devices with their start and end apart: 10, of which 5 were waited for; matrix products, arithmetic and copies ran while one was open for 0% of the time, Pallas kernels for 18%

profile of v10, /device:TPU:0, one launch (start us, length us, event | category | flops | bytes accessed | tf_op | source)
XLA Modules:
  0.0 70.6 jit_solution(13761010441197032761)
XLA Ops:
  0.6 3.1 %shard_map.139 = (f32[3,16,2048]{2,1,0:T(8,128)S(1)}, f32[32,1,768]{2,1,0:T(1,128)}, f32[6,16,2048]{2,1,0:T(8,128)S(1)}) custom-call(s32[1,256]{1,0:T(1,128)} %bitcast.7, s32[1,256]{1,0:T(1,128)} %bitcast.9, f32[1,256]{1,0:T(1,128)} %bitcast.4, f32[3,3,16,2048]{3,2,1,0:T(8,128)} %refs_9_.1, f32[3,3,16,2048]{3,2,1,0:T(8,128)} %wts_in.1, ...), custom_call_target="tpu_custom_call" | custom-call | tf_op jit(solution)/shard_map/pallas_call | solution.py:588
  3.8 0.5 collective-permute-start
  4.3 7.0 %all-to-all-start = ((f32[32,1,768]{2,1,0:T(1,128)}), f32[32,1,768]{2,1,0:T(1,128)S(1)}, u32[]{:S(2)}, u32[]{:S(2)}) async-start(f32[32,1,768]{2,1,0:T(1,128)} %get-tuple-element.36), calls=%async_computation | async-start | bytes 196608 | tf_op jit(solution)/shard_map/all_to_all | solution.py:569
  11.3 0.0 collective-permute-done.refs_1_.refs_2_.refs_3_
  11.3 0.0 copy-start
  11.3 2.2 %shard_map.140 = (f32[12,1,2048]{2,1,0:T(1,128)S(1)}, f32[12,1,2048]{2,1,0:T(1,128)S(1)}, f32[1,768]{1,0:T(1,128)S(1)}, f32[3,16,2048]{2,1,0:T(8,128)S(1)}) custom-call(f32[6,16,2048]{2,1,0:T(8,128)S(1)} %get-tuple-element.37.refs_0_, f32[6,16,2048]{2,1,0:T(8,128)S(1)} %collective-permute-done.refs_1_.refs_2_.refs_3_, ...), custom_call_target="tpu_custom_call" | custom-call | tf_op jit(solution)/shard_map/pallas_call | solution.py:56
  13.5 0.0 copy-done
  13.6 5.5 %all-to-all-done.recv.refs_1_ = f32[32,1,768]{2,1,0:T(1,128)S(1)} async-done(((f32[32,1,768]{2,1,0:T(1,128)}), f32[32,1,768]{2,1,0:T(1,128)S(1)}, u32[]{:S(2)}, u32[]{:S(2)}) %all-to-all-start) | async-done | bytes 98336 | tf_op jit(solution)/shard_map/all_to_all | solution.py:569
  19.1 0.3 collective-permute-start.1
  19.4 5.0 %shard_map.141 = f32[32,1,1280]{2,1,0:T(1,128)} custom-call(f32[32,1,768]{2,1,0:T(1,128)S(1)} %all-to-all-done.recv.refs_1_, f32[1,1024]{1,0:T(1,128)S(1)} %pad_maximum_fusion.found, f32[256,8192]{1,0:T(8,128)} %inverse.1), custom_call_target="tpu_custom_call" | custom-call | tf_op jit(solution)/shard_map/pallas_call | solution.py:623
  24.4 2.7 %all-to-all-start.1 = ((f32[32,1,1280]{2,1,0:T(1,128)}), f32[32,1,1280]{2,1,0:T(1,128)S(1)}, u32[]{:S(2)}, u32[]{:S(2)}) async-start(f32[32,1,1280]{2,1,0:T(1,128)} %shard_map.141), calls=%async_computation.1 | async-start | bytes 327680 | tf_op jit(solution)/shard_map/all_to_all | solution.py:569
  27.1 3.3 %collective-permute-done.1.refs_3_.refs_4_ = f32[3,16,2048]{2,1,0:T(8,128)S(1)} collective-permute-done((f32[3,16,2048]{2,1,0:T(8,128)S(1)}, f32[3,16,2048]{2,1,0:T(8,128)S(1)}, u32[]{:S(2)}, u32[]{:S(2)}) %collective-permute-start.1) | collective-permute-done | bytes 393248 | tf_op jit(solution)/shard_map/ppermute | solution.py:560
  30.4 0.1 shard_map.142
  30.4 0.7 collective-permute-start.2
  31.1 2.2 %collective-permute-start.3 = (f32[21,1,2048]{2,1,0:T(1,128)S(1)}, f32[21,1,2048]{2,1,0:T(1,128)S(1)}, u32[]{:S(2)}, u32[]{:S(2)}) collective-permute-start(f32[21,1,2048]{2,1,0:T(1,128)S(1)} %get-tuple-element.50), channel_id=1, source_target_pairs={{0,4},{4,0},{8,12},{12,8},{16,20},{20,16},{24,28},{28,24},{1,5},{5... | collective-permute-start | bytes 516104 | tf_op jit(solution)/shard_map/ppermute | solution.py:560
  33.3 2.4 %all-to-all-done.1.refs_0_ = f32[32,1,1280]{2,1,0:T(1,128)S(1)} async-done(((f32[32,1,1280]{2,1,0:T(1,128)}), f32[32,1,1280]{2,1,0:T(1,128)S(1)}, u32[]{:S(2)}, u32[]{:S(2)}) %all-to-all-start.1) | async-done | bytes 163872 | tf_op jit(solution)/shard_map/all_to_all | solution.py:569
  35.7 4.1 %shard_map.143 = (f32[3,16,2048]{2,1,0:T(8,128)S(1)}, f32[3,16,2048]{2,1,0:T(8,128)S(1)}, f32[3,16,2048]{2,1,0:T(8,128)S(1)}, f32[3,16,2048]{2,1,0:T(8,128)}, f3...) custom-call(f32[32,1,1280]{2,1,0:T(1,128)S(1)} %all-to-all-done.1.refs_0_, ...), custom_call_target="tpu_custom_call" | custom-call | tf_op jit(solution)/shard_map/pallas_call | solution.py:56
  39.8 0.0 collective-permute-done.2.refs_2_
  39.8 0.3 collective-permute-done.3.refs_3_
  40.1 4.2 %shard_map.144 = (f32[3,3,16,2048]{3,2,1,0:T(8,128)S(1)}, f32[3,16,2048]{2,1,0:T(8,128)S(1)}, f32[3,3,1,2048]{3,2,1,0:T(1,128)S(1)}, f32[3,3,1,2048]{3,2,1,0:T(1...) custom-call(f32[32,1,1280]{2,1,0:T(1,128)S(1)} %all-to-all-done.1.re, ...), custom_call_target="tpu_custom_call" | custom-call | tf_op jit(solution)/shard_map/pallas_call | solution.py:56
  44.3 0.7 collective-permute-start.4
  45.0 2.6 %collective-permute-start.7 = (f32[3,16,2048]{2,1,0:T(8,128)S(1)}, f32[3,16,2048]{2,1,0:T(8,128)S(1)}, u32[]{:S(2)}, u32[]{:S(2)}) collective-permute-start(f32[3,16,2048]{2,1,0:T(8,128)S(1)} %get-tuple-element.62), channel_id=1, source_target_pairs={{0,1},{1,0},{2,3},{3,2},{4,5},{5,4},{6,7},{7,6},{8,9},{9,8},{10,11... | collective-permute-start | bytes 1179656 | tf_op jit(solution)/shard_map/ppermute | solution.py:560
  47.7 0.7 collective-permute-start.5
  48.3 5.1 %collective-permute-start.6 = (f32[3,3,1,2048]{3,2,1,0:T(1,128)S(1)}, f32[3,3,1,2048]{3,2,1,0:T(1,128)S(1)}, u32[]{:S(2)}, u32[]{:S(2)}) collective-permute-start(f32[3,3,1,2048]{3,2,1,0:T(1,128)S(1)} %get-tuple-element.61), channel_id=1, source_target_pairs={{0,4},{4,0},{8,12},{12,8},{16,20},{20,16},{24,28},{28,24},{1,5},{5... | collective-permute-start | bytes 221192 | tf_op jit(solution)/shard_map/ppermute | solution.py:560
  53.5 1.2 %shard_map.145.refs_0_ = f32[3,3,16,2048]{3,2,1,0:T(8,128)S(1)} custom-call(f32[3,3,16,2048]{3,2,1,0:T(8,128)S(1)} %get-tuple-element.56.refs_0_.refs_1_, f32[3,3,3,16,2048]{4,3,2,1,0:T(8,128)S(1)} %get-tuple-element.57.refs_1_, f32[3,16,2048]{2,1,0:T(8,128)S(1)} %get-tuple-element.54.refs_7_.refs_2_.refs_6_, ...), custom_call_target="tpu_custom_call" | custom-call | tf_op jit(solution)/shard_map/pallas_call | solution.py:56
  54.7 0.0 collective-permute-done.5.refs_2_
  54.7 1.5 %collective-permute-done.6.refs_3_ = f32[3,3,1,2048]{3,2,1,0:T(1,128)S(1)} collective-permute-done((f32[3,3,1,2048]{3,2,1,0:T(1,128)S(1)}, f32[3,3,1,2048]{3,2,1,0:T(1,128)S(1)}, u32[]{:S(2)}, u32[]{:S(2)}) %collective-permute-start.6) | collective-permute-done | bytes 73760 | tf_op jit(solution)/shard_map/ppermute | solution.py:560
  56.2 0.0 collective-permute-done.4.refs_1_
  56.2 0.0 collective-permute-done.7.refs_4_
  56.2 1.2 %shard_map.146 = (f32[3,3,16,2048]{3,2,1,0:T(8,128)S(1)}, f32[32,1,128]{2,1,0:T(1,128)S(1)}) custom-call(f32[3,3,16,2048]{3,2,1,0:T(8,128)S(1)} %shard_map.145.refs_0_, f32[3,16,2048]{2,1,0:T(8,128)S(1)} %collective-permute-done.4.refs_1_, f32[3,3,1,2048]{3,2,1,0:T(1,128)S(1)} %collective-permute-done.5.refs_2_, ...), custom_call_target="tpu_custom_call" | custom-call | tf_op jit(solution)/shard_map/pallas_call | solution.py:56
  57.4 11.5 %all_to_all.15.refs_0_ = f32[32,1,128]{2,1,0:T(1,128)S(1)} all-to-all(f32[32,1,128]{2,1,0:T(1,128)S(1)} %get-tuple-element.64), channel_id=1, replica_groups=mesh['tile'=8,'layer'=4] {'tile','layer'}, dimensions={0} | all-to-all | bytes 32768 | tf_op jit(solution)/shard_map/all_to_all | solution.py:569
  68.9 1.7 %shard_map.147 = (f32[3,3,16,2048]{3,2,1,0:T(8,128)}, f32[3,3,16,2048]{3,2,1,0:T(8,128)}, f32[1,1]{1,0:T(1,128)}) custom-call(f32[32,1,128]{2,1,0:T(1,128)S(1)} %all_to_all.15.refs_0_, f32[3,3,16,2048]{3,2,1,0:T(8,128)S(1)} %get-tuple-element.56.refs_0_.refs_1_, f32[3,3,16,2048]{3,2,1,0:T(8,128)S(1)} %get-tuple-element.65.refs_2_, ...), custom_call_target="tpu_custom_call" | custom-call | tf_op jit(solution)/shard_map/pallas_call | solution.py:56
  (1 shorter events, 0.0 us)
Async XLA Ops:
  3.8 7.5 %collective-permute-start = (f32[6,16,2048]{2,1,0:T(8,128)S(1)}, f32[6,16,2048]{2,1,0:T(8,128)S(1)}, u32[]{:S(2)}, u32[]{:S(2)}) collective-permute-start(f32[6,16,2048]{2,1,0:T(8,128)S(1)} %get-tuple-element.37.refs_0_), channel_id=1, source_target_pairs={{0,1},{1,0},{2,3},{3,2},{4,5},{5,4},{6,7},{7,6},{8,9},{9,8},{10,11... | collective-permute-start | bytes 2359304 | tf_op jit(solution)/shard_map/ppermute | solution.py:560
  4.3 14.8 %all-to-all-start = ((f32[32,1,768]{2,1,0:T(1,128)}), f32[32,1,768]{2,1,0:T(1,128)S(1)}, u32[]{:S(2)}, u32[]{:S(2)}) async-start(f32[32,1,768]{2,1,0:T(1,128)} %get-tuple-element.36), calls=%async_computation | async-start | bytes 196608 | tf_op jit(solution)/shard_map/all_to_all | solution.py:569
  11.3 2.3 %copy-start = (f32[256]{0:T(256)S(1)}, f32[256]{0:T(256)}, u32[]{:S(2)}) copy-start(f32[256]{0:T(256)} %param.22) | copy-start | bytes 3076
  19.1 11.3 %collective-permute-start.1 = (f32[3,16,2048]{2,1,0:T(8,128)S(1)}, f32[3,16,2048]{2,1,0:T(8,128)S(1)}, u32[]{:S(2)}, u32[]{:S(2)}) collective-permute-start(f32[3,16,2048]{2,1,0:T(8,128)S(1)} %get-tuple-element.48), channel_id=1, source_target_pairs={{0,2},{1,3},{2,0},{3,1},{4,6},{5,7},{6,4},{7,5},{8,10},{9,11},{10,... | collective-permute-start | bytes 1179656 | tf_op jit(solution)/shard_map/ppermute | solution.py:560
  24.4 11.3 %all-to-all-start.1 = ((f32[32,1,1280]{2,1,0:T(1,128)}), f32[32,1,1280]{2,1,0:T(1,128)S(1)}, u32[]{:S(2)}, u32[]{:S(2)}) async-start(f32[32,1,1280]{2,1,0:T(1,128)} %shard_map.141), calls=%async_computation.1 | async-start | bytes 327680 | tf_op jit(solution)/shard_map/all_to_all | solution.py:569
  30.4 9.4 %collective-permute-start.2 = (f32[21,1,2048]{2,1,0:T(1,128)S(1)}, f32[21,1,2048]{2,1,0:T(1,128)S(1)}, u32[]{:S(2)}, u32[]{:S(2)}) collective-permute-start(f32[21,1,2048]{2,1,0:T(1,128)S(1)} %get-tuple-element.49), channel_id=1, source_target_pairs={{4,8},{12,16},{20,24},{8,4},{16,12},{24,20},{5,9},{13,17},{21,25},... | collective-permute-start | bytes 516104 | tf_op jit(solution)/shard_map/ppermute | solution.py:565
  31.1 9.0 %collective-permute-start.3 = (f32[21,1,2048]{2,1,0:T(1,128)S(1)}, f32[21,1,2048]{2,1,0:T(1,128)S(1)}, u32[]{:S(2)}, u32[]{:S(2)}) collective-permute-start(f32[21,1,2048]{2,1,0:T(1,128)S(1)} %get-tuple-element.50), channel_id=1, source_target_pairs={{0,4},{4,0},{8,12},{12,8},{16,20},{20,16},{24,28},{28,24},{1,5},{5... | collective-permute-start | bytes 516104 | tf_op jit(solution)/shard_map/ppermute | solution.py:560
  44.3 11.9 %collective-permute-start.4 = (f32[3,16,2048]{2,1,0:T(8,128)S(1)}, f32[3,16,2048]{2,1,0:T(8,128)S(1)}, u32[]{:S(2)}, u32[]{:S(2)}) collective-permute-start(f32[3,16,2048]{2,1,0:T(8,128)S(1)} %get-tuple-element.59), channel_id=1, source_target_pairs={{1,2},{2,1},{5,6},{6,5},{9,10},{10,9},{13,14},{14,13},{17,18},{18,... | collective-permute-start | bytes 1179656 | tf_op jit(solution)/shard_map/ppermute | solution.py:565
  45.0 11.2 %collective-permute-start.7 = (f32[3,16,2048]{2,1,0:T(8,128)S(1)}, f32[3,16,2048]{2,1,0:T(8,128)S(1)}, u32[]{:S(2)}, u32[]{:S(2)}) collective-permute-start(f32[3,16,2048]{2,1,0:T(8,128)S(1)} %get-tuple-element.62), channel_id=1, source_target_pairs={{0,1},{1,0},{2,3},{3,2},{4,5},{5,4},{6,7},{7,6},{8,9},{9,8},{10,11... | collective-permute-start | bytes 1179656 | tf_op jit(solution)/shard_map/ppermute | solution.py:560
  47.7 7.0 %collective-permute-start.5 = (f32[3,3,1,2048]{3,2,1,0:T(1,128)S(1)}, f32[3,3,1,2048]{3,2,1,0:T(1,128)S(1)}, u32[]{:S(2)}, u32[]{:S(2)}) collective-permute-start(f32[3,3,1,2048]{3,2,1,0:T(1,128)S(1)} %get-tuple-element.60), channel_id=1, source_target_pairs={{4,8},{12,16},{20,24},{8,4},{16,12},{24,20},{5,9},{13,17},{21,25},... | collective-permute-start | bytes 221192 | tf_op jit(solution)/shard_map/ppermute | solution.py:565
  48.3 7.9 %collective-permute-start.6 = (f32[3,3,1,2048]{3,2,1,0:T(1,128)S(1)}, f32[3,3,1,2048]{3,2,1,0:T(1,128)S(1)}, u32[]{:S(2)}, u32[]{:S(2)}) collective-permute-start(f32[3,3,1,2048]{3,2,1,0:T(1,128)S(1)} %get-tuple-element.61), channel_id=1, source_target_pairs={{0,4},{4,0},{8,12},{12,8},{16,20},{20,16},{24,28},{28,24},{1,5},{5... | collective-permute-start | bytes 221192 | tf_op jit(solution)/shard_map/ppermute | solution.py:560

commit v11 on v10

--- a/solution.py
+++ b/solution.py
@@ -315,7 +315,7 @@
     two[...] = jnp.where(odd, last, first)
 
 
-def table_kernel(lists, shape, terms, hots, side=False):
+def table_kernel(lists, shape, terms, hots, only=None):
     _, width, long = shape
     rows_hot, lanes_hot, sol_hot, sol_row, layer = hots
     lanes = 128
@@ -323,17 +323,15 @@
     count = terms.shape[2] // 3
     at = 0
     for members in lists:
-        for k, device in enumerate(members):
+        for device in members:
             entry = terms[device]
             index = entry[:, count : 2 * count].astype(I32)
             cell = entry[:, 2 * count :].astype(I32)
             y, x = lax.rem(cell, long), lax.rem(lax.div(cell, long), width)
-            if not side:
+            if only is None:
                 row = lax.div(y, lanes) * width + x
-            elif k % 2 == 0:
-                row = jnp.where(x == 0, lax.div(y, lanes) * 8, -1)
             else:
-                row = jnp.where(x == width - 1, lax.div(y, lanes) * 8 + 7, -1)
+                row = jnp.where(x == only, lax.div(y, lanes) * 8, -1)
             here = pl.ds(at, count)
             rows_hot[:, here] = onehot(row, rows_hot.shape[0]).astype(BF16)
             lanes_hot[:, here] = onehot(lax.rem(y, lanes), lanes).astype(BF16)
@@ -406,9 +404,10 @@
     return [y[z] + first[z] * above + final[z] * below for z in range(depth)], above, below, tzp
 
 
-def pressure_kernel(levels, recv, terms, pres, *refs):
-    sib, (tz, store, tx, binv, p, coupled_z, *hots) = (refs[:levels], refs[levels:])
-    depth = pres.shape[0]
+def pressure_kernel(levels, ready, recv, terms, pres, *refs):
+    sib, (tz, store, tx, _, p, coupled_z, one, *hots) = (refs[:levels], refs[levels:])
+    depth, width, _ = pres.shape
+    odd = is_right(0, "tile")
     lists = groups_of(levels)
     table_kernel(lists, pres.shape, terms, hots)
     tzs = [tz[z] for z in range(depth)]
@@ -418,51 +417,51 @@
     is_last = lax.axis_index("layer") == (1 << levels) - 1
     for z in range(depth):
         p[z] = values[z]
+        one[z] = jnp.where(odd, values[z][0:1], (tx[z] * values[z])[width - 1 :])
         total = above + tzp * values[z] if z == 0 else tzs[z - 1] * values[z - 1]
         if z == depth - 1:
             coupled_z[z] = total + jnp.where(is_last, 0.0, below + tzs[z] * values[z])
         else:
             coupled_z[z] = total + tzs[z] * values[z + 1]
+    ready()
 
 
 def edge_kernel(levels, low, high, *refs):
-    sib, (one, two) = (refs[:levels], refs[levels:])
-    for ref in (one, two):
-        ref[...] = jnp.zeros(ref.shape, F32)
+    sib, two = (refs[:levels], refs[levels])
+    odd = is_right(0, "tile")
     n = low.shape[0]
-    tile_rows(low[...], high[...], one.at[pl.ds(0, n)], two.at[pl.ds(0, n)])
+    two[pl.ds(0, n)] = jnp.where(odd, high[...], low[...])
     at = n
     for block in sib:
         width = block.shape[1]
         for i in range(block.shape[0]):
-            tile_rows(block[i, 0:1], block[i, width - 1 : width], one.at[at], two.at[at])
+            two[at] = jnp.where(odd, block[i, width - 1 : width], block[i, 0:1])
             at += 1
 
 
-def search_kernel(levels, shapes, ready, recv, terms, two, one, p, coupled_z, tx, tz, binv, rhs, diag, ty, *refs):
-    (s, outer, row_two, row_one, inner), (planes, *hots) = (refs[:5], refs[5:])
-    depth, width, long = p.shape
+def first_three(kernel, ready, one, two, three, _rhs, _diag, _ty, *rest):
+    kernel(one, two, three, *rest)
+    ready()
+
+
+def beyond_kernel(levels, shapes, shape, recv, terms, two, row, planes, *hots):
+    depth, width, long = shape
     tiles, layers = (lax.axis_size("tile"), lax.axis_size("layer"))
     tile = lax.axis_index("tile")
-    odd, right = (is_right(0, "tile"), is_right(0))
-    row = iota(p.shape[1:], 0)
+    odd = is_right(0, "tile")
     planes[...] = jnp.zeros(planes.shape, F32)
     for i in range(planes.shape[0]):
-        planes[i, 0:1] = jnp.where(odd, two[i], one[i])
-        planes[i, 7:8] = jnp.where(odd, one[i], two[i])
-    lists = [
-        [jnp.clip(device + step, 0, tiles * layers - 1) for device in members for step in (layers, -layers)]
-        for members in groups_of(levels)
-    ]
-    table_kernel(lists, p.shape, terms, hots, side=True)
-    has_next, has_last = ((tile < tiles - 1).astype(F32), (tile > 0).astype(F32))
-    real = jnp.where(iota((8, long), 0) < 4, has_next, has_last)
+        planes[i, 0:1] = two[i]
+    step = jnp.where(odd, layers, -layers)
+    lists = [[jnp.clip(device + step, 0, tiles * layers - 1) for device in members] for members in groups_of(levels)]
+    table_kernel(lists, shape, terms, hots, jnp.where(odd, 0, width - 1))
+    exists = jnp.where(odd, (tile < tiles - 1).astype(F32), (tile > 0).astype(F32)) + jnp.zeros((1, long), F32)
     blocks = []
     at = 4 * depth
     for size in shapes:
         blocks.append([planes[at + i] for i in range(size)])
         at += size
-    beyond, _, _, _ = column_solve(
+    values, _, _, _ = column_solve(
         levels,
         recv,
         lists,
@@ -472,12 +471,20 @@
         [planes[2 * depth + z] for z in range(depth)],
         blocks,
     )
-    ready()
+    for z in range(depth):
+        found = jnp.where(exists > 0.0, values[z][0:1], 0.0)
+        row[z] = jnp.where(odd, found, found * two[3 * depth + z])
+
+
+def search_kernel(p, coupled_z, two, one, tx, ty, tz, rhs, diag, binv, s, outer, row_two, row_one, inner):
+    depth, width, _ = p.shape
+    odd = is_right(0, "tile")
+    right = is_right(0)
+    row = iota(p.shape[1:], 0)
     for z in range(depth):
         centre = p[z]
-        far = jnp.where(real > 0.0, beyond[z], 0.0)
-        after = far[0:1]
-        before = (planes[3 * depth + z] * far)[7:8]
+        after = jnp.where(odd, two[z], one[z])
+        before = jnp.where(odd, one[z], two[z])
         coupled = coupled_z[z] + beside(centre, tx[z], ty[z])
         coupled = coupled + jnp.where(row == 0, before, 0.0) + jnp.where(row == width - 1, tx[z] * after, 0.0)
         remain = [rhs[c, z] - diag[c, 0, z] * centre for c in range(3)]
@@ -631,39 +638,47 @@
     sizes = [block.shape[0] for block in sib]
     rim = vmem((4 * depth + sum(sizes), 1, long))
     send, low, high = lax.optimization_barrier((send, low, high))
-    one, two = call(functools.partial(edge_kernel, levels), (rim, rim), (low, high, *sib))
+    (two,) = call(functools.partial(edge_kernel, levels), (rim,), (low, high, *sib))
     sol = everywhere(send)
-    two, one = (neighbour(two, "tile"), flip(one, 0, "tile"))
-
-    def hots(high, long_list, short_list):
+    two = neighbour(two, "tile")
+
+    def hots(high):
         return (
-            vmem((high * long // 128, long_list), BF16),
-            vmem((128, long_list), BF16),
-            vmem((rows, long_list), BF16),
-            vmem((1, long_list), I32),
-            vmem((1, short_list), I32),
+            vmem((high * long // 128, lists), BF16),
+            vmem((128, lists), BF16),
+            vmem((rows, lists), BF16),
+            vmem((1, lists), I32),
+            vmem((1, count), I32),
         )
 
     at = 3 + levels
-    p, coupled_z, tz, _, tx, block_inv = call(
+    row3 = vmem((depth, 1, long))
+    p, coupled_z, one, tz, _, tx, block_inv = call(
         functools.partial(pressure_kernel, levels),
-        (field, field),
+        (field, field, row3),
         (sol, terms, pres, *sib, tz, store, tx, block_inv),
         far=range(at, at + 4),
         keep=range(at, at + 4),
-        late=(),
-        scratch=hots(width, lists, count),
+        late=(at + 3,),
+        scratch=hots(width),
+    )
+    sol, one, terms = lax.optimization_barrier((sol, one, terms))
+    one = flip(one, 0, "tile")
+    two, rhs, block_diag, ty = call(
+        functools.partial(first_three, functools.partial(beyond_kernel, levels, sizes, (depth, width, long))),
+        (row3,),
+        (sol, terms, two, rhs, block_diag, ty),
+        far=(3, 4, 5),
+        keep=(3, 4, 5),
+        late=(3, 4, 5),
+        scratch=(vmem((4 * depth + sum(sizes), 8, long)), *hots(8)),
     )
     row9 = vmem((3, depth, 1, long))
     plane3 = planes(3)
-    s, outer, row_two, row_one, inner, rhs, block_diag, ty = call(
-        functools.partial(search_kernel, levels, sizes),
+    s, outer, row_two, row_one, inner = call(
+        search_kernel,
         (vmem(rhs.shape), plane3, row9, row9, plane3),
-        (sol, terms, two, one, p, coupled_z, tx, tz, block_inv, rhs, block_diag, ty),
-        far=(9, 10, 11),
-        keep=(9, 10, 11),
-        late=(9, 10, 11),
-        scratch=(vmem((4 * depth + sum(sizes), 8, long)), *hots(8, 2 * lists, 2 * count)),
+        (p, coupled_z, two, one, tx, ty, tz, rhs, block_diag, block_inv),
     )
     outer, row_two = (neighbour(outer), neighbour(row_two, "tile"))
     row_one, inner = (flip(row_one, 0, "tile"), flip(inner, 0))

time: 70.9 us -> 68 us (0.959)
  starting transfers between devices: 22.5 us -> 19.1 us
  waiting for transfers between devices: 13 us -> 15.1 us
  Pallas kernels: 22.8 us -> 21.9 us
    ppermute x5, starting transfers between devices: 10.9 us -> 7.42 us  [flip(): lax.ppermute(x, axis, [(i, i ^ 1 << level) for i in range(lax.axis_size(a...]
    all_to_all x2, waiting for transfers between devices: 7.87 us -> 10.1 us  [everywhere(): return lax.all_to_all(x, BOTH, split_axis=0, concat_axis=0, tiled=True)]
    pallas_call x7 -> x8, Pallas kernels: 14.7 us -> 13.8 us  [call(): pl.pallas_call(functools.partial(staged, kernel, where, len(outs), tuple(...]
  transfers between devices with their start and end apart: 10 -> 10, of which waited for: 5 -> 4; matrix products, arithmetic and copies ran while one was open for 0% -> 0% of each run, Pallas kernels for 18% -> 22%
where the time goes in v11:
time: 68 us; the launch traced here: 67.7 us
  Pallas kernels  21.9 us (32%)
  starting transfers between devices  19.1 us (28%)
  waiting for transfers between devices  15.1 us (22%)
  blocking collectives  10.8 us (16%)
  between operations  0.8 us (1%)
    pallas_call x8, Pallas kernels, call(): pl.pallas_call(functools.partial(staged, kernel, where, len(outs), tuple(...  13.8 us
    all_to_all x1, blocking collectives, everywhere(): return lax.all_to_all(x, BOTH, split_axis=0, concat_axis=0, tiled=True)  10.8 us
    all_to_all x2, waiting for transfers between devices, everywhere(): return lax.all_to_all(x, BOTH, split_axis=0, concat_axis=0, tiled=True)  10.1 us
    all_to_all x2, starting transfers between devices, everywhere(): return lax.all_to_all(x, BOTH, split_axis=0, concat_axis=0, tiled=True)  9.63 us
    ppermute x5, starting transfers between devices, flip(): lax.ppermute(x, axis, [(i, i ^ 1 << level) for i in range(lax.axis_size(a...  7.42 us
    ppermute x5, waiting for transfers between devices, flip(): lax.ppermute(x, axis, [(i, i ^ 1 << level) for i in range(lax.axis_size(a...  5.02 us
    pallas_call x1, Pallas kernels, shards(): pl.pallas_call(front_kernel, out_shape=vmem((devices, 1, rows + 2 * level...  5 us
    pallas_call x1, Pallas kernels, shards(): pl.pallas_call(pres_kernel, out_shape=(field, vmem((devices, 1, 3 * count...  3.13 us
  transfers between devices with their start and end apart: 10, of which 4 were waited for; matrix products, arithmetic and copies ran while one was open for 0% of the time, Pallas kernels for 22%

profile of v11, /device:TPU:0, one launch (start us, length us, event | category | flops | bytes accessed | tf_op | source)
XLA Modules:
  0.0 67.7 jit_solution(47597373944152983)
XLA Ops:
  0.6 3.1 %shard_map.139 = (f32[3,16,2048]{2,1,0:T(8,128)S(1)}, f32[32,1,768]{2,1,0:T(1,128)}, f32[6,16,2048]{2,1,0:T(8,128)S(1)}) custom-call(s32[1,256]{1,0:T(1,128)} %bitcast.7, s32[1,256]{1,0:T(1,128)} %bitcast.9, f32[1,256]{1,0:T(1,128)} %bitcast.4, f32[3,3,16,2048]{3,2,1,0:T(8,128)} %refs_3_.3, f32[3,3,16,2048]{3,2,1,0:T(8,128)} %wts_in.1, ...), custom_call_target="tpu_custom_call" | custom-call | tf_op jit(solution)/shard_map/pallas_call | solution.py:595
  3.8 0.5 collective-permute-start
  4.3 7.0 %all-to-all-start = ((f32[32,1,768]{2,1,0:T(1,128)}), f32[32,1,768]{2,1,0:T(1,128)S(1)}, u32[]{:S(2)}, u32[]{:S(2)}) async-start(f32[32,1,768]{2,1,0:T(1,128)} %get-tuple-element.39), calls=%async_computation | async-start | bytes 196608 | tf_op jit(solution)/shard_map/all_to_all | solution.py:576
  11.3 0.0 collective-permute-done.refs_1_.refs_3_.refs_2_
  11.3 0.0 copy-start
  11.3 2.2 %shard_map.140 = (f32[12,1,2048]{2,1,0:T(1,128)S(1)}, f32[12,1,2048]{2,1,0:T(1,128)S(1)}, f32[1,768]{1,0:T(1,128)S(1)}, f32[3,16,2048]{2,1,0:T(8,128)S(1)}) custom-call(f32[6,16,2048]{2,1,0:T(8,128)S(1)} %get-tuple-element.40.refs_0_, f32[6,16,2048]{2,1,0:T(8,128)S(1)} %collective-permute-done.refs_1_.refs_3_.refs_2_, ...), custom_call_target="tpu_custom_call" | custom-call | tf_op jit(solution)/shard_map/pallas_call | solution.py:56
  13.5 0.0 copy-done
  13.6 5.5 %all-to-all-done.recv.refs_1_ = f32[32,1,768]{2,1,0:T(1,128)S(1)} async-done(((f32[32,1,768]{2,1,0:T(1,128)}), f32[32,1,768]{2,1,0:T(1,128)S(1)}, u32[]{:S(2)}, u32[]{:S(2)}) %all-to-all-start) | async-done | bytes 98336 | tf_op jit(solution)/shard_map/all_to_all | solution.py:576
  19.1 0.3 collective-permute-start.1
  19.4 5.0 %shard_map.141 = f32[32,1,1280]{2,1,0:T(1,128)} custom-call(f32[32,1,768]{2,1,0:T(1,128)S(1)} %all-to-all-done.recv.refs_1_, f32[1,1024]{1,0:T(1,128)S(1)} %pad_maximum_fusion.found, f32[256,8192]{1,0:T(8,128)} %inverse.1), custom_call_target="tpu_custom_call" | custom-call | tf_op jit(solution)/shard_map/pallas_call | solution.py:630
  24.4 2.7 %all-to-all-start.1 = ((f32[32,1,1280]{2,1,0:T(1,128)}), f32[32,1,1280]{2,1,0:T(1,128)S(1)}, u32[]{:S(2)}, u32[]{:S(2)}) async-start(f32[32,1,1280]{2,1,0:T(1,128)} %shard_map.141), calls=%async_computation.1 | async-start | bytes 327680 | tf_op jit(solution)/shard_map/all_to_all | solution.py:576
  27.1 3.3 %collective-permute-done.1.refs_4_.refs_3_ = f32[3,16,2048]{2,1,0:T(8,128)S(1)} collective-permute-done((f32[3,16,2048]{2,1,0:T(8,128)S(1)}, f32[3,16,2048]{2,1,0:T(8,128)S(1)}, u32[]{:S(2)}, u32[]{:S(2)}) %collective-permute-start.1) | collective-permute-done | bytes 393248 | tf_op jit(solution)/shard_map/ppermute | solution.py:567
  30.4 0.7 collective-permute-start.2
  31.1 4.6 %all-to-all-done.1.refs_0_ = f32[32,1,1280]{2,1,0:T(1,128)S(1)} async-done(((f32[32,1,1280]{2,1,0:T(1,128)}), f32[32,1,1280]{2,1,0:T(1,128)S(1)}, u32[]{:S(2)}, u32[]{:S(2)}) %all-to-all-start.1) | async-done | bytes 163872 | tf_op jit(solution)/shard_map/all_to_all | solution.py:576
  35.7 3.2 %shard_map.142 = (f32[3,16,2048]{2,1,0:T(8,128)S(1)}, f32[3,16,2048]{2,1,0:T(8,128)S(1)}, f32[3,1,2048]{2,1,0:T(1,128)S(1)}, f32[3,16,2048]{2,1,0:T(8,128)S(1)},...) custom-call(f32[32,1,1280]{2,1,0:T(1,128)S(1)} %all-to-all-done.1.refs_0_, ...), custom_call_target="tpu_custom_call" | custom-call | tf_op jit(solution)/shard_map/pallas_call | solution.py:56
  38.9 0.9 %collective-permute-start.3 = (f32[3,1,2048]{2,1,0:T(1,128)S(1)}, f32[3,1,2048]{2,1,0:T(1,128)S(1)}, u32[]{:S(2)}, u32[]{:S(2)}) collective-permute-start(f32[3,1,2048]{2,1,0:T(1,128)S(1)} %get-tuple-element.58), channel_id=1, source_target_pairs={{0,4},{4,0},{8,12},{12,8},{16,20},{20,16},{24,28},{28,24},{1,5},{5... | collective-permute-start | bytes 73736 | tf_op jit(solution)/shard_map/ppermute | solution.py:567
  39.9 0.0 collective-permute-done.2.refs_2_
  39.9 3.3 %shard_map.144 = (f32[3,1,2048]{2,1,0:T(1,128)S(1)}, f32[3,3,16,2048]{3,2,1,0:T(8,128)S(1)}, f32[3,3,3,16,2048]{4,3,2,1,0:T(8,128)S(1)}, f32[3,16,2048]{2,1,0:T(8,128)S(1)}) custom-call(f32[32,1,1280]{2,1,0:T(1,128)S(1)} %all-to-all-done.1.refs_0_, f32[32,1,768]{2,1,0:T(1,128)S(1)} %all-to-all-done.recv.refs_1_, ...), custom_call_target="tpu_custom_call" | custom-call | tf_op jit(solution)/shard_map/pallas_call | solution.py:56
  43.1 0.0 collective-permute-done.3.refs_3_
  43.1 0.9 %shard_map.145 = (f32[3,3,16,2048]{3,2,1,0:T(8,128)S(1)}, f32[3,16,2048]{2,1,0:T(8,128)S(1)}, f32[3,3,1,2048]{3,2,1,0:T(1,128)S(1)}, f32[3,3,1,2048]{3,2,1,0:T(1,128)S(1)}, f32[3,16,2048]{2,1,0:T(8,128)S(1)}) custom-call(f32[3,16,2048]{2,1,0:T(8,128)S(1)} %get-tuple-element.50.refs_0_, f32[3,16,2048]{2,1,0:T(8,128)S(1)} %get-tuple-element.51.refs_1_, ...), custom_call_target="tpu_custom_call" | custom-call | tf_op jit(solution)/shard_map/pallas_call | solution.py:56
  44.1 0.7 %collective-permute-start.4 = (f32[3,16,2048]{2,1,0:T(8,128)S(1)}, f32[3,16,2048]{2,1,0:T(8,128)S(1)}, u32[]{:S(2)}, u32[]{:S(2)}) collective-permute-start(f32[3,16,2048]{2,1,0:T(8,128)S(1)} %get-tuple-element.66), channel_id=1, source_target_pairs={{1,2},{2,1},{5,6},{6,5},{9,10},{10,9},{13,14},{14,13},{17,18},{18,... | collective-permute-start | bytes 1179656 | tf_op jit(solution)/shard_map/ppermute | solution.py:572
  44.8 2.1 %collective-permute-start.7 = (f32[3,16,2048]{2,1,0:T(8,128)S(1)}, f32[3,16,2048]{2,1,0:T(8,128)S(1)}, u32[]{:S(2)}, u32[]{:S(2)}) collective-permute-start(f32[3,16,2048]{2,1,0:T(8,128)S(1)} %get-tuple-element.69), channel_id=1, source_target_pairs={{0,1},{1,0},{2,3},{3,2},{4,5},{5,4},{6,7},{7,6},{8,9},{9,8},{10,11... | collective-permute-start | bytes 1179656 | tf_op jit(solution)/shard_map/ppermute | solution.py:567
  46.9 0.7 collective-permute-start.5
  47.6 3.5 %collective-permute-start.6 = (f32[3,3,1,2048]{3,2,1,0:T(1,128)S(1)}, f32[3,3,1,2048]{3,2,1,0:T(1,128)S(1)}, u32[]{:S(2)}, u32[]{:S(2)}) collective-permute-start(f32[3,3,1,2048]{3,2,1,0:T(1,128)S(1)} %get-tuple-element.68), channel_id=1, source_target_pairs={{0,4},{4,0},{8,12},{12,8},{16,20},{20,16},{24,28},{28,24},{1,5},{5... | collective-permute-start | bytes 221192 | tf_op jit(solution)/shard_map/ppermute | solution.py:567
  51.1 1.2 %shard_map.146.refs_0_ = f32[3,3,16,2048]{3,2,1,0:T(8,128)S(1)} custom-call(f32[3,3,16,2048]{3,2,1,0:T(8,128)S(1)} %get-tuple-element.65.refs_0_.refs_1_, f32[3,3,3,16,2048]{4,3,2,1,0:T(8,128)S(1)} %get-tuple-element.63.refs_8_.refs_1_, f32[3,16,2048]{2,1,0:T(8,128)S(1)} %get-tuple-element.61.refs_6_.refs_2_, ...), custom_call_target="tpu_custom_call" | custom-call | tf_op jit(solution)/shard_map/pallas_call | solution.py:56
  52.3 0.0 collective-permute-done.5.refs_2_
  52.3 1.7 %collective-permute-done.6.refs_3_ = f32[3,3,1,2048]{3,2,1,0:T(1,128)S(1)} collective-permute-done((f32[3,3,1,2048]{3,2,1,0:T(1,128)S(1)}, f32[3,3,1,2048]{3,2,1,0:T(1,128)S(1)}, u32[]{:S(2)}, u32[]{:S(2)}) %collective-permute-start.6) | collective-permute-done | bytes 73760 | tf_op jit(solution)/shard_map/ppermute | solution.py:567
  54.0 0.0 collective-permute-done.4.refs_1_
  54.0 0.0 collective-permute-done.7.refs_4_
  54.0 1.2 %shard_map.147 = (f32[3,3,16,2048]{3,2,1,0:T(8,128)S(1)}, f32[32,1,128]{2,1,0:T(1,128)S(1)}) custom-call(f32[3,3,16,2048]{3,2,1,0:T(8,128)S(1)} %shard_map.146.refs_0_, f32[3,16,2048]{2,1,0:T(8,128)S(1)} %collective-permute-done.4.refs_1_, f32[3,3,1,2048]{3,2,1,0:T(1,128)S(1)} %collective-permute-done.5.refs_2_, ...), custom_call_target="tpu_custom_call" | custom-call | tf_op jit(solution)/shard_map/pallas_call | solution.py:56
  55.2 10.8 %all_to_all.15.refs_0_ = f32[32,1,128]{2,1,0:T(1,128)S(1)} all-to-all(f32[32,1,128]{2,1,0:T(1,128)S(1)} %get-tuple-element.70), channel_id=1, replica_groups=mesh['tile'=8,'layer'=4] {'tile','layer'}, dimensions={0} | all-to-all | bytes 32768 | tf_op jit(solution)/shard_map/all_to_all | solution.py:576
  66.1 1.7 %shard_map.148 = (f32[3,3,16,2048]{3,2,1,0:T(8,128)}, f32[3,3,16,2048]{3,2,1,0:T(8,128)}, f32[1,1]{1,0:T(1,128)}) custom-call(f32[32,1,128]{2,1,0:T(1,128)S(1)} %all_to_all.15.refs_0_, f32[3,3,16,2048]{3,2,1,0:T(8,128)S(1)} %get-tuple-element.65.refs_0_.refs_1_, f32[3,3,16,2048]{3,2,1,0:T(8,128)S(1)} %get-tuple-element.71.refs_2_, ...), custom_call_target="tpu_custom_call" | custom-call | tf_op jit(solution)/shard_map/pallas_call | solution.py:56
  (2 shorter events, 0.1 us)
Async XLA Ops:
  3.8 7.5 %collective-permute-start = (f32[6,16,2048]{2,1,0:T(8,128)S(1)}, f32[6,16,2048]{2,1,0:T(8,128)S(1)}, u32[]{:S(2)}, u32[]{:S(2)}) collective-permute-start(f32[6,16,2048]{2,1,0:T(8,128)S(1)} %get-tuple-element.40.refs_0_), channel_id=1, source_target_pairs={{0,1},{1,0},{2,3},{3,2},{4,5},{5,4},{6,7},{7,6},{8,9},{9,8},{10,11... | collective-permute-start | bytes 2359304 | tf_op jit(solution)/shard_map/ppermute | solution.py:567
  4.3 14.8 %all-to-all-start = ((f32[32,1,768]{2,1,0:T(1,128)}), f32[32,1,768]{2,1,0:T(1,128)S(1)}, u32[]{:S(2)}, u32[]{:S(2)}) async-start(f32[32,1,768]{2,1,0:T(1,128)} %get-tuple-element.39), calls=%async_computation | async-start | bytes 196608 | tf_op jit(solution)/shard_map/all_to_all | solution.py:576
  11.3 2.3 %copy-start = (f32[256]{0:T(256)S(1)}, f32[256]{0:T(256)}, u32[]{:S(2)}) copy-start(f32[256]{0:T(256)} %param.22) | copy-start | bytes 3076
  19.1 11.3 %collective-permute-start.1 = (f32[3,16,2048]{2,1,0:T(8,128)S(1)}, f32[3,16,2048]{2,1,0:T(8,128)S(1)}, u32[]{:S(2)}, u32[]{:S(2)}) collective-permute-start(f32[3,16,2048]{2,1,0:T(8,128)S(1)} %get-tuple-element.49), channel_id=1, source_target_pairs={{0,2},{1,3},{2,0},{3,1},{4,6},{5,7},{6,4},{7,5},{8,10},{9,11},{10,... | collective-permute-start | bytes 1179656 | tf_op jit(solution)/shard_map/ppermute | solution.py:567
  24.4 11.3 %all-to-all-start.1 = ((f32[32,1,1280]{2,1,0:T(1,128)}), f32[32,1,1280]{2,1,0:T(1,128)S(1)}, u32[]{:S(2)}, u32[]{:S(2)}) async-start(f32[32,1,1280]{2,1,0:T(1,128)} %shard_map.141), calls=%async_computation.1 | async-start | bytes 327680 | tf_op jit(solution)/shard_map/all_to_all | solution.py:576
  30.4 9.4 %collective-permute-start.2 = (f32[21,1,2048]{2,1,0:T(1,128)S(1)}, f32[21,1,2048]{2,1,0:T(1,128)S(1)}, u32[]{:S(2)}, u32[]{:S(2)}) collective-permute-start(f32[21,1,2048]{2,1,0:T(1,128)S(1)} %shard_map.143), channel_id=1, source_target_pairs={{4,8},{12,16},{20,24},{8,4},{16,12},{24,20},{5,9},{13,17},{21,25},... | collective-permute-start | bytes 516104 | tf_op jit(solution)/shard_map/ppermute | solution.py:572
  38.9 4.2 %collective-permute-start.3 = (f32[3,1,2048]{2,1,0:T(1,128)S(1)}, f32[3,1,2048]{2,1,0:T(1,128)S(1)}, u32[]{:S(2)}, u32[]{:S(2)}) collective-permute-start(f32[3,1,2048]{2,1,0:T(1,128)S(1)} %get-tuple-element.58), channel_id=1, source_target_pairs={{0,4},{4,0},{8,12},{12,8},{16,20},{20,16},{24,28},{28,24},{1,5},{5... | collective-permute-start | bytes 73736 | tf_op jit(solution)/shard_map/ppermute | solution.py:567
  44.1 9.9 %collective-permute-start.4 = (f32[3,16,2048]{2,1,0:T(8,128)S(1)}, f32[3,16,2048]{2,1,0:T(8,128)S(1)}, u32[]{:S(2)}, u32[]{:S(2)}) collective-permute-start(f32[3,16,2048]{2,1,0:T(8,128)S(1)} %get-tuple-element.66), channel_id=1, source_target_pairs={{1,2},{2,1},{5,6},{6,5},{9,10},{10,9},{13,14},{14,13},{17,18},{18,... | collective-permute-start | bytes 1179656 | tf_op jit(solution)/shard_map/ppermute | solution.py:572
  44.8 9.2 %collective-permute-start.7 = (f32[3,16,2048]{2,1,0:T(8,128)S(1)}, f32[3,16,2048]{2,1,0:T(8,128)S(1)}, u32[]{:S(2)}, u32[]{:S(2)}) collective-permute-start(f32[3,16,2048]{2,1,0:T(8,128)S(1)} %get-tuple-element.69), channel_id=1, source_target_pairs={{0,1},{1,0},{2,3},{3,2},{4,5},{5,4},{6,7},{7,6},{8,9},{9,8},{10,11... | collective-permute-start | bytes 1179656 | tf_op jit(solution)/shard_map/ppermute | solution.py:567
  46.9 5.4 %collective-permute-start.5 = (f32[3,3,1,2048]{3,2,1,0:T(1,128)S(1)}, f32[3,3,1,2048]{3,2,1,0:T(1,128)S(1)}, u32[]{:S(2)}, u32[]{:S(2)}) collective-permute-start(f32[3,3,1,2048]{3,2,1,0:T(1,128)S(1)} %get-tuple-element.67), channel_id=1, source_target_pairs={{4,8},{12,16},{20,24},{8,4},{16,12},{24,20},{5,9},{13,17},{21,25},... | collective-permute-start | bytes 221192 | tf_op jit(solution)/shard_map/ppermute | solution.py:572
  47.6 6.5 %collective-permute-start.6 = (f32[3,3,1,2048]{3,2,1,0:T(1,128)S(1)}, f32[3,3,1,2048]{3,2,1,0:T(1,128)S(1)}, u32[]{:S(2)}, u32[]{:S(2)}) collective-permute-start(f32[3,3,1,2048]{3,2,1,0:T(1,128)S(1)} %get-tuple-element.68), channel_id=1, source_target_pairs={{0,4},{4,0},{8,12},{12,8},{16,20},{20,16},{24,28},{28,24},{1,5},{5... | collective-permute-start | bytes 221192 | tf_op jit(solution)/shard_map/ppermute | solution.py:567

commit v12 on v11

--- a/solution.py
+++ b/solution.py
@@ -38,13 +38,15 @@
             operands.append(to)
         else:
             operands.append(refs[i])
-    for copy in copies:
-        copy.start()
     places = [i for i, far in enumerate(where) if far]
     rest = [copy for i, copy in zip(places, copies) if i in late]
-    for i, copy in zip(places, copies):
-        if i not in late:
-            copy.wait()
+    early = [copy for i, copy in zip(places, copies) if i not in late]
+    for copy in early:
+        copy.start()
+    for copy in early:
+        copy.wait()
+    for copy in rest:
+        copy.start()
     more = (lambda: [copy.wait() for copy in rest],) if late else ()
     kernel(*more, *operands, *refs[count : count + outs], *extra)
 

time: 68 us -> 68.9 us (1.013)
  Pallas kernels: 21.9 us -> 22.7 us
    pallas_call x8, Pallas kernels: 13.8 us -> 14.6 us  [call(): pl.pallas_call(functools.partial(staged, kernel, where, len(outs), tuple(...]
  transfers between devices with their start and end apart: 10 -> 10, of which waited for: 4 -> 4; matrix products, arithmetic and copies ran while one was open for 0% -> 0% of each run, Pallas kernels for 22% -> 23%
where the time goes in v12:
time: 68.9 us; the launch traced here: 68.5 us
  Pallas kernels  22.7 us (33%)
  starting transfers between devices  19.1 us (28%)
  waiting for transfers between devices  15.1 us (22%)
  blocking collectives  10.8 us (16%)
  between operations  0.8 us (1%)
    pallas_call x8, Pallas kernels, call(): pl.pallas_call(functools.partial(staged, kernel, where, len(outs), tuple(...  14.6 us
    all_to_all x1, blocking collectives, everywhere(): return lax.all_to_all(x, BOTH, split_axis=0, concat_axis=0, tiled=True)  10.8 us
    all_to_all x2, waiting for transfers between devices, everywhere(): return lax.all_to_all(x, BOTH, split_axis=0, concat_axis=0, tiled=True)  10.1 us
    all_to_all x2, starting transfers between devices, everywhere(): return lax.all_to_all(x, BOTH, split_axis=0, concat_axis=0, tiled=True)  9.63 us
    ppermute x5, starting transfers between devices, flip(): lax.ppermute(x, axis, [(i, i ^ 1 << level) for i in range(lax.axis_size(a...  7.42 us
    ppermute x5, waiting for transfers between devices, flip(): lax.ppermute(x, axis, [(i, i ^ 1 << level) for i in range(lax.axis_size(a...  5.02 us
    pallas_call x1, Pallas kernels, shards(): pl.pallas_call(front_kernel, out_shape=vmem((devices, 1, rows + 2 * level...  5 us
    pallas_call x1, Pallas kernels, shards(): pl.pallas_call(pres_kernel, out_shape=(field, vmem((devices, 1, 3 * count...  3.13 us
  transfers between devices with their start and end apart: 10, of which 4 were waited for; matrix products, arithmetic and copies ran while one was open for 0% of the time, Pallas kernels for 23%

profile of v12, /device:TPU:0, one launch (start us, length us, event | category | flops | bytes accessed | tf_op | source)
XLA Modules:
  0.0 68.5 jit_solution(4862238517627582532)
XLA Ops:
  0.6 3.1 %shard_map.139 = (f32[3,16,2048]{2,1,0:T(8,128)S(1)}, f32[32,1,768]{2,1,0:T(1,128)}, f32[6,16,2048]{2,1,0:T(8,128)S(1)}) custom-call(s32[1,256]{1,0:T(1,128)} %bitcast.7, s32[1,256]{1,0:T(1,128)} %bitcast.9, f32[1,256]{1,0:T(1,128)} %bitcast.4, f32[3,3,16,2048]{3,2,1,0:T(8,128)} %refs_3_.3, f32[3,3,16,2048]{3,2,1,0:T(8,128)} %wts_in.1, ...), custom_call_target="tpu_custom_call" | custom-call | tf_op jit(solution)/shard_map/pallas_call | solution.py:597
  3.8 0.5 collective-permute-start
  4.3 7.0 %all-to-all-start = ((f32[32,1,768]{2,1,0:T(1,128)}), f32[32,1,768]{2,1,0:T(1,128)S(1)}, u32[]{:S(2)}, u32[]{:S(2)}) async-start(f32[32,1,768]{2,1,0:T(1,128)} %get-tuple-element.39), calls=%async_computation | async-start | bytes 196608 | tf_op jit(solution)/shard_map/all_to_all | solution.py:578
  11.3 0.0 collective-permute-done.refs_1_.refs_3_.refs_2_
  11.3 0.0 copy-start
  11.3 2.2 %shard_map.140 = (f32[12,1,2048]{2,1,0:T(1,128)S(1)}, f32[12,1,2048]{2,1,0:T(1,128)S(1)}, f32[1,768]{1,0:T(1,128)S(1)}, f32[3,16,2048]{2,1,0:T(8,128)S(1)}) custom-call(f32[6,16,2048]{2,1,0:T(8,128)S(1)} %get-tuple-element.40.refs_0_, f32[6,16,2048]{2,1,0:T(8,128)S(1)} %collective-permute-done.refs_1_.refs_3_.refs_2_, ...), custom_call_target="tpu_custom_call" | custom-call | tf_op jit(solution)/shard_map/pallas_call | solution.py:58
  13.5 0.0 copy-done
  13.6 5.5 %all-to-all-done.recv.refs_1_ = f32[32,1,768]{2,1,0:T(1,128)S(1)} async-done(((f32[32,1,768]{2,1,0:T(1,128)}), f32[32,1,768]{2,1,0:T(1,128)S(1)}, u32[]{:S(2)}, u32[]{:S(2)}) %all-to-all-start) | async-done | bytes 98336 | tf_op jit(solution)/shard_map/all_to_all | solution.py:578
  19.1 0.3 collective-permute-start.1
  19.4 5.0 %shard_map.141 = f32[32,1,1280]{2,1,0:T(1,128)} custom-call(f32[32,1,768]{2,1,0:T(1,128)S(1)} %all-to-all-done.recv.refs_1_, f32[1,1024]{1,0:T(1,128)S(1)} %pad_maximum_fusion.found, f32[256,8192]{1,0:T(8,128)} %inverse.1), custom_call_target="tpu_custom_call" | custom-call | tf_op jit(solution)/shard_map/pallas_call | solution.py:632
  24.4 2.7 %all-to-all-start.1 = ((f32[32,1,1280]{2,1,0:T(1,128)}), f32[32,1,1280]{2,1,0:T(1,128)S(1)}, u32[]{:S(2)}, u32[]{:S(2)}) async-start(f32[32,1,1280]{2,1,0:T(1,128)} %shard_map.141), calls=%async_computation.1 | async-start | bytes 327680 | tf_op jit(solution)/shard_map/all_to_all | solution.py:578
  27.1 3.3 %collective-permute-done.1.refs_4_.refs_3_ = f32[3,16,2048]{2,1,0:T(8,128)S(1)} collective-permute-done((f32[3,16,2048]{2,1,0:T(8,128)S(1)}, f32[3,16,2048]{2,1,0:T(8,128)S(1)}, u32[]{:S(2)}, u32[]{:S(2)}) %collective-permute-start.1) | collective-permute-done | bytes 393248 | tf_op jit(solution)/shard_map/ppermute | solution.py:569
  30.4 0.7 collective-permute-start.2
  31.1 4.6 %all-to-all-done.1.refs_0_ = f32[32,1,1280]{2,1,0:T(1,128)S(1)} async-done(((f32[32,1,1280]{2,1,0:T(1,128)}), f32[32,1,1280]{2,1,0:T(1,128)S(1)}, u32[]{:S(2)}, u32[]{:S(2)}) %all-to-all-start.1) | async-done | bytes 163872 | tf_op jit(solution)/shard_map/all_to_all | solution.py:578
  35.7 4.0 %shard_map.142 = (f32[3,16,2048]{2,1,0:T(8,128)S(1)}, f32[3,16,2048]{2,1,0:T(8,128)S(1)}, f32[3,1,2048]{2,1,0:T(1,128)S(1)}, f32[3,16,2048]{2,1,0:T(8,128)S(1)},...) custom-call(f32[32,1,1280]{2,1,0:T(1,128)S(1)} %all-to-all-done.1.refs_0_, ...), custom_call_target="tpu_custom_call" | custom-call | tf_op jit(solution)/shard_map/pallas_call | solution.py:58
  39.7 0.9 %collective-permute-start.3 = (f32[3,1,2048]{2,1,0:T(1,128)S(1)}, f32[3,1,2048]{2,1,0:T(1,128)S(1)}, u32[]{:S(2)}, u32[]{:S(2)}) collective-permute-start(f32[3,1,2048]{2,1,0:T(1,128)S(1)} %get-tuple-element.58), channel_id=1, source_target_pairs={{0,4},{4,0},{8,12},{12,8},{16,20},{20,16},{24,28},{28,24},{1,5},{5... | collective-permute-start | bytes 73736 | tf_op jit(solution)/shard_map/ppermute | solution.py:569
  40.7 0.0 collective-permute-done.2.refs_2_
  40.7 3.3 %shard_map.144 = (f32[3,1,2048]{2,1,0:T(1,128)S(1)}, f32[3,3,16,2048]{3,2,1,0:T(8,128)S(1)}, f32[3,3,3,16,2048]{4,3,2,1,0:T(8,128)S(1)}, f32[3,16,2048]{2,1,0:T(8,128)S(1)}) custom-call(f32[32,1,1280]{2,1,0:T(1,128)S(1)} %all-to-all-done.1.refs_0_, f32[32,1,768]{2,1,0:T(1,128)S(1)} %all-to-all-done.recv.refs_1_, ...), custom_call_target="tpu_custom_call" | custom-call | tf_op jit(solution)/shard_map/pallas_call | solution.py:58
  43.9 0.0 collective-permute-done.3.refs_3_
  43.9 0.9 %shard_map.145 = (f32[3,3,16,2048]{3,2,1,0:T(8,128)S(1)}, f32[3,16,2048]{2,1,0:T(8,128)S(1)}, f32[3,3,1,2048]{3,2,1,0:T(1,128)S(1)}, f32[3,3,1,2048]{3,2,1,0:T(1,128)S(1)}, f32[3,16,2048]{2,1,0:T(8,128)S(1)}) custom-call(f32[3,16,2048]{2,1,0:T(8,128)S(1)} %get-tuple-element.50.refs_0_, f32[3,16,2048]{2,1,0:T(8,128)S(1)} %get-tuple-element.51.refs_1_, ...), custom_call_target="tpu_custom_call" | custom-call | tf_op jit(solution)/shard_map/pallas_call | solution.py:58
  44.9 0.7 %collective-permute-start.4 = (f32[3,16,2048]{2,1,0:T(8,128)S(1)}, f32[3,16,2048]{2,1,0:T(8,128)S(1)}, u32[]{:S(2)}, u32[]{:S(2)}) collective-permute-start(f32[3,16,2048]{2,1,0:T(8,128)S(1)} %get-tuple-element.66), channel_id=1, source_target_pairs={{1,2},{2,1},{5,6},{6,5},{9,10},{10,9},{13,14},{14,13},{17,18},{18,... | collective-permute-start | bytes 1179656 | tf_op jit(solution)/shard_map/ppermute | solution.py:574
  45.6 2.1 %collective-permute-start.7 = (f32[3,16,2048]{2,1,0:T(8,128)S(1)}, f32[3,16,2048]{2,1,0:T(8,128)S(1)}, u32[]{:S(2)}, u32[]{:S(2)}) collective-permute-start(f32[3,16,2048]{2,1,0:T(8,128)S(1)} %get-tuple-element.69), channel_id=1, source_target_pairs={{0,1},{1,0},{2,3},{3,2},{4,5},{5,4},{6,7},{7,6},{8,9},{9,8},{10,11... | collective-permute-start | bytes 1179656 | tf_op jit(solution)/shard_map/ppermute | solution.py:569
  47.7 0.7 collective-permute-start.5
  48.4 3.5 %collective-permute-start.6 = (f32[3,3,1,2048]{3,2,1,0:T(1,128)S(1)}, f32[3,3,1,2048]{3,2,1,0:T(1,128)S(1)}, u32[]{:S(2)}, u32[]{:S(2)}) collective-permute-start(f32[3,3,1,2048]{3,2,1,0:T(1,128)S(1)} %get-tuple-element.68), channel_id=1, source_target_pairs={{0,4},{4,0},{8,12},{12,8},{16,20},{20,16},{24,28},{28,24},{1,5},{5... | collective-permute-start | bytes 221192 | tf_op jit(solution)/shard_map/ppermute | solution.py:569
  51.9 1.2 %shard_map.146.refs_0_ = f32[3,3,16,2048]{3,2,1,0:T(8,128)S(1)} custom-call(f32[3,3,16,2048]{3,2,1,0:T(8,128)S(1)} %get-tuple-element.65.refs_0_.refs_1_, f32[3,3,3,16,2048]{4,3,2,1,0:T(8,128)S(1)} %get-tuple-element.63.refs_8_.refs_1_, f32[3,16,2048]{2,1,0:T(8,128)S(1)} %get-tuple-element.61.refs_6_.refs_2_, ...), custom_call_target="tpu_custom_call" | custom-call | tf_op jit(solution)/shard_map/pallas_call | solution.py:58
  53.1 0.0 collective-permute-done.5.refs_2_
  53.1 1.7 %collective-permute-done.6.refs_3_ = f32[3,3,1,2048]{3,2,1,0:T(1,128)S(1)} collective-permute-done((f32[3,3,1,2048]{3,2,1,0:T(1,128)S(1)}, f32[3,3,1,2048]{3,2,1,0:T(1,128)S(1)}, u32[]{:S(2)}, u32[]{:S(2)}) %collective-permute-start.6) | collective-permute-done | bytes 73760 | tf_op jit(solution)/shard_map/ppermute | solution.py:569
  54.8 0.0 collective-permute-done.4.refs_1_
  54.8 0.0 collective-permute-done.7.refs_4_
  54.8 1.2 %shard_map.147 = (f32[3,3,16,2048]{3,2,1,0:T(8,128)S(1)}, f32[32,1,128]{2,1,0:T(1,128)S(1)}) custom-call(f32[3,3,16,2048]{3,2,1,0:T(8,128)S(1)} %shard_map.146.refs_0_, f32[3,16,2048]{2,1,0:T(8,128)S(1)} %collective-permute-done.4.refs_1_, f32[3,3,1,2048]{3,2,1,0:T(1,128)S(1)} %collective-permute-done.5.refs_2_, ...), custom_call_target="tpu_custom_call" | custom-call | tf_op jit(solution)/shard_map/pallas_call | solution.py:58
  56.0 10.8 %all_to_all.15.refs_0_ = f32[32,1,128]{2,1,0:T(1,128)S(1)} all-to-all(f32[32,1,128]{2,1,0:T(1,128)S(1)} %get-tuple-element.70), channel_id=1, replica_groups=mesh['tile'=8,'layer'=4] {'tile','layer'}, dimensions={0} | all-to-all | bytes 32768 | tf_op jit(solution)/shard_map/all_to_all | solution.py:578
  66.9 1.7 %shard_map.148 = (f32[3,3,16,2048]{3,2,1,0:T(8,128)}, f32[3,3,16,2048]{3,2,1,0:T(8,128)}, f32[1,1]{1,0:T(1,128)}) custom-call(f32[32,1,128]{2,1,0:T(1,128)S(1)} %all_to_all.15.refs_0_, f32[3,3,16,2048]{3,2,1,0:T(8,128)S(1)} %get-tuple-element.65.refs_0_.refs_1_, f32[3,3,16,2048]{3,2,1,0:T(8,128)S(1)} %get-tuple-element.71.refs_2_, ...), custom_call_target="tpu_custom_call" | custom-call | tf_op jit(solution)/shard_map/pallas_call | solution.py:58
  (2 shorter events, 0.1 us)
Async XLA Ops:
  3.8 7.5 %collective-permute-start = (f32[6,16,2048]{2,1,0:T(8,128)S(1)}, f32[6,16,2048]{2,1,0:T(8,128)S(1)}, u32[]{:S(2)}, u32[]{:S(2)}) collective-permute-start(f32[6,16,2048]{2,1,0:T(8,128)S(1)} %get-tuple-element.40.refs_0_), channel_id=1, source_target_pairs={{0,1},{1,0},{2,3},{3,2},{4,5},{5,4},{6,7},{7,6},{8,9},{9,8},{10,11... | collective-permute-start | bytes 2359304 | tf_op jit(solution)/shard_map/ppermute | solution.py:569
  4.3 14.8 %all-to-all-start = ((f32[32,1,768]{2,1,0:T(1,128)}), f32[32,1,768]{2,1,0:T(1,128)S(1)}, u32[]{:S(2)}, u32[]{:S(2)}) async-start(f32[32,1,768]{2,1,0:T(1,128)} %get-tuple-element.39), calls=%async_computation | async-start | bytes 196608 | tf_op jit(solution)/shard_map/all_to_all | solution.py:578
  11.3 2.3 %copy-start = (f32[256]{0:T(256)S(1)}, f32[256]{0:T(256)}, u32[]{:S(2)}) copy-start(f32[256]{0:T(256)} %param.22) | copy-start | bytes 3076
  19.1 11.3 %collective-permute-start.1 = (f32[3,16,2048]{2,1,0:T(8,128)S(1)}, f32[3,16,2048]{2,1,0:T(8,128)S(1)}, u32[]{:S(2)}, u32[]{:S(2)}) collective-permute-start(f32[3,16,2048]{2,1,0:T(8,128)S(1)} %get-tuple-element.49), channel_id=1, source_target_pairs={{0,2},{1,3},{2,0},{3,1},{4,6},{5,7},{6,4},{7,5},{8,10},{9,11},{10,... | collective-permute-start | bytes 1179656 | tf_op jit(solution)/shard_map/ppermute | solution.py:569
  24.4 11.3 %all-to-all-start.1 = ((f32[32,1,1280]{2,1,0:T(1,128)}), f32[32,1,1280]{2,1,0:T(1,128)S(1)}, u32[]{:S(2)}, u32[]{:S(2)}) async-start(f32[32,1,1280]{2,1,0:T(1,128)} %shard_map.141), calls=%async_computation.1 | async-start | bytes 327680 | tf_op jit(solution)/shard_map/all_to_all | solution.py:578
  30.4 10.2 %collective-permute-start.2 = (f32[21,1,2048]{2,1,0:T(1,128)S(1)}, f32[21,1,2048]{2,1,0:T(1,128)S(1)}, u32[]{:S(2)}, u32[]{:S(2)}) collective-permute-start(f32[21,1,2048]{2,1,0:T(1,128)S(1)} %shard_map.143), channel_id=1, source_target_pairs={{4,8},{12,16},{20,24},{8,4},{16,12},{24,20},{5,9},{13,17},{21,25},... | collective-permute-start | bytes 516104 | tf_op jit(solution)/shard_map/ppermute | solution.py:574
  39.7 4.2 %collective-permute-start.3 = (f32[3,1,2048]{2,1,0:T(1,128)S(1)}, f32[3,1,2048]{2,1,0:T(1,128)S(1)}, u32[]{:S(2)}, u32[]{:S(2)}) collective-permute-start(f32[3,1,2048]{2,1,0:T(1,128)S(1)} %get-tuple-element.58), channel_id=1, source_target_pairs={{0,4},{4,0},{8,12},{12,8},{16,20},{20,16},{24,28},{28,24},{1,5},{5... | collective-permute-start | bytes 73736 | tf_op jit(solution)/shard_map/ppermute | solution.py:569
  44.9 9.9 %collective-permute-start.4 = (f32[3,16,2048]{2,1,0:T(8,128)S(1)}, f32[3,16,2048]{2,1,0:T(8,128)S(1)}, u32[]{:S(2)}, u32[]{:S(2)}) collective-permute-start(f32[3,16,2048]{2,1,0:T(8,128)S(1)} %get-tuple-element.66), channel_id=1, source_target_pairs={{1,2},{2,1},{5,6},{6,5},{9,10},{10,9},{13,14},{14,13},{17,18},{18,... | collective-permute-start | bytes 1179656 | tf_op jit(solution)/shard_map/ppermute | solution.py:574
  45.6 9.2 %collective-permute-start.7 = (f32[3,16,2048]{2,1,0:T(8,128)S(1)}, f32[3,16,2048]{2,1,0:T(8,128)S(1)}, u32[]{:S(2)}, u32[]{:S(2)}) collective-permute-start(f32[3,16,2048]{2,1,0:T(8,128)S(1)} %get-tuple-element.69), channel_id=1, source_target_pairs={{0,1},{1,0},{2,3},{3,2},{4,5},{5,4},{6,7},{7,6},{8,9},{9,8},{10,11... | collective-permute-start | bytes 1179656 | tf_op jit(solution)/shard_map/ppermute | solution.py:569
  47.7 5.4 %collective-permute-start.5 = (f32[3,3,1,2048]{3,2,1,0:T(1,128)S(1)}, f32[3,3,1,2048]{3,2,1,0:T(1,128)S(1)}, u32[]{:S(2)}, u32[]{:S(2)}) collective-permute-start(f32[3,3,1,2048]{3,2,1,0:T(1,128)S(1)} %get-tuple-element.67), channel_id=1, source_target_pairs={{4,8},{12,16},{20,24},{8,4},{16,12},{24,20},{5,9},{13,17},{21,25},... | collective-permute-start | bytes 221192 | tf_op jit(solution)/shard_map/ppermute | solution.py:574
  48.4 6.5 %collective-permute-start.6 = (f32[3,3,1,2048]{3,2,1,0:T(1,128)S(1)}, f32[3,3,1,2048]{3,2,1,0:T(1,128)S(1)}, u32[]{:S(2)}, u32[]{:S(2)}) collective-permute-start(f32[3,3,1,2048]{3,2,1,0:T(1,128)S(1)} %get-tuple-element.68), channel_id=1, source_target_pairs={{0,4},{4,0},{8,12},{12,8},{16,20},{20,16},{24,28},{28,24},{1,5},{5... | collective-permute-start | bytes 221192 | tf_op jit(solution)/shard_map/ppermute | solution.py:569

commit v13 on v11

--- a/solution.py
+++ b/solution.py
@@ -38,14 +38,19 @@
             operands.append(to)
         else:
             operands.append(refs[i])
+    places = [i for i, far in enumerate(where) if far]
     for copy in copies:
         copy.start()
-    places = [i for i, far in enumerate(where) if far]
-    rest = [copy for i, copy in zip(places, copies) if i in late]
     for i, copy in zip(places, copies):
-        if i not in late:
+        if not any(i in group for group in late):
             copy.wait()
-    more = (lambda: [copy.wait() for copy in rest],) if late else ()
+
+    def ready(k):
+        for i, copy in zip(places, copies):
+            if i in late[k]:
+                copy.wait()
+
+    more = (ready,) if late else ()
     kernel(*more, *operands, *refs[count : count + outs], *extra)
 
 
@@ -342,10 +347,8 @@
             at += count
 
 
-def column_solve(levels, recv, lists, hots, tz, store, pres, sib):
+def column_solve(levels, recv, lists, hots, planes_of, sib):
     rows_hot, lanes_hot, sol_hot, sol_row, layer = hots
-    depth = len(tz)
-    high = tz[0].shape[0]
     rows, count = (sol_hot.shape[0], recv.shape[2])
     count = (count - rows) // (2 * levels)
     table = jnp.concatenate(split(recv[...].reshape(recv.shape[0], recv.shape[2])[:, :rows]), 0)
@@ -357,6 +360,9 @@
         at = rows + column * count
         return jnp.concatenate([recv[device][:, at : at + count] for device in group], 1)
 
+    tz, store, pres = planes_of()
+    depth = len(tz)
+    high = tz[0].shape[0]
     gs, invs, first, final, coefs = factors(tz, store)
     own = [coefs]
     start = layer.shape[1]
@@ -410,10 +416,13 @@
     odd = is_right(0, "tile")
     lists = groups_of(levels)
     table_kernel(lists, pres.shape, terms, hots)
+
+    def planes_of():
+        ready(0)
+        return tuple([ref[z] for z in range(depth)] for ref in (tz, store, pres))
+
+    values, above, below, tzp = column_solve(levels, recv, lists, hots, planes_of, sib)
     tzs = [tz[z] for z in range(depth)]
-    values, above, below, tzp = column_solve(
-        levels, recv, lists, hots, tzs, [store[z] for z in range(depth)], [pres[z] for z in range(depth)], sib
-    )
     is_last = lax.axis_index("layer") == (1 << levels) - 1
     for z in range(depth):
         p[z] = values[z]
@@ -423,7 +432,7 @@
             coupled_z[z] = total + jnp.where(is_last, 0.0, below + tzs[z] * values[z])
         else:
             coupled_z[z] = total + tzs[z] * values[z + 1]
-    ready()
+    ready(1)
 
 
 def edge_kernel(levels, low, high, *refs):
@@ -441,7 +450,7 @@
 
 def first_three(kernel, ready, one, two, three, _rhs, _diag, _ty, *rest):
     kernel(one, two, three, *rest)
-    ready()
+    ready(0)
 
 
 def beyond_kernel(levels, shapes, shape, recv, terms, two, row, planes, *hots):
@@ -461,16 +470,16 @@
     for size in shapes:
         blocks.append([planes[at + i] for i in range(size)])
         at += size
-    values, _, _, _ = column_solve(
-        levels,
-        recv,
-        lists,
-        hots,
-        [planes[z] for z in range(depth)],
-        [jnp.where(planes[depth + z] == 0.0, 1.0, planes[depth + z]) for z in range(depth)],
-        [planes[2 * depth + z] for z in range(depth)],
-        blocks,
-    )
+
+    def planes_of():
+        kept = [planes[depth + z] for z in range(depth)]
+        return (
+            [planes[z] for z in range(depth)],
+            [jnp.where(value == 0.0, 1.0, value) for value in kept],
+            [planes[2 * depth + z] for z in range(depth)],
+        )
+
+    values, _, _, _ = column_solve(levels, recv, lists, hots, planes_of, blocks)
     for z in range(depth):
         found = jnp.where(exists > 0.0, values[z][0:1], 0.0)
         row[z] = jnp.where(odd, found, found * two[3 * depth + z])
@@ -659,7 +668,7 @@
         (sol, terms, pres, *sib, tz, store, tx, block_inv),
         far=range(at, at + 4),
         keep=range(at, at + 4),
-        late=(at + 3,),
+        late=(range(at, at + 3), (at + 3,)),
         scratch=hots(width),
     )
     sol, one, terms = lax.optimization_barrier((sol, one, terms))
@@ -670,7 +679,7 @@
         (sol, terms, two, rhs, block_diag, ty),
         far=(3, 4, 5),
         keep=(3, 4, 5),
-        late=(3, 4, 5),
+        late=((3, 4, 5),),
         scratch=(vmem((4 * depth + sum(sizes), 8, long)), *hots(8)),
     )
     row9 = vmem((3, depth, 1, long))

time: 68 us -> 68 us (level)
  no operation moved by 1% of the time
where the time goes in v13:
time: 68 us; the launch traced here: 67.6 us
  Pallas kernels  21.8 us (32%)
  starting transfers between devices  19.1 us (28%)
  waiting for transfers between devices  15.1 us (22%)
  blocking collectives  10.8 us (16%)
  between operations  0.8 us (1%)
    pallas_call x8, Pallas kernels, call(): pl.pallas_call(functools.partial(staged, kernel, where, len(outs), tuple(...  13.7 us
    all_to_all x1, blocking collectives, everywhere(): return lax.all_to_all(x, BOTH, split_axis=0, concat_axis=0, tiled=True)  10.8 us
    all_to_all x2, waiting for transfers between devices, everywhere(): return lax.all_to_all(x, BOTH, split_axis=0, concat_axis=0, tiled=True)  10.1 us
    all_to_all x2, starting transfers between devices, everywhere(): return lax.all_to_all(x, BOTH, split_axis=0, concat_axis=0, tiled=True)  9.63 us
    ppermute x5, starting transfers between devices, flip(): lax.ppermute(x, axis, [(i, i ^ 1 << level) for i in range(lax.axis_size(a...  7.42 us
    ppermute x5, waiting for transfers between devices, flip(): lax.ppermute(x, axis, [(i, i ^ 1 << level) for i in range(lax.axis_size(a...  5.02 us
    pallas_call x1, Pallas kernels, shards(): pl.pallas_call(front_kernel, out_shape=vmem((devices, 1, rows + 2 * level...  5 us
    pallas_call x1, Pallas kernels, shards(): pl.pallas_call(pres_kernel, out_shape=(field, vmem((devices, 1, 3 * count...  3.13 us
  transfers between devices with their start and end apart: 10, of which 4 were waited for; matrix products, arithmetic and copies ran while one was open for 0% of the time, Pallas kernels for 22%

profile of v13, /device:TPU:0, one launch (start us, length us, event | category | flops | bytes accessed | tf_op | source)
XLA Modules:
  0.0 67.6 jit_solution(13928049421819242703)
XLA Ops:
  0.6 3.1 %shard_map.139 = (f32[3,16,2048]{2,1,0:T(8,128)S(1)}, f32[32,1,768]{2,1,0:T(1,128)}, f32[6,16,2048]{2,1,0:T(8,128)S(1)}) custom-call(s32[1,256]{1,0:T(1,128)} %bitcast.7, s32[1,256]{1,0:T(1,128)} %bitcast.9, f32[1,256]{1,0:T(1,128)} %bitcast.4, f32[3,3,16,2048]{3,2,1,0:T(8,128)} %refs_3_.3, f32[3,3,16,2048]{3,2,1,0:T(8,128)} %wts_in.1, ...), custom_call_target="tpu_custom_call" | custom-call | tf_op jit(solution)/shard_map/pallas_call | solution.py:604
  3.8 0.5 collective-permute-start
  4.3 7.0 %all-to-all-start = ((f32[32,1,768]{2,1,0:T(1,128)}), f32[32,1,768]{2,1,0:T(1,128)S(1)}, u32[]{:S(2)}, u32[]{:S(2)}) async-start(f32[32,1,768]{2,1,0:T(1,128)} %get-tuple-element.39), calls=%async_computation | async-start | bytes 196608 | tf_op jit(solution)/shard_map/all_to_all | solution.py:585
  11.3 0.0 collective-permute-done.refs_1_.refs_3_.refs_2_
  11.3 0.0 copy-start
  11.3 2.2 %shard_map.140 = (f32[12,1,2048]{2,1,0:T(1,128)S(1)}, f32[12,1,2048]{2,1,0:T(1,128)S(1)}, f32[1,768]{1,0:T(1,128)S(1)}, f32[3,16,2048]{2,1,0:T(8,128)S(1)}) custom-call(f32[6,16,2048]{2,1,0:T(8,128)S(1)} %get-tuple-element.40.refs_0_, f32[6,16,2048]{2,1,0:T(8,128)S(1)} %collective-permute-done.refs_1_.refs_3_.refs_2_, ...), custom_call_target="tpu_custom_call" | custom-call | tf_op jit(solution)/shard_map/pallas_call | solution.py:61
  13.5 0.0 copy-done
  13.6 5.5 %all-to-all-done.recv.refs_1_ = f32[32,1,768]{2,1,0:T(1,128)S(1)} async-done(((f32[32,1,768]{2,1,0:T(1,128)}), f32[32,1,768]{2,1,0:T(1,128)S(1)}, u32[]{:S(2)}, u32[]{:S(2)}) %all-to-all-start) | async-done | bytes 98336 | tf_op jit(solution)/shard_map/all_to_all | solution.py:585
  19.1 0.3 collective-permute-start.1
  19.4 5.0 %shard_map.141 = f32[32,1,1280]{2,1,0:T(1,128)} custom-call(f32[32,1,768]{2,1,0:T(1,128)S(1)} %all-to-all-done.recv.refs_1_, f32[1,1024]{1,0:T(1,128)S(1)} %pad_maximum_fusion.found, f32[256,8192]{1,0:T(8,128)} %inverse.1), custom_call_target="tpu_custom_call" | custom-call | tf_op jit(solution)/shard_map/pallas_call | solution.py:639
  24.4 2.7 %all-to-all-start.1 = ((f32[32,1,1280]{2,1,0:T(1,128)}), f32[32,1,1280]{2,1,0:T(1,128)S(1)}, u32[]{:S(2)}, u32[]{:S(2)}) async-start(f32[32,1,1280]{2,1,0:T(1,128)} %shard_map.141), calls=%async_computation.1 | async-start | bytes 327680 | tf_op jit(solution)/shard_map/all_to_all | solution.py:585
  27.1 3.3 %collective-permute-done.1.refs_4_.refs_3_ = f32[3,16,2048]{2,1,0:T(8,128)S(1)} collective-permute-done((f32[3,16,2048]{2,1,0:T(8,128)S(1)}, f32[3,16,2048]{2,1,0:T(8,128)S(1)}, u32[]{:S(2)}, u32[]{:S(2)}) %collective-permute-start.1) | collective-permute-done | bytes 393248 | tf_op jit(solution)/shard_map/ppermute | solution.py:576
  30.4 0.7 collective-permute-start.2
  31.1 4.6 %all-to-all-done.1.refs_0_ = f32[32,1,1280]{2,1,0:T(1,128)S(1)} async-done(((f32[32,1,1280]{2,1,0:T(1,128)}), f32[32,1,1280]{2,1,0:T(1,128)S(1)}, u32[]{:S(2)}, u32[]{:S(2)}) %all-to-all-start.1) | async-done | bytes 163872 | tf_op jit(solution)/shard_map/all_to_all | solution.py:585
  35.7 3.2 %shard_map.142 = (f32[3,16,2048]{2,1,0:T(8,128)S(1)}, f32[3,16,2048]{2,1,0:T(8,128)S(1)}, f32[3,1,2048]{2,1,0:T(1,128)S(1)}, f32[3,16,2048]{2,1,0:T(8,128)S(1)},...) custom-call(f32[32,1,1280]{2,1,0:T(1,128)S(1)} %all-to-all-done.1.refs_0_, ...), custom_call_target="tpu_custom_call" | custom-call | tf_op jit(solution)/shard_map/pallas_call | solution.py:61
  38.8 0.9 %collective-permute-start.3 = (f32[3,1,2048]{2,1,0:T(1,128)S(1)}, f32[3,1,2048]{2,1,0:T(1,128)S(1)}, u32[]{:S(2)}, u32[]{:S(2)}) collective-permute-start(f32[3,1,2048]{2,1,0:T(1,128)S(1)} %get-tuple-element.58), channel_id=1, source_target_pairs={{0,4},{4,0},{8,12},{12,8},{16,20},{20,16},{24,28},{28,24},{1,5},{5... | collective-permute-start | bytes 73736 | tf_op jit(solution)/shard_map/ppermute | solution.py:576
  39.8 0.0 collective-permute-done.2.refs_2_
  39.8 3.3 %shard_map.144 = (f32[3,1,2048]{2,1,0:T(1,128)S(1)}, f32[3,3,16,2048]{3,2,1,0:T(8,128)S(1)}, f32[3,3,3,16,2048]{4,3,2,1,0:T(8,128)S(1)}, f32[3,16,2048]{2,1,0:T(8,128)S(1)}) custom-call(f32[32,1,1280]{2,1,0:T(1,128)S(1)} %all-to-all-done.1.refs_0_, f32[32,1,768]{2,1,0:T(1,128)S(1)} %all-to-all-done.recv.refs_1_, ...), custom_call_target="tpu_custom_call" | custom-call | tf_op jit(solution)/shard_map/pallas_call | solution.py:61
  43.1 0.0 collective-permute-done.3.refs_3_
  43.1 0.9 %shard_map.145 = (f32[3,3,16,2048]{3,2,1,0:T(8,128)S(1)}, f32[3,16,2048]{2,1,0:T(8,128)S(1)}, f32[3,3,1,2048]{3,2,1,0:T(1,128)S(1)}, f32[3,3,1,2048]{3,2,1,0:T(1,128)S(1)}, f32[3,16,2048]{2,1,0:T(8,128)S(1)}) custom-call(f32[3,16,2048]{2,1,0:T(8,128)S(1)} %get-tuple-element.50.refs_0_, f32[3,16,2048]{2,1,0:T(8,128)S(1)} %get-tuple-element.51.refs_1_, ...), custom_call_target="tpu_custom_call" | custom-call | tf_op jit(solution)/shard_map/pallas_call | solution.py:61
  44.0 0.7 %collective-permute-start.4 = (f32[3,16,2048]{2,1,0:T(8,128)S(1)}, f32[3,16,2048]{2,1,0:T(8,128)S(1)}, u32[]{:S(2)}, u32[]{:S(2)}) collective-permute-start(f32[3,16,2048]{2,1,0:T(8,128)S(1)} %get-tuple-element.66), channel_id=1, source_target_pairs={{1,2},{2,1},{5,6},{6,5},{9,10},{10,9},{13,14},{14,13},{17,18},{18,... | collective-permute-start | bytes 1179656 | tf_op jit(solution)/shard_map/ppermute | solution.py:581
  44.7 2.1 %collective-permute-start.7 = (f32[3,16,2048]{2,1,0:T(8,128)S(1)}, f32[3,16,2048]{2,1,0:T(8,128)S(1)}, u32[]{:S(2)}, u32[]{:S(2)}) collective-permute-start(f32[3,16,2048]{2,1,0:T(8,128)S(1)} %get-tuple-element.69), channel_id=1, source_target_pairs={{0,1},{1,0},{2,3},{3,2},{4,5},{5,4},{6,7},{7,6},{8,9},{9,8},{10,11... | collective-permute-start | bytes 1179656 | tf_op jit(solution)/shard_map/ppermute | solution.py:576
  46.8 0.7 collective-permute-start.5
  47.5 3.5 %collective-permute-start.6 = (f32[3,3,1,2048]{3,2,1,0:T(1,128)S(1)}, f32[3,3,1,2048]{3,2,1,0:T(1,128)S(1)}, u32[]{:S(2)}, u32[]{:S(2)}) collective-permute-start(f32[3,3,1,2048]{3,2,1,0:T(1,128)S(1)} %get-tuple-element.68), channel_id=1, source_target_pairs={{0,4},{4,0},{8,12},{12,8},{16,20},{20,16},{24,28},{28,24},{1,5},{5... | collective-permute-start | bytes 221192 | tf_op jit(solution)/shard_map/ppermute | solution.py:576
  51.0 1.2 %shard_map.146.refs_0_ = f32[3,3,16,2048]{3,2,1,0:T(8,128)S(1)} custom-call(f32[3,3,16,2048]{3,2,1,0:T(8,128)S(1)} %get-tuple-element.65.refs_0_.refs_1_, f32[3,3,3,16,2048]{4,3,2,1,0:T(8,128)S(1)} %get-tuple-element.63.refs_8_.refs_1_, f32[3,16,2048]{2,1,0:T(8,128)S(1)} %get-tuple-element.61.refs_6_.refs_2_, ...), custom_call_target="tpu_custom_call" | custom-call | tf_op jit(solution)/shard_map/pallas_call | solution.py:61
  52.2 0.0 collective-permute-done.5.refs_2_
  52.2 1.7 %collective-permute-done.6.refs_3_ = f32[3,3,1,2048]{3,2,1,0:T(1,128)S(1)} collective-permute-done((f32[3,3,1,2048]{3,2,1,0:T(1,128)S(1)}, f32[3,3,1,2048]{3,2,1,0:T(1,128)S(1)}, u32[]{:S(2)}, u32[]{:S(2)}) %collective-permute-start.6) | collective-permute-done | bytes 73760 | tf_op jit(solution)/shard_map/ppermute | solution.py:576
  53.9 0.0 collective-permute-done.4.refs_1_
  53.9 0.0 collective-permute-done.7.refs_4_
  53.9 1.2 %shard_map.147 = (f32[3,3,16,2048]{3,2,1,0:T(8,128)S(1)}, f32[32,1,128]{2,1,0:T(1,128)S(1)}) custom-call(f32[3,3,16,2048]{3,2,1,0:T(8,128)S(1)} %shard_map.146.refs_0_, f32[3,16,2048]{2,1,0:T(8,128)S(1)} %collective-permute-done.4.refs_1_, f32[3,3,1,2048]{3,2,1,0:T(1,128)S(1)} %collective-permute-done.5.refs_2_, ...), custom_call_target="tpu_custom_call" | custom-call | tf_op jit(solution)/shard_map/pallas_call | solution.py:61
  55.1 10.8 %all_to_all.15.refs_0_ = f32[32,1,128]{2,1,0:T(1,128)S(1)} all-to-all(f32[32,1,128]{2,1,0:T(1,128)S(1)} %get-tuple-element.70), channel_id=1, replica_groups=mesh['tile'=8,'layer'=4] {'tile','layer'}, dimensions={0} | all-to-all | bytes 32768 | tf_op jit(solution)/shard_map/all_to_all | solution.py:585
  66.0 1.7 %shard_map.148 = (f32[3,3,16,2048]{3,2,1,0:T(8,128)}, f32[3,3,16,2048]{3,2,1,0:T(8,128)}, f32[1,1]{1,0:T(1,128)}) custom-call(f32[32,1,128]{2,1,0:T(1,128)S(1)} %all_to_all.15.refs_0_, f32[3,3,16,2048]{3,2,1,0:T(8,128)S(1)} %get-tuple-element.65.refs_0_.refs_1_, f32[3,3,16,2048]{3,2,1,0:T(8,128)S(1)} %get-tuple-element.71.refs_2_, ...), custom_call_target="tpu_custom_call" | custom-call | tf_op jit(solution)/shard_map/pallas_call | solution.py:61
  (2 shorter events, 0.1 us)
Async XLA Ops:
  3.8 7.5 %collective-permute-start = (f32[6,16,2048]{2,1,0:T(8,128)S(1)}, f32[6,16,2048]{2,1,0:T(8,128)S(1)}, u32[]{:S(2)}, u32[]{:S(2)}) collective-permute-start(f32[6,16,2048]{2,1,0:T(8,128)S(1)} %get-tuple-element.40.refs_0_), channel_id=1, source_target_pairs={{0,1},{1,0},{2,3},{3,2},{4,5},{5,4},{6,7},{7,6},{8,9},{9,8},{10,11... | collective-permute-start | bytes 2359304 | tf_op jit(solution)/shard_map/ppermute | solution.py:576
  4.3 14.8 %all-to-all-start = ((f32[32,1,768]{2,1,0:T(1,128)}), f32[32,1,768]{2,1,0:T(1,128)S(1)}, u32[]{:S(2)}, u32[]{:S(2)}) async-start(f32[32,1,768]{2,1,0:T(1,128)} %get-tuple-element.39), calls=%async_computation | async-start | bytes 196608 | tf_op jit(solution)/shard_map/all_to_all | solution.py:585
  11.3 2.3 %copy-start = (f32[256]{0:T(256)S(1)}, f32[256]{0:T(256)}, u32[]{:S(2)}) copy-start(f32[256]{0:T(256)} %param.22) | copy-start | bytes 3076
  19.1 11.3 %collective-permute-start.1 = (f32[3,16,2048]{2,1,0:T(8,128)S(1)}, f32[3,16,2048]{2,1,0:T(8,128)S(1)}, u32[]{:S(2)}, u32[]{:S(2)}) collective-permute-start(f32[3,16,2048]{2,1,0:T(8,128)S(1)} %get-tuple-element.49), channel_id=1, source_target_pairs={{0,2},{1,3},{2,0},{3,1},{4,6},{5,7},{6,4},{7,5},{8,10},{9,11},{10,... | collective-permute-start | bytes 1179656 | tf_op jit(solution)/shard_map/ppermute | solution.py:576
  24.4 11.3 %all-to-all-start.1 = ((f32[32,1,1280]{2,1,0:T(1,128)}), f32[32,1,1280]{2,1,0:T(1,128)S(1)}, u32[]{:S(2)}, u32[]{:S(2)}) async-start(f32[32,1,1280]{2,1,0:T(1,128)} %shard_map.141), calls=%async_computation.1 | async-start | bytes 327680 | tf_op jit(solution)/shard_map/all_to_all | solution.py:585
  30.4 9.3 %collective-permute-start.2 = (f32[21,1,2048]{2,1,0:T(1,128)S(1)}, f32[21,1,2048]{2,1,0:T(1,128)S(1)}, u32[]{:S(2)}, u32[]{:S(2)}) collective-permute-start(f32[21,1,2048]{2,1,0:T(1,128)S(1)} %shard_map.143), channel_id=1, source_target_pairs={{4,8},{12,16},{20,24},{8,4},{16,12},{24,20},{5,9},{13,17},{21,25},... | collective-permute-start | bytes 516104 | tf_op jit(solution)/shard_map/ppermute | solution.py:581
  38.8 4.2 %collective-permute-start.3 = (f32[3,1,2048]{2,1,0:T(1,128)S(1)}, f32[3,1,2048]{2,1,0:T(1,128)S(1)}, u32[]{:S(2)}, u32[]{:S(2)}) collective-permute-start(f32[3,1,2048]{2,1,0:T(1,128)S(1)} %get-tuple-element.58), channel_id=1, source_target_pairs={{0,4},{4,0},{8,12},{12,8},{16,20},{20,16},{24,28},{28,24},{1,5},{5... | collective-permute-start | bytes 73736 | tf_op jit(solution)/shard_map/ppermute | solution.py:576
  44.0 9.9 %collective-permute-start.4 = (f32[3,16,2048]{2,1,0:T(8,128)S(1)}, f32[3,16,2048]{2,1,0:T(8,128)S(1)}, u32[]{:S(2)}, u32[]{:S(2)}) collective-permute-start(f32[3,16,2048]{2,1,0:T(8,128)S(1)} %get-tuple-element.66), channel_id=1, source_target_pairs={{1,2},{2,1},{5,6},{6,5},{9,10},{10,9},{13,14},{14,13},{17,18},{18,... | collective-permute-start | bytes 1179656 | tf_op jit(solution)/shard_map/ppermute | solution.py:581
  44.7 9.2 %collective-permute-start.7 = (f32[3,16,2048]{2,1,0:T(8,128)S(1)}, f32[3,16,2048]{2,1,0:T(8,128)S(1)}, u32[]{:S(2)}, u32[]{:S(2)}) collective-permute-start(f32[3,16,2048]{2,1,0:T(8,128)S(1)} %get-tuple-element.69), channel_id=1, source_target_pairs={{0,1},{1,0},{2,3},{3,2},{4,5},{5,4},{6,7},{7,6},{8,9},{9,8},{10,11... | collective-permute-start | bytes 1179656 | tf_op jit(solution)/shard_map/ppermute | solution.py:576
  46.8 5.4 %collective-permute-start.5 = (f32[3,3,1,2048]{3,2,1,0:T(1,128)S(1)}, f32[3,3,1,2048]{3,2,1,0:T(1,128)S(1)}, u32[]{:S(2)}, u32[]{:S(2)}) collective-permute-start(f32[3,3,1,2048]{3,2,1,0:T(1,128)S(1)} %get-tuple-element.67), channel_id=1, source_target_pairs={{4,8},{12,16},{20,24},{8,4},{16,12},{24,20},{5,9},{13,17},{21,25},... | collective-permute-start | bytes 221192 | tf_op jit(solution)/shard_map/ppermute | solution.py:581
  47.5 6.5 %collective-permute-start.6 = (f32[3,3,1,2048]{3,2,1,0:T(1,128)S(1)}, f32[3,3,1,2048]{3,2,1,0:T(1,128)S(1)}, u32[]{:S(2)}, u32[]{:S(2)}) collective-permute-start(f32[3,3,1,2048]{3,2,1,0:T(1,128)S(1)} %get-tuple-element.68), channel_id=1, source_target_pairs={{0,4},{4,0},{8,12},{12,8},{16,20},{20,16},{24,28},{28,24},{1,5},{5... | collective-permute-start | bytes 221192 | tf_op jit(solution)/shard_map/ppermute | solution.py:576

commit v14 on v13

--- a/solution.py
+++ b/solution.py
@@ -129,14 +129,17 @@
         copy.wait()
     for z in range(depth):
         pres[z] = wts[0, z] * rhs[0, z] + wts[1, z] * rhs[1, z] + wts[2, z] * rhs[2, z]
-    (found,) = pick([pres[...].reshape(depth * width, long)], lax.div(where, long), hot)
+    tzs = [tz[z] for z in range(depth)]
+    gs, invs, first, final, coefs = factors(tzs, [store[z] for z in range(depth)])
+    tables = [pres[...].reshape(depth * width, long), jnp.concatenate(first, 0), jnp.concatenate(final, 0)]
+    found, kf, kl = pick(tables, lax.div(where, long), hot)
     both = jnp.concatenate([prod[...] * found, front[...].astype(F32), where.astype(F32)], 1)
     send[...] = jnp.broadcast_to(both[:, None], send.shape)
-    tzs = [tz[z] for z in range(depth)]
-    gs, invs, _, _, coefs = factors(tzs, [store[z] for z in range(depth)])
     y = local_solve([pres[z] for z in range(depth)], gs, invs, tzs)
     for i, value in enumerate((*coefs, y[0], y[-1], tzs[-1])):
         ends[i] = value
+    ends[6] = jnp.zeros((width, long), F32)
+    ends[6, 0:1, : 2 * where.shape[1]] = jnp.concatenate([prod[...] * kf, prod[...] * kl], 1)
 
 
 def is_right(level, axis="layer"):
@@ -174,7 +177,11 @@
     for z in range(depth - 2, -1, -1):
         first[z] = first[z] + gs[z] * first[z + 1]
         final[z] = gs[z] * final[z + 1]
-    return gs, invs, first, final, (first[0], first[-1], final[-1] + 1.0 / jnp.maximum(tz[-1], 1e-30))
+    return gs, invs, first, final, block_ends(first, final, tz)
+
+
+def block_ends(first, final, tz):
+    return (first[0], first[-1], final[-1] + 1.0 / jnp.maximum(tz[-1], 1e-30))
 
 
 def pair(level, own, sib):
@@ -197,13 +204,15 @@
     return (yf - c * flux, yl_ + c_ * flux)
 
 
-def first_join_kernel(final, own, sib, pres, tz, store, tx, cell, prod, low, high, *outs):
+def first_join_kernel(final, own, sib, pres, tz, store, tx, cell, prod, kept, low, high, *outs):
     depth, width, _ = tz.shape
     for k, ref in enumerate((tz, store, pres, tx)):
         for z in range(depth):
             low[k * depth + z] = ref[z, 0:1]
             high[k * depth + z] = ref[z, width - 1 : width]
-    _, _, first, last, _ = factors([tz[z] for z in range(depth)], [store[z] for z in range(depth)])
+    gs, invs, first, last, _ = factors([tz[z] for z in range(depth)], [store[z] for z in range(depth)])
+    for i, value in enumerate(gs + invs + first + last):
+        kept[i] = value
     join(0, final, own, sib, first + last, cell, prod, *outs)
 
 
@@ -225,7 +234,7 @@
         kf, kl = (answers[z], answers[depth + z])
         tops.append(jnp.where(right, cg * kf, kf - cg * kl))
         bottoms.append(jnp.where(right, kl - cg_ * kf, cg_ * kl))
-    tables = [answers[:depth], answers[depth:]]
+    tables = [answers[:depth], answers[depth:]] if level else []
     if final:
         (face,) = outs
         face[0], face[1] = (jnp.where(later, first, last), jnp.where(later, yf, yl))
@@ -237,11 +246,13 @@
             out[i] = value
         for i, value in enumerate(tops + bottoms):
             more[i] = value
-    where = cell[...]
-    hot = onehot(lax.rem(where, long), long).astype(BF16)
-    stack = [jnp.concatenate(t, 0) for t in tables]
-    got = pick(stack, lax.div(where, long), hot)
-    found[...] = jnp.concatenate([prod[...] * value for value in got], 1)
+    if tables:
+        where = cell[...]
+        hot = onehot(lax.rem(where, long), long).astype(BF16)
+        got = pick([jnp.concatenate(t, 0) for t in tables], lax.div(where, long), hot)
+        found[...] = jnp.concatenate([prod[...] * value for value in got], 1)
+    else:
+        found[...] = jnp.zeros(found.shape, F32)
 
 
 def groups_of(levels):
@@ -287,7 +298,9 @@
             acc = acc + held[:, r * lanes : (r + 1) * lanes] * total[r : r + 1]
     parts = jnp.concatenate(split(acc), 1)
     out = dot_nt(jnp.ones((8, parts.shape[1]), BF16), parts)
-    send[...] = jnp.broadcast_to(jnp.concatenate([out[0:1], found], 1)[:, None], send.shape)
+    pad = send.shape[2] - out.shape[1] - found.shape[1]
+    pieces = [out[0:1], found] + ([jnp.zeros((1, pad), F32)] if pad else [])
+    send[...] = jnp.broadcast_to(jnp.concatenate(pieces, 1)[:, None], send.shape)
 
 
 def gathered(values, rows_hot, lanes_hot, start, size, ext, parts):
@@ -347,10 +360,9 @@
             at += count
 
 
-def column_solve(levels, recv, lists, hots, planes_of, sib):
+def column_solve(levels, recv, lists, hots, listing, planes_of, sib):
     rows_hot, lanes_hot, sol_hot, sol_row, layer = hots
-    rows, count = (sol_hot.shape[0], recv.shape[2])
-    count = (count - rows) // (2 * levels)
+    rows, count = (sol_hot.shape[0], layer.shape[1])
     table = jnp.concatenate(split(recv[...].reshape(recv.shape[0], recv.shape[2])[:, :rows]), 0)
     sol = fold(dot(table, sol_hot[...]))
     sol = jnp.sum(jnp.where(iota(sol.shape, 0) == sol_row[...], sol, 0.0), axis=0, keepdims=True)
@@ -360,13 +372,13 @@
         at = rows + column * count
         return jnp.concatenate([recv[device][:, at : at + count] for device in group], 1)
 
-    tz, store, pres = planes_of()
+    mine_list, sib_list = listing
+    tz, pres, (gs, invs, first, final, coefs) = planes_of()
     depth = len(tz)
     high = tz[0].shape[0]
-    gs, invs, first, final, coefs = factors(tz, store)
     own = [coefs]
     start = layer.shape[1]
-    value = listed(lists[0], 0) * sol[:, :start]
+    value = mine_list * sol[:, :start]
     values = [jnp.where(layer == z, value, 0.0) for z in range(depth)]
     change = gathered(values, rows_hot, lanes_hot, 0, start, high, PARTS)
     y = local_solve([pres[z] - change[z] for z in range(depth)], gs, invs, tz)
@@ -375,8 +387,12 @@
     for level in range(levels):
         size = len(lists[level + 1]) * count
         top = level == levels - 1
-        columns = [1 + 2 * level] if top else [1 + 2 * level, 2 + 2 * level]
-        values = [listed(lists[level + 1], c) * sol[:, start : start + size] for c in columns]
+        if level:
+            columns = [2 * level - 2] if top else [2 * level - 2, 2 * level - 1]
+            values = [listed(lists[level + 1], c) for c in columns]
+        else:
+            values = [sib_list[:, i * count : (i + 1) * count] for i in range(2)]
+        values = [value * sol[:, start : start + size] for value in values]
         change = gathered(values, rows_hot, lanes_hot, start, size, high, PARTS)
         start += size
         if top:
@@ -411,17 +427,20 @@
 
 
 def pressure_kernel(levels, ready, recv, terms, pres, *refs):
-    sib, (tz, store, tx, _, p, coupled_z, one, *hots) = (refs[:levels], refs[levels:])
+    sib, (tz, kept, tx, prod, _, p, coupled_z, one, *hots) = (refs[:levels], refs[levels:])
     depth, width, _ = pres.shape
     odd = is_right(0, "tile")
     lists = groups_of(levels)
     table_kernel(lists, pres.shape, terms, hots)
 
     def planes_of():
-        ready(0)
-        return tuple([ref[z] for z in range(depth)] for ref in (tz, store, pres))
-
-    values, above, below, tzp = column_solve(levels, recv, lists, hots, planes_of, sib)
+        tzs, pressures = ([ref[z] for z in range(depth)] for ref in (tz, pres))
+        gs, invs, first, final = ([kept[k * depth + z] for z in range(depth)] for k in range(4))
+        return tzs, pressures, (gs, invs, first, final, block_ends(first, final, tzs))
+
+    ready(0)
+    listing = (prod[...], sib[0][6, 0:1])
+    values, above, below, tzp = column_solve(levels, recv, lists, hots, listing, planes_of, sib)
     tzs = [tz[z] for z in range(depth)]
     is_last = lax.axis_index("layer") == (1 << levels) - 1
     for z in range(depth):
@@ -435,7 +454,7 @@
     ready(1)
 
 
-def edge_kernel(levels, low, high, *refs):
+def edge_kernel(levels, low, high, prod, *refs):
     sib, two = (refs[:levels], refs[levels])
     odd = is_right(0, "tile")
     n = low.shape[0]
@@ -443,9 +462,12 @@
     at = n
     for block in sib:
         width = block.shape[1]
-        for i in range(block.shape[0]):
+        for i in range(min(6, block.shape[0])):
             two[at] = jnp.where(odd, block[i, width - 1 : width], block[i, 0:1])
             at += 1
+    two[at] = sib[0][6, 0:1]
+    two[at + 1] = jnp.zeros((1, two.shape[2]), F32)
+    two[at + 1, :, : prod.shape[1]] = prod[...]
 
 
 def first_three(kernel, ready, one, two, three, _rhs, _diag, _ty, *rest):
@@ -459,7 +481,8 @@
     tile = lax.axis_index("tile")
     odd = is_right(0, "tile")
     planes[...] = jnp.zeros(planes.shape, F32)
-    for i in range(planes.shape[0]):
+    count = planes.shape[0]
+    for i in range(count):
         planes[i, 0:1] = two[i]
     step = jnp.where(odd, layers, -layers)
     lists = [[jnp.clip(device + step, 0, tiles * layers - 1) for device in members] for members in groups_of(levels)]
@@ -473,13 +496,12 @@
 
     def planes_of():
         kept = [planes[depth + z] for z in range(depth)]
-        return (
-            [planes[z] for z in range(depth)],
-            [jnp.where(value == 0.0, 1.0, value) for value in kept],
-            [planes[2 * depth + z] for z in range(depth)],
-        )
-
-    values, _, _, _ = column_solve(levels, recv, lists, hots, planes_of, blocks)
+        tzs = [planes[z] for z in range(depth)]
+        found = factors(tzs, [jnp.where(value == 0.0, 1.0, value) for value in kept])
+        return tzs, [planes[2 * depth + z] for z in range(depth)], found
+
+    listing = (two[count + 1, :, : terms.shape[2] // 3], two[count])
+    values, _, _, _ = column_solve(levels, recv, lists, hots, listing, planes_of, blocks)
     for z in range(depth):
         found = jnp.where(exists > 0.0, values[z][0:1], 0.0)
         row[z] = jnp.where(odd, found, found * two[3 * depth + z])
@@ -603,23 +625,24 @@
     given = (cell, front, prod, rhs, weights, tz, store)
     pres, send, ends = pl.pallas_call(
         pres_kernel,
-        out_shape=(field, vmem((devices, 1, 3 * count)), planes(6)),
+        out_shape=(field, vmem((devices, 1, 3 * count)), planes(7)),
         in_specs=[hbm_spec] * len(given),
         out_specs=(VM,) * 3,
         scratch_shapes=[vmem(a.shape, a.dtype) for a in given] + [pltpu.SemaphoreType.DMA((len(given),))],
         compiler_params=pltpu.CompilerParams(vmem_limit_bytes=LIMIT),
     )(*[pltpu.with_memory_space_constraint(a, pltpu.HBM) for a in given])
     terms = everywhere(send)
-    sib, found = ([], [prod])
+    sib, found = ([], [])
     for level in range(levels - 1):
         sib.append(flip(ends, level))
         final = level == levels - 2
-        outs = (vmem((1, (3 if final else 2) * count)), *((planes(3),) if final else (planes(6), planes(2 * depth))))
+        many = (2 if level else 0) + (1 if final else 0)
+        outs = (vmem((1, max(1, many) * count)), *((planes(3),) if final else (planes(6), planes(2 * depth))))
         if level == 0:
             rim = vmem((4 * depth, 1, long))
-            low, high, *got = call(
+            kept, low, high, *got = call(
                 functools.partial(first_join_kernel, final),
-                (rim, rim, *outs),
+                (hbm((4 * depth, width, long)), rim, rim, *outs),
                 (ends, sib[-1], pres, tz, store, tx, cell, prod),
                 far=range(3, 8),
             )
@@ -627,27 +650,28 @@
             got = call(
                 functools.partial(join_kernel, level, final), outs, (ends, sib[-1], answers, cell, prod), far=(3, 4)
             )
-        found.append(got[0])
+        if many:
+            found.append(got[0])
         if final:
             face = got[1]
         else:
             ends, answers = got[1:]
-    found = jnp.concatenate(found, 1)
+    found = found[0] if len(found) == 1 else jnp.concatenate(found, 1)
     terms, face, found = lax.optimization_barrier((terms, face, found))
     sib.append(flip(face, levels - 1))
     chunks = 8
     send = pl.pallas_call(
         front_kernel,
-        out_shape=vmem((devices, 1, rows + 2 * levels * count)),
+        out_shape=vmem((devices, 1, max(rows + found.shape[1], 3 * count))),
         in_specs=[VM, VM, hbm_spec],
         out_specs=VM,
         scratch_shapes=[vmem(inverse.shape), pltpu.SemaphoreType.DMA((chunks,))],
         compiler_params=pltpu.CompilerParams(vmem_limit_bytes=LIMIT),
     )(terms, found, pltpu.with_memory_space_constraint(inverse, pltpu.HBM))
-    sizes = [block.shape[0] for block in sib]
-    rim = vmem((4 * depth + sum(sizes), 1, long))
+    sizes = [min(6, block.shape[0]) for block in sib]
+    rim = vmem((4 * depth + sum(sizes) + 2, 1, long))
     send, low, high = lax.optimization_barrier((send, low, high))
-    (two,) = call(functools.partial(edge_kernel, levels), (rim,), (low, high, *sib))
+    (two,) = call(functools.partial(edge_kernel, levels), (rim,), (low, high, prod, *sib))
     sol = everywhere(send)
     two = neighbour(two, "tile")
 
@@ -662,13 +686,13 @@
 
     at = 3 + levels
     row3 = vmem((depth, 1, long))
-    p, coupled_z, one, tz, _, tx, block_inv = call(
+    p, coupled_z, one, tz, tx, block_inv = call(
         functools.partial(pressure_kernel, levels),
         (field, field, row3),
-        (sol, terms, pres, *sib, tz, store, tx, block_inv),
-        far=range(at, at + 4),
-        keep=range(at, at + 4),
-        late=(range(at, at + 3), (at + 3,)),
+        (sol, terms, pres, *sib, tz, kept, tx, prod, block_inv),
+        far=range(at, at + 5),
+        keep=(at, at + 2, at + 4),
+        late=(range(at, at + 4), (at + 4,)),
         scratch=hots(width),
     )
     sol, one, terms = lax.optimization_barrier((sol, one, terms))

time: 68 us -> 67.3 us (0.990)
  waiting for transfers between devices: 15.1 us -> 13 us
  local copies, waits for them, and re-layouts: 0.01 us -> 1.17 us
  blocking collectives: 10.8 us -> 11.5 us
    all_to_all x2, waiting for transfers between devices: 10.1 us -> 8.32 us  [everywhere(): return lax.all_to_all(x, BOTH, split_axis=0, concat_axis=0, tiled=True)]
    unnamed x2 -> x4, local copies, waits for them, and re-layouts: 0.01 us -> 1.17 us
where the time goes in v14:
time: 67.3 us; the launch traced here: 67 us
  Pallas kernels  21.4 us (32%)
  starting transfers between devices  19.1 us (28%)
  waiting for transfers between devices  13 us (19%)
  blocking collectives  11.5 us (17%)
  local copies, waits for them, and re-layouts  1.17 us (2%)
  between operations  0.78 us (1%)
    pallas_call x8, Pallas kernels, call(): pl.pallas_call(functools.partial(staged, kernel, where, len(outs), tuple(...  13.2 us
    all_to_all x1, blocking collectives, everywhere(): return lax.all_to_all(x, BOTH, split_axis=0, concat_axis=0, tiled=True)  11.5 us
    all_to_all x2, starting transfers between devices, everywhere(): return lax.all_to_all(x, BOTH, split_axis=0, concat_axis=0, tiled=True)  9.63 us
    all_to_all x2, waiting for transfers between devices, everywhere(): return lax.all_to_all(x, BOTH, split_axis=0, concat_axis=0, tiled=True)  8.32 us
    ppermute x5, starting transfers between devices, flip(): lax.ppermute(x, axis, [(i, i ^ 1 << level) for i in range(lax.axis_size(a...  7.45 us
    pallas_call x1, Pallas kernels, shards(): pl.pallas_call(front_kernel, out_shape=vmem((devices, 1, max(rows + found...  4.97 us
    ppermute x5, waiting for transfers between devices, flip(): lax.ppermute(x, axis, [(i, i ^ 1 << level) for i in range(lax.axis_size(a...  4.72 us
    pallas_call x1, Pallas kernels, shards(): pl.pallas_call(pres_kernel, out_shape=(field, vmem((devices, 1, 3 * count...  3.25 us
  transfers between devices with their start and end apart: 10, of which 4 were waited for; matrix products, arithmetic and copies ran while one was open for 0% of the time, Pallas kernels for 22%

profile of v14, /device:TPU:0, one launch (start us, length us, event | category | flops | bytes accessed | tf_op | source)
XLA Modules:
  0.0 67.0 jit_solution(7045944314252690102)
XLA Ops:
  0.6 3.2 %shard_map.139 = (f32[3,16,2048]{2,1,0:T(8,128)S(1)}, f32[32,1,768]{2,1,0:T(1,128)}, f32[7,16,2048]{2,1,0:T(8,128)S(1)}) custom-call(s32[1,256]{1,0:T(1,128)} %bitcast.8, s32[1,256]{1,0:T(1,128)} %bitcast.10, f32[1,256]{1,0:T(1,128)} %bitcast.4, f32[3,3,16,2048]{3,2,1,0:T(8,128)} %refs_3_.3, f32[3,3,16,2048]{3,2,1,0:T(8,128)} %wts_in.1, ...), custom_call_target="tpu_custom_call" | custom-call | tf_op jit(solution)/shard_map/pallas_call | solution.py:626
  3.9 0.5 collective-permute-start
  4.4 7.0 %all-to-all-start = ((f32[32,1,768]{2,1,0:T(1,128)}), f32[32,1,768]{2,1,0:T(1,128)S(1)}, u32[]{:S(2)}, u32[]{:S(2)}) async-start(f32[32,1,768]{2,1,0:T(1,128)} %get-tuple-element.40), calls=%async_computation | async-start | bytes 196608 | tf_op jit(solution)/shard_map/all_to_all | solution.py:607
  11.4 0.0 collective-permute-done.refs_1_.refs_3_
  11.4 2.1 %shard_map.140 = (f32[12,16,2048]{2,1,0:T(8,128)S(1)}, f32[12,1,2048]{2,1,0:T(1,128)S(1)}, f32[12,1,2048]{2,1,0:T(1,128)S(1)}, f32[1,256]{1,0:T(1,128)S(1)}, f32[3,16,2048]{2,1,0:T(8,128)S(1)}) custom-call(f32[7,16,2048]{2,1,0:T(8,128)S(1)} %get-tuple-element.41.refs_0_, f32[7,16,2048]{2,1,0:T(8,128)S(1)} %collective-permute-done.refs_1_.refs_3_, ...), custom_call_target="tpu_custom_call" | custom-call | tf_op jit(solution)/shard_map/pallas_call | solution.py:61
  13.5 1.2 %copy-done = f32[12,16,2048]{2,1,0:T(8,128)} copy-done((f32[12,16,2048]{2,1,0:T(8,128)}, f32[12,16,2048]{2,1,0:T(8,128)S(1)}, u32[]{:S(2)}) %copy-start) | copy-done | bytes 1572888
  14.7 4.5 %all-to-all-done.recv.refs_1_ = f32[32,1,768]{2,1,0:T(1,128)S(1)} async-done(((f32[32,1,768]{2,1,0:T(1,128)}), f32[32,1,768]{2,1,0:T(1,128)S(1)}, u32[]{:S(2)}, u32[]{:S(2)}) %all-to-all-start) | async-done | bytes 98336 | tf_op jit(solution)/shard_map/all_to_all | solution.py:607
  19.2 0.3 collective-permute-start.1
  19.5 5.0 %shard_map.141 = f32[32,1,768]{2,1,0:T(1,128)} custom-call(f32[32,1,768]{2,1,0:T(1,128)S(1)} %all-to-all-done.recv.refs_1_, f32[1,256]{1,0:T(1,128)S(1)} %get-tuple-element.46.found, f32[256,8192]{1,0:T(8,128)} %inverse.1), custom_call_target="tpu_custom_call" | custom-call | tf_op jit(solution)/shard_map/pallas_call | solution.py:663
  24.5 2.7 %all-to-all-start.1 = ((f32[32,1,768]{2,1,0:T(1,128)}), f32[32,1,768]{2,1,0:T(1,128)S(1)}, u32[]{:S(2)}, u32[]{:S(2)}) async-start(f32[32,1,768]{2,1,0:T(1,128)} %shard_map.141), calls=%async_computation.1 | async-start | bytes 196608 | tf_op jit(solution)/shard_map/all_to_all | solution.py:607
  27.2 3.3 %collective-permute-done.1.refs_4_ = f32[3,16,2048]{2,1,0:T(8,128)S(1)} collective-permute-done((f32[3,16,2048]{2,1,0:T(8,128)S(1)}, f32[3,16,2048]{2,1,0:T(8,128)S(1)}, u32[]{:S(2)}, u32[]{:S(2)}) %collective-permute-start.1) | collective-permute-done | bytes 393248 | tf_op jit(solution)/shard_map/ppermute | solution.py:598
  30.5 0.1 shard_map.143
  30.5 0.7 %collective-permute-start.2 = (f32[23,1,2048]{2,1,0:T(1,128)S(1)}, f32[23,1,2048]{2,1,0:T(1,128)S(1)}, u32[]{:S(2)}, u32[]{:S(2)}) collective-permute-start(f32[23,1,2048]{2,1,0:T(1,128)S(1)} %shard_map.143), channel_id=1, source_target_pairs={{4,8},{12,16},{20,24},{8,4},{16,12},{24,20},{5,9},{13,17},{21,25},... | collective-permute-start | bytes 565256 | tf_op jit(solution)/shard_map/ppermute | solution.py:603
  31.2 3.8 %all-to-all-done.1.refs_0_ = f32[32,1,768]{2,1,0:T(1,128)S(1)} async-done(((f32[32,1,768]{2,1,0:T(1,128)}), f32[32,1,768]{2,1,0:T(1,128)S(1)}, u32[]{:S(2)}, u32[]{:S(2)}) %all-to-all-start.1) | async-done | bytes 98336 | tf_op jit(solution)/shard_map/all_to_all | solution.py:607
  35.0 2.8 %shard_map.142 = (f32[3,16,2048]{2,1,0:T(8,128)S(1)}, f32[3,16,2048]{2,1,0:T(8,128)S(1)}, f32[3,1,2048]{2,1,0:T(1,128)S(1)}, f32[3,16,2048]{2,1,0:T(8,128)S(1)},...) custom-call(f32[32,1,768]{2,1,0:T(1,128)S(1)} %all-to-all-done.1.refs_0_, ...), custom_call_target="tpu_custom_call" | custom-call | tf_op jit(solution)/shard_map/pallas_call | solution.py:61
  37.8 0.7 %collective-permute-start.3 = (f32[3,1,2048]{2,1,0:T(1,128)S(1)}, f32[3,1,2048]{2,1,0:T(1,128)S(1)}, u32[]{:S(2)}, u32[]{:S(2)}) collective-permute-start(f32[3,1,2048]{2,1,0:T(1,128)S(1)} %get-tuple-element.60), channel_id=1, source_target_pairs={{0,4},{4,0},{8,12},{12,8},{16,20},{20,16},{24,28},{28,24},{1,5},{5... | collective-permute-start | bytes 73736 | tf_op jit(solution)/shard_map/ppermute | solution.py:598
  38.5 0.0 collective-permute-done.2.refs_2_
  38.5 3.3 %shard_map.144 = (f32[3,1,2048]{2,1,0:T(1,128)S(1)}, f32[3,3,16,2048]{3,2,1,0:T(8,128)S(1)}, f32[3,3,3,16,2048]{4,3,2,1,0:T(8,128)S(1)}, f32[3,16,2048]{2,1,0:T(8,128)S(1)}) custom-call(f32[32,1,768]{2,1,0:T(1,128)S(1)} %all-to-all-done.1.refs_0_, f32[32,1,768]{2,1,0:T(1,128)S(1)} %all-to-all-done.recv.refs_1_, ...), custom_call_target="tpu_custom_call" | custom-call | tf_op jit(solution)/shard_map/pallas_call | solution.py:61
  41.8 0.0 collective-permute-done.3.refs_3_
  41.8 0.9 %shard_map.145 = (f32[3,3,16,2048]{3,2,1,0:T(8,128)S(1)}, f32[3,16,2048]{2,1,0:T(8,128)S(1)}, f32[3,3,1,2048]{3,2,1,0:T(1,128)S(1)}, f32[3,3,1,2048]{3,2,1,0:T(1,128)S(1)}, f32[3,16,2048]{2,1,0:T(8,128)S(1)}) custom-call(f32[3,16,2048]{2,1,0:T(8,128)S(1)} %get-tuple-element.52.refs_0_, f32[3,16,2048]{2,1,0:T(8,128)S(1)} %get-tuple-element.53.refs_1_, ...), custom_call_target="tpu_custom_call" | custom-call | tf_op jit(solution)/shard_map/pallas_call | solution.py:61
  42.7 0.7 %collective-permute-start.4 = (f32[3,16,2048]{2,1,0:T(8,128)S(1)}, f32[3,16,2048]{2,1,0:T(8,128)S(1)}, u32[]{:S(2)}, u32[]{:S(2)}) collective-permute-start(f32[3,16,2048]{2,1,0:T(8,128)S(1)} %get-tuple-element.68), channel_id=1, source_target_pairs={{1,2},{2,1},{5,6},{6,5},{9,10},{10,9},{13,14},{14,13},{17,18},{18,... | collective-permute-start | bytes 1179656 | tf_op jit(solution)/shard_map/ppermute | solution.py:603
  43.4 2.1 %collective-permute-start.7 = (f32[3,16,2048]{2,1,0:T(8,128)S(1)}, f32[3,16,2048]{2,1,0:T(8,128)S(1)}, u32[]{:S(2)}, u32[]{:S(2)}) collective-permute-start(f32[3,16,2048]{2,1,0:T(8,128)S(1)} %get-tuple-element.71), channel_id=1, source_target_pairs={{0,1},{1,0},{2,3},{3,2},{4,5},{5,4},{6,7},{7,6},{8,9},{9,8},{10,11... | collective-permute-start | bytes 1179656 | tf_op jit(solution)/shard_map/ppermute | solution.py:598
  45.5 0.7 collective-permute-start.5
  46.2 3.8 %collective-permute-start.6 = (f32[3,3,1,2048]{3,2,1,0:T(1,128)S(1)}, f32[3,3,1,2048]{3,2,1,0:T(1,128)S(1)}, u32[]{:S(2)}, u32[]{:S(2)}) collective-permute-start(f32[3,3,1,2048]{3,2,1,0:T(1,128)S(1)} %get-tuple-element.70), channel_id=1, source_target_pairs={{0,4},{4,0},{8,12},{12,8},{16,20},{20,16},{24,28},{28,24},{1,5},{5... | collective-permute-start | bytes 221192 | tf_op jit(solution)/shard_map/ppermute | solution.py:598
  50.0 1.2 %shard_map.146.refs_0_ = f32[3,3,16,2048]{3,2,1,0:T(8,128)S(1)} custom-call(f32[3,3,16,2048]{3,2,1,0:T(8,128)S(1)} %get-tuple-element.67.refs_0_.refs_1_, f32[3,3,3,16,2048]{4,3,2,1,0:T(8,128)S(1)} %get-tuple-element.65.refs_8_.refs_1_, f32[3,16,2048]{2,1,0:T(8,128)S(1)} %get-tuple-element.63.refs_6_.refs_2_, ...), custom_call_target="tpu_custom_call" | custom-call | tf_op jit(solution)/shard_map/pallas_call | solution.py:61
  51.2 0.0 collective-permute-done.5.refs_2_
  51.2 1.5 %collective-permute-done.6.refs_3_ = f32[3,3,1,2048]{3,2,1,0:T(1,128)S(1)} collective-permute-done((f32[3,3,1,2048]{3,2,1,0:T(1,128)S(1)}, f32[3,3,1,2048]{3,2,1,0:T(1,128)S(1)}, u32[]{:S(2)}, u32[]{:S(2)}) %collective-permute-start.6) | collective-permute-done | bytes 73760 | tf_op jit(solution)/shard_map/ppermute | solution.py:598
  52.6 0.0 collective-permute-done.4.refs_1_
  52.6 0.0 collective-permute-done.7.refs_4_
  52.6 1.2 %shard_map.147 = (f32[3,3,16,2048]{3,2,1,0:T(8,128)S(1)}, f32[32,1,128]{2,1,0:T(1,128)S(1)}) custom-call(f32[3,3,16,2048]{3,2,1,0:T(8,128)S(1)} %shard_map.146.refs_0_, f32[3,16,2048]{2,1,0:T(8,128)S(1)} %collective-permute-done.4.refs_1_, f32[3,3,1,2048]{3,2,1,0:T(1,128)S(1)} %collective-permute-done.5.refs_2_, ...), custom_call_target="tpu_custom_call" | custom-call | tf_op jit(solution)/shard_map/pallas_call | solution.py:61
  53.8 11.5 %all_to_all.15.refs_0_ = f32[32,1,128]{2,1,0:T(1,128)S(1)} all-to-all(f32[32,1,128]{2,1,0:T(1,128)S(1)} %get-tuple-element.72), channel_id=1, replica_groups=mesh['tile'=8,'layer'=4] {'tile','layer'}, dimensions={0} | all-to-all | bytes 32768 | tf_op jit(solution)/shard_map/all_to_all | solution.py:607
  65.3 1.7 %shard_map.148 = (f32[3,3,16,2048]{3,2,1,0:T(8,128)}, f32[3,3,16,2048]{3,2,1,0:T(8,128)}, f32[1,1]{1,0:T(1,128)}) custom-call(f32[32,1,128]{2,1,0:T(1,128)S(1)} %all_to_all.15.refs_0_, f32[3,3,16,2048]{3,2,1,0:T(8,128)S(1)} %get-tuple-element.67.refs_0_.refs_1_, f32[3,3,16,2048]{3,2,1,0:T(8,128)S(1)} %get-tuple-element.73.refs_2_, ...), custom_call_target="tpu_custom_call" | custom-call | tf_op jit(solution)/shard_map/pallas_call | solution.py:61
  (3 shorter events, 0.0 us)
Async XLA Ops:
  3.9 7.5 %collective-permute-start = (f32[7,16,2048]{2,1,0:T(8,128)S(1)}, f32[7,16,2048]{2,1,0:T(8,128)S(1)}, u32[]{:S(2)}, u32[]{:S(2)}) collective-permute-start(f32[7,16,2048]{2,1,0:T(8,128)S(1)} %get-tuple-element.41.refs_0_), channel_id=1, source_target_pairs={{0,1},{1,0},{2,3},{3,2},{4,5},{5,4},{6,7},{7,6},{8,9},{9,8},{10,11... | collective-permute-start | bytes 2752520 | tf_op jit(solution)/shard_map/ppermute | solution.py:598
  4.4 14.8 %all-to-all-start = ((f32[32,1,768]{2,1,0:T(1,128)}), f32[32,1,768]{2,1,0:T(1,128)S(1)}, u32[]{:S(2)}, u32[]{:S(2)}) async-start(f32[32,1,768]{2,1,0:T(1,128)} %get-tuple-element.40), calls=%async_computation | async-start | bytes 196608 | tf_op jit(solution)/shard_map/all_to_all | solution.py:607
  13.5 1.2 %copy-start = (f32[12,16,2048]{2,1,0:T(8,128)}, f32[12,16,2048]{2,1,0:T(8,128)S(1)}, u32[]{:S(2)}) copy-start(f32[12,16,2048]{2,1,0:T(8,128)S(1)} %get-tuple-element.51.refs_6_) | copy-start | bytes 4718596
  19.2 11.3 %copy-start.1 = (f32[256]{0:T(256)S(1)}, f32[256]{0:T(256)}, u32[]{:S(2)}) copy-start(f32[256]{0:T(256)} %param.22) | copy-start | bytes 3076
  19.2 11.3 %collective-permute-start.1 = (f32[3,16,2048]{2,1,0:T(8,128)S(1)}, f32[3,16,2048]{2,1,0:T(8,128)S(1)}, u32[]{:S(2)}, u32[]{:S(2)}) collective-permute-start(f32[3,16,2048]{2,1,0:T(8,128)S(1)} %get-tuple-element.50), channel_id=1, source_target_pairs={{0,2},{1,3},{2,0},{3,1},{4,6},{5,7},{6,4},{7,5},{8,10},{9,11},{10,... | collective-permute-start | bytes 1179656 | tf_op jit(solution)/shard_map/ppermute | solution.py:598
  24.5 10.5 %all-to-all-start.1 = ((f32[32,1,768]{2,1,0:T(1,128)}), f32[32,1,768]{2,1,0:T(1,128)S(1)}, u32[]{:S(2)}, u32[]{:S(2)}) async-start(f32[32,1,768]{2,1,0:T(1,128)} %shard_map.141), calls=%async_computation.1 | async-start | bytes 196608 | tf_op jit(solution)/shard_map/all_to_all | solution.py:607
  30.5 8.0 %collective-permute-start.2 = (f32[23,1,2048]{2,1,0:T(1,128)S(1)}, f32[23,1,2048]{2,1,0:T(1,128)S(1)}, u32[]{:S(2)}, u32[]{:S(2)}) collective-permute-start(f32[23,1,2048]{2,1,0:T(1,128)S(1)} %shard_map.143), channel_id=1, source_target_pairs={{4,8},{12,16},{20,24},{8,4},{16,12},{24,20},{5,9},{13,17},{21,25},... | collective-permute-start | bytes 565256 | tf_op jit(solution)/shard_map/ppermute | solution.py:603
  37.8 4.0 %collective-permute-start.3 = (f32[3,1,2048]{2,1,0:T(1,128)S(1)}, f32[3,1,2048]{2,1,0:T(1,128)S(1)}, u32[]{:S(2)}, u32[]{:S(2)}) collective-permute-start(f32[3,1,2048]{2,1,0:T(1,128)S(1)} %get-tuple-element.60), channel_id=1, source_target_pairs={{0,4},{4,0},{8,12},{12,8},{16,20},{20,16},{24,28},{28,24},{1,5},{5... | collective-permute-start | bytes 73736 | tf_op jit(solution)/shard_map/ppermute | solution.py:598
  42.7 9.9 %collective-permute-start.4 = (f32[3,16,2048]{2,1,0:T(8,128)S(1)}, f32[3,16,2048]{2,1,0:T(8,128)S(1)}, u32[]{:S(2)}, u32[]{:S(2)}) collective-permute-start(f32[3,16,2048]{2,1,0:T(8,128)S(1)} %get-tuple-element.68), channel_id=1, source_target_pairs={{1,2},{2,1},{5,6},{6,5},{9,10},{10,9},{13,14},{14,13},{17,18},{18,... | collective-permute-start | bytes 1179656 | tf_op jit(solution)/shard_map/ppermute | solution.py:603
  43.4 9.2 %collective-permute-start.7 = (f32[3,16,2048]{2,1,0:T(8,128)S(1)}, f32[3,16,2048]{2,1,0:T(8,128)S(1)}, u32[]{:S(2)}, u32[]{:S(2)}) collective-permute-start(f32[3,16,2048]{2,1,0:T(8,128)S(1)} %get-tuple-element.71), channel_id=1, source_target_pairs={{0,1},{1,0},{2,3},{3,2},{4,5},{5,4},{6,7},{7,6},{8,9},{9,8},{10,11... | collective-permute-start | bytes 1179656 | tf_op jit(solution)/shard_map/ppermute | solution.py:598
  45.5 5.6 %collective-permute-start.5 = (f32[3,3,1,2048]{3,2,1,0:T(1,128)S(1)}, f32[3,3,1,2048]{3,2,1,0:T(1,128)S(1)}, u32[]{:S(2)}, u32[]{:S(2)}) collective-permute-start(f32[3,3,1,2048]{3,2,1,0:T(1,128)S(1)} %get-tuple-element.69), channel_id=1, source_target_pairs={{4,8},{12,16},{20,24},{8,4},{16,12},{24,20},{5,9},{13,17},{21,25},... | collective-permute-start | bytes 221192 | tf_op jit(solution)/shard_map/ppermute | solution.py:603
  46.2 6.4 %collective-permute-start.6 = (f32[3,3,1,2048]{3,2,1,0:T(1,128)S(1)}, f32[3,3,1,2048]{3,2,1,0:T(1,128)S(1)}, u32[]{:S(2)}, u32[]{:S(2)}) collective-permute-start(f32[3,3,1,2048]{3,2,1,0:T(1,128)S(1)} %get-tuple-element.70), channel_id=1, source_target_pairs={{0,4},{4,0},{8,12},{12,8},{16,20},{20,16},{24,28},{28,24},{1,5},{5... | collective-permute-start | bytes 221192 | tf_op jit(solution)/shard_map/ppermute | solution.py:598

commit v15 on v14

--- a/solution.py
+++ b/solution.py
@@ -57,17 +57,14 @@
 def call(kernel, outs, args, far=(), keep=(), column=(), late=(), scratch=(), limit=LIMIT):
     where = [i in far for i in range(len(args))]
     spaces = [pltpu.HBM if w else pltpu.VMEM for w in where]
-    every = (*outs, *(vmem(args[i].shape, args[i].dtype) for i in keep))
+    shapes = [a.shape[:1] + a.shape[2:] if i in column else a.shape for i, a in enumerate(args)]
+    every = (*outs, *(vmem(shapes[i], args[i].dtype) for i in keep))
     return pl.pallas_call(
         functools.partial(staged, kernel, where, len(outs), tuple(keep), tuple(column), tuple(late)),
         out_shape=every,
         in_specs=[pl.BlockSpec(memory_space=s) for s in spaces],
         out_specs=(VM,) * len(every),
-        scratch_shapes=[
-            vmem(a.shape[:1] + a.shape[2:] if i in column else a.shape, a.dtype)
-            for i, a in enumerate(args)
-            if where[i] and i not in keep
-        ]
+        scratch_shapes=[vmem(shapes[i], a.dtype) for i, a in enumerate(args) if where[i] and i not in keep]
         + [*scratch, pltpu.SemaphoreType.DMA((max(1, sum(where)),))],
         compiler_params=pltpu.CompilerParams(vmem_limit_bytes=limit),
     )(*[pltpu.with_memory_space_constraint(a, s) for a, s in zip(args, spaces)])
@@ -116,7 +113,7 @@
 
 def pres_kernel(cell_in, front_in, prod_in, rhs_in, wts_in, tz_in, store_in, pres, send, ends, *scratch):
     (cell, front, prod, rhs, wts, tz, store), sems = scratch[:-1], scratch[-1]
-    pairs = ((cell_in, cell), (front_in, front), (prod_in, prod), (rhs_in, rhs), (wts_in, wts), (tz_in, tz), (store_in, store))
+    pairs = ((cell_in, cell), (front_in, front), (prod_in, prod), (tz_in, tz), (store_in, store), (rhs_in, rhs), (wts_in, wts))
     copies = [pltpu.make_async_copy(a, b, sems.at[i]) for i, (a, b) in enumerate(pairs)]
     for copy in copies:
         copy.start()
@@ -125,12 +122,14 @@
     depth, width, long = pres.shape
     where = cell[...]
     hot = onehot(lax.rem(where, long), long).astype(BF16)
-    for copy in copies[3:]:
+    for copy in copies[3:5]:
         copy.wait()
-    for z in range(depth):
-        pres[z] = wts[0, z] * rhs[0, z] + wts[1, z] * rhs[1, z] + wts[2, z] * rhs[2, z]
     tzs = [tz[z] for z in range(depth)]
     gs, invs, first, final, coefs = factors(tzs, [store[z] for z in range(depth)])
+    for copy in copies[5:]:
+        copy.wait()
+    for z in range(depth):
+        pres[z] = wts[0, z] * rhs[0, z] + wts[1, z] * rhs[1, z] + wts[2, z] * rhs[2, z]
     tables = [pres[...].reshape(depth * width, long), jnp.concatenate(first, 0), jnp.concatenate(final, 0)]
     found, kf, kl = pick(tables, lax.div(where, long), hot)
     both = jnp.concatenate([prod[...] * found, front[...].astype(F32), where.astype(F32)], 1)
@@ -349,7 +348,7 @@
             if only is None:
                 row = lax.div(y, lanes) * width + x
             else:
-                row = jnp.where(x == only, lax.div(y, lanes) * 8, -1)
+                row = jnp.where(x == only, lax.div(y, lanes), -1)
             here = pl.ds(at, count)
             rows_hot[:, here] = onehot(row, rows_hot.shape[0]).astype(BF16)
             lanes_hot[:, here] = onehot(lax.rem(y, lanes), lanes).astype(BF16)
@@ -475,15 +474,13 @@
     ready(0)
 
 
-def beyond_kernel(levels, shapes, shape, recv, terms, two, row, planes, *hots):
+def beyond_kernel(levels, shapes, shape, recv, terms, two, row, *hots):
     depth, width, long = shape
     tiles, layers = (lax.axis_size("tile"), lax.axis_size("layer"))
     tile = lax.axis_index("tile")
     odd = is_right(0, "tile")
-    planes[...] = jnp.zeros(planes.shape, F32)
-    count = planes.shape[0]
-    for i in range(count):
-        planes[i, 0:1] = two[i]
+    count = 4 * depth + sum(shapes)
+    planes = [two[i] for i in range(count)]
     step = jnp.where(odd, layers, -layers)
     lists = [[jnp.clip(device + step, 0, tiles * layers - 1) for device in members] for members in groups_of(levels)]
     table_kernel(lists, shape, terms, hots, jnp.where(odd, 0, width - 1))
@@ -503,11 +500,11 @@
     listing = (two[count + 1, :, : terms.shape[2] // 3], two[count])
     values, _, _, _ = column_solve(levels, recv, lists, hots, listing, planes_of, blocks)
     for z in range(depth):
-        found = jnp.where(exists > 0.0, values[z][0:1], 0.0)
+        found = jnp.where(exists > 0.0, values[z], 0.0)
         row[z] = jnp.where(odd, found, found * two[3 * depth + z])
 
 
-def search_kernel(p, coupled_z, two, one, tx, ty, tz, rhs, diag, binv, s, outer, row_two, row_one, inner):
+def search_kernel(p, coupled_z, two, one, tx, ty, tz, rhs, column, binv, s, outer, row_two, row_one, inner):
     depth, width, _ = p.shape
     odd = is_right(0, "tile")
     right = is_right(0)
@@ -518,7 +515,7 @@
         before = jnp.where(odd, one[z], two[z])
         coupled = coupled_z[z] + beside(centre, tx[z], ty[z])
         coupled = coupled + jnp.where(row == 0, before, 0.0) + jnp.where(row == width - 1, tx[z] * after, 0.0)
-        remain = [rhs[c, z] - diag[c, 0, z] * centre for c in range(3)]
+        remain = [rhs[c, z] - column[c, z] * centre for c in range(3)]
         remain[0] = remain[0] + coupled
         for c in range(3):
             value = binv[c, 0, z] * remain[0] + binv[c, 1, z] * remain[1] + binv[c, 2, z] * remain[2]
@@ -532,17 +529,21 @@
         outer[c] = jnp.where(right, bottom, top)
 
 
-def inner_kernel(s, diag, tz, tx, ty, image):
+def inner_kernel(ready, s, diag, tz, tx, ty, image):
     depth = s.shape[1]
+    for z in range(depth):
+        for c in range(3):
+            total = beside(s[c, z], tx[z], ty[z])
+            if z:
+                total = total + tz[z - 1] * s[c, z - 1]
+            if z < depth - 1:
+                total = total + tz[z] * s[c, z + 1]
+            image[c, z] = total
+    ready(0)
     for z in range(depth):
         for c in range(3):
             total = diag[c, 0, z] * s[0, z] + diag[c, 1, z] * s[1, z] + diag[c, 2, z] * s[2, z]
-            total = total - beside(s[c, z], tx[z], ty[z])
-            if z:
-                total = total - tz[z - 1] * s[c, z - 1]
-            if z < depth - 1:
-                total = total - tz[z] * s[c, z + 1]
-            image[c, z] = total
+            image[c, z] = total - image[c, z]
 
 
 def image_kernel(part, outer, row_two, row_one, inner, rhs, tz, tx, image, send):
@@ -697,25 +698,26 @@
     )
     sol, one, terms = lax.optimization_barrier((sol, one, terms))
     one = flip(one, 0, "tile")
-    two, rhs, block_diag, ty = call(
+    two, rhs, first_column, ty = call(
         functools.partial(first_three, functools.partial(beyond_kernel, levels, sizes, (depth, width, long))),
         (row3,),
         (sol, terms, two, rhs, block_diag, ty),
         far=(3, 4, 5),
         keep=(3, 4, 5),
+        column=(4,),
         late=((3, 4, 5),),
-        scratch=(vmem((4 * depth + sum(sizes), 8, long)), *hots(8)),
+        scratch=hots(1),
     )
     row9 = vmem((3, depth, 1, long))
     plane3 = planes(3)
     s, outer, row_two, row_one, inner = call(
         search_kernel,
         (vmem(rhs.shape), plane3, row9, row9, plane3),
-        (p, coupled_z, two, one, tx, ty, tz, rhs, block_diag, block_inv),
+        (p, coupled_z, two, one, tx, ty, tz, rhs, first_column, block_inv),
     )
     outer, row_two = (neighbour(outer), neighbour(row_two, "tile"))
     row_one, inner = (flip(row_one, 0, "tile"), flip(inner, 0))
-    (part,) = call(inner_kernel, (vmem(rhs.shape),), (s, block_diag, tz, tx, ty))
+    (part,) = call(inner_kernel, (vmem(rhs.shape),), (s, block_diag, tz, tx, ty), far=(1,), late=((1,),))
     image, send = call(
         image_kernel,
         (vmem(rhs.shape), vmem((devices, 1, 128))),

time: 67.3 us -> 66.2 us (0.984)
  starting transfers between devices: 19.1 us -> 18.4 us
  blocking collectives: 11.5 us -> 10.8 us
    all_to_all x1, blocking collectives: 11.5 us -> 10.8 us  [everywhere(): return lax.all_to_all(x, BOTH, split_axis=0, concat_axis=0, tiled=True)]
    ppermute x5, starting transfers between devices: 7.45 us -> 6.76 us  [flip(): lax.ppermute(x, axis, [(i, i ^ 1 << level) for i in range(lax.axis_size(a...]
  transfers between devices with their start and end apart: 10 -> 10, of which waited for: 4 -> 5; matrix products, arithmetic and copies ran while one was open for 0% -> 0% of each run, Pallas kernels for 22% -> 22%
where the time goes in v15:
time: 66.2 us; the launch traced here: 65.8 us
  Pallas kernels  21.4 us (32%)
  starting transfers between devices  18.4 us (28%)
  waiting for transfers between devices  13.3 us (20%)
  blocking collectives  10.8 us (16%)
  local copies, waits for them, and re-layouts  1.17 us (2%)
  between operations  0.77 us (1%)
    pallas_call x8, Pallas kernels, call(): pl.pallas_call(functools.partial(staged, kernel, where, len(outs), tuple(...  13.2 us
    all_to_all x1, blocking collectives, everywhere(): return lax.all_to_all(x, BOTH, split_axis=0, concat_axis=0, tiled=True)  10.8 us
    all_to_all x2, starting transfers between devices, everywhere(): return lax.all_to_all(x, BOTH, split_axis=0, concat_axis=0, tiled=True)  9.63 us
    all_to_all x2, waiting for transfers between devices, everywhere(): return lax.all_to_all(x, BOTH, split_axis=0, concat_axis=0, tiled=True)  8.32 us
    ppermute x5, starting transfers between devices, flip(): lax.ppermute(x, axis, [(i, i ^ 1 << level) for i in range(lax.axis_size(a...  6.76 us
    pallas_call x1, Pallas kernels, shards(): pl.pallas_call(front_kernel, out_shape=vmem((devices, 1, max(rows + found...  4.98 us
    ppermute x5, waiting for transfers between devices, flip(): lax.ppermute(x, axis, [(i, i ^ 1 << level) for i in range(lax.axis_size(a...  4.95 us
    pallas_call x1, Pallas kernels, shards(): pl.pallas_call(pres_kernel, out_shape=(field, vmem((devices, 1, 3 * count...  3.25 us
  transfers between devices with their start and end apart: 10, of which 5 were waited for; matrix products, arithmetic and copies ran while one was open for 0% of the time, Pallas kernels for 22%

profile of v15, /device:TPU:0, one launch (start us, length us, event | category | flops | bytes accessed | tf_op | source)
XLA Modules:
  0.0 65.8 jit_solution(17940644090814776715)
XLA Ops:
  0.6 3.2 %shard_map.139 = (f32[3,16,2048]{2,1,0:T(8,128)S(1)}, f32[32,1,768]{2,1,0:T(1,128)}, f32[7,16,2048]{2,1,0:T(8,128)S(1)}) custom-call(s32[1,256]{1,0:T(1,128)} %bitcast.8, s32[1,256]{1,0:T(1,128)} %bitcast.10, f32[1,256]{1,0:T(1,128)} %bitcast.4, f32[3,3,16,2048]{3,2,1,0:T(8,128)} %refs_3_.3, f32[3,3,16,2048]{3,2,1,0:T(8,128)} %wts_in.1, ...), custom_call_target="tpu_custom_call" | custom-call | tf_op jit(solution)/shard_map/pallas_call | solution.py:627
  3.9 0.5 collective-permute-start
  4.4 7.0 %all-to-all-start = ((f32[32,1,768]{2,1,0:T(1,128)}), f32[32,1,768]{2,1,0:T(1,128)S(1)}, u32[]{:S(2)}, u32[]{:S(2)}) async-start(f32[32,1,768]{2,1,0:T(1,128)} %get-tuple-element.40), calls=%async_computation | async-start | bytes 196608 | tf_op jit(solution)/shard_map/all_to_all | solution.py:608
  11.4 0.0 collective-permute-done.refs_1_.refs_3_
  11.4 2.1 %shard_map.140 = (f32[12,16,2048]{2,1,0:T(8,128)S(1)}, f32[12,1,2048]{2,1,0:T(1,128)S(1)}, f32[12,1,2048]{2,1,0:T(1,128)S(1)}, f32[1,256]{1,0:T(1,128)S(1)}, f32[3,16,2048]{2,1,0:T(8,128)S(1)}) custom-call(f32[7,16,2048]{2,1,0:T(8,128)S(1)} %get-tuple-element.41.refs_0_, f32[7,16,2048]{2,1,0:T(8,128)S(1)} %collective-permute-done.refs_1_.refs_3_, ...), custom_call_target="tpu_custom_call" | custom-call | tf_op jit(solution)/shard_map/pallas_call | solution.py:62
  13.5 1.2 %copy-done = f32[12,16,2048]{2,1,0:T(8,128)} copy-done((f32[12,16,2048]{2,1,0:T(8,128)}, f32[12,16,2048]{2,1,0:T(8,128)S(1)}, u32[]{:S(2)}) %copy-start) | copy-done | bytes 1572888
  14.7 4.5 %all-to-all-done.recv.refs_1_ = f32[32,1,768]{2,1,0:T(1,128)S(1)} async-done(((f32[32,1,768]{2,1,0:T(1,128)}), f32[32,1,768]{2,1,0:T(1,128)S(1)}, u32[]{:S(2)}, u32[]{:S(2)}) %all-to-all-start) | async-done | bytes 98336 | tf_op jit(solution)/shard_map/all_to_all | solution.py:608
  19.2 0.3 collective-permute-start.1
  19.5 5.0 %shard_map.141 = f32[32,1,768]{2,1,0:T(1,128)} custom-call(f32[32,1,768]{2,1,0:T(1,128)S(1)} %all-to-all-done.recv.refs_1_, f32[1,256]{1,0:T(1,128)S(1)} %get-tuple-element.46.found, f32[256,8192]{1,0:T(8,128)} %inverse.1), custom_call_target="tpu_custom_call" | custom-call | tf_op jit(solution)/shard_map/pallas_call | solution.py:664
  24.5 2.7 %all-to-all-start.1 = ((f32[32,1,768]{2,1,0:T(1,128)}), f32[32,1,768]{2,1,0:T(1,128)S(1)}, u32[]{:S(2)}, u32[]{:S(2)}) async-start(f32[32,1,768]{2,1,0:T(1,128)} %shard_map.141), calls=%async_computation.1 | async-start | bytes 196608 | tf_op jit(solution)/shard_map/all_to_all | solution.py:608
  27.2 3.3 %collective-permute-done.1.refs_4_ = f32[3,16,2048]{2,1,0:T(8,128)S(1)} collective-permute-done((f32[3,16,2048]{2,1,0:T(8,128)S(1)}, f32[3,16,2048]{2,1,0:T(8,128)S(1)}, u32[]{:S(2)}, u32[]{:S(2)}) %collective-permute-start.1) | collective-permute-done | bytes 393248 | tf_op jit(solution)/shard_map/ppermute | solution.py:599
  30.5 0.1 shard_map.143
  30.5 0.7 %collective-permute-start.2 = (f32[23,1,2048]{2,1,0:T(1,128)S(1)}, f32[23,1,2048]{2,1,0:T(1,128)S(1)}, u32[]{:S(2)}, u32[]{:S(2)}) collective-permute-start(f32[23,1,2048]{2,1,0:T(1,128)S(1)} %shard_map.143), channel_id=1, source_target_pairs={{4,8},{12,16},{20,24},{8,4},{16,12},{24,20},{5,9},{13,17},{21,25},... | collective-permute-start | bytes 565256 | tf_op jit(solution)/shard_map/ppermute | solution.py:604
  31.2 3.8 %all-to-all-done.1.refs_0_ = f32[32,1,768]{2,1,0:T(1,128)S(1)} async-done(((f32[32,1,768]{2,1,0:T(1,128)}), f32[32,1,768]{2,1,0:T(1,128)S(1)}, u32[]{:S(2)}, u32[]{:S(2)}) %all-to-all-start.1) | async-done | bytes 98336 | tf_op jit(solution)/shard_map/all_to_all | solution.py:608
  35.0 2.8 %shard_map.142 = (f32[3,16,2048]{2,1,0:T(8,128)S(1)}, f32[3,16,2048]{2,1,0:T(8,128)S(1)}, f32[3,1,2048]{2,1,0:T(1,128)S(1)}, f32[3,16,2048]{2,1,0:T(8,128)S(1)},...) custom-call(f32[32,1,768]{2,1,0:T(1,128)S(1)} %all-to-all-done.1.refs_0_, ...), custom_call_target="tpu_custom_call" | custom-call | tf_op jit(solution)/shard_map/pallas_call | solution.py:62
  37.8 0.7 %collective-permute-start.3 = (f32[3,1,2048]{2,1,0:T(1,128)S(1)}, f32[3,1,2048]{2,1,0:T(1,128)S(1)}, u32[]{:S(2)}, u32[]{:S(2)}) collective-permute-start(f32[3,1,2048]{2,1,0:T(1,128)S(1)} %get-tuple-element.60), channel_id=1, source_target_pairs={{0,4},{4,0},{8,12},{12,8},{16,20},{20,16},{24,28},{28,24},{1,5},{5... | collective-permute-start | bytes 73736 | tf_op jit(solution)/shard_map/ppermute | solution.py:599
  38.5 0.0 collective-permute-done.2.refs_2_
  38.5 2.1 %shard_map.144 = (f32[3,1,2048]{2,1,0:T(1,128)S(1)}, f32[3,3,16,2048]{3,2,1,0:T(8,128)S(1)}, f32[3,3,16,2048]{3,2,1,0:T(8,128)S(1)}, f32[3,16,2048]{2,1,0:T(8,128)S(1)}) custom-call(f32[32,1,768]{2,1,0:T(1,128)S(1)} %all-to-all-done.1.refs_0_, f32[32,1,768]{2,1,0:T(1,128)S(1)} %all-to-all-done.recv.refs_1_, ...), custom_call_target="tpu_custom_call" | custom-call | tf_op jit(solution)/shard_map/pallas_call | solution.py:62
  40.6 1.1 %collective-permute-done.3.refs_3_ = f32[3,1,2048]{2,1,0:T(1,128)S(1)} collective-permute-done((f32[3,1,2048]{2,1,0:T(1,128)S(1)}, f32[3,1,2048]{2,1,0:T(1,128)S(1)}, u32[]{:S(2)}, u32[]{:S(2)}) %collective-permute-start.3) | collective-permute-done | bytes 24608 | tf_op jit(solution)/shard_map/ppermute | solution.py:599
  41.7 0.9 %shard_map.145 = (f32[3,3,16,2048]{3,2,1,0:T(8,128)S(1)}, f32[3,16,2048]{2,1,0:T(8,128)S(1)}, f32[3,3,1,2048]{3,2,1,0:T(1,128)S(1)}, f32[3,3,1,2048]{3,2,1,0:T(1,128)S(1)}, f32[3,16,2048]{2,1,0:T(8,128)S(1)}) custom-call(f32[3,16,2048]{2,1,0:T(8,128)S(1)} %get-tuple-element.52.refs_0_, f32[3,16,2048]{2,1,0:T(8,128)S(1)} %get-tuple-element.53.refs_1_, ...), custom_call_target="tpu_custom_call" | custom-call | tf_op jit(solution)/shard_map/pallas_call | solution.py:62
  42.6 0.7 %collective-permute-start.4 = (f32[3,16,2048]{2,1,0:T(8,128)S(1)}, f32[3,16,2048]{2,1,0:T(8,128)S(1)}, u32[]{:S(2)}, u32[]{:S(2)}) collective-permute-start(f32[3,16,2048]{2,1,0:T(8,128)S(1)} %get-tuple-element.68), channel_id=1, source_target_pairs={{1,2},{2,1},{5,6},{6,5},{9,10},{10,9},{13,14},{14,13},{17,18},{18,... | collective-permute-start | bytes 1179656 | tf_op jit(solution)/shard_map/ppermute | solution.py:604
  43.3 1.8 %collective-permute-start.7 = (f32[3,16,2048]{2,1,0:T(8,128)S(1)}, f32[3,16,2048]{2,1,0:T(8,128)S(1)}, u32[]{:S(2)}, u32[]{:S(2)}) collective-permute-start(f32[3,16,2048]{2,1,0:T(8,128)S(1)} %get-tuple-element.71), channel_id=1, source_target_pairs={{0,1},{1,0},{2,3},{3,2},{4,5},{5,4},{6,7},{7,6},{8,9},{9,8},{10,11... | collective-permute-start | bytes 1179656 | tf_op jit(solution)/shard_map/ppermute | solution.py:599
  45.1 0.7 collective-permute-start.5
  45.8 3.4 %collective-permute-start.6 = (f32[3,3,1,2048]{3,2,1,0:T(1,128)S(1)}, f32[3,3,1,2048]{3,2,1,0:T(1,128)S(1)}, u32[]{:S(2)}, u32[]{:S(2)}) collective-permute-start(f32[3,3,1,2048]{3,2,1,0:T(1,128)S(1)} %get-tuple-element.70), channel_id=1, source_target_pairs={{0,4},{4,0},{8,12},{12,8},{16,20},{20,16},{24,28},{28,24},{1,5},{5... | collective-permute-start | bytes 221192 | tf_op jit(solution)/shard_map/ppermute | solution.py:599
  49.2 2.4 %shard_map.146.refs_0_ = f32[3,3,16,2048]{3,2,1,0:T(8,128)S(1)} custom-call(f32[3,3,16,2048]{3,2,1,0:T(8,128)S(1)} %get-tuple-element.67.refs_0_.refs_1_, f32[3,3,3,16,2048]{4,3,2,1,0:T(8,128)} %refs_1_.1, f32[3,16,2048]{2,1,0:T(8,128)S(1)} %get-tuple-element.63.refs_6_.refs_2_, f32[3,16,2048]{2,1,0:T(8,128)S(1)} %get-tuple-element.61.refs_4_.refs_3_.refs_7_, ...), custom_call_target="tpu_custom_call" | custom-call | tf_op jit(solution)/shard_map/pallas_call | solution.py:62
  51.5 0.0 collective-permute-done.5.refs_2_
  51.5 0.6 collective-permute-done.6.refs_3_
  52.2 0.0 collective-permute-done.4.refs_1_
  52.2 0.0 collective-permute-done.7.refs_4_
  52.2 1.2 %shard_map.147 = (f32[3,3,16,2048]{3,2,1,0:T(8,128)S(1)}, f32[32,1,128]{2,1,0:T(1,128)S(1)}) custom-call(f32[3,3,16,2048]{3,2,1,0:T(8,128)S(1)} %shard_map.146.refs_0_, f32[3,16,2048]{2,1,0:T(8,128)S(1)} %collective-permute-done.4.refs_1_, f32[3,3,1,2048]{3,2,1,0:T(1,128)S(1)} %collective-permute-done.5.refs_2_, ...), custom_call_target="tpu_custom_call" | custom-call | tf_op jit(solution)/shard_map/pallas_call | solution.py:62
  53.4 10.8 %all_to_all.15.refs_0_ = f32[32,1,128]{2,1,0:T(1,128)S(1)} all-to-all(f32[32,1,128]{2,1,0:T(1,128)S(1)} %get-tuple-element.72), channel_id=1, replica_groups=mesh['tile'=8,'layer'=4] {'tile','layer'}, dimensions={0} | all-to-all | bytes 32768 | tf_op jit(solution)/shard_map/all_to_all | solution.py:608
  64.2 1.7 %shard_map.148 = (f32[3,3,16,2048]{3,2,1,0:T(8,128)}, f32[3,3,16,2048]{3,2,1,0:T(8,128)}, f32[1,1]{1,0:T(1,128)}) custom-call(f32[32,1,128]{2,1,0:T(1,128)S(1)} %all_to_all.15.refs_0_, f32[3,3,16,2048]{3,2,1,0:T(8,128)S(1)} %get-tuple-element.67.refs_0_.refs_1_, f32[3,3,16,2048]{3,2,1,0:T(8,128)S(1)} %get-tuple-element.73.refs_2_, ...), custom_call_target="tpu_custom_call" | custom-call | tf_op jit(solution)/shard_map/pallas_call | solution.py:62
  (3 shorter events, 0.0 us)
Async XLA Ops:
  3.9 7.5 %collective-permute-start = (f32[7,16,2048]{2,1,0:T(8,128)S(1)}, f32[7,16,2048]{2,1,0:T(8,128)S(1)}, u32[]{:S(2)}, u32[]{:S(2)}) collective-permute-start(f32[7,16,2048]{2,1,0:T(8,128)S(1)} %get-tuple-element.41.refs_0_), channel_id=1, source_target_pairs={{0,1},{1,0},{2,3},{3,2},{4,5},{5,4},{6,7},{7,6},{8,9},{9,8},{10,11... | collective-permute-start | bytes 2752520 | tf_op jit(solution)/shard_map/ppermute | solution.py:599
  4.4 14.8 %all-to-all-start = ((f32[32,1,768]{2,1,0:T(1,128)}), f32[32,1,768]{2,1,0:T(1,128)S(1)}, u32[]{:S(2)}, u32[]{:S(2)}) async-start(f32[32,1,768]{2,1,0:T(1,128)} %get-tuple-element.40), calls=%async_computation | async-start | bytes 196608 | tf_op jit(solution)/shard_map/all_to_all | solution.py:608
  13.5 1.2 %copy-start = (f32[12,16,2048]{2,1,0:T(8,128)}, f32[12,16,2048]{2,1,0:T(8,128)S(1)}, u32[]{:S(2)}) copy-start(f32[12,16,2048]{2,1,0:T(8,128)S(1)} %get-tuple-element.51.refs_6_) | copy-start | bytes 4718596
  19.2 11.3 %copy-start.1 = (f32[256]{0:T(256)S(1)}, f32[256]{0:T(256)}, u32[]{:S(2)}) copy-start(f32[256]{0:T(256)} %param.22) | copy-start | bytes 3076
  19.2 11.3 %collective-permute-start.1 = (f32[3,16,2048]{2,1,0:T(8,128)S(1)}, f32[3,16,2048]{2,1,0:T(8,128)S(1)}, u32[]{:S(2)}, u32[]{:S(2)}) collective-permute-start(f32[3,16,2048]{2,1,0:T(8,128)S(1)} %get-tuple-element.50), channel_id=1, source_target_pairs={{0,2},{1,3},{2,0},{3,1},{4,6},{5,7},{6,4},{7,5},{8,10},{9,11},{10,... | collective-permute-start | bytes 1179656 | tf_op jit(solution)/shard_map/ppermute | solution.py:599
  24.5 10.5 %all-to-all-start.1 = ((f32[32,1,768]{2,1,0:T(1,128)}), f32[32,1,768]{2,1,0:T(1,128)S(1)}, u32[]{:S(2)}, u32[]{:S(2)}) async-start(f32[32,1,768]{2,1,0:T(1,128)} %shard_map.141), calls=%async_computation.1 | async-start | bytes 196608 | tf_op jit(solution)/shard_map/all_to_all | solution.py:608
  30.5 8.0 %collective-permute-start.2 = (f32[23,1,2048]{2,1,0:T(1,128)S(1)}, f32[23,1,2048]{2,1,0:T(1,128)S(1)}, u32[]{:S(2)}, u32[]{:S(2)}) collective-permute-start(f32[23,1,2048]{2,1,0:T(1,128)S(1)} %shard_map.143), channel_id=1, source_target_pairs={{4,8},{12,16},{20,24},{8,4},{16,12},{24,20},{5,9},{13,17},{21,25},... | collective-permute-start | bytes 565256 | tf_op jit(solution)/shard_map/ppermute | solution.py:604
  37.8 3.9 %collective-permute-start.3 = (f32[3,1,2048]{2,1,0:T(1,128)S(1)}, f32[3,1,2048]{2,1,0:T(1,128)S(1)}, u32[]{:S(2)}, u32[]{:S(2)}) collective-permute-start(f32[3,1,2048]{2,1,0:T(1,128)S(1)} %get-tuple-element.60), channel_id=1, source_target_pairs={{0,4},{4,0},{8,12},{12,8},{16,20},{20,16},{24,28},{28,24},{1,5},{5... | collective-permute-start | bytes 73736 | tf_op jit(solution)/shard_map/ppermute | solution.py:599
  42.6 9.5 %collective-permute-start.4 = (f32[3,16,2048]{2,1,0:T(8,128)S(1)}, f32[3,16,2048]{2,1,0:T(8,128)S(1)}, u32[]{:S(2)}, u32[]{:S(2)}) collective-permute-start(f32[3,16,2048]{2,1,0:T(8,128)S(1)} %get-tuple-element.68), channel_id=1, source_target_pairs={{1,2},{2,1},{5,6},{6,5},{9,10},{10,9},{13,14},{14,13},{17,18},{18,... | collective-permute-start | bytes 1179656 | tf_op jit(solution)/shard_map/ppermute | solution.py:604
  43.3 8.8 %collective-permute-start.7 = (f32[3,16,2048]{2,1,0:T(8,128)S(1)}, f32[3,16,2048]{2,1,0:T(8,128)S(1)}, u32[]{:S(2)}, u32[]{:S(2)}) collective-permute-start(f32[3,16,2048]{2,1,0:T(8,128)S(1)} %get-tuple-element.71), channel_id=1, source_target_pairs={{0,1},{1,0},{2,3},{3,2},{4,5},{5,4},{6,7},{7,6},{8,9},{9,8},{10,11... | collective-permute-start | bytes 1179656 | tf_op jit(solution)/shard_map/ppermute | solution.py:599
  45.1 6.5 %collective-permute-start.5 = (f32[3,3,1,2048]{3,2,1,0:T(1,128)S(1)}, f32[3,3,1,2048]{3,2,1,0:T(1,128)S(1)}, u32[]{:S(2)}, u32[]{:S(2)}) collective-permute-start(f32[3,3,1,2048]{3,2,1,0:T(1,128)S(1)} %get-tuple-element.69), channel_id=1, source_target_pairs={{4,8},{12,16},{20,24},{8,4},{16,12},{24,20},{5,9},{13,17},{21,25},... | collective-permute-start | bytes 221192 | tf_op jit(solution)/shard_map/ppermute | solution.py:604
  45.8 6.4 %collective-permute-start.6 = (f32[3,3,1,2048]{3,2,1,0:T(1,128)S(1)}, f32[3,3,1,2048]{3,2,1,0:T(1,128)S(1)}, u32[]{:S(2)}, u32[]{:S(2)}) collective-permute-start(f32[3,3,1,2048]{3,2,1,0:T(1,128)S(1)} %get-tuple-element.70), channel_id=1, source_target_pairs={{0,4},{4,0},{8,12},{12,8},{16,20},{20,16},{24,28},{28,24},{1,5},{5... | collective-permute-start | bytes 221192 | tf_op jit(solution)/shard_map/ppermute | solution.py:599

commit v16 on v15

--- a/solution.py
+++ b/solution.py
@@ -126,12 +126,13 @@
         copy.wait()
     tzs = [tz[z] for z in range(depth)]
     gs, invs, first, final, coefs = factors(tzs, [store[z] for z in range(depth)])
+    row = lax.div(where, long)
+    kf, kl = pick([jnp.concatenate(first, 0), jnp.concatenate(final, 0)], row, hot)
     for copy in copies[5:]:
         copy.wait()
     for z in range(depth):
         pres[z] = wts[0, z] * rhs[0, z] + wts[1, z] * rhs[1, z] + wts[2, z] * rhs[2, z]
-    tables = [pres[...].reshape(depth * width, long), jnp.concatenate(first, 0), jnp.concatenate(final, 0)]
-    found, kf, kl = pick(tables, lax.div(where, long), hot)
+    (found,) = pick([pres[...].reshape(depth * width, long)], row, hot)
     both = jnp.concatenate([prod[...] * found, front[...].astype(F32), where.astype(F32)], 1)
     send[...] = jnp.broadcast_to(both[:, None], send.shape)
     y = local_solve([pres[z] for z in range(depth)], gs, invs, tzs)
@@ -546,7 +547,7 @@
             image[c, z] = total - image[c, z]
 
 
-def image_kernel(part, outer, row_two, row_one, inner, rhs, tz, tx, image, send):
+def image_kernel(part, inner, outer, row_two, row_one, rhs, tz, tx, image, send):
     depth, width = part.shape[1:3]
     right, odd = (is_right(0), is_right(0, "tile"))
     row = iota(part.shape[2:], 0)
@@ -721,7 +722,7 @@
     image, send = call(
         image_kernel,
         (vmem(rhs.shape), vmem((devices, 1, 128))),
-        (part, outer, row_two, row_one, inner, rhs, tz, tx),
+        (part, inner, outer, row_two, row_one, rhs, tz, tx),
     )
     sums = everywhere(send)
     update, lin_res, ratio = call(

time: 66.2 us -> 65.7 us (level)
  starting transfers between devices: 18.4 us -> 16.8 us
  blocking collectives: 10.8 us -> 11.8 us
    ppermute x5, starting transfers between devices: 6.76 us -> 5.19 us  [flip(): lax.ppermute(x, axis, [(i, i ^ 1 << level) for i in range(lax.axis_size(a...]
    all_to_all x1, blocking collectives: 10.8 us -> 11.8 us  [everywhere(): return lax.all_to_all(x, BOTH, split_axis=0, concat_axis=0, tiled=True)]
where the time goes in v16:
time: 65.7 us; the launch traced here: 65.3 us
  Pallas kernels  21.3 us (32%)
  starting transfers between devices  16.8 us (26%)
  waiting for transfers between devices  13.5 us (21%)
  blocking collectives  11.8 us (18%)
  local copies, waits for them, and re-layouts  1.17 us (2%)
  between operations  0.78 us (1%)
    pallas_call x8, Pallas kernels, call(): pl.pallas_call(functools.partial(staged, kernel, where, len(outs), tuple(...  13.2 us
    all_to_all x1, blocking collectives, everywhere(): return lax.all_to_all(x, BOTH, split_axis=0, concat_axis=0, tiled=True)  11.8 us
    all_to_all x2, starting transfers between devices, everywhere(): return lax.all_to_all(x, BOTH, split_axis=0, concat_axis=0, tiled=True)  9.63 us
    all_to_all x2, waiting for transfers between devices, everywhere(): return lax.all_to_all(x, BOTH, split_axis=0, concat_axis=0, tiled=True)  8.32 us
    ppermute x5, starting transfers between devices, flip(): lax.ppermute(x, axis, [(i, i ^ 1 << level) for i in range(lax.axis_size(a...  5.19 us
    ppermute x5, waiting for transfers between devices, flip(): lax.ppermute(x, axis, [(i, i ^ 1 << level) for i in range(lax.axis_size(a...  5.14 us
    pallas_call x1, Pallas kernels, shards(): pl.pallas_call(front_kernel, out_shape=vmem((devices, 1, max(rows + found...  4.97 us
    pallas_call x1, Pallas kernels, shards(): pl.pallas_call(pres_kernel, out_shape=(field, vmem((devices, 1, 3 * count...  3.14 us
  transfers between devices with their start and end apart: 10, of which 5 were waited for; matrix products, arithmetic and copies ran while one was open for 0% of the time, Pallas kernels for 22%

profile of v16, /device:TPU:0, one launch (start us, length us, event | category | flops | bytes accessed | tf_op | source)
XLA Modules:
  0.0 65.3 jit_solution(10424216610218511599)
XLA Ops:
  0.6 3.1 %shard_map.139 = (f32[3,16,2048]{2,1,0:T(8,128)S(1)}, f32[32,1,768]{2,1,0:T(1,128)}, f32[7,16,2048]{2,1,0:T(8,128)S(1)}) custom-call(s32[1,256]{1,0:T(1,128)} %bitcast.8, s32[1,256]{1,0:T(1,128)} %bitcast.10, f32[1,256]{1,0:T(1,128)} %bitcast.4, f32[3,3,16,2048]{3,2,1,0:T(8,128)} %refs_3_.3, f32[3,3,16,2048]{3,2,1,0:T(8,128)} %wts_in.1, ...), custom_call_target="tpu_custom_call" | custom-call | tf_op jit(solution)/shard_map/pallas_call | solution.py:628
  3.8 0.5 collective-permute-start
  4.3 7.0 %all-to-all-start = ((f32[32,1,768]{2,1,0:T(1,128)}), f32[32,1,768]{2,1,0:T(1,128)S(1)}, u32[]{:S(2)}, u32[]{:S(2)}) async-start(f32[32,1,768]{2,1,0:T(1,128)} %get-tuple-element.40), calls=%async_computation | async-start | bytes 196608 | tf_op jit(solution)/shard_map/all_to_all | solution.py:609
  11.3 0.0 collective-permute-done.refs_1_.refs_3_
  11.3 2.1 %shard_map.140 = (f32[12,16,2048]{2,1,0:T(8,128)S(1)}, f32[12,1,2048]{2,1,0:T(1,128)S(1)}, f32[12,1,2048]{2,1,0:T(1,128)S(1)}, f32[1,256]{1,0:T(1,128)S(1)}, f32[3,16,2048]{2,1,0:T(8,128)S(1)}) custom-call(f32[7,16,2048]{2,1,0:T(8,128)S(1)} %get-tuple-element.41.refs_0_, f32[7,16,2048]{2,1,0:T(8,128)S(1)} %collective-permute-done.refs_1_.refs_3_, ...), custom_call_target="tpu_custom_call" | custom-call | tf_op jit(solution)/shard_map/pallas_call | solution.py:62
  13.4 1.2 %copy-done = f32[12,16,2048]{2,1,0:T(8,128)} copy-done((f32[12,16,2048]{2,1,0:T(8,128)}, f32[12,16,2048]{2,1,0:T(8,128)S(1)}, u32[]{:S(2)}) %copy-start) | copy-done | bytes 1572888
  14.6 4.5 %all-to-all-done.recv.refs_1_ = f32[32,1,768]{2,1,0:T(1,128)S(1)} async-done(((f32[32,1,768]{2,1,0:T(1,128)}), f32[32,1,768]{2,1,0:T(1,128)S(1)}, u32[]{:S(2)}, u32[]{:S(2)}) %all-to-all-start) | async-done | bytes 98336 | tf_op jit(solution)/shard_map/all_to_all | solution.py:609
  19.1 0.3 collective-permute-start.1
  19.4 5.0 %shard_map.141 = f32[32,1,768]{2,1,0:T(1,128)} custom-call(f32[32,1,768]{2,1,0:T(1,128)S(1)} %all-to-all-done.recv.refs_1_, f32[1,256]{1,0:T(1,128)S(1)} %get-tuple-element.46.found, f32[256,8192]{1,0:T(8,128)} %inverse.1), custom_call_target="tpu_custom_call" | custom-call | tf_op jit(solution)/shard_map/pallas_call | solution.py:665
  24.4 2.7 %all-to-all-start.1 = ((f32[32,1,768]{2,1,0:T(1,128)}), f32[32,1,768]{2,1,0:T(1,128)S(1)}, u32[]{:S(2)}, u32[]{:S(2)}) async-start(f32[32,1,768]{2,1,0:T(1,128)} %shard_map.141), calls=%async_computation.1 | async-start | bytes 196608 | tf_op jit(solution)/shard_map/all_to_all | solution.py:609
  27.1 3.3 %collective-permute-done.1.refs_4_ = f32[3,16,2048]{2,1,0:T(8,128)S(1)} collective-permute-done((f32[3,16,2048]{2,1,0:T(8,128)S(1)}, f32[3,16,2048]{2,1,0:T(8,128)S(1)}, u32[]{:S(2)}, u32[]{:S(2)}) %collective-permute-start.1) | collective-permute-done | bytes 393248 | tf_op jit(solution)/shard_map/ppermute | solution.py:600
  30.3 0.1 shard_map.143
  30.4 0.7 %collective-permute-start.2 = (f32[23,1,2048]{2,1,0:T(1,128)S(1)}, f32[23,1,2048]{2,1,0:T(1,128)S(1)}, u32[]{:S(2)}, u32[]{:S(2)}) collective-permute-start(f32[23,1,2048]{2,1,0:T(1,128)S(1)} %shard_map.143), channel_id=1, source_target_pairs={{4,8},{12,16},{20,24},{8,4},{16,12},{24,20},{5,9},{13,17},{21,25},... | collective-permute-start | bytes 565256 | tf_op jit(solution)/shard_map/ppermute | solution.py:605
  31.1 3.8 %all-to-all-done.1.refs_0_ = f32[32,1,768]{2,1,0:T(1,128)S(1)} async-done(((f32[32,1,768]{2,1,0:T(1,128)}), f32[32,1,768]{2,1,0:T(1,128)S(1)}, u32[]{:S(2)}, u32[]{:S(2)}) %all-to-all-start.1) | async-done | bytes 98336 | tf_op jit(solution)/shard_map/all_to_all | solution.py:609
  34.9 2.8 %shard_map.142 = (f32[3,16,2048]{2,1,0:T(8,128)S(1)}, f32[3,16,2048]{2,1,0:T(8,128)S(1)}, f32[3,1,2048]{2,1,0:T(1,128)S(1)}, f32[3,16,2048]{2,1,0:T(8,128)S(1)},...) custom-call(f32[32,1,768]{2,1,0:T(1,128)S(1)} %all-to-all-done.1.refs_0_, ...), custom_call_target="tpu_custom_call" | custom-call | tf_op jit(solution)/shard_map/pallas_call | solution.py:62
  37.7 0.7 %collective-permute-start.3 = (f32[3,1,2048]{2,1,0:T(1,128)S(1)}, f32[3,1,2048]{2,1,0:T(1,128)S(1)}, u32[]{:S(2)}, u32[]{:S(2)}) collective-permute-start(f32[3,1,2048]{2,1,0:T(1,128)S(1)} %get-tuple-element.60), channel_id=1, source_target_pairs={{0,4},{4,0},{8,12},{12,8},{16,20},{20,16},{24,28},{28,24},{1,5},{5... | collective-permute-start | bytes 73736 | tf_op jit(solution)/shard_map/ppermute | solution.py:600
  38.4 0.0 collective-permute-done.2.refs_2_
  38.4 2.1 %shard_map.144 = (f32[3,1,2048]{2,1,0:T(1,128)S(1)}, f32[3,3,16,2048]{3,2,1,0:T(8,128)S(1)}, f32[3,3,16,2048]{3,2,1,0:T(8,128)S(1)}, f32[3,16,2048]{2,1,0:T(8,128)S(1)}) custom-call(f32[32,1,768]{2,1,0:T(1,128)S(1)} %all-to-all-done.1.refs_0_, f32[32,1,768]{2,1,0:T(1,128)S(1)} %all-to-all-done.recv.refs_1_, ...), custom_call_target="tpu_custom_call" | custom-call | tf_op jit(solution)/shard_map/pallas_call | solution.py:62
  40.5 1.1 %collective-permute-done.3.refs_3_ = f32[3,1,2048]{2,1,0:T(1,128)S(1)} collective-permute-done((f32[3,1,2048]{2,1,0:T(1,128)S(1)}, f32[3,1,2048]{2,1,0:T(1,128)S(1)}, u32[]{:S(2)}, u32[]{:S(2)}) %collective-permute-start.3) | collective-permute-done | bytes 24608 | tf_op jit(solution)/shard_map/ppermute | solution.py:600
  41.6 0.9 %shard_map.145 = (f32[3,3,16,2048]{3,2,1,0:T(8,128)S(1)}, f32[3,16,2048]{2,1,0:T(8,128)S(1)}, f32[3,3,1,2048]{3,2,1,0:T(1,128)S(1)}, f32[3,3,1,2048]{3,2,1,0:T(1,128)S(1)}, f32[3,16,2048]{2,1,0:T(8,128)S(1)}) custom-call(f32[3,16,2048]{2,1,0:T(8,128)S(1)} %get-tuple-element.52.refs_0_, f32[3,16,2048]{2,1,0:T(8,128)S(1)} %get-tuple-element.53.refs_1_, ...), custom_call_target="tpu_custom_call" | custom-call | tf_op jit(solution)/shard_map/pallas_call | solution.py:62
  42.5 0.1 collective-permute-start.4
  42.6 0.7 %collective-permute-start.5 = (f32[3,16,2048]{2,1,0:T(8,128)S(1)}, f32[3,16,2048]{2,1,0:T(8,128)S(1)}, u32[]{:S(2)}, u32[]{:S(2)}) collective-permute-start(f32[3,16,2048]{2,1,0:T(8,128)S(1)} %get-tuple-element.69), channel_id=1, source_target_pairs={{1,2},{2,1},{5,6},{6,5},{9,10},{10,9},{13,14},{14,13},{17,18},{18,... | collective-permute-start | bytes 1179656 | tf_op jit(solution)/shard_map/ppermute | solution.py:605
  43.3 0.7 %collective-permute-start.6 = (f32[3,3,1,2048]{3,2,1,0:T(1,128)S(1)}, f32[3,3,1,2048]{3,2,1,0:T(1,128)S(1)}, u32[]{:S(2)}, u32[]{:S(2)}) collective-permute-start(f32[3,3,1,2048]{3,2,1,0:T(1,128)S(1)} %get-tuple-element.70), channel_id=1, source_target_pairs={{4,8},{12,16},{20,24},{8,4},{16,12},{24,20},{5,9},{13,17},{21,25},... | collective-permute-start | bytes 221192 | tf_op jit(solution)/shard_map/ppermute | solution.py:605
  44.0 3.5 %collective-permute-start.7 = (f32[3,3,1,2048]{3,2,1,0:T(1,128)S(1)}, f32[3,3,1,2048]{3,2,1,0:T(1,128)S(1)}, u32[]{:S(2)}, u32[]{:S(2)}) collective-permute-start(f32[3,3,1,2048]{3,2,1,0:T(1,128)S(1)} %get-tuple-element.71), channel_id=1, source_target_pairs={{0,4},{4,0},{8,12},{12,8},{16,20},{20,16},{24,28},{28,24},{1,5},{5... | collective-permute-start | bytes 221192 | tf_op jit(solution)/shard_map/ppermute | solution.py:600
  47.5 2.4 %shard_map.146.refs_0_ = f32[3,3,16,2048]{3,2,1,0:T(8,128)S(1)} custom-call(f32[3,3,16,2048]{3,2,1,0:T(8,128)S(1)} %get-tuple-element.67.refs_0_.refs_1_, f32[3,3,3,16,2048]{4,3,2,1,0:T(8,128)} %refs_1_.1, f32[3,16,2048]{2,1,0:T(8,128)S(1)} %get-tuple-element.63.refs_6_.refs_2_, f32[3,16,2048]{2,1,0:T(8,128)S(1)} %get-tuple-element.61.refs_4_.refs_3_.refs_7_, ...), custom_call_target="tpu_custom_call" | custom-call | tf_op jit(solution)/shard_map/pallas_call | solution.py:62
  49.9 0.0 collective-permute-done.6.refs_3_
  49.9 0.8 %collective-permute-done.7.refs_4_ = f32[3,3,1,2048]{3,2,1,0:T(1,128)S(1)} collective-permute-done((f32[3,3,1,2048]{3,2,1,0:T(1,128)S(1)}, f32[3,3,1,2048]{3,2,1,0:T(1,128)S(1)}, u32[]{:S(2)}, u32[]{:S(2)}) %collective-permute-start.7) | collective-permute-done | bytes 73760 | tf_op jit(solution)/shard_map/ppermute | solution.py:600
  50.7 0.0 collective-permute-done.4.refs_1_
  50.7 0.0 collective-permute-done.5.refs_2_
  50.7 1.2 %shard_map.147 = (f32[3,3,16,2048]{3,2,1,0:T(8,128)S(1)}, f32[32,1,128]{2,1,0:T(1,128)S(1)}) custom-call(f32[3,3,16,2048]{3,2,1,0:T(8,128)S(1)} %shard_map.146.refs_0_, f32[3,16,2048]{2,1,0:T(8,128)S(1)} %collective-permute-done.4.refs_1_, f32[3,16,2048]{2,1,0:T(8,128)S(1)} %collective-permute-done.5.refs_2_, ...), custom_call_target="tpu_custom_call" | custom-call | tf_op jit(solution)/shard_map/pallas_call | solution.py:62
  51.9 11.8 %all_to_all.15.refs_0_ = f32[32,1,128]{2,1,0:T(1,128)S(1)} all-to-all(f32[32,1,128]{2,1,0:T(1,128)S(1)} %get-tuple-element.72), channel_id=1, replica_groups=mesh['tile'=8,'layer'=4] {'tile','layer'}, dimensions={0} | all-to-all | bytes 32768 | tf_op jit(solution)/shard_map/all_to_all | solution.py:609
  63.7 1.7 %shard_map.148 = (f32[3,3,16,2048]{3,2,1,0:T(8,128)}, f32[3,3,16,2048]{3,2,1,0:T(8,128)}, f32[1,1]{1,0:T(1,128)}) custom-call(f32[32,1,128]{2,1,0:T(1,128)S(1)} %all_to_all.15.refs_0_, f32[3,3,16,2048]{3,2,1,0:T(8,128)S(1)} %get-tuple-element.67.refs_0_.refs_1_, f32[3,3,16,2048]{3,2,1,0:T(8,128)S(1)} %get-tuple-element.73.refs_2_, ...), custom_call_target="tpu_custom_call" | custom-call | tf_op jit(solution)/shard_map/pallas_call | solution.py:62
  (3 shorter events, 0.0 us)
Async XLA Ops:
  3.8 7.5 %collective-permute-start = (f32[7,16,2048]{2,1,0:T(8,128)S(1)}, f32[7,16,2048]{2,1,0:T(8,128)S(1)}, u32[]{:S(2)}, u32[]{:S(2)}) collective-permute-start(f32[7,16,2048]{2,1,0:T(8,128)S(1)} %get-tuple-element.41.refs_0_), channel_id=1, source_target_pairs={{0,1},{1,0},{2,3},{3,2},{4,5},{5,4},{6,7},{7,6},{8,9},{9,8},{10,11... | collective-permute-start | bytes 2752520 | tf_op jit(solution)/shard_map/ppermute | solution.py:600
  4.3 14.8 %all-to-all-start = ((f32[32,1,768]{2,1,0:T(1,128)}), f32[32,1,768]{2,1,0:T(1,128)S(1)}, u32[]{:S(2)}, u32[]{:S(2)}) async-start(f32[32,1,768]{2,1,0:T(1,128)} %get-tuple-element.40), calls=%async_computation | async-start | bytes 196608 | tf_op jit(solution)/shard_map/all_to_all | solution.py:609
  13.4 1.2 %copy-start = (f32[12,16,2048]{2,1,0:T(8,128)}, f32[12,16,2048]{2,1,0:T(8,128)S(1)}, u32[]{:S(2)}) copy-start(f32[12,16,2048]{2,1,0:T(8,128)S(1)} %get-tuple-element.51.refs_6_) | copy-start | bytes 4718596
  19.1 11.3 %copy-start.1 = (f32[256]{0:T(256)S(1)}, f32[256]{0:T(256)}, u32[]{:S(2)}) copy-start(f32[256]{0:T(256)} %param.22) | copy-start | bytes 3076
  19.1 11.3 %collective-permute-start.1 = (f32[3,16,2048]{2,1,0:T(8,128)S(1)}, f32[3,16,2048]{2,1,0:T(8,128)S(1)}, u32[]{:S(2)}, u32[]{:S(2)}) collective-permute-start(f32[3,16,2048]{2,1,0:T(8,128)S(1)} %get-tuple-element.50), channel_id=1, source_target_pairs={{0,2},{1,3},{2,0},{3,1},{4,6},{5,7},{6,4},{7,5},{8,10},{9,11},{10,... | collective-permute-start | bytes 1179656 | tf_op jit(solution)/shard_map/ppermute | solution.py:600
  24.4 10.5 %all-to-all-start.1 = ((f32[32,1,768]{2,1,0:T(1,128)}), f32[32,1,768]{2,1,0:T(1,128)S(1)}, u32[]{:S(2)}, u32[]{:S(2)}) async-start(f32[32,1,768]{2,1,0:T(1,128)} %shard_map.141), calls=%async_computation.1 | async-start | bytes 196608 | tf_op jit(solution)/shard_map/all_to_all | solution.py:609
  30.4 8.0 %collective-permute-start.2 = (f32[23,1,2048]{2,1,0:T(1,128)S(1)}, f32[23,1,2048]{2,1,0:T(1,128)S(1)}, u32[]{:S(2)}, u32[]{:S(2)}) collective-permute-start(f32[23,1,2048]{2,1,0:T(1,128)S(1)} %shard_map.143), channel_id=1, source_target_pairs={{4,8},{12,16},{20,24},{8,4},{16,12},{24,20},{5,9},{13,17},{21,25},... | collective-permute-start | bytes 565256 | tf_op jit(solution)/shard_map/ppermute | solution.py:605
  37.7 3.9 %collective-permute-start.3 = (f32[3,1,2048]{2,1,0:T(1,128)S(1)}, f32[3,1,2048]{2,1,0:T(1,128)S(1)}, u32[]{:S(2)}, u32[]{:S(2)}) collective-permute-start(f32[3,1,2048]{2,1,0:T(1,128)S(1)} %get-tuple-element.60), channel_id=1, source_target_pairs={{0,4},{4,0},{8,12},{12,8},{16,20},{20,16},{24,28},{28,24},{1,5},{5... | collective-permute-start | bytes 73736 | tf_op jit(solution)/shard_map/ppermute | solution.py:600
  42.5 8.2 %collective-permute-start.4 = (f32[3,16,2048]{2,1,0:T(8,128)S(1)}, f32[3,16,2048]{2,1,0:T(8,128)S(1)}, u32[]{:S(2)}, u32[]{:S(2)}) collective-permute-start(f32[3,16,2048]{2,1,0:T(8,128)S(1)} %get-tuple-element.68), channel_id=1, source_target_pairs={{0,1},{1,0},{2,3},{3,2},{4,5},{5,4},{6,7},{7,6},{8,9},{9,8},{10,11... | collective-permute-start | bytes 1179656 | tf_op jit(solution)/shard_map/ppermute | solution.py:600
  42.6 8.1 %collective-permute-start.5 = (f32[3,16,2048]{2,1,0:T(8,128)S(1)}, f32[3,16,2048]{2,1,0:T(8,128)S(1)}, u32[]{:S(2)}, u32[]{:S(2)}) collective-permute-start(f32[3,16,2048]{2,1,0:T(8,128)S(1)} %get-tuple-element.69), channel_id=1, source_target_pairs={{1,2},{2,1},{5,6},{6,5},{9,10},{10,9},{13,14},{14,13},{17,18},{18,... | collective-permute-start | bytes 1179656 | tf_op jit(solution)/shard_map/ppermute | solution.py:605
  43.3 6.6 %collective-permute-start.6 = (f32[3,3,1,2048]{3,2,1,0:T(1,128)S(1)}, f32[3,3,1,2048]{3,2,1,0:T(1,128)S(1)}, u32[]{:S(2)}, u32[]{:S(2)}) collective-permute-start(f32[3,3,1,2048]{3,2,1,0:T(1,128)S(1)} %get-tuple-element.70), channel_id=1, source_target_pairs={{4,8},{12,16},{20,24},{8,4},{16,12},{24,20},{5,9},{13,17},{21,25},... | collective-permute-start | bytes 221192 | tf_op jit(solution)/shard_map/ppermute | solution.py:605
  44.0 6.7 %collective-permute-start.7 = (f32[3,3,1,2048]{3,2,1,0:T(1,128)S(1)}, f32[3,3,1,2048]{3,2,1,0:T(1,128)S(1)}, u32[]{:S(2)}, u32[]{:S(2)}) collective-permute-start(f32[3,3,1,2048]{3,2,1,0:T(1,128)S(1)} %get-tuple-element.71), channel_id=1, source_target_pairs={{0,4},{4,0},{8,12},{12,8},{16,20},{20,16},{24,28},{28,24},{1,5},{5... | collective-permute-start | bytes 221192 | tf_op jit(solution)/shard_map/ppermute | solution.py:600

commit v17 on v16

--- a/solution.py
+++ b/solution.py
@@ -23,7 +23,7 @@
     return pltpu.VMEM(shape, dtype)
 
 
-def staged(kernel, where, outs, kept, column, late, *refs):
+def staged(kernel, where, outs, kept, column, cut, late, *refs):
     count, sems = (len(where), refs[-1])
     held = list(refs[count + outs + len(kept) : -1])
     target_count = sum(where) - len(kept)
@@ -33,7 +33,7 @@
     for i, far in enumerate(where):
         if far:
             to = target[i] if i in target else held.pop(0)
-            part = refs[i].at[:, 0] if i in column else refs[i]
+            part = refs[i].at[:, 0] if i in column else refs[i].at[cut[i][0] : cut[i][1]] if i in cut else refs[i]
             copies.append(pltpu.make_async_copy(part, to, sems.at[len(copies)]))
             operands.append(to)
         else:
@@ -54,13 +54,14 @@
     kernel(*more, *operands, *refs[count : count + outs], *extra)
 
 
-def call(kernel, outs, args, far=(), keep=(), column=(), late=(), scratch=(), limit=LIMIT):
+def call(kernel, outs, args, far=(), keep=(), column=(), cut={}, late=(), scratch=(), limit=LIMIT):
     where = [i in far for i in range(len(args))]
     spaces = [pltpu.HBM if w else pltpu.VMEM for w in where]
     shapes = [a.shape[:1] + a.shape[2:] if i in column else a.shape for i, a in enumerate(args)]
+    shapes = [(cut[i][1] - cut[i][0], *a[1:]) if i in cut else a for i, a in enumerate(shapes)]
     every = (*outs, *(vmem(shapes[i], args[i].dtype) for i in keep))
     return pl.pallas_call(
-        functools.partial(staged, kernel, where, len(outs), tuple(keep), tuple(column), tuple(late)),
+        functools.partial(staged, kernel, where, len(outs), tuple(keep), tuple(column), cut, tuple(late)),
         out_shape=every,
         in_specs=[pl.BlockSpec(memory_space=s) for s in spaces],
         out_specs=(VM,) * len(every),
@@ -285,19 +286,19 @@
     parts = [p.astype(F32) for p in split(terms)[:PARTS]]
     row_of = iota((length // lanes, count), 0).astype(F32)
     lane_of = iota((lanes, count), 0).astype(F32)
-    total = jnp.zeros((length // lanes, lanes), F32)
+    flipped = jnp.zeros((lanes, PARTS * (length // lanes)), F32)
     for d in range(devices):
         hit = row_of == high[d : d + 1]
         left = jnp.concatenate([jnp.where(hit, p[d : d + 1], 0.0).astype(BF16) for p in parts], 0)
         right = jnp.where(lane_of == low[d : d + 1], 1.0, 0.0).astype(BF16)
-        total = total + fold(dot_nt(left, right), PARTS)
+        flipped = flipped + dot_nt(right, left)
+    total = fold(jnp.transpose(flipped), PARTS)
     acc = jnp.zeros((rows, lanes), F32)
     for i in range(chunks):
         copies[i].wait()
         for r in range(i * wide // lanes, (i + 1) * wide // lanes):
             acc = acc + held[:, r * lanes : (r + 1) * lanes] * total[r : r + 1]
-    parts = jnp.concatenate(split(acc), 1)
-    out = dot_nt(jnp.ones((8, parts.shape[1]), BF16), parts)
+    out = jnp.transpose(jnp.broadcast_to(jnp.sum(acc, axis=1, keepdims=True), (rows, lanes)))
     pad = send.shape[2] - out.shape[1] - found.shape[1]
     pieces = [out[0:1], found] + ([jnp.zeros((1, pad), F32)] if pad else [])
     send[...] = jnp.broadcast_to(jnp.concatenate(pieces, 1)[:, None], send.shape)
@@ -470,7 +471,7 @@
     two[at + 1, :, : prod.shape[1]] = prod[...]
 
 
-def first_three(kernel, ready, one, two, three, _rhs, _diag, _ty, *rest):
+def first_three(kernel, ready, one, two, three, _rhs, _diag, _ty, _binv, *rest):
     kernel(one, two, three, *rest)
     ready(0)
 
@@ -505,7 +506,7 @@
         row[z] = jnp.where(odd, found, found * two[3 * depth + z])
 
 
-def search_kernel(p, coupled_z, two, one, tx, ty, tz, rhs, column, binv, s, outer, row_two, row_one, inner):
+def search_kernel(p, coupled_z, two, one, tx, ty, tz, rhs, column, first_inv, later_inv, s, outer, row_two, row_one, inner):
     depth, width, _ = p.shape
     odd = is_right(0, "tile")
     right = is_right(0)
@@ -519,7 +520,8 @@
         remain = [rhs[c, z] - column[c, z] * centre for c in range(3)]
         remain[0] = remain[0] + coupled
         for c in range(3):
-            value = binv[c, 0, z] * remain[0] + binv[c, 1, z] * remain[1] + binv[c, 2, z] * remain[2]
+            binv = [later_inv[c - 1, d, z] if c else first_inv[0, d, z] for d in range(3)]
+            value = binv[0] * remain[0] + binv[1] * remain[1] + binv[2] * remain[2]
             if c == 0:
                 value = centre + value
             s[c, z] = value
@@ -688,25 +690,27 @@
 
     at = 3 + levels
     row3 = vmem((depth, 1, long))
-    p, coupled_z, one, tz, tx, block_inv = call(
+    p, coupled_z, one, tz, tx, later_inv = call(
         functools.partial(pressure_kernel, levels),
         (field, field, row3),
         (sol, terms, pres, *sib, tz, kept, tx, prod, block_inv),
         far=range(at, at + 5),
         keep=(at, at + 2, at + 4),
+        cut={at + 4: (1, 3)},
         late=(range(at, at + 4), (at + 4,)),
         scratch=hots(width),
     )
     sol, one, terms = lax.optimization_barrier((sol, one, terms))
     one = flip(one, 0, "tile")
-    two, rhs, first_column, ty = call(
+    two, rhs, first_column, ty, first_inv = call(
         functools.partial(first_three, functools.partial(beyond_kernel, levels, sizes, (depth, width, long))),
         (row3,),
-        (sol, terms, two, rhs, block_diag, ty),
-        far=(3, 4, 5),
-        keep=(3, 4, 5),
+        (sol, terms, two, rhs, block_diag, ty, block_inv),
+        far=(3, 4, 5, 6),
+        keep=(3, 4, 5, 6),
         column=(4,),
-        late=((3, 4, 5),),
+        cut={6: (0, 1)},
+        late=((3, 4, 5, 6),),
         scratch=hots(1),
     )
     row9 = vmem((3, depth, 1, long))
@@ -714,7 +718,7 @@
     s, outer, row_two, row_one, inner = call(
         search_kernel,
         (vmem(rhs.shape), plane3, row9, row9, plane3),
-        (p, coupled_z, two, one, tx, ty, tz, rhs, first_column, block_inv),
+        (p, coupled_z, two, one, tx, ty, tz, rhs, first_column, first_inv, later_inv),
     )
     outer, row_two = (neighbour(outer), neighbour(row_two, "tile"))
     row_one, inner = (flip(row_one, 0, "tile"), flip(inner, 0))

time: 65.7 us -> 65.8 us (level)
  no operation moved by 1% of the time
where the time goes in v17:
time: 65.8 us; the launch traced here: 65.4 us
  Pallas kernels  21.6 us (33%)
  starting transfers between devices  16.9 us (26%)
  waiting for transfers between devices  13.1 us (20%)
  blocking collectives  11.8 us (18%)
  local copies, waits for them, and re-layouts  1.17 us (2%)
  between operations  0.78 us (1%)
    pallas_call x8, Pallas kernels, call(): pl.pallas_call(functools.partial(staged, kernel, where, len(outs), tuple(...  13.6 us
    all_to_all x1, blocking collectives, everywhere(): return lax.all_to_all(x, BOTH, split_axis=0, concat_axis=0, tiled=True)  11.8 us
    all_to_all x2, starting transfers between devices, everywhere(): return lax.all_to_all(x, BOTH, split_axis=0, concat_axis=0, tiled=True)  9.63 us
    all_to_all x2, waiting for transfers between devices, everywhere(): return lax.all_to_all(x, BOTH, split_axis=0, concat_axis=0, tiled=True)  8.24 us
    ppermute x5, starting transfers between devices, flip(): lax.ppermute(x, axis, [(i, i ^ 1 << level) for i in range(lax.axis_size(a...  5.28 us
    pallas_call x1, Pallas kernels, shards(): pl.pallas_call(front_kernel, out_shape=vmem((devices, 1, max(rows + found...  4.9 us
    ppermute x5, waiting for transfers between devices, flip(): lax.ppermute(x, axis, [(i, i ^ 1 << level) for i in range(lax.axis_size(a...  4.87 us
    pallas_call x1, Pallas kernels, shards(): pl.pallas_call(pres_kernel, out_shape=(field, vmem((devices, 1, 3 * count...  3.14 us
  transfers between devices with their start and end apart: 10, of which 5 were waited for; matrix products, arithmetic and copies ran while one was open for 0% of the time, Pallas kernels for 22%

profile of v17, /device:TPU:0, one launch (start us, length us, event | category | flops | bytes accessed | tf_op | source)
XLA Modules:
  0.0 65.4 jit_solution(17133058687910294411)
XLA Ops:
  0.6 3.1 %shard_map.139 = (f32[3,16,2048]{2,1,0:T(8,128)S(1)}, f32[32,1,768]{2,1,0:T(1,128)}, f32[7,16,2048]{2,1,0:T(8,128)S(1)}) custom-call(s32[1,256]{1,0:T(1,128)} %bitcast.8, s32[1,256]{1,0:T(1,128)} %bitcast.10, f32[1,256]{1,0:T(1,128)} %bitcast.4, f32[3,3,16,2048]{3,2,1,0:T(8,128)} %refs_3_.3, f32[3,3,16,2048]{3,2,1,0:T(8,128)} %wts_in.1, ...), custom_call_target="tpu_custom_call" | custom-call | tf_op jit(solution)/shard_map/pallas_call | solution.py:630
  3.8 0.5 collective-permute-start
  4.3 7.0 %all-to-all-start = ((f32[32,1,768]{2,1,0:T(1,128)}), f32[32,1,768]{2,1,0:T(1,128)S(1)}, u32[]{:S(2)}, u32[]{:S(2)}) async-start(f32[32,1,768]{2,1,0:T(1,128)} %get-tuple-element.41), calls=%async_computation | async-start | bytes 196608 | tf_op jit(solution)/shard_map/all_to_all | solution.py:611
  11.3 0.0 collective-permute-done.refs_1_.refs_3_
  11.3 2.1 %shard_map.140 = (f32[12,16,2048]{2,1,0:T(8,128)S(1)}, f32[12,1,2048]{2,1,0:T(1,128)S(1)}, f32[12,1,2048]{2,1,0:T(1,128)S(1)}, f32[1,256]{1,0:T(1,128)S(1)}, f32[3,16,2048]{2,1,0:T(8,128)S(1)}) custom-call(f32[7,16,2048]{2,1,0:T(8,128)S(1)} %get-tuple-element.42.refs_0_, f32[7,16,2048]{2,1,0:T(8,128)S(1)} %collective-permute-done.refs_1_.refs_3_, ...), custom_call_target="tpu_custom_call" | custom-call | tf_op jit(solution)/shard_map/pallas_call | solution.py:63
  13.4 1.2 %copy-done = f32[12,16,2048]{2,1,0:T(8,128)} copy-done((f32[12,16,2048]{2,1,0:T(8,128)}, f32[12,16,2048]{2,1,0:T(8,128)S(1)}, u32[]{:S(2)}) %copy-start) | copy-done | bytes 1572888
  14.6 4.5 %all-to-all-done.recv.refs_1_ = f32[32,1,768]{2,1,0:T(1,128)S(1)} async-done(((f32[32,1,768]{2,1,0:T(1,128)}), f32[32,1,768]{2,1,0:T(1,128)S(1)}, u32[]{:S(2)}, u32[]{:S(2)}) %all-to-all-start) | async-done | bytes 98336 | tf_op jit(solution)/shard_map/all_to_all | solution.py:611
  19.1 0.3 collective-permute-start.1
  19.4 4.9 %shard_map.141 = f32[32,1,768]{2,1,0:T(1,128)} custom-call(f32[32,1,768]{2,1,0:T(1,128)S(1)} %all-to-all-done.recv.refs_1_, f32[1,256]{1,0:T(1,128)S(1)} %get-tuple-element.47.found, f32[256,8192]{1,0:T(8,128)} %inverse.1), custom_call_target="tpu_custom_call" | custom-call | tf_op jit(solution)/shard_map/pallas_call | solution.py:667
  24.3 2.7 %all-to-all-start.1 = ((f32[32,1,768]{2,1,0:T(1,128)}), f32[32,1,768]{2,1,0:T(1,128)S(1)}, u32[]{:S(2)}, u32[]{:S(2)}) async-start(f32[32,1,768]{2,1,0:T(1,128)} %shard_map.141), calls=%async_computation.1 | async-start | bytes 196608 | tf_op jit(solution)/shard_map/all_to_all | solution.py:611
  27.0 3.3 %collective-permute-done.1.refs_4_ = f32[3,16,2048]{2,1,0:T(8,128)S(1)} collective-permute-done((f32[3,16,2048]{2,1,0:T(8,128)S(1)}, f32[3,16,2048]{2,1,0:T(8,128)S(1)}, u32[]{:S(2)}, u32[]{:S(2)}) %collective-permute-start.1) | collective-permute-done | bytes 393248 | tf_op jit(solution)/shard_map/ppermute | solution.py:602
  30.3 0.1 shard_map.143
  30.4 0.7 %collective-permute-start.2 = (f32[23,1,2048]{2,1,0:T(1,128)S(1)}, f32[23,1,2048]{2,1,0:T(1,128)S(1)}, u32[]{:S(2)}, u32[]{:S(2)}) collective-permute-start(f32[23,1,2048]{2,1,0:T(1,128)S(1)} %shard_map.143), channel_id=1, source_target_pairs={{4,8},{12,16},{20,24},{8,4},{16,12},{24,20},{5,9},{13,17},{21,25},... | collective-permute-start | bytes 565256 | tf_op jit(solution)/shard_map/ppermute | solution.py:607
  31.1 3.7 %all-to-all-done.1.refs_0_ = f32[32,1,768]{2,1,0:T(1,128)S(1)} async-done(((f32[32,1,768]{2,1,0:T(1,128)}), f32[32,1,768]{2,1,0:T(1,128)S(1)}, u32[]{:S(2)}, u32[]{:S(2)}) %all-to-all-start.1) | async-done | bytes 98336 | tf_op jit(solution)/shard_map/all_to_all | solution.py:611
  34.8 2.8 %shard_map.142 = (f32[3,16,2048]{2,1,0:T(8,128)S(1)}, f32[3,16,2048]{2,1,0:T(8,128)S(1)}, f32[3,1,2048]{2,1,0:T(1,128)S(1)}, f32[3,16,2048]{2,1,0:T(8,128)S(1)},...) custom-call(f32[32,1,768]{2,1,0:T(1,128)S(1)} %all-to-all-done.1.refs_0_, ...), custom_call_target="tpu_custom_call" | custom-call | tf_op jit(solution)/shard_map/pallas_call | solution.py:63
  37.6 0.8 %collective-permute-start.3 = (f32[3,1,2048]{2,1,0:T(1,128)S(1)}, f32[3,1,2048]{2,1,0:T(1,128)S(1)}, u32[]{:S(2)}, u32[]{:S(2)}) collective-permute-start(f32[3,1,2048]{2,1,0:T(1,128)S(1)} %get-tuple-element.61), channel_id=1, source_target_pairs={{0,4},{4,0},{8,12},{12,8},{16,20},{20,16},{24,28},{28,24},{1,5},{5... | collective-permute-start | bytes 73736 | tf_op jit(solution)/shard_map/ppermute | solution.py:602
  38.4 0.0 collective-permute-done.2.refs_2_
  38.4 2.5 %shard_map.144 = (f32[3,1,2048]{2,1,0:T(1,128)S(1)}, f32[3,3,16,2048]{3,2,1,0:T(8,128)S(1)}, f32[3,3,16,2048]{3,2,1,0:T(8,128)S(1)}, f32[3,16,2048]{2,1,0:T(8,128)S(1)}, f32[1,3,3,16,2048]{4,3,2,1,0:T(8,128)S(1)}) custom-call(f32[32,1,768]{2,1,0:T(1,128)S(1)} %all-to-all-done.1.refs_0_, f32[32,1,768]{2,1,0:T(1,128)S(1)} %all-to-all-done.recv.refs_1_, ...), custom_call_target="tpu_custom_call" | custom-call | tf_op jit(solution)/shard_map/pallas_call | solution.py:63
  40.9 0.6 collective-permute-done.3.refs_3_
  41.5 0.9 %shard_map.145 = (f32[3,3,16,2048]{3,2,1,0:T(8,128)S(1)}, f32[3,16,2048]{2,1,0:T(8,128)S(1)}, f32[3,3,1,2048]{3,2,1,0:T(1,128)S(1)}, f32[3,3,1,2048]{3,2,1,0:T(1,128)S(1)}, f32[3,16,2048]{2,1,0:T(8,128)S(1)}) custom-call(f32[3,16,2048]{2,1,0:T(8,128)S(1)} %get-tuple-element.53.refs_0_, f32[3,16,2048]{2,1,0:T(8,128)S(1)} %get-tuple-element.54.refs_1_, ...), custom_call_target="tpu_custom_call" | custom-call | tf_op jit(solution)/shard_map/pallas_call | solution.py:63
  42.4 0.1 collective-permute-start.4
  42.5 0.7 %collective-permute-start.5 = (f32[3,16,2048]{2,1,0:T(8,128)S(1)}, f32[3,16,2048]{2,1,0:T(8,128)S(1)}, u32[]{:S(2)}, u32[]{:S(2)}) collective-permute-start(f32[3,16,2048]{2,1,0:T(8,128)S(1)} %get-tuple-element.71), channel_id=1, source_target_pairs={{1,2},{2,1},{5,6},{6,5},{9,10},{10,9},{13,14},{14,13},{17,18},{18,... | collective-permute-start | bytes 1179656 | tf_op jit(solution)/shard_map/ppermute | solution.py:607
  43.2 0.7 %collective-permute-start.6 = (f32[3,3,1,2048]{3,2,1,0:T(1,128)S(1)}, f32[3,3,1,2048]{3,2,1,0:T(1,128)S(1)}, u32[]{:S(2)}, u32[]{:S(2)}) collective-permute-start(f32[3,3,1,2048]{3,2,1,0:T(1,128)S(1)} %get-tuple-element.72), channel_id=1, source_target_pairs={{4,8},{12,16},{20,24},{8,4},{16,12},{24,20},{5,9},{13,17},{21,25},... | collective-permute-start | bytes 221192 | tf_op jit(solution)/shard_map/ppermute | solution.py:607
  43.9 3.5 %collective-permute-start.7 = (f32[3,3,1,2048]{3,2,1,0:T(1,128)S(1)}, f32[3,3,1,2048]{3,2,1,0:T(1,128)S(1)}, u32[]{:S(2)}, u32[]{:S(2)}) collective-permute-start(f32[3,3,1,2048]{3,2,1,0:T(1,128)S(1)} %get-tuple-element.73), channel_id=1, source_target_pairs={{0,4},{4,0},{8,12},{12,8},{16,20},{20,16},{24,28},{28,24},{1,5},{5... | collective-permute-start | bytes 221192 | tf_op jit(solution)/shard_map/ppermute | solution.py:602
  47.4 2.4 %shard_map.146.refs_0_ = f32[3,3,16,2048]{3,2,1,0:T(8,128)S(1)} custom-call(f32[3,3,16,2048]{3,2,1,0:T(8,128)S(1)} %get-tuple-element.69.refs_0_.refs_1_, f32[3,3,3,16,2048]{4,3,2,1,0:T(8,128)} %refs_1_.1, f32[3,16,2048]{2,1,0:T(8,128)S(1)} %get-tuple-element.64.refs_6_.refs_2_, f32[3,16,2048]{2,1,0:T(8,128)S(1)} %get-tuple-element.62.refs_4_.refs_3_.refs_7_, ...), custom_call_target="tpu_custom_call" | custom-call | tf_op jit(solution)/shard_map/pallas_call | solution.py:63
  49.8 0.0 collective-permute-done.6.refs_3_
  49.8 1.0 %collective-permute-done.7.refs_4_ = f32[3,3,1,2048]{3,2,1,0:T(1,128)S(1)} collective-permute-done((f32[3,3,1,2048]{3,2,1,0:T(1,128)S(1)}, f32[3,3,1,2048]{3,2,1,0:T(1,128)S(1)}, u32[]{:S(2)}, u32[]{:S(2)}) %collective-permute-start.7) | collective-permute-done | bytes 73760 | tf_op jit(solution)/shard_map/ppermute | solution.py:602
  50.8 0.0 collective-permute-done.4.refs_1_
  50.8 0.0 collective-permute-done.5.refs_2_
  50.8 1.2 %shard_map.147 = (f32[3,3,16,2048]{3,2,1,0:T(8,128)S(1)}, f32[32,1,128]{2,1,0:T(1,128)S(1)}) custom-call(f32[3,3,16,2048]{3,2,1,0:T(8,128)S(1)} %shard_map.146.refs_0_, f32[3,16,2048]{2,1,0:T(8,128)S(1)} %collective-permute-done.4.refs_1_, f32[3,16,2048]{2,1,0:T(8,128)S(1)} %collective-permute-done.5.refs_2_, ...), custom_call_target="tpu_custom_call" | custom-call | tf_op jit(solution)/shard_map/pallas_call | solution.py:63
  52.0 11.8 %all_to_all.15.refs_0_ = f32[32,1,128]{2,1,0:T(1,128)S(1)} all-to-all(f32[32,1,128]{2,1,0:T(1,128)S(1)} %get-tuple-element.74), channel_id=1, replica_groups=mesh['tile'=8,'layer'=4] {'tile','layer'}, dimensions={0} | all-to-all | bytes 32768 | tf_op jit(solution)/shard_map/all_to_all | solution.py:611
  63.8 1.7 %shard_map.148 = (f32[3,3,16,2048]{3,2,1,0:T(8,128)}, f32[3,3,16,2048]{3,2,1,0:T(8,128)}, f32[1,1]{1,0:T(1,128)}) custom-call(f32[32,1,128]{2,1,0:T(1,128)S(1)} %all_to_all.15.refs_0_, f32[3,3,16,2048]{3,2,1,0:T(8,128)S(1)} %get-tuple-element.69.refs_0_.refs_1_, f32[3,3,16,2048]{3,2,1,0:T(8,128)S(1)} %get-tuple-element.75.refs_2_, ...), custom_call_target="tpu_custom_call" | custom-call | tf_op jit(solution)/shard_map/pallas_call | solution.py:63
  (3 shorter events, 0.0 us)
Async XLA Ops:
  3.8 7.5 %collective-permute-start = (f32[7,16,2048]{2,1,0:T(8,128)S(1)}, f32[7,16,2048]{2,1,0:T(8,128)S(1)}, u32[]{:S(2)}, u32[]{:S(2)}) collective-permute-start(f32[7,16,2048]{2,1,0:T(8,128)S(1)} %get-tuple-element.42.refs_0_), channel_id=1, source_target_pairs={{0,1},{1,0},{2,3},{3,2},{4,5},{5,4},{6,7},{7,6},{8,9},{9,8},{10,11... | collective-permute-start | bytes 2752520 | tf_op jit(solution)/shard_map/ppermute | solution.py:602
  4.3 14.8 %all-to-all-start = ((f32[32,1,768]{2,1,0:T(1,128)}), f32[32,1,768]{2,1,0:T(1,128)S(1)}, u32[]{:S(2)}, u32[]{:S(2)}) async-start(f32[32,1,768]{2,1,0:T(1,128)} %get-tuple-element.41), calls=%async_computation | async-start | bytes 196608 | tf_op jit(solution)/shard_map/all_to_all | solution.py:611
  13.4 1.2 %copy-start = (f32[12,16,2048]{2,1,0:T(8,128)}, f32[12,16,2048]{2,1,0:T(8,128)S(1)}, u32[]{:S(2)}) copy-start(f32[12,16,2048]{2,1,0:T(8,128)S(1)} %get-tuple-element.52.refs_6_) | copy-start | bytes 4718596
  19.1 11.3 %copy-start.1 = (f32[256]{0:T(256)S(1)}, f32[256]{0:T(256)}, u32[]{:S(2)}) copy-start(f32[256]{0:T(256)} %param.22) | copy-start | bytes 3076
  19.1 11.3 %collective-permute-start.1 = (f32[3,16,2048]{2,1,0:T(8,128)S(1)}, f32[3,16,2048]{2,1,0:T(8,128)S(1)}, u32[]{:S(2)}, u32[]{:S(2)}) collective-permute-start(f32[3,16,2048]{2,1,0:T(8,128)S(1)} %get-tuple-element.51), channel_id=1, source_target_pairs={{0,2},{1,3},{2,0},{3,1},{4,6},{5,7},{6,4},{7,5},{8,10},{9,11},{10,... | collective-permute-start | bytes 1179656 | tf_op jit(solution)/shard_map/ppermute | solution.py:602
  24.3 10.5 %all-to-all-start.1 = ((f32[32,1,768]{2,1,0:T(1,128)}), f32[32,1,768]{2,1,0:T(1,128)S(1)}, u32[]{:S(2)}, u32[]{:S(2)}) async-start(f32[32,1,768]{2,1,0:T(1,128)} %shard_map.141), calls=%async_computation.1 | async-start | bytes 196608 | tf_op jit(solution)/shard_map/all_to_all | solution.py:611
  30.4 8.0 %collective-permute-start.2 = (f32[23,1,2048]{2,1,0:T(1,128)S(1)}, f32[23,1,2048]{2,1,0:T(1,128)S(1)}, u32[]{:S(2)}, u32[]{:S(2)}) collective-permute-start(f32[23,1,2048]{2,1,0:T(1,128)S(1)} %shard_map.143), channel_id=1, source_target_pairs={{4,8},{12,16},{20,24},{8,4},{16,12},{24,20},{5,9},{13,17},{21,25},... | collective-permute-start | bytes 565256 | tf_op jit(solution)/shard_map/ppermute | solution.py:607
  37.6 3.9 %collective-permute-start.3 = (f32[3,1,2048]{2,1,0:T(1,128)S(1)}, f32[3,1,2048]{2,1,0:T(1,128)S(1)}, u32[]{:S(2)}, u32[]{:S(2)}) collective-permute-start(f32[3,1,2048]{2,1,0:T(1,128)S(1)} %get-tuple-element.61), channel_id=1, source_target_pairs={{0,4},{4,0},{8,12},{12,8},{16,20},{20,16},{24,28},{28,24},{1,5},{5... | collective-permute-start | bytes 73736 | tf_op jit(solution)/shard_map/ppermute | solution.py:602
  42.4 8.3 %collective-permute-start.4 = (f32[3,16,2048]{2,1,0:T(8,128)S(1)}, f32[3,16,2048]{2,1,0:T(8,128)S(1)}, u32[]{:S(2)}, u32[]{:S(2)}) collective-permute-start(f32[3,16,2048]{2,1,0:T(8,128)S(1)} %get-tuple-element.70), channel_id=1, source_target_pairs={{0,1},{1,0},{2,3},{3,2},{4,5},{5,4},{6,7},{7,6},{8,9},{9,8},{10,11... | collective-permute-start | bytes 1179656 | tf_op jit(solution)/shard_map/ppermute | solution.py:602
  42.5 8.3 %collective-permute-start.5 = (f32[3,16,2048]{2,1,0:T(8,128)S(1)}, f32[3,16,2048]{2,1,0:T(8,128)S(1)}, u32[]{:S(2)}, u32[]{:S(2)}) collective-permute-start(f32[3,16,2048]{2,1,0:T(8,128)S(1)} %get-tuple-element.71), channel_id=1, source_target_pairs={{1,2},{2,1},{5,6},{6,5},{9,10},{10,9},{13,14},{14,13},{17,18},{18,... | collective-permute-start | bytes 1179656 | tf_op jit(solution)/shard_map/ppermute | solution.py:607
  43.2 6.6 %collective-permute-start.6 = (f32[3,3,1,2048]{3,2,1,0:T(1,128)S(1)}, f32[3,3,1,2048]{3,2,1,0:T(1,128)S(1)}, u32[]{:S(2)}, u32[]{:S(2)}) collective-permute-start(f32[3,3,1,2048]{3,2,1,0:T(1,128)S(1)} %get-tuple-element.72), channel_id=1, source_target_pairs={{4,8},{12,16},{20,24},{8,4},{16,12},{24,20},{5,9},{13,17},{21,25},... | collective-permute-start | bytes 221192 | tf_op jit(solution)/shard_map/ppermute | solution.py:607
  43.9 6.9 %collective-permute-start.7 = (f32[3,3,1,2048]{3,2,1,0:T(1,128)S(1)}, f32[3,3,1,2048]{3,2,1,0:T(1,128)S(1)}, u32[]{:S(2)}, u32[]{:S(2)}) collective-permute-start(f32[3,3,1,2048]{3,2,1,0:T(1,128)S(1)} %get-tuple-element.73), channel_id=1, source_target_pairs={{0,4},{4,0},{8,12},{12,8},{16,20},{20,16},{24,28},{28,24},{1,5},{5... | collective-permute-start | bytes 221192 | tf_op jit(solution)/shard_map/ppermute | solution.py:602

commit v18 on v16

--- a/solution.py
+++ b/solution.py
@@ -285,19 +285,19 @@
     parts = [p.astype(F32) for p in split(terms)[:PARTS]]
     row_of = iota((length // lanes, count), 0).astype(F32)
     lane_of = iota((lanes, count), 0).astype(F32)
-    total = jnp.zeros((length // lanes, lanes), F32)
+    flipped = jnp.zeros((lanes, PARTS * (length // lanes)), F32)
     for d in range(devices):
         hit = row_of == high[d : d + 1]
         left = jnp.concatenate([jnp.where(hit, p[d : d + 1], 0.0).astype(BF16) for p in parts], 0)
         right = jnp.where(lane_of == low[d : d + 1], 1.0, 0.0).astype(BF16)
-        total = total + fold(dot_nt(left, right), PARTS)
+        flipped = flipped + dot_nt(right, left)
+    total = fold(jnp.transpose(flipped), PARTS)
     acc = jnp.zeros((rows, lanes), F32)
     for i in range(chunks):
         copies[i].wait()
         for r in range(i * wide // lanes, (i + 1) * wide // lanes):
             acc = acc + held[:, r * lanes : (r + 1) * lanes] * total[r : r + 1]
-    parts = jnp.concatenate(split(acc), 1)
-    out = dot_nt(jnp.ones((8, parts.shape[1]), BF16), parts)
+    out = jnp.transpose(jnp.broadcast_to(jnp.sum(acc, axis=1, keepdims=True), (rows, lanes)))
     pad = send.shape[2] - out.shape[1] - found.shape[1]
     pieces = [out[0:1], found] + ([jnp.zeros((1, pad), F32)] if pad else [])
     send[...] = jnp.broadcast_to(jnp.concatenate(pieces, 1)[:, None], send.shape)
@@ -426,12 +426,11 @@
     return [y[z] + first[z] * above + final[z] * below for z in range(depth)], above, below, tzp
 
 
-def pressure_kernel(levels, ready, recv, terms, pres, *refs):
-    sib, (tz, kept, tx, prod, _, p, coupled_z, one, *hots) = (refs[:levels], refs[levels:])
+def pressure_kernel(levels, ready, recv, pres, *refs):
+    hots, sib, (tz, kept, tx, prod, _, p, coupled_z, one) = (refs[:5], refs[5 : 5 + levels], refs[5 + levels :])
     depth, width, _ = pres.shape
     odd = is_right(0, "tile")
     lists = groups_of(levels)
-    table_kernel(lists, pres.shape, terms, hots)
 
     def planes_of():
         tzs, pressures = ([ref[z] for z in range(depth)] for ref in (tz, pres))
@@ -454,8 +453,9 @@
     ready(1)
 
 
-def edge_kernel(levels, low, high, prod, *refs):
-    sib, two = (refs[:levels], refs[levels])
+def edge_kernel(levels, shape, low, high, prod, terms, *refs):
+    sib, two, hots = (refs[:levels], refs[levels], refs[levels + 1 :])
+    table_kernel(groups_of(levels), shape, terms, hots)
     odd = is_right(0, "tile")
     n = low.shape[0]
     two[pl.ds(0, n)] = jnp.where(odd, high[...], low[...])
@@ -673,9 +673,6 @@
     sizes = [min(6, block.shape[0]) for block in sib]
     rim = vmem((4 * depth + sum(sizes) + 2, 1, long))
     send, low, high = lax.optimization_barrier((send, low, high))
-    (two,) = call(functools.partial(edge_kernel, levels), (rim,), (low, high, prod, *sib))
-    sol = everywhere(send)
-    two = neighbour(two, "tile")
 
     def hots(high):
         return (
@@ -686,16 +683,22 @@
             vmem((1, count), I32),
         )
 
-    at = 3 + levels
+    two, *made = call(
+        functools.partial(edge_kernel, levels, (depth, width, long)),
+        (rim, *hots(width)),
+        (low, high, prod, terms, *sib),
+    )
+    sol = everywhere(send)
+    two = neighbour(two, "tile")
+    at = 7 + levels
     row3 = vmem((depth, 1, long))
     p, coupled_z, one, tz, tx, block_inv = call(
         functools.partial(pressure_kernel, levels),
         (field, field, row3),
-        (sol, terms, pres, *sib, tz, kept, tx, prod, block_inv),
+        (sol, pres, *made, *sib, tz, kept, tx, prod, block_inv),
         far=range(at, at + 5),
         keep=(at, at + 2, at + 4),
         late=(range(at, at + 4), (at + 4,)),
-        scratch=hots(width),
     )
     sol, one, terms = lax.optimization_barrier((sol, one, terms))
     one = flip(one, 0, "tile")

time: 65.7 us -> 66.3 us (level)
    all_to_all x2, waiting for transfers between devices: 8.32 us -> 7.56 us  [everywhere(): return lax.all_to_all(x, BOTH, split_axis=0, concat_axis=0, tiled=True)]
    pallas_call x8, Pallas kernels: 13.2 us -> 13.9 us  [call(): pl.pallas_call(functools.partial(staged, kernel, where, len(outs), tuple(...]
  transfers between devices with their start and end apart: 10 -> 10, of which waited for: 5 -> 5; matrix products, arithmetic and copies ran while one was open for 0% -> 0% of each run, Pallas kernels for 22% -> 23%
where the time goes in v18:
time: 66.3 us; the launch traced here: 66 us
  Pallas kernels  21.9 us (33%)
  starting transfers between devices  16.7 us (25%)
  waiting for transfers between devices  13.1 us (20%)
  blocking collectives  12.2 us (18%)
  local copies, waits for them, and re-layouts  1.17 us (2%)
  between operations  0.78 us (1%)
    pallas_call x8, Pallas kernels, call(): pl.pallas_call(functools.partial(staged, kernel, where, len(outs), tuple(...  13.9 us
    all_to_all x1, blocking collectives, everywhere(): return lax.all_to_all(x, BOTH, split_axis=0, concat_axis=0, tiled=True)  12.2 us
    all_to_all x2, starting transfers between devices, everywhere(): return lax.all_to_all(x, BOTH, split_axis=0, concat_axis=0, tiled=True)  9.63 us
    all_to_all x2, waiting for transfers between devices, everywhere(): return lax.all_to_all(x, BOTH, split_axis=0, concat_axis=0, tiled=True)  7.56 us
    ppermute x5, waiting for transfers between devices, flip(): lax.ppermute(x, axis, [(i, i ^ 1 << level) for i in range(lax.axis_size(a...  5.56 us
    ppermute x5, starting transfers between devices, flip(): lax.ppermute(x, axis, [(i, i ^ 1 << level) for i in range(lax.axis_size(a...  5.06 us
    pallas_call x1, Pallas kernels, shards(): pl.pallas_call(front_kernel, out_shape=vmem((devices, 1, max(rows + found...  4.9 us
    pallas_call x1, Pallas kernels, shards(): pl.pallas_call(pres_kernel, out_shape=(field, vmem((devices, 1, 3 * count...  3.14 us
  transfers between devices with their start and end apart: 10, of which 5 were waited for; matrix products, arithmetic and copies ran while one was open for 0% of the time, Pallas kernels for 23%

profile of v18, /device:TPU:0, one launch (start us, length us, event | category | flops | bytes accessed | tf_op | source)
XLA Modules:
  0.0 66.0 jit_solution(13932924632690729215)
XLA Ops:
  0.6 3.1 %shard_map.139 = (f32[3,16,2048]{2,1,0:T(8,128)S(1)}, f32[32,1,768]{2,1,0:T(1,128)}, f32[7,16,2048]{2,1,0:T(8,128)S(1)}) custom-call(s32[1,256]{1,0:T(1,128)} %bitcast.8, s32[1,256]{1,0:T(1,128)} %bitcast.10, f32[1,256]{1,0:T(1,128)} %bitcast.4, f32[3,3,16,2048]{3,2,1,0:T(8,128)} %refs_3_.3, f32[3,3,16,2048]{3,2,1,0:T(8,128)} %wts_in.1, ...), custom_call_target="tpu_custom_call" | custom-call | tf_op jit(solution)/shard_map/pallas_call | solution.py:628
  3.8 0.5 collective-permute-start
  4.3 7.0 %all-to-all-start = ((f32[32,1,768]{2,1,0:T(1,128)}), f32[32,1,768]{2,1,0:T(1,128)S(1)}, u32[]{:S(2)}, u32[]{:S(2)}) async-start(f32[32,1,768]{2,1,0:T(1,128)} %get-tuple-element.46), calls=%async_computation | async-start | bytes 196608 | tf_op jit(solution)/shard_map/all_to_all | solution.py:609
  11.3 0.0 collective-permute-done.refs_1_.refs_4_.refs_7_
  11.3 2.1 %shard_map.140 = (f32[12,16,2048]{2,1,0:T(8,128)S(1)}, f32[12,1,2048]{2,1,0:T(1,128)S(1)}, f32[12,1,2048]{2,1,0:T(1,128)S(1)}, f32[1,256]{1,0:T(1,128)S(1)}, f32[3,16,2048]{2,1,0:T(8,128)S(1)}) custom-call(f32[7,16,2048]{2,1,0:T(8,128)S(1)} %get-tuple-element.47.refs_0_, f32[7,16,2048]{2,1,0:T(8,128)S(1)} %collective-permute-done.refs_1_.refs_4_.refs_7_, ...), custom_call_target="tpu_custom_call" | custom-call | tf_op jit(solution)/shard_map/pallas_call | solution.py:62
  13.4 1.2 %copy-done = f32[12,16,2048]{2,1,0:T(8,128)} copy-done((f32[12,16,2048]{2,1,0:T(8,128)}, f32[12,16,2048]{2,1,0:T(8,128)S(1)}, u32[]{:S(2)}) %copy-start) | copy-done | bytes 1572888
  14.6 4.5 %all-to-all-done.recv.refs_3_.refs_1_ = f32[32,1,768]{2,1,0:T(1,128)S(1)} async-done(((f32[32,1,768]{2,1,0:T(1,128)}), f32[32,1,768]{2,1,0:T(1,128)S(1)}, u32[]{:S(2)}, u32[]{:S(2)}) %all-to-all-start) | async-done | bytes 98336 | tf_op jit(solution)/shard_map/all_to_all | solution.py:609
  19.1 0.3 collective-permute-start.1
  19.4 4.9 %shard_map.141 = f32[32,1,768]{2,1,0:T(1,128)} custom-call(f32[32,1,768]{2,1,0:T(1,128)S(1)} %all-to-all-done.recv.refs_3_.refs_1_, f32[1,256]{1,0:T(1,128)S(1)} %get-tuple-element.52.found, f32[256,8192]{1,0:T(8,128)} %inverse.1), custom_call_target="tpu_custom_call" | custom-call | tf_op jit(solution)/shard_map/pallas_call | solution.py:665
  24.3 2.7 %all-to-all-start.1 = ((f32[32,1,768]{2,1,0:T(1,128)}), f32[32,1,768]{2,1,0:T(1,128)S(1)}, u32[]{:S(2)}, u32[]{:S(2)}) async-start(f32[32,1,768]{2,1,0:T(1,128)} %shard_map.141), calls=%async_computation.1 | async-start | bytes 196608 | tf_op jit(solution)/shard_map/all_to_all | solution.py:609
  27.0 3.3 %collective-permute-done.1.refs_5_.refs_8_ = f32[3,16,2048]{2,1,0:T(8,128)S(1)} collective-permute-done((f32[3,16,2048]{2,1,0:T(8,128)S(1)}, f32[3,16,2048]{2,1,0:T(8,128)S(1)}, u32[]{:S(2)}, u32[]{:S(2)}) %collective-permute-start.1) | collective-permute-done | bytes 393248 | tf_op jit(solution)/shard_map/ppermute | solution.py:600
  30.3 0.7 %shard_map.142 = (f32[23,1,2048]{2,1,0:T(1,128)}, bf16[256,1024]{1,0:T(8,128)(2,1)S(1)}, bf16[128,1024]{1,0:T(8,128)(2,1)S(1)}, bf16[256,1024]{1,0:T(8,128)(2,1)...) custom-call(f32[12,1,2048]{2,1,0:T(1,128)S(1)} %get-tuple-element.56.refs_0_, ...), custom_call_target="tpu_custom_call" | custom-call | tf_op jit(solution)/shard_map/pallas_call | solution.py:62
  31.1 0.7 %collective-permute-start.2 = (f32[23,1,2048]{2,1,0:T(1,128)}, f32[23,1,2048]{2,1,0:T(1,128)S(1)}, u32[]{:S(2)}, u32[]{:S(2)}) collective-permute-start(f32[23,1,2048]{2,1,0:T(1,128)} %get-tuple-element.70), channel_id=1, source_target_pairs={{4,8},{12,16},{20,24},{8,4},{16,12},{24,20},{5,9},{13,17},{21,25},... | collective-permute-start | bytes 565256 | tf_op jit(solution)/shard_map/ppermute | solution.py:605
  31.8 3.1 %all-to-all-done.1.refs_0_ = f32[32,1,768]{2,1,0:T(1,128)S(1)} async-done(((f32[32,1,768]{2,1,0:T(1,128)}), f32[32,1,768]{2,1,0:T(1,128)S(1)}, u32[]{:S(2)}, u32[]{:S(2)}) %all-to-all-start.1) | async-done | bytes 98336 | tf_op jit(solution)/shard_map/all_to_all | solution.py:609
  34.8 2.8 %shard_map.143 = (f32[3,16,2048]{2,1,0:T(8,128)S(1)}, f32[3,16,2048]{2,1,0:T(8,128)S(1)}, f32[3,1,2048]{2,1,0:T(1,128)S(1)}, f32[3,16,2048]{2,1,0:T(8,128)S(1)},...) custom-call(f32[32,1,768]{2,1,0:T(1,128)S(1)} %all-to-all-done.1.refs_0_, ...), custom_call_target="tpu_custom_call" | custom-call | tf_op jit(solution)/shard_map/pallas_call | solution.py:62
  37.6 0.7 %collective-permute-start.3 = (f32[3,1,2048]{2,1,0:T(1,128)S(1)}, f32[3,1,2048]{2,1,0:T(1,128)S(1)}, u32[]{:S(2)}, u32[]{:S(2)}) collective-permute-start(f32[3,1,2048]{2,1,0:T(1,128)S(1)} %get-tuple-element.72), channel_id=1, source_target_pairs={{0,4},{4,0},{8,12},{12,8},{16,20},{20,16},{24,28},{28,24},{1,5},{5... | collective-permute-start | bytes 73736 | tf_op jit(solution)/shard_map/ppermute | solution.py:600
  38.3 0.0 collective-permute-done.2.refs_2_
  38.3 2.1 %shard_map.144 = (f32[3,1,2048]{2,1,0:T(1,128)S(1)}, f32[3,3,16,2048]{3,2,1,0:T(8,128)S(1)}, f32[3,3,16,2048]{3,2,1,0:T(8,128)S(1)}, f32[3,16,2048]{2,1,0:T(8,128)S(1)}) custom-call(f32[32,1,768]{2,1,0:T(1,128)S(1)} %all-to-all-done.1.refs_0_, f32[32,1,768]{2,1,0:T(1,128)S(1)} %all-to-all-done.recv.refs_3_.refs_1_, ...), custom_call_target="tpu_custom_call" | custom-call | tf_op jit(solution)/shard_map/pallas_call | solution.py:62
  40.4 1.1 %collective-permute-done.3.refs_3_ = f32[3,1,2048]{2,1,0:T(1,128)S(1)} collective-permute-done((f32[3,1,2048]{2,1,0:T(1,128)S(1)}, f32[3,1,2048]{2,1,0:T(1,128)S(1)}, u32[]{:S(2)}, u32[]{:S(2)}) %collective-permute-start.3) | collective-permute-done | bytes 24608 | tf_op jit(solution)/shard_map/ppermute | solution.py:600
  41.5 1.0 %shard_map.145 = (f32[3,3,16,2048]{3,2,1,0:T(8,128)S(1)}, f32[3,16,2048]{2,1,0:T(8,128)S(1)}, f32[3,3,1,2048]{3,2,1,0:T(1,128)S(1)}, f32[3,3,1,2048]{3,2,1,0:T(1,128)S(1)}, f32[3,16,2048]{2,1,0:T(8,128)S(1)}) custom-call(f32[3,16,2048]{2,1,0:T(8,128)S(1)} %get-tuple-element.65.refs_0_, f32[3,16,2048]{2,1,0:T(8,128)S(1)} %get-tuple-element.66.refs_1_, ...), custom_call_target="tpu_custom_call" | custom-call | tf_op jit(solution)/shard_map/pallas_call | solution.py:62
  42.5 0.1 collective-permute-start.4
  42.6 0.7 %collective-permute-start.5 = (f32[3,16,2048]{2,1,0:T(8,128)S(1)}, f32[3,16,2048]{2,1,0:T(8,128)S(1)}, u32[]{:S(2)}, u32[]{:S(2)}) collective-permute-start(f32[3,16,2048]{2,1,0:T(8,128)S(1)} %get-tuple-element.81), channel_id=1, source_target_pairs={{1,2},{2,1},{5,6},{6,5},{9,10},{10,9},{13,14},{14,13},{17,18},{18,... | collective-permute-start | bytes 1179656 | tf_op jit(solution)/shard_map/ppermute | solution.py:605
  43.3 0.7 %collective-permute-start.6 = (f32[3,3,1,2048]{3,2,1,0:T(1,128)S(1)}, f32[3,3,1,2048]{3,2,1,0:T(1,128)S(1)}, u32[]{:S(2)}, u32[]{:S(2)}) collective-permute-start(f32[3,3,1,2048]{3,2,1,0:T(1,128)S(1)} %get-tuple-element.82), channel_id=1, source_target_pairs={{4,8},{12,16},{20,24},{8,4},{16,12},{24,20},{5,9},{13,17},{21,25},... | collective-permute-start | bytes 221192 | tf_op jit(solution)/shard_map/ppermute | solution.py:605
  43.9 3.4 %collective-permute-start.7 = (f32[3,3,1,2048]{3,2,1,0:T(1,128)S(1)}, f32[3,3,1,2048]{3,2,1,0:T(1,128)S(1)}, u32[]{:S(2)}, u32[]{:S(2)}) collective-permute-start(f32[3,3,1,2048]{3,2,1,0:T(1,128)S(1)} %get-tuple-element.83), channel_id=1, source_target_pairs={{0,4},{4,0},{8,12},{12,8},{16,20},{20,16},{24,28},{28,24},{1,5},{5... | collective-permute-start | bytes 221192 | tf_op jit(solution)/shard_map/ppermute | solution.py:600
  47.4 2.4 %shard_map.146.refs_0_ = f32[3,3,16,2048]{3,2,1,0:T(8,128)S(1)} custom-call(f32[3,3,16,2048]{3,2,1,0:T(8,128)S(1)} %get-tuple-element.79.refs_0_.refs_1_, f32[3,3,3,16,2048]{4,3,2,1,0:T(8,128)} %refs_1_.1, f32[3,16,2048]{2,1,0:T(8,128)S(1)} %get-tuple-element.75.refs_6_.refs_2_, f32[3,16,2048]{2,1,0:T(8,128)S(1)} %get-tuple-element.73.refs_4_.refs_3_.refs_7_, ...), custom_call_target="tpu_custom_call" | custom-call | tf_op jit(solution)/shard_map/pallas_call | solution.py:62
  49.7 0.0 collective-permute-done.6.refs_3_
  49.7 1.1 %collective-permute-done.7.refs_4_ = f32[3,3,1,2048]{3,2,1,0:T(1,128)S(1)} collective-permute-done((f32[3,3,1,2048]{3,2,1,0:T(1,128)S(1)}, f32[3,3,1,2048]{3,2,1,0:T(1,128)S(1)}, u32[]{:S(2)}, u32[]{:S(2)}) %collective-permute-start.7) | collective-permute-done | bytes 73760 | tf_op jit(solution)/shard_map/ppermute | solution.py:600
  50.9 0.0 collective-permute-done.4.refs_1_
  50.9 0.0 collective-permute-done.5.refs_2_
  50.9 1.2 %shard_map.147 = (f32[3,3,16,2048]{3,2,1,0:T(8,128)S(1)}, f32[32,1,128]{2,1,0:T(1,128)S(1)}) custom-call(f32[3,3,16,2048]{3,2,1,0:T(8,128)S(1)} %shard_map.146.refs_0_, f32[3,16,2048]{2,1,0:T(8,128)S(1)} %collective-permute-done.4.refs_1_, f32[3,16,2048]{2,1,0:T(8,128)S(1)} %collective-permute-done.5.refs_2_, ...), custom_call_target="tpu_custom_call" | custom-call | tf_op jit(solution)/shard_map/pallas_call | solution.py:62
  52.1 12.2 %all_to_all.15.refs_0_ = f32[32,1,128]{2,1,0:T(1,128)S(1)} all-to-all(f32[32,1,128]{2,1,0:T(1,128)S(1)} %get-tuple-element.84), channel_id=1, replica_groups=mesh['tile'=8,'layer'=4] {'tile','layer'}, dimensions={0} | all-to-all | bytes 32768 | tf_op jit(solution)/shard_map/all_to_all | solution.py:609
  64.3 1.7 %shard_map.148 = (f32[3,3,16,2048]{3,2,1,0:T(8,128)}, f32[3,3,16,2048]{3,2,1,0:T(8,128)}, f32[1,1]{1,0:T(1,128)}) custom-call(f32[32,1,128]{2,1,0:T(1,128)S(1)} %all_to_all.15.refs_0_, f32[3,3,16,2048]{3,2,1,0:T(8,128)S(1)} %get-tuple-element.79.refs_0_.refs_1_, f32[3,3,16,2048]{3,2,1,0:T(8,128)S(1)} %get-tuple-element.85.refs_2_, ...), custom_call_target="tpu_custom_call" | custom-call | tf_op jit(solution)/shard_map/pallas_call | solution.py:62
  (3 shorter events, 0.0 us)
Async XLA Ops:
  3.8 7.5 %collective-permute-start = (f32[7,16,2048]{2,1,0:T(8,128)S(1)}, f32[7,16,2048]{2,1,0:T(8,128)S(1)}, u32[]{:S(2)}, u32[]{:S(2)}) collective-permute-start(f32[7,16,2048]{2,1,0:T(8,128)S(1)} %get-tuple-element.47.refs_0_), channel_id=1, source_target_pairs={{0,1},{1,0},{2,3},{3,2},{4,5},{5,4},{6,7},{7,6},{8,9},{9,8},{10,11... | collective-permute-start | bytes 2752520 | tf_op jit(solution)/shard_map/ppermute | solution.py:600
  4.3 14.8 %all-to-all-start = ((f32[32,1,768]{2,1,0:T(1,128)}), f32[32,1,768]{2,1,0:T(1,128)S(1)}, u32[]{:S(2)}, u32[]{:S(2)}) async-start(f32[32,1,768]{2,1,0:T(1,128)} %get-tuple-element.46), calls=%async_computation | async-start | bytes 196608 | tf_op jit(solution)/shard_map/all_to_all | solution.py:609
  13.4 1.2 %copy-start = (f32[12,16,2048]{2,1,0:T(8,128)}, f32[12,16,2048]{2,1,0:T(8,128)S(1)}, u32[]{:S(2)}) copy-start(f32[12,16,2048]{2,1,0:T(8,128)S(1)} %get-tuple-element.64.refs_10_) | copy-start | bytes 4718596
  19.1 11.3 %copy-start.1 = (f32[256]{0:T(256)S(1)}, f32[256]{0:T(256)}, u32[]{:S(2)}) copy-start(f32[256]{0:T(256)} %param.22) | copy-start | bytes 3076
  19.1 11.3 %collective-permute-start.1 = (f32[3,16,2048]{2,1,0:T(8,128)S(1)}, f32[3,16,2048]{2,1,0:T(8,128)S(1)}, u32[]{:S(2)}, u32[]{:S(2)}) collective-permute-start(f32[3,16,2048]{2,1,0:T(8,128)S(1)} %get-tuple-element.58), channel_id=1, source_target_pairs={{0,2},{1,3},{2,0},{3,1},{4,6},{5,7},{6,4},{7,5},{8,10},{9,11},{10,... | collective-permute-start | bytes 1179656 | tf_op jit(solution)/shard_map/ppermute | solution.py:600
  24.3 10.5 %all-to-all-start.1 = ((f32[32,1,768]{2,1,0:T(1,128)}), f32[32,1,768]{2,1,0:T(1,128)S(1)}, u32[]{:S(2)}, u32[]{:S(2)}) async-start(f32[32,1,768]{2,1,0:T(1,128)} %shard_map.141), calls=%async_computation.1 | async-start | bytes 196608 | tf_op jit(solution)/shard_map/all_to_all | solution.py:609
  31.1 7.2 %collective-permute-start.2 = (f32[23,1,2048]{2,1,0:T(1,128)}, f32[23,1,2048]{2,1,0:T(1,128)S(1)}, u32[]{:S(2)}, u32[]{:S(2)}) collective-permute-start(f32[23,1,2048]{2,1,0:T(1,128)} %get-tuple-element.70), channel_id=1, source_target_pairs={{4,8},{12,16},{20,24},{8,4},{16,12},{24,20},{5,9},{13,17},{21,25},... | collective-permute-start | bytes 565256 | tf_op jit(solution)/shard_map/ppermute | solution.py:605
  37.6 3.9 %collective-permute-start.3 = (f32[3,1,2048]{2,1,0:T(1,128)S(1)}, f32[3,1,2048]{2,1,0:T(1,128)S(1)}, u32[]{:S(2)}, u32[]{:S(2)}) collective-permute-start(f32[3,1,2048]{2,1,0:T(1,128)S(1)} %get-tuple-element.72), channel_id=1, source_target_pairs={{0,4},{4,0},{8,12},{12,8},{16,20},{20,16},{24,28},{28,24},{1,5},{5... | collective-permute-start | bytes 73736 | tf_op jit(solution)/shard_map/ppermute | solution.py:600
  42.5 8.4 %collective-permute-start.4 = (f32[3,16,2048]{2,1,0:T(8,128)S(1)}, f32[3,16,2048]{2,1,0:T(8,128)S(1)}, u32[]{:S(2)}, u32[]{:S(2)}) collective-permute-start(f32[3,16,2048]{2,1,0:T(8,128)S(1)} %get-tuple-element.80), channel_id=1, source_target_pairs={{0,1},{1,0},{2,3},{3,2},{4,5},{5,4},{6,7},{7,6},{8,9},{9,8},{10,11... | collective-permute-start | bytes 1179656 | tf_op jit(solution)/shard_map/ppermute | solution.py:600
  42.6 8.3 %collective-permute-start.5 = (f32[3,16,2048]{2,1,0:T(8,128)S(1)}, f32[3,16,2048]{2,1,0:T(8,128)S(1)}, u32[]{:S(2)}, u32[]{:S(2)}) collective-permute-start(f32[3,16,2048]{2,1,0:T(8,128)S(1)} %get-tuple-element.81), channel_id=1, source_target_pairs={{1,2},{2,1},{5,6},{6,5},{9,10},{10,9},{13,14},{14,13},{17,18},{18,... | collective-permute-start | bytes 1179656 | tf_op jit(solution)/shard_map/ppermute | solution.py:605
  43.3 6.5 %collective-permute-start.6 = (f32[3,3,1,2048]{3,2,1,0:T(1,128)S(1)}, f32[3,3,1,2048]{3,2,1,0:T(1,128)S(1)}, u32[]{:S(2)}, u32[]{:S(2)}) collective-permute-start(f32[3,3,1,2048]{3,2,1,0:T(1,128)S(1)} %get-tuple-element.82), channel_id=1, source_target_pairs={{4,8},{12,16},{20,24},{8,4},{16,12},{24,20},{5,9},{13,17},{21,25},... | collective-permute-start | bytes 221192 | tf_op jit(solution)/shard_map/ppermute | solution.py:605
  43.9 6.9 %collective-permute-start.7 = (f32[3,3,1,2048]{3,2,1,0:T(1,128)S(1)}, f32[3,3,1,2048]{3,2,1,0:T(1,128)S(1)}, u32[]{:S(2)}, u32[]{:S(2)}) collective-permute-start(f32[3,3,1,2048]{3,2,1,0:T(1,128)S(1)} %get-tuple-element.83), channel_id=1, source_target_pairs={{0,4},{4,0},{8,12},{12,8},{16,20},{20,16},{24,28},{28,24},{1,5},{5... | collective-permute-start | bytes 221192 | tf_op jit(solution)/shard_map/ppermute | solution.py:600

commit v19 on v17

--- a/solution.py
+++ b/solution.py
@@ -427,12 +427,11 @@
     return [y[z] + first[z] * above + final[z] * below for z in range(depth)], above, below, tzp
 
 
-def pressure_kernel(levels, ready, recv, terms, pres, *refs):
-    sib, (tz, kept, tx, prod, _, p, coupled_z, one, *hots) = (refs[:levels], refs[levels:])
+def pressure_kernel(levels, ready, recv, pres, *refs):
+    hots, sib, (tz, kept, tx, prod, _, p, coupled_z, one) = (refs[:5], refs[5 : 5 + levels], refs[5 + levels :])
     depth, width, _ = pres.shape
     odd = is_right(0, "tile")
     lists = groups_of(levels)
-    table_kernel(lists, pres.shape, terms, hots)
 
     def planes_of():
         tzs, pressures = ([ref[z] for z in range(depth)] for ref in (tz, pres))
@@ -455,8 +454,9 @@
     ready(1)
 
 
-def edge_kernel(levels, low, high, prod, *refs):
-    sib, two = (refs[:levels], refs[levels])
+def edge_kernel(levels, shape, low, high, prod, terms, *refs):
+    sib, two, hots = (refs[:levels], refs[levels], refs[levels + 1 :])
+    table_kernel(groups_of(levels), shape, terms, hots)
     odd = is_right(0, "tile")
     n = low.shape[0]
     two[pl.ds(0, n)] = jnp.where(odd, high[...], low[...])
@@ -675,9 +675,6 @@
     sizes = [min(6, block.shape[0]) for block in sib]
     rim = vmem((4 * depth + sum(sizes) + 2, 1, long))
     send, low, high = lax.optimization_barrier((send, low, high))
-    (two,) = call(functools.partial(edge_kernel, levels), (rim,), (low, high, prod, *sib))
-    sol = everywhere(send)
-    two = neighbour(two, "tile")
 
     def hots(high):
         return (
@@ -688,17 +685,23 @@
             vmem((1, count), I32),
         )
 
-    at = 3 + levels
+    two, *made = call(
+        functools.partial(edge_kernel, levels, (depth, width, long)),
+        (rim, *hots(width)),
+        (low, high, prod, terms, *sib),
+    )
+    sol = everywhere(send)
+    two = neighbour(two, "tile")
+    at = 7 + levels
     row3 = vmem((depth, 1, long))
     p, coupled_z, one, tz, tx, later_inv = call(
         functools.partial(pressure_kernel, levels),
         (field, field, row3),
-        (sol, terms, pres, *sib, tz, kept, tx, prod, block_inv),
+        (sol, pres, *made, *sib, tz, kept, tx, prod, block_inv),
         far=range(at, at + 5),
         keep=(at, at + 2, at + 4),
         cut={at + 4: (1, 3)},
         late=(range(at, at + 4), (at + 4,)),
-        scratch=hots(width),
     )
     sol, one, terms = lax.optimization_barrier((sol, one, terms))
     one = flip(one, 0, "tile")

time: 65.8 us -> 66.7 us (1.014)
  Pallas kernels: 21.6 us -> 22.3 us
    ppermute x5, waiting for transfers between devices: 4.87 us -> 5.61 us  [flip(): lax.ppermute(x, axis, [(i, i ^ 1 << level) for i in range(lax.axis_size(a...]
    pallas_call x8, Pallas kernels: 13.6 us -> 14.3 us  [call(): pl.pallas_call(functools.partial(staged, kernel, where, len(outs), tuple(...]
    all_to_all x2, waiting for transfers between devices: 8.24 us -> 7.56 us  [everywhere(): return lax.all_to_all(x, BOTH, split_axis=0, concat_axis=0, tiled=True)]
  transfers between devices with their start and end apart: 10 -> 10, of which waited for: 5 -> 5; matrix products, arithmetic and copies ran while one was open for 0% -> 0% of each run, Pallas kernels for 22% -> 23%
where the time goes in v19:
time: 66.7 us; the launch traced here: 66.4 us
  Pallas kernels  22.3 us (33%)
  starting transfers between devices  16.7 us (25%)
  waiting for transfers between devices  13.2 us (20%)
  blocking collectives  12.2 us (18%)
  local copies, waits for them, and re-layouts  1.17 us (2%)
  between operations  0.78 us (1%)
    pallas_call x8, Pallas kernels, call(): pl.pallas_call(functools.partial(staged, kernel, where, len(outs), tuple(...  14.3 us
    all_to_all x1, blocking collectives, everywhere(): return lax.all_to_all(x, BOTH, split_axis=0, concat_axis=0, tiled=True)  12.2 us
    all_to_all x2, starting transfers between devices, everywhere(): return lax.all_to_all(x, BOTH, split_axis=0, concat_axis=0, tiled=True)  9.63 us
    all_to_all x2, waiting for transfers between devices, everywhere(): return lax.all_to_all(x, BOTH, split_axis=0, concat_axis=0, tiled=True)  7.56 us
    ppermute x5, waiting for transfers between devices, flip(): lax.ppermute(x, axis, [(i, i ^ 1 << level) for i in range(lax.axis_size(a...  5.61 us
    ppermute x5, starting transfers between devices, flip(): lax.ppermute(x, axis, [(i, i ^ 1 << level) for i in range(lax.axis_size(a...  5.07 us
    pallas_call x1, Pallas kernels, shards(): pl.pallas_call(front_kernel, out_shape=vmem((devices, 1, max(rows + found...  4.9 us
    pallas_call x1, Pallas kernels, shards(): pl.pallas_call(pres_kernel, out_shape=(field, vmem((devices, 1, 3 * count...  3.14 us
  transfers between devices with their start and end apart: 10, of which 5 were waited for; matrix products, arithmetic and copies ran while one was open for 0% of the time, Pallas kernels for 23%

profile of v19, /device:TPU:0, one launch (start us, length us, event | category | flops | bytes accessed | tf_op | source)
XLA Modules:
  0.0 66.4 jit_solution(16419674122928659336)
XLA Ops:
  0.6 3.1 %shard_map.139 = (f32[3,16,2048]{2,1,0:T(8,128)S(1)}, f32[32,1,768]{2,1,0:T(1,128)}, f32[7,16,2048]{2,1,0:T(8,128)S(1)}) custom-call(s32[1,256]{1,0:T(1,128)} %bitcast.8, s32[1,256]{1,0:T(1,128)} %bitcast.10, f32[1,256]{1,0:T(1,128)} %bitcast.4, f32[3,3,16,2048]{3,2,1,0:T(8,128)} %refs_3_.3, f32[3,3,16,2048]{3,2,1,0:T(8,128)} %wts_in.1, ...), custom_call_target="tpu_custom_call" | custom-call | tf_op jit(solution)/shard_map/pallas_call | solution.py:630
  3.8 0.5 collective-permute-start
  4.3 7.0 %all-to-all-start = ((f32[32,1,768]{2,1,0:T(1,128)}), f32[32,1,768]{2,1,0:T(1,128)S(1)}, u32[]{:S(2)}, u32[]{:S(2)}) async-start(f32[32,1,768]{2,1,0:T(1,128)} %get-tuple-element.47), calls=%async_computation | async-start | bytes 196608 | tf_op jit(solution)/shard_map/all_to_all | solution.py:611
  11.3 0.0 collective-permute-done.refs_1_.refs_4_.refs_7_
  11.3 2.1 %shard_map.140 = (f32[12,16,2048]{2,1,0:T(8,128)S(1)}, f32[12,1,2048]{2,1,0:T(1,128)S(1)}, f32[12,1,2048]{2,1,0:T(1,128)S(1)}, f32[1,256]{1,0:T(1,128)S(1)}, f32[3,16,2048]{2,1,0:T(8,128)S(1)}) custom-call(f32[7,16,2048]{2,1,0:T(8,128)S(1)} %get-tuple-element.48.refs_0_, f32[7,16,2048]{2,1,0:T(8,128)S(1)} %collective-permute-done.refs_1_.refs_4_.refs_7_, ...), custom_call_target="tpu_custom_call" | custom-call | tf_op jit(solution)/shard_map/pallas_call | solution.py:63
  13.4 1.2 %copy-done = f32[12,16,2048]{2,1,0:T(8,128)} copy-done((f32[12,16,2048]{2,1,0:T(8,128)}, f32[12,16,2048]{2,1,0:T(8,128)S(1)}, u32[]{:S(2)}) %copy-start) | copy-done | bytes 1572888
  14.6 4.5 %all-to-all-done.recv.refs_3_.refs_1_ = f32[32,1,768]{2,1,0:T(1,128)S(1)} async-done(((f32[32,1,768]{2,1,0:T(1,128)}), f32[32,1,768]{2,1,0:T(1,128)S(1)}, u32[]{:S(2)}, u32[]{:S(2)}) %all-to-all-start) | async-done | bytes 98336 | tf_op jit(solution)/shard_map/all_to_all | solution.py:611
  19.1 0.3 collective-permute-start.1
  19.4 4.9 %shard_map.141 = f32[32,1,768]{2,1,0:T(1,128)} custom-call(f32[32,1,768]{2,1,0:T(1,128)S(1)} %all-to-all-done.recv.refs_3_.refs_1_, f32[1,256]{1,0:T(1,128)S(1)} %get-tuple-element.53.found, f32[256,8192]{1,0:T(8,128)} %inverse.1), custom_call_target="tpu_custom_call" | custom-call | tf_op jit(solution)/shard_map/pallas_call | solution.py:667
  24.3 2.7 %all-to-all-start.1 = ((f32[32,1,768]{2,1,0:T(1,128)}), f32[32,1,768]{2,1,0:T(1,128)S(1)}, u32[]{:S(2)}, u32[]{:S(2)}) async-start(f32[32,1,768]{2,1,0:T(1,128)} %shard_map.141), calls=%async_computation.1 | async-start | bytes 196608 | tf_op jit(solution)/shard_map/all_to_all | solution.py:611
  27.0 3.3 %collective-permute-done.1.refs_5_.refs_8_ = f32[3,16,2048]{2,1,0:T(8,128)S(1)} collective-permute-done((f32[3,16,2048]{2,1,0:T(8,128)S(1)}, f32[3,16,2048]{2,1,0:T(8,128)S(1)}, u32[]{:S(2)}, u32[]{:S(2)}) %collective-permute-start.1) | collective-permute-done | bytes 393248 | tf_op jit(solution)/shard_map/ppermute | solution.py:602
  30.3 0.7 %shard_map.142 = (f32[23,1,2048]{2,1,0:T(1,128)}, bf16[256,1024]{1,0:T(8,128)(2,1)S(1)}, bf16[128,1024]{1,0:T(8,128)(2,1)S(1)}, bf16[256,1024]{1,0:T(8,128)(2,1)...) custom-call(f32[12,1,2048]{2,1,0:T(1,128)S(1)} %get-tuple-element.57.refs_0_, ...), custom_call_target="tpu_custom_call" | custom-call | tf_op jit(solution)/shard_map/pallas_call | solution.py:63
  31.1 0.7 %collective-permute-start.2 = (f32[23,1,2048]{2,1,0:T(1,128)}, f32[23,1,2048]{2,1,0:T(1,128)S(1)}, u32[]{:S(2)}, u32[]{:S(2)}) collective-permute-start(f32[23,1,2048]{2,1,0:T(1,128)} %get-tuple-element.71), channel_id=1, source_target_pairs={{4,8},{12,16},{20,24},{8,4},{16,12},{24,20},{5,9},{13,17},{21,25},... | collective-permute-start | bytes 565256 | tf_op jit(solution)/shard_map/ppermute | solution.py:607
  31.8 3.1 %all-to-all-done.1.refs_0_ = f32[32,1,768]{2,1,0:T(1,128)S(1)} async-done(((f32[32,1,768]{2,1,0:T(1,128)}), f32[32,1,768]{2,1,0:T(1,128)S(1)}, u32[]{:S(2)}, u32[]{:S(2)}) %all-to-all-start.1) | async-done | bytes 98336 | tf_op jit(solution)/shard_map/all_to_all | solution.py:611
  34.8 2.7 %shard_map.143 = (f32[3,16,2048]{2,1,0:T(8,128)S(1)}, f32[3,16,2048]{2,1,0:T(8,128)S(1)}, f32[3,1,2048]{2,1,0:T(1,128)S(1)}, f32[3,16,2048]{2,1,0:T(8,128)S(1)},...) custom-call(f32[32,1,768]{2,1,0:T(1,128)S(1)} %all-to-all-done.1.refs_0_, ...), custom_call_target="tpu_custom_call" | custom-call | tf_op jit(solution)/shard_map/pallas_call | solution.py:63
  37.6 0.7 %collective-permute-start.3 = (f32[3,1,2048]{2,1,0:T(1,128)S(1)}, f32[3,1,2048]{2,1,0:T(1,128)S(1)}, u32[]{:S(2)}, u32[]{:S(2)}) collective-permute-start(f32[3,1,2048]{2,1,0:T(1,128)S(1)} %get-tuple-element.73), channel_id=1, source_target_pairs={{0,4},{4,0},{8,12},{12,8},{16,20},{20,16},{24,28},{28,24},{1,5},{5... | collective-permute-start | bytes 73736 | tf_op jit(solution)/shard_map/ppermute | solution.py:602
  38.3 0.0 collective-permute-done.2.refs_2_
  38.3 2.5 %shard_map.144 = (f32[3,1,2048]{2,1,0:T(1,128)S(1)}, f32[3,3,16,2048]{3,2,1,0:T(8,128)S(1)}, f32[3,3,16,2048]{3,2,1,0:T(8,128)S(1)}, f32[3,16,2048]{2,1,0:T(8,128)S(1)}, f32[1,3,3,16,2048]{4,3,2,1,0:T(8,128)S(1)}) custom-call(f32[32,1,768]{2,1,0:T(1,128)S(1)} %all-to-all-done.1.refs_0_, f32[32,1,768]{2,1,0:T(1,128)S(1)} %all-to-all-done.recv.refs_3_.refs_1_, ...), custom_call_target="tpu_custom_call" | custom-call | tf_op jit(solution)/shard_map/pallas_call | solution.py:63
  40.8 0.7 collective-permute-done.3.refs_3_
  41.4 1.0 %shard_map.145 = (f32[3,3,16,2048]{3,2,1,0:T(8,128)S(1)}, f32[3,16,2048]{2,1,0:T(8,128)S(1)}, f32[3,3,1,2048]{3,2,1,0:T(1,128)S(1)}, f32[3,3,1,2048]{3,2,1,0:T(1,128)S(1)}, f32[3,16,2048]{2,1,0:T(8,128)S(1)}) custom-call(f32[3,16,2048]{2,1,0:T(8,128)S(1)} %get-tuple-element.66.refs_0_, f32[3,16,2048]{2,1,0:T(8,128)S(1)} %get-tuple-element.67.refs_1_, ...), custom_call_target="tpu_custom_call" | custom-call | tf_op jit(solution)/shard_map/pallas_call | solution.py:63
  42.4 0.1 collective-permute-start.4
  42.5 0.7 %collective-permute-start.5 = (f32[3,16,2048]{2,1,0:T(8,128)S(1)}, f32[3,16,2048]{2,1,0:T(8,128)S(1)}, u32[]{:S(2)}, u32[]{:S(2)}) collective-permute-start(f32[3,16,2048]{2,1,0:T(8,128)S(1)} %get-tuple-element.83), channel_id=1, source_target_pairs={{1,2},{2,1},{5,6},{6,5},{9,10},{10,9},{13,14},{14,13},{17,18},{18,... | collective-permute-start | bytes 1179656 | tf_op jit(solution)/shard_map/ppermute | solution.py:607
  43.2 0.7 %collective-permute-start.6 = (f32[3,3,1,2048]{3,2,1,0:T(1,128)S(1)}, f32[3,3,1,2048]{3,2,1,0:T(1,128)S(1)}, u32[]{:S(2)}, u32[]{:S(2)}) collective-permute-start(f32[3,3,1,2048]{3,2,1,0:T(1,128)S(1)} %get-tuple-element.84), channel_id=1, source_target_pairs={{4,8},{12,16},{20,24},{8,4},{16,12},{24,20},{5,9},{13,17},{21,25},... | collective-permute-start | bytes 221192 | tf_op jit(solution)/shard_map/ppermute | solution.py:607
  43.9 3.4 %collective-permute-start.7 = (f32[3,3,1,2048]{3,2,1,0:T(1,128)S(1)}, f32[3,3,1,2048]{3,2,1,0:T(1,128)S(1)}, u32[]{:S(2)}, u32[]{:S(2)}) collective-permute-start(f32[3,3,1,2048]{3,2,1,0:T(1,128)S(1)} %get-tuple-element.85), channel_id=1, source_target_pairs={{0,4},{4,0},{8,12},{12,8},{16,20},{20,16},{24,28},{28,24},{1,5},{5... | collective-permute-start | bytes 221192 | tf_op jit(solution)/shard_map/ppermute | solution.py:602
  47.3 2.4 %shard_map.146.refs_0_ = f32[3,3,16,2048]{3,2,1,0:T(8,128)S(1)} custom-call(f32[3,3,16,2048]{3,2,1,0:T(8,128)S(1)} %get-tuple-element.81.refs_0_.refs_1_, f32[3,3,3,16,2048]{4,3,2,1,0:T(8,128)} %refs_1_.1, f32[3,16,2048]{2,1,0:T(8,128)S(1)} %get-tuple-element.76.refs_6_.refs_2_, f32[3,16,2048]{2,1,0:T(8,128)S(1)} %get-tuple-element.74.refs_4_.refs_3_.refs_7_, ...), custom_call_target="tpu_custom_call" | custom-call | tf_op jit(solution)/shard_map/pallas_call | solution.py:63
  49.7 0.0 collective-permute-done.6.refs_3_
  49.7 1.6 %collective-permute-done.7.refs_4_ = f32[3,3,1,2048]{3,2,1,0:T(1,128)S(1)} collective-permute-done((f32[3,3,1,2048]{3,2,1,0:T(1,128)S(1)}, f32[3,3,1,2048]{3,2,1,0:T(1,128)S(1)}, u32[]{:S(2)}, u32[]{:S(2)}) %collective-permute-start.7) | collective-permute-done | bytes 73760 | tf_op jit(solution)/shard_map/ppermute | solution.py:602
  51.3 0.0 collective-permute-done.4.refs_1_
  51.3 0.0 collective-permute-done.5.refs_2_
  51.3 1.2 %shard_map.147 = (f32[3,3,16,2048]{3,2,1,0:T(8,128)S(1)}, f32[32,1,128]{2,1,0:T(1,128)S(1)}) custom-call(f32[3,3,16,2048]{3,2,1,0:T(8,128)S(1)} %shard_map.146.refs_0_, f32[3,16,2048]{2,1,0:T(8,128)S(1)} %collective-permute-done.4.refs_1_, f32[3,16,2048]{2,1,0:T(8,128)S(1)} %collective-permute-done.5.refs_2_, ...), custom_call_target="tpu_custom_call" | custom-call | tf_op jit(solution)/shard_map/pallas_call | solution.py:63
  52.5 12.2 %all_to_all.15.refs_0_ = f32[32,1,128]{2,1,0:T(1,128)S(1)} all-to-all(f32[32,1,128]{2,1,0:T(1,128)S(1)} %get-tuple-element.86), channel_id=1, replica_groups=mesh['tile'=8,'layer'=4] {'tile','layer'}, dimensions={0} | all-to-all | bytes 32768 | tf_op jit(solution)/shard_map/all_to_all | solution.py:611
  64.7 1.7 %shard_map.148 = (f32[3,3,16,2048]{3,2,1,0:T(8,128)}, f32[3,3,16,2048]{3,2,1,0:T(8,128)}, f32[1,1]{1,0:T(1,128)}) custom-call(f32[32,1,128]{2,1,0:T(1,128)S(1)} %all_to_all.15.refs_0_, f32[3,3,16,2048]{3,2,1,0:T(8,128)S(1)} %get-tuple-element.81.refs_0_.refs_1_, f32[3,3,16,2048]{3,2,1,0:T(8,128)S(1)} %get-tuple-element.87.refs_2_, ...), custom_call_target="tpu_custom_call" | custom-call | tf_op jit(solution)/shard_map/pallas_call | solution.py:63
  (3 shorter events, 0.0 us)
Async XLA Ops:
  3.8 7.5 %collective-permute-start = (f32[7,16,2048]{2,1,0:T(8,128)S(1)}, f32[7,16,2048]{2,1,0:T(8,128)S(1)}, u32[]{:S(2)}, u32[]{:S(2)}) collective-permute-start(f32[7,16,2048]{2,1,0:T(8,128)S(1)} %get-tuple-element.48.refs_0_), channel_id=1, source_target_pairs={{0,1},{1,0},{2,3},{3,2},{4,5},{5,4},{6,7},{7,6},{8,9},{9,8},{10,11... | collective-permute-start | bytes 2752520 | tf_op jit(solution)/shard_map/ppermute | solution.py:602
  4.3 14.8 %all-to-all-start = ((f32[32,1,768]{2,1,0:T(1,128)}), f32[32,1,768]{2,1,0:T(1,128)S(1)}, u32[]{:S(2)}, u32[]{:S(2)}) async-start(f32[32,1,768]{2,1,0:T(1,128)} %get-tuple-element.47), calls=%async_computation | async-start | bytes 196608 | tf_op jit(solution)/shard_map/all_to_all | solution.py:611
  13.4 1.2 %copy-start = (f32[12,16,2048]{2,1,0:T(8,128)}, f32[12,16,2048]{2,1,0:T(8,128)S(1)}, u32[]{:S(2)}) copy-start(f32[12,16,2048]{2,1,0:T(8,128)S(1)} %get-tuple-element.65.refs_10_) | copy-start | bytes 4718596
  19.1 11.3 %copy-start.1 = (f32[256]{0:T(256)S(1)}, f32[256]{0:T(256)}, u32[]{:S(2)}) copy-start(f32[256]{0:T(256)} %param.22) | copy-start | bytes 3076
  19.1 11.3 %collective-permute-start.1 = (f32[3,16,2048]{2,1,0:T(8,128)S(1)}, f32[3,16,2048]{2,1,0:T(8,128)S(1)}, u32[]{:S(2)}, u32[]{:S(2)}) collective-permute-start(f32[3,16,2048]{2,1,0:T(8,128)S(1)} %get-tuple-element.59), channel_id=1, source_target_pairs={{0,2},{1,3},{2,0},{3,1},{4,6},{5,7},{6,4},{7,5},{8,10},{9,11},{10,... | collective-permute-start | bytes 1179656 | tf_op jit(solution)/shard_map/ppermute | solution.py:602
  24.3 10.5 %all-to-all-start.1 = ((f32[32,1,768]{2,1,0:T(1,128)}), f32[32,1,768]{2,1,0:T(1,128)S(1)}, u32[]{:S(2)}, u32[]{:S(2)}) async-start(f32[32,1,768]{2,1,0:T(1,128)} %shard_map.141), calls=%async_computation.1 | async-start | bytes 196608 | tf_op jit(solution)/shard_map/all_to_all | solution.py:611
  31.1 7.2 %collective-permute-start.2 = (f32[23,1,2048]{2,1,0:T(1,128)}, f32[23,1,2048]{2,1,0:T(1,128)S(1)}, u32[]{:S(2)}, u32[]{:S(2)}) collective-permute-start(f32[23,1,2048]{2,1,0:T(1,128)} %get-tuple-element.71), channel_id=1, source_target_pairs={{4,8},{12,16},{20,24},{8,4},{16,12},{24,20},{5,9},{13,17},{21,25},... | collective-permute-start | bytes 565256 | tf_op jit(solution)/shard_map/ppermute | solution.py:607
  37.6 3.9 %collective-permute-start.3 = (f32[3,1,2048]{2,1,0:T(1,128)S(1)}, f32[3,1,2048]{2,1,0:T(1,128)S(1)}, u32[]{:S(2)}, u32[]{:S(2)}) collective-permute-start(f32[3,1,2048]{2,1,0:T(1,128)S(1)} %get-tuple-element.73), channel_id=1, source_target_pairs={{0,4},{4,0},{8,12},{12,8},{16,20},{20,16},{24,28},{28,24},{1,5},{5... | collective-permute-start | bytes 73736 | tf_op jit(solution)/shard_map/ppermute | solution.py:602
  42.4 8.9 %collective-permute-start.4 = (f32[3,16,2048]{2,1,0:T(8,128)S(1)}, f32[3,16,2048]{2,1,0:T(8,128)S(1)}, u32[]{:S(2)}, u32[]{:S(2)}) collective-permute-start(f32[3,16,2048]{2,1,0:T(8,128)S(1)} %get-tuple-element.82), channel_id=1, source_target_pairs={{0,1},{1,0},{2,3},{3,2},{4,5},{5,4},{6,7},{7,6},{8,9},{9,8},{10,11... | collective-permute-start | bytes 1179656 | tf_op jit(solution)/shard_map/ppermute | solution.py:602
  42.5 8.8 %collective-permute-start.5 = (f32[3,16,2048]{2,1,0:T(8,128)S(1)}, f32[3,16,2048]{2,1,0:T(8,128)S(1)}, u32[]{:S(2)}, u32[]{:S(2)}) collective-permute-start(f32[3,16,2048]{2,1,0:T(8,128)S(1)} %get-tuple-element.83), channel_id=1, source_target_pairs={{1,2},{2,1},{5,6},{6,5},{9,10},{10,9},{13,14},{14,13},{17,18},{18,... | collective-permute-start | bytes 1179656 | tf_op jit(solution)/shard_map/ppermute | solution.py:607
  43.2 6.5 %collective-permute-start.6 = (f32[3,3,1,2048]{3,2,1,0:T(1,128)S(1)}, f32[3,3,1,2048]{3,2,1,0:T(1,128)S(1)}, u32[]{:S(2)}, u32[]{:S(2)}) collective-permute-start(f32[3,3,1,2048]{3,2,1,0:T(1,128)S(1)} %get-tuple-element.84), channel_id=1, source_target_pairs={{4,8},{12,16},{20,24},{8,4},{16,12},{24,20},{5,9},{13,17},{21,25},... | collective-permute-start | bytes 221192 | tf_op jit(solution)/shard_map/ppermute | solution.py:607
  43.9 7.4 %collective-permute-start.7 = (f32[3,3,1,2048]{3,2,1,0:T(1,128)S(1)}, f32[3,3,1,2048]{3,2,1,0:T(1,128)S(1)}, u32[]{:S(2)}, u32[]{:S(2)}) collective-permute-start(f32[3,3,1,2048]{3,2,1,0:T(1,128)S(1)} %get-tuple-element.85), channel_id=1, source_target_pairs={{0,4},{4,0},{8,12},{12,8},{16,20},{20,16},{24,28},{28,24},{1,5},{5... | collective-permute-start | bytes 221192 | tf_op jit(solution)/shard_map/ppermute | solution.py:602

commit v20 on v16

--- a/solution.py
+++ b/solution.py
@@ -285,19 +285,19 @@
     parts = [p.astype(F32) for p in split(terms)[:PARTS]]
     row_of = iota((length // lanes, count), 0).astype(F32)
     lane_of = iota((lanes, count), 0).astype(F32)
-    total = jnp.zeros((length // lanes, lanes), F32)
+    flipped = jnp.zeros((lanes, PARTS * (length // lanes)), F32)
     for d in range(devices):
         hit = row_of == high[d : d + 1]
         left = jnp.concatenate([jnp.where(hit, p[d : d + 1], 0.0).astype(BF16) for p in parts], 0)
         right = jnp.where(lane_of == low[d : d + 1], 1.0, 0.0).astype(BF16)
-        total = total + fold(dot_nt(left, right), PARTS)
+        flipped = flipped + dot_nt(right, left)
+    total = fold(jnp.transpose(flipped), PARTS)
     acc = jnp.zeros((rows, lanes), F32)
     for i in range(chunks):
         copies[i].wait()
         for r in range(i * wide // lanes, (i + 1) * wide // lanes):
             acc = acc + held[:, r * lanes : (r + 1) * lanes] * total[r : r + 1]
-    parts = jnp.concatenate(split(acc), 1)
-    out = dot_nt(jnp.ones((8, parts.shape[1]), BF16), parts)
+    out = jnp.transpose(jnp.broadcast_to(jnp.sum(acc, axis=1, keepdims=True), (rows, lanes)))
     pad = send.shape[2] - out.shape[1] - found.shape[1]
     pieces = [out[0:1], found] + ([jnp.zeros((1, pad), F32)] if pad else [])
     send[...] = jnp.broadcast_to(jnp.concatenate(pieces, 1)[:, None], send.shape)
@@ -547,7 +547,7 @@
             image[c, z] = total - image[c, z]
 
 
-def image_kernel(part, inner, outer, row_two, row_one, rhs, tz, tx, image, send):
+def image_kernel(part, inner, outer, row_one, row_two, rhs, tz, tx, image, send):
     depth, width = part.shape[1:3]
     right, odd = (is_right(0), is_right(0, "tile"))
     row = iota(part.shape[2:], 0)
@@ -722,7 +722,7 @@
     image, send = call(
         image_kernel,
         (vmem(rhs.shape), vmem((devices, 1, 128))),
-        (part, inner, outer, row_two, row_one, rhs, tz, tx),
+        (part, inner, outer, row_one, row_two, rhs, tz, tx),
     )
     sums = everywhere(send)
     update, lin_res, ratio = call(

time: 65.7 us -> 66 us (level)
  blocking collectives: 11.8 us -> 15 us
  starting transfers between devices: 16.8 us -> 14.2 us
    all_to_all x1, blocking collectives: 11.8 us -> 15 us  [everywhere(): return lax.all_to_all(x, BOTH, split_axis=0, concat_axis=0, tiled=True)]
    ppermute x5, starting transfers between devices: 5.19 us -> 2.53 us  [flip(): lax.ppermute(x, axis, [(i, i ^ 1 << level) for i in range(lax.axis_size(a...]
where the time goes in v20:
time: 66 us; the launch traced here: 65.6 us
  Pallas kernels  21.2 us (32%)
  blocking collectives  15 us (23%)
  starting transfers between devices  14.2 us (22%)
  waiting for transfers between devices  13.2 us (20%)
  local copies, waits for them, and re-layouts  1.17 us (2%)
  between operations  0.78 us (1%)
    all_to_all x1, blocking collectives, everywhere(): return lax.all_to_all(x, BOTH, split_axis=0, concat_axis=0, tiled=True)  15 us
    pallas_call x8, Pallas kernels, call(): pl.pallas_call(functools.partial(staged, kernel, where, len(outs), tuple(...  13.2 us
    all_to_all x2, starting transfers between devices, everywhere(): return lax.all_to_all(x, BOTH, split_axis=0, concat_axis=0, tiled=True)  9.63 us
    all_to_all x2, waiting for transfers between devices, everywhere(): return lax.all_to_all(x, BOTH, split_axis=0, concat_axis=0, tiled=True)  8.24 us
    ppermute x5, waiting for transfers between devices, flip(): lax.ppermute(x, axis, [(i, i ^ 1 << level) for i in range(lax.axis_size(a...  5 us
    pallas_call x1, Pallas kernels, shards(): pl.pallas_call(front_kernel, out_shape=vmem((devices, 1, max(rows + found...  4.9 us
    pallas_call x1, Pallas kernels, shards(): pl.pallas_call(pres_kernel, out_shape=(field, vmem((devices, 1, 3 * count...  3.14 us
    ppermute x5, starting transfers between devices, flip(): lax.ppermute(x, axis, [(i, i ^ 1 << level) for i in range(lax.axis_size(a...  2.53 us
  transfers between devices with their start and end apart: 10, of which 5 were waited for; matrix products, arithmetic and copies ran while one was open for 0% of the time, Pallas kernels for 22%

profile of v20, /device:TPU:0, one launch (start us, length us, event | category | flops | bytes accessed | tf_op | source)
XLA Modules:
  0.0 65.6 jit_solution(190337190957848751)
XLA Ops:
  0.6 3.1 %shard_map.139 = (f32[3,16,2048]{2,1,0:T(8,128)S(1)}, f32[32,1,768]{2,1,0:T(1,128)}, f32[7,16,2048]{2,1,0:T(8,128)S(1)}) custom-call(s32[1,256]{1,0:T(1,128)} %bitcast.8, s32[1,256]{1,0:T(1,128)} %bitcast.10, f32[1,256]{1,0:T(1,128)} %bitcast.4, f32[3,3,16,2048]{3,2,1,0:T(8,128)} %refs_3_.3, f32[3,3,16,2048]{3,2,1,0:T(8,128)} %wts_in.1, ...), custom_call_target="tpu_custom_call" | custom-call | tf_op jit(solution)/shard_map/pallas_call | solution.py:628
  3.8 0.5 collective-permute-start
  4.3 7.0 %all-to-all-start = ((f32[32,1,768]{2,1,0:T(1,128)}), f32[32,1,768]{2,1,0:T(1,128)S(1)}, u32[]{:S(2)}, u32[]{:S(2)}) async-start(f32[32,1,768]{2,1,0:T(1,128)} %get-tuple-element.40), calls=%async_computation | async-start | bytes 196608 | tf_op jit(solution)/shard_map/all_to_all | solution.py:609
  11.3 0.0 collective-permute-done.refs_1_.refs_3_
  11.3 2.1 %shard_map.140 = (f32[12,16,2048]{2,1,0:T(8,128)S(1)}, f32[12,1,2048]{2,1,0:T(1,128)S(1)}, f32[12,1,2048]{2,1,0:T(1,128)S(1)}, f32[1,256]{1,0:T(1,128)S(1)}, f32[3,16,2048]{2,1,0:T(8,128)S(1)}) custom-call(f32[7,16,2048]{2,1,0:T(8,128)S(1)} %get-tuple-element.41.refs_0_, f32[7,16,2048]{2,1,0:T(8,128)S(1)} %collective-permute-done.refs_1_.refs_3_, ...), custom_call_target="tpu_custom_call" | custom-call | tf_op jit(solution)/shard_map/pallas_call | solution.py:62
  13.4 1.2 %copy-done = f32[12,16,2048]{2,1,0:T(8,128)} copy-done((f32[12,16,2048]{2,1,0:T(8,128)}, f32[12,16,2048]{2,1,0:T(8,128)S(1)}, u32[]{:S(2)}) %copy-start) | copy-done | bytes 1572888
  14.6 4.5 %all-to-all-done.recv.refs_1_ = f32[32,1,768]{2,1,0:T(1,128)S(1)} async-done(((f32[32,1,768]{2,1,0:T(1,128)}), f32[32,1,768]{2,1,0:T(1,128)S(1)}, u32[]{:S(2)}, u32[]{:S(2)}) %all-to-all-start) | async-done | bytes 98336 | tf_op jit(solution)/shard_map/all_to_all | solution.py:609
  19.1 0.3 collective-permute-start.1
  19.4 4.9 %shard_map.141 = f32[32,1,768]{2,1,0:T(1,128)} custom-call(f32[32,1,768]{2,1,0:T(1,128)S(1)} %all-to-all-done.recv.refs_1_, f32[1,256]{1,0:T(1,128)S(1)} %get-tuple-element.46.found, f32[256,8192]{1,0:T(8,128)} %inverse.1), custom_call_target="tpu_custom_call" | custom-call | tf_op jit(solution)/shard_map/pallas_call | solution.py:665
  24.3 2.7 %all-to-all-start.1 = ((f32[32,1,768]{2,1,0:T(1,128)}), f32[32,1,768]{2,1,0:T(1,128)S(1)}, u32[]{:S(2)}, u32[]{:S(2)}) async-start(f32[32,1,768]{2,1,0:T(1,128)} %shard_map.141), calls=%async_computation.1 | async-start | bytes 196608 | tf_op jit(solution)/shard_map/all_to_all | solution.py:609
  27.0 3.3 %collective-permute-done.1.refs_4_ = f32[3,16,2048]{2,1,0:T(8,128)S(1)} collective-permute-done((f32[3,16,2048]{2,1,0:T(8,128)S(1)}, f32[3,16,2048]{2,1,0:T(8,128)S(1)}, u32[]{:S(2)}, u32[]{:S(2)}) %collective-permute-start.1) | collective-permute-done | bytes 393248 | tf_op jit(solution)/shard_map/ppermute | solution.py:600
  30.3 0.1 shard_map.143
  30.4 0.7 %collective-permute-start.2 = (f32[23,1,2048]{2,1,0:T(1,128)S(1)}, f32[23,1,2048]{2,1,0:T(1,128)S(1)}, u32[]{:S(2)}, u32[]{:S(2)}) collective-permute-start(f32[23,1,2048]{2,1,0:T(1,128)S(1)} %shard_map.143), channel_id=1, source_target_pairs={{4,8},{12,16},{20,24},{8,4},{16,12},{24,20},{5,9},{13,17},{21,25},... | collective-permute-start | bytes 565256 | tf_op jit(solution)/shard_map/ppermute | solution.py:605
  31.1 3.7 %all-to-all-done.1.refs_0_ = f32[32,1,768]{2,1,0:T(1,128)S(1)} async-done(((f32[32,1,768]{2,1,0:T(1,128)}), f32[32,1,768]{2,1,0:T(1,128)S(1)}, u32[]{:S(2)}, u32[]{:S(2)}) %all-to-all-start.1) | async-done | bytes 98336 | tf_op jit(solution)/shard_map/all_to_all | solution.py:609
  34.8 2.8 %shard_map.142 = (f32[3,16,2048]{2,1,0:T(8,128)S(1)}, f32[3,16,2048]{2,1,0:T(8,128)S(1)}, f32[3,1,2048]{2,1,0:T(1,128)S(1)}, f32[3,16,2048]{2,1,0:T(8,128)S(1)},...) custom-call(f32[32,1,768]{2,1,0:T(1,128)S(1)} %all-to-all-done.1.refs_0_, ...), custom_call_target="tpu_custom_call" | custom-call | tf_op jit(solution)/shard_map/pallas_call | solution.py:62
  37.6 0.8 %collective-permute-start.3 = (f32[3,1,2048]{2,1,0:T(1,128)S(1)}, f32[3,1,2048]{2,1,0:T(1,128)S(1)}, u32[]{:S(2)}, u32[]{:S(2)}) collective-permute-start(f32[3,1,2048]{2,1,0:T(1,128)S(1)} %get-tuple-element.60), channel_id=1, source_target_pairs={{0,4},{4,0},{8,12},{12,8},{16,20},{20,16},{24,28},{28,24},{1,5},{5... | collective-permute-start | bytes 73736 | tf_op jit(solution)/shard_map/ppermute | solution.py:600
  38.4 0.0 collective-permute-done.2.refs_2_
  38.4 2.1 %shard_map.144 = (f32[3,1,2048]{2,1,0:T(1,128)S(1)}, f32[3,3,16,2048]{3,2,1,0:T(8,128)S(1)}, f32[3,3,16,2048]{3,2,1,0:T(8,128)S(1)}, f32[3,16,2048]{2,1,0:T(8,128)S(1)}) custom-call(f32[32,1,768]{2,1,0:T(1,128)S(1)} %all-to-all-done.1.refs_0_, f32[32,1,768]{2,1,0:T(1,128)S(1)} %all-to-all-done.recv.refs_1_, ...), custom_call_target="tpu_custom_call" | custom-call | tf_op jit(solution)/shard_map/pallas_call | solution.py:62
  40.5 1.0 %collective-permute-done.3.refs_3_ = f32[3,1,2048]{2,1,0:T(1,128)S(1)} collective-permute-done((f32[3,1,2048]{2,1,0:T(1,128)S(1)}, f32[3,1,2048]{2,1,0:T(1,128)S(1)}, u32[]{:S(2)}, u32[]{:S(2)}) %collective-permute-start.3) | collective-permute-done | bytes 24608 | tf_op jit(solution)/shard_map/ppermute | solution.py:600
  41.5 0.9 %shard_map.145 = (f32[3,3,16,2048]{3,2,1,0:T(8,128)S(1)}, f32[3,16,2048]{2,1,0:T(8,128)S(1)}, f32[3,3,1,2048]{3,2,1,0:T(1,128)S(1)}, f32[3,3,1,2048]{3,2,1,0:T(1,128)S(1)}, f32[3,16,2048]{2,1,0:T(8,128)S(1)}) custom-call(f32[3,16,2048]{2,1,0:T(8,128)S(1)} %get-tuple-element.52.refs_0_, f32[3,16,2048]{2,1,0:T(8,128)S(1)} %get-tuple-element.53.refs_1_, ...), custom_call_target="tpu_custom_call" | custom-call | tf_op jit(solution)/shard_map/pallas_call | solution.py:62
  42.5 0.1 collective-permute-start.4
  42.5 0.7 %collective-permute-start.5 = (f32[3,16,2048]{2,1,0:T(8,128)S(1)}, f32[3,16,2048]{2,1,0:T(8,128)S(1)}, u32[]{:S(2)}, u32[]{:S(2)}) collective-permute-start(f32[3,16,2048]{2,1,0:T(8,128)S(1)} %get-tuple-element.69), channel_id=1, source_target_pairs={{1,2},{2,1},{5,6},{6,5},{9,10},{10,9},{13,14},{14,13},{17,18},{18,... | collective-permute-start | bytes 1179656 | tf_op jit(solution)/shard_map/ppermute | solution.py:605
  43.2 0.8 %collective-permute-start.6 = (f32[3,3,1,2048]{3,2,1,0:T(1,128)S(1)}, f32[3,3,1,2048]{3,2,1,0:T(1,128)S(1)}, u32[]{:S(2)}, u32[]{:S(2)}) collective-permute-start(f32[3,3,1,2048]{3,2,1,0:T(1,128)S(1)} %get-tuple-element.70), channel_id=1, source_target_pairs={{0,4},{4,0},{8,12},{12,8},{16,20},{20,16},{24,28},{28,24},{1,5},{5... | collective-permute-start | bytes 221192 | tf_op jit(solution)/shard_map/ppermute | solution.py:600
  44.0 0.7 collective-permute-start.7
  44.7 2.4 %shard_map.146.refs_0_ = f32[3,3,16,2048]{3,2,1,0:T(8,128)S(1)} custom-call(f32[3,3,16,2048]{3,2,1,0:T(8,128)S(1)} %get-tuple-element.67.refs_0_.refs_1_, f32[3,3,3,16,2048]{4,3,2,1,0:T(8,128)} %refs_1_.1, f32[3,16,2048]{2,1,0:T(8,128)S(1)} %get-tuple-element.63.refs_6_.refs_2_, f32[3,16,2048]{2,1,0:T(8,128)S(1)} %get-tuple-element.61.refs_4_.refs_3_.refs_7_, ...), custom_call_target="tpu_custom_call" | custom-call | tf_op jit(solution)/shard_map/pallas_call | solution.py:62
  47.1 0.7 %collective-permute-done.6.refs_3_ = f32[3,3,1,2048]{3,2,1,0:T(1,128)S(1)} collective-permute-done((f32[3,3,1,2048]{3,2,1,0:T(1,128)S(1)}, f32[3,3,1,2048]{3,2,1,0:T(1,128)S(1)}, u32[]{:S(2)}, u32[]{:S(2)}) %collective-permute-start.6) | collective-permute-done | bytes 73760 | tf_op jit(solution)/shard_map/ppermute | solution.py:600
  47.7 0.0 collective-permute-done.7.refs_4_
  47.7 0.0 collective-permute-done.4.refs_1_
  47.7 0.0 collective-permute-done.5.refs_2_
  47.7 1.2 %shard_map.147 = (f32[3,3,16,2048]{3,2,1,0:T(8,128)S(1)}, f32[32,1,128]{2,1,0:T(1,128)S(1)}) custom-call(f32[3,3,16,2048]{3,2,1,0:T(8,128)S(1)} %shard_map.146.refs_0_, f32[3,16,2048]{2,1,0:T(8,128)S(1)} %collective-permute-done.4.refs_1_, f32[3,16,2048]{2,1,0:T(8,128)S(1)} %collective-permute-done.5.refs_2_, ...), custom_call_target="tpu_custom_call" | custom-call | tf_op jit(solution)/shard_map/pallas_call | solution.py:62
  48.9 15.0 %all_to_all.15.refs_0_ = f32[32,1,128]{2,1,0:T(1,128)S(1)} all-to-all(f32[32,1,128]{2,1,0:T(1,128)S(1)} %get-tuple-element.72), channel_id=1, replica_groups=mesh['tile'=8,'layer'=4] {'tile','layer'}, dimensions={0} | all-to-all | bytes 32768 | tf_op jit(solution)/shard_map/all_to_all | solution.py:609
  64.0 1.7 %shard_map.148 = (f32[3,3,16,2048]{3,2,1,0:T(8,128)}, f32[3,3,16,2048]{3,2,1,0:T(8,128)}, f32[1,1]{1,0:T(1,128)}) custom-call(f32[32,1,128]{2,1,0:T(1,128)S(1)} %all_to_all.15.refs_0_, f32[3,3,16,2048]{3,2,1,0:T(8,128)S(1)} %get-tuple-element.67.refs_0_.refs_1_, f32[3,3,16,2048]{3,2,1,0:T(8,128)S(1)} %get-tuple-element.73.refs_2_, ...), custom_call_target="tpu_custom_call" | custom-call | tf_op jit(solution)/shard_map/pallas_call | solution.py:62
  (3 shorter events, 0.0 us)
Async XLA Ops:
  3.8 7.5 %collective-permute-start = (f32[7,16,2048]{2,1,0:T(8,128)S(1)}, f32[7,16,2048]{2,1,0:T(8,128)S(1)}, u32[]{:S(2)}, u32[]{:S(2)}) collective-permute-start(f32[7,16,2048]{2,1,0:T(8,128)S(1)} %get-tuple-element.41.refs_0_), channel_id=1, source_target_pairs={{0,1},{1,0},{2,3},{3,2},{4,5},{5,4},{6,7},{7,6},{8,9},{9,8},{10,11... | collective-permute-start | bytes 2752520 | tf_op jit(solution)/shard_map/ppermute | solution.py:600
  4.3 14.8 %all-to-all-start = ((f32[32,1,768]{2,1,0:T(1,128)}), f32[32,1,768]{2,1,0:T(1,128)S(1)}, u32[]{:S(2)}, u32[]{:S(2)}) async-start(f32[32,1,768]{2,1,0:T(1,128)} %get-tuple-element.40), calls=%async_computation | async-start | bytes 196608 | tf_op jit(solution)/shard_map/all_to_all | solution.py:609
  13.4 1.2 %copy-start = (f32[12,16,2048]{2,1,0:T(8,128)}, f32[12,16,2048]{2,1,0:T(8,128)S(1)}, u32[]{:S(2)}) copy-start(f32[12,16,2048]{2,1,0:T(8,128)S(1)} %get-tuple-element.51.refs_6_) | copy-start | bytes 4718596
  19.1 11.3 %copy-start.1 = (f32[256]{0:T(256)S(1)}, f32[256]{0:T(256)}, u32[]{:S(2)}) copy-start(f32[256]{0:T(256)} %param.22) | copy-start | bytes 3076
  19.1 11.3 %collective-permute-start.1 = (f32[3,16,2048]{2,1,0:T(8,128)S(1)}, f32[3,16,2048]{2,1,0:T(8,128)S(1)}, u32[]{:S(2)}, u32[]{:S(2)}) collective-permute-start(f32[3,16,2048]{2,1,0:T(8,128)S(1)} %get-tuple-element.50), channel_id=1, source_target_pairs={{0,2},{1,3},{2,0},{3,1},{4,6},{5,7},{6,4},{7,5},{8,10},{9,11},{10,... | collective-permute-start | bytes 1179656 | tf_op jit(solution)/shard_map/ppermute | solution.py:600
  24.3 10.5 %all-to-all-start.1 = ((f32[32,1,768]{2,1,0:T(1,128)}), f32[32,1,768]{2,1,0:T(1,128)S(1)}, u32[]{:S(2)}, u32[]{:S(2)}) async-start(f32[32,1,768]{2,1,0:T(1,128)} %shard_map.141), calls=%async_computation.1 | async-start | bytes 196608 | tf_op jit(solution)/shard_map/all_to_all | solution.py:609
  30.4 8.0 %collective-permute-start.2 = (f32[23,1,2048]{2,1,0:T(1,128)S(1)}, f32[23,1,2048]{2,1,0:T(1,128)S(1)}, u32[]{:S(2)}, u32[]{:S(2)}) collective-permute-start(f32[23,1,2048]{2,1,0:T(1,128)S(1)} %shard_map.143), channel_id=1, source_target_pairs={{4,8},{12,16},{20,24},{8,4},{16,12},{24,20},{5,9},{13,17},{21,25},... | collective-permute-start | bytes 565256 | tf_op jit(solution)/shard_map/ppermute | solution.py:605
  37.6 3.9 %collective-permute-start.3 = (f32[3,1,2048]{2,1,0:T(1,128)S(1)}, f32[3,1,2048]{2,1,0:T(1,128)S(1)}, u32[]{:S(2)}, u32[]{:S(2)}) collective-permute-start(f32[3,1,2048]{2,1,0:T(1,128)S(1)} %get-tuple-element.60), channel_id=1, source_target_pairs={{0,4},{4,0},{8,12},{12,8},{16,20},{20,16},{24,28},{28,24},{1,5},{5... | collective-permute-start | bytes 73736 | tf_op jit(solution)/shard_map/ppermute | solution.py:600
  42.5 5.3 %collective-permute-start.4 = (f32[3,16,2048]{2,1,0:T(8,128)S(1)}, f32[3,16,2048]{2,1,0:T(8,128)S(1)}, u32[]{:S(2)}, u32[]{:S(2)}) collective-permute-start(f32[3,16,2048]{2,1,0:T(8,128)S(1)} %get-tuple-element.68), channel_id=1, source_target_pairs={{0,1},{1,0},{2,3},{3,2},{4,5},{5,4},{6,7},{7,6},{8,9},{9,8},{10,11... | collective-permute-start | bytes 1179656 | tf_op jit(solution)/shard_map/ppermute | solution.py:600
  42.5 5.2 %collective-permute-start.5 = (f32[3,16,2048]{2,1,0:T(8,128)S(1)}, f32[3,16,2048]{2,1,0:T(8,128)S(1)}, u32[]{:S(2)}, u32[]{:S(2)}) collective-permute-start(f32[3,16,2048]{2,1,0:T(8,128)S(1)} %get-tuple-element.69), channel_id=1, source_target_pairs={{1,2},{2,1},{5,6},{6,5},{9,10},{10,9},{13,14},{14,13},{17,18},{18,... | collective-permute-start | bytes 1179656 | tf_op jit(solution)/shard_map/ppermute | solution.py:605
  43.2 4.5 %collective-permute-start.6 = (f32[3,3,1,2048]{3,2,1,0:T(1,128)S(1)}, f32[3,3,1,2048]{3,2,1,0:T(1,128)S(1)}, u32[]{:S(2)}, u32[]{:S(2)}) collective-permute-start(f32[3,3,1,2048]{3,2,1,0:T(1,128)S(1)} %get-tuple-element.70), channel_id=1, source_target_pairs={{0,4},{4,0},{8,12},{12,8},{16,20},{20,16},{24,28},{28,24},{1,5},{5... | collective-permute-start | bytes 221192 | tf_op jit(solution)/shard_map/ppermute | solution.py:600
  44.0 3.7 %collective-permute-start.7 = (f32[3,3,1,2048]{3,2,1,0:T(1,128)S(1)}, f32[3,3,1,2048]{3,2,1,0:T(1,128)S(1)}, u32[]{:S(2)}, u32[]{:S(2)}) collective-permute-start(f32[3,3,1,2048]{3,2,1,0:T(1,128)S(1)} %get-tuple-element.71), channel_id=1, source_target_pairs={{4,8},{12,16},{20,24},{8,4},{16,12},{24,20},{5,9},{13,17},{21,25},... | collective-permute-start | bytes 221192 | tf_op jit(solution)/shard_map/ppermute | solution.py:605

commit v21 on v20

--- a/solution.py
+++ b/solution.py
@@ -547,7 +547,7 @@
             image[c, z] = total - image[c, z]
 
 
-def image_kernel(part, inner, outer, row_one, row_two, rhs, tz, tx, image, send):
+def image_kernel(part, inner, outer, row_two, row_one, rhs, tz, tx, image, send):
     depth, width = part.shape[1:3]
     right, odd = (is_right(0), is_right(0, "tile"))
     row = iota(part.shape[2:], 0)
@@ -722,7 +722,7 @@
     image, send = call(
         image_kernel,
         (vmem(rhs.shape), vmem((devices, 1, 128))),
-        (part, inner, outer, row_one, row_two, rhs, tz, tx),
+        (part, inner, outer, row_two, row_one, rhs, tz, tx),
     )
     sums = everywhere(send)
     update, lin_res, ratio = call(

time: 66 us -> 65.7 us (level)
  blocking collectives: 15 us -> 11.6 us
  starting transfers between devices: 14.2 us -> 16.9 us
    all_to_all x1, blocking collectives: 15 us -> 11.6 us  [everywhere(): return lax.all_to_all(x, BOTH, split_axis=0, concat_axis=0, tiled=True)]
    ppermute x5, starting transfers between devices: 2.53 us -> 5.27 us  [flip(): lax.ppermute(x, axis, [(i, i ^ 1 << level) for i in range(lax.axis_size(a...]
where the time goes in v21:
time: 65.7 us; the launch traced here: 65.3 us
  Pallas kernels  21.2 us (32%)
  starting transfers between devices  16.9 us (26%)
  waiting for transfers between devices  13.5 us (21%)
  blocking collectives  11.6 us (18%)
  local copies, waits for them, and re-layouts  1.17 us (2%)
  between operations  0.78 us (1%)
    pallas_call x8, Pallas kernels, call(): pl.pallas_call(functools.partial(staged, kernel, where, len(outs), tuple(...  13.2 us
    all_to_all x1, blocking collectives, everywhere(): return lax.all_to_all(x, BOTH, split_axis=0, concat_axis=0, tiled=True)  11.6 us
    all_to_all x2, starting transfers between devices, everywhere(): return lax.all_to_all(x, BOTH, split_axis=0, concat_axis=0, tiled=True)  9.63 us
    all_to_all x2, waiting for transfers between devices, everywhere(): return lax.all_to_all(x, BOTH, split_axis=0, concat_axis=0, tiled=True)  8.24 us
    ppermute x5, waiting for transfers between devices, flip(): lax.ppermute(x, axis, [(i, i ^ 1 << level) for i in range(lax.axis_size(a...  5.29 us
    ppermute x5, starting transfers between devices, flip(): lax.ppermute(x, axis, [(i, i ^ 1 << level) for i in range(lax.axis_size(a...  5.27 us
    pallas_call x1, Pallas kernels, shards(): pl.pallas_call(front_kernel, out_shape=vmem((devices, 1, max(rows + found...  4.9 us
    pallas_call x1, Pallas kernels, shards(): pl.pallas_call(pres_kernel, out_shape=(field, vmem((devices, 1, 3 * count...  3.14 us
  transfers between devices with their start and end apart: 10, of which 5 were waited for; matrix products, arithmetic and copies ran while one was open for 0% of the time, Pallas kernels for 22%

profile of v21, /device:TPU:0, one launch (start us, length us, event | category | flops | bytes accessed | tf_op | source)
XLA Modules:
  0.0 65.3 jit_solution(1926693759605402477)
XLA Ops:
  0.6 3.1 %shard_map.139 = (f32[3,16,2048]{2,1,0:T(8,128)S(1)}, f32[32,1,768]{2,1,0:T(1,128)}, f32[7,16,2048]{2,1,0:T(8,128)S(1)}) custom-call(s32[1,256]{1,0:T(1,128)} %bitcast.8, s32[1,256]{1,0:T(1,128)} %bitcast.10, f32[1,256]{1,0:T(1,128)} %bitcast.4, f32[3,3,16,2048]{3,2,1,0:T(8,128)} %refs_3_.3, f32[3,3,16,2048]{3,2,1,0:T(8,128)} %wts_in.1, ...), custom_call_target="tpu_custom_call" | custom-call | tf_op jit(solution)/shard_map/pallas_call | solution.py:628
  3.8 0.5 collective-permute-start
  4.3 7.0 %all-to-all-start = ((f32[32,1,768]{2,1,0:T(1,128)}), f32[32,1,768]{2,1,0:T(1,128)S(1)}, u32[]{:S(2)}, u32[]{:S(2)}) async-start(f32[32,1,768]{2,1,0:T(1,128)} %get-tuple-element.40), calls=%async_computation | async-start | bytes 196608 | tf_op jit(solution)/shard_map/all_to_all | solution.py:609
  11.3 0.0 collective-permute-done.refs_1_.refs_3_
  11.3 2.1 %shard_map.140 = (f32[12,16,2048]{2,1,0:T(8,128)S(1)}, f32[12,1,2048]{2,1,0:T(1,128)S(1)}, f32[12,1,2048]{2,1,0:T(1,128)S(1)}, f32[1,256]{1,0:T(1,128)S(1)}, f32[3,16,2048]{2,1,0:T(8,128)S(1)}) custom-call(f32[7,16,2048]{2,1,0:T(8,128)S(1)} %get-tuple-element.41.refs_0_, f32[7,16,2048]{2,1,0:T(8,128)S(1)} %collective-permute-done.refs_1_.refs_3_, ...), custom_call_target="tpu_custom_call" | custom-call | tf_op jit(solution)/shard_map/pallas_call | solution.py:62
  13.4 1.2 %copy-done = f32[12,16,2048]{2,1,0:T(8,128)} copy-done((f32[12,16,2048]{2,1,0:T(8,128)}, f32[12,16,2048]{2,1,0:T(8,128)S(1)}, u32[]{:S(2)}) %copy-start) | copy-done | bytes 1572888
  14.6 4.5 %all-to-all-done.recv.refs_1_ = f32[32,1,768]{2,1,0:T(1,128)S(1)} async-done(((f32[32,1,768]{2,1,0:T(1,128)}), f32[32,1,768]{2,1,0:T(1,128)S(1)}, u32[]{:S(2)}, u32[]{:S(2)}) %all-to-all-start) | async-done | bytes 98336 | tf_op jit(solution)/shard_map/all_to_all | solution.py:609
  19.1 0.3 collective-permute-start.1
  19.4 4.9 %shard_map.141 = f32[32,1,768]{2,1,0:T(1,128)} custom-call(f32[32,1,768]{2,1,0:T(1,128)S(1)} %all-to-all-done.recv.refs_1_, f32[1,256]{1,0:T(1,128)S(1)} %get-tuple-element.46.found, f32[256,8192]{1,0:T(8,128)} %inverse.1), custom_call_target="tpu_custom_call" | custom-call | tf_op jit(solution)/shard_map/pallas_call | solution.py:665
  24.3 2.7 %all-to-all-start.1 = ((f32[32,1,768]{2,1,0:T(1,128)}), f32[32,1,768]{2,1,0:T(1,128)S(1)}, u32[]{:S(2)}, u32[]{:S(2)}) async-start(f32[32,1,768]{2,1,0:T(1,128)} %shard_map.141), calls=%async_computation.1 | async-start | bytes 196608 | tf_op jit(solution)/shard_map/all_to_all | solution.py:609
  27.0 3.3 %collective-permute-done.1.refs_4_ = f32[3,16,2048]{2,1,0:T(8,128)S(1)} collective-permute-done((f32[3,16,2048]{2,1,0:T(8,128)S(1)}, f32[3,16,2048]{2,1,0:T(8,128)S(1)}, u32[]{:S(2)}, u32[]{:S(2)}) %collective-permute-start.1) | collective-permute-done | bytes 393248 | tf_op jit(solution)/shard_map/ppermute | solution.py:600
  30.3 0.1 shard_map.143
  30.4 0.7 %collective-permute-start.2 = (f32[23,1,2048]{2,1,0:T(1,128)S(1)}, f32[23,1,2048]{2,1,0:T(1,128)S(1)}, u32[]{:S(2)}, u32[]{:S(2)}) collective-permute-start(f32[23,1,2048]{2,1,0:T(1,128)S(1)} %shard_map.143), channel_id=1, source_target_pairs={{4,8},{12,16},{20,24},{8,4},{16,12},{24,20},{5,9},{13,17},{21,25},... | collective-permute-start | bytes 565256 | tf_op jit(solution)/shard_map/ppermute | solution.py:605
  31.1 3.7 %all-to-all-done.1.refs_0_ = f32[32,1,768]{2,1,0:T(1,128)S(1)} async-done(((f32[32,1,768]{2,1,0:T(1,128)}), f32[32,1,768]{2,1,0:T(1,128)S(1)}, u32[]{:S(2)}, u32[]{:S(2)}) %all-to-all-start.1) | async-done | bytes 98336 | tf_op jit(solution)/shard_map/all_to_all | solution.py:609
  34.8 2.8 %shard_map.142 = (f32[3,16,2048]{2,1,0:T(8,128)S(1)}, f32[3,16,2048]{2,1,0:T(8,128)S(1)}, f32[3,1,2048]{2,1,0:T(1,128)S(1)}, f32[3,16,2048]{2,1,0:T(8,128)S(1)},...) custom-call(f32[32,1,768]{2,1,0:T(1,128)S(1)} %all-to-all-done.1.refs_0_, ...), custom_call_target="tpu_custom_call" | custom-call | tf_op jit(solution)/shard_map/pallas_call | solution.py:62
  37.6 0.8 %collective-permute-start.3 = (f32[3,1,2048]{2,1,0:T(1,128)S(1)}, f32[3,1,2048]{2,1,0:T(1,128)S(1)}, u32[]{:S(2)}, u32[]{:S(2)}) collective-permute-start(f32[3,1,2048]{2,1,0:T(1,128)S(1)} %get-tuple-element.60), channel_id=1, source_target_pairs={{0,4},{4,0},{8,12},{12,8},{16,20},{20,16},{24,28},{28,24},{1,5},{5... | collective-permute-start | bytes 73736 | tf_op jit(solution)/shard_map/ppermute | solution.py:600
  38.4 0.0 collective-permute-done.2.refs_2_
  38.4 2.1 %shard_map.144 = (f32[3,1,2048]{2,1,0:T(1,128)S(1)}, f32[3,3,16,2048]{3,2,1,0:T(8,128)S(1)}, f32[3,3,16,2048]{3,2,1,0:T(8,128)S(1)}, f32[3,16,2048]{2,1,0:T(8,128)S(1)}) custom-call(f32[32,1,768]{2,1,0:T(1,128)S(1)} %all-to-all-done.1.refs_0_, f32[32,1,768]{2,1,0:T(1,128)S(1)} %all-to-all-done.recv.refs_1_, ...), custom_call_target="tpu_custom_call" | custom-call | tf_op jit(solution)/shard_map/pallas_call | solution.py:62
  40.5 1.0 %collective-permute-done.3.refs_3_ = f32[3,1,2048]{2,1,0:T(1,128)S(1)} collective-permute-done((f32[3,1,2048]{2,1,0:T(1,128)S(1)}, f32[3,1,2048]{2,1,0:T(1,128)S(1)}, u32[]{:S(2)}, u32[]{:S(2)}) %collective-permute-start.3) | collective-permute-done | bytes 24608 | tf_op jit(solution)/shard_map/ppermute | solution.py:600
  41.5 0.9 %shard_map.145 = (f32[3,3,16,2048]{3,2,1,0:T(8,128)S(1)}, f32[3,16,2048]{2,1,0:T(8,128)S(1)}, f32[3,3,1,2048]{3,2,1,0:T(1,128)S(1)}, f32[3,3,1,2048]{3,2,1,0:T(1,128)S(1)}, f32[3,16,2048]{2,1,0:T(8,128)S(1)}) custom-call(f32[3,16,2048]{2,1,0:T(8,128)S(1)} %get-tuple-element.52.refs_0_, f32[3,16,2048]{2,1,0:T(8,128)S(1)} %get-tuple-element.53.refs_1_, ...), custom_call_target="tpu_custom_call" | custom-call | tf_op jit(solution)/shard_map/pallas_call | solution.py:62
  42.5 0.1 collective-permute-start.4
  42.5 0.7 %collective-permute-start.5 = (f32[3,16,2048]{2,1,0:T(8,128)S(1)}, f32[3,16,2048]{2,1,0:T(8,128)S(1)}, u32[]{:S(2)}, u32[]{:S(2)}) collective-permute-start(f32[3,16,2048]{2,1,0:T(8,128)S(1)} %get-tuple-element.69), channel_id=1, source_target_pairs={{1,2},{2,1},{5,6},{6,5},{9,10},{10,9},{13,14},{14,13},{17,18},{18,... | collective-permute-start | bytes 1179656 | tf_op jit(solution)/shard_map/ppermute | solution.py:605
  43.2 0.7 %collective-permute-start.6 = (f32[3,3,1,2048]{3,2,1,0:T(1,128)S(1)}, f32[3,3,1,2048]{3,2,1,0:T(1,128)S(1)}, u32[]{:S(2)}, u32[]{:S(2)}) collective-permute-start(f32[3,3,1,2048]{3,2,1,0:T(1,128)S(1)} %get-tuple-element.70), channel_id=1, source_target_pairs={{4,8},{12,16},{20,24},{8,4},{16,12},{24,20},{5,9},{13,17},{21,25},... | collective-permute-start | bytes 221192 | tf_op jit(solution)/shard_map/ppermute | solution.py:605
  43.9 3.5 %collective-permute-start.7 = (f32[3,3,1,2048]{3,2,1,0:T(1,128)S(1)}, f32[3,3,1,2048]{3,2,1,0:T(1,128)S(1)}, u32[]{:S(2)}, u32[]{:S(2)}) collective-permute-start(f32[3,3,1,2048]{3,2,1,0:T(1,128)S(1)} %get-tuple-element.71), channel_id=1, source_target_pairs={{0,4},{4,0},{8,12},{12,8},{16,20},{20,16},{24,28},{28,24},{1,5},{5... | collective-permute-start | bytes 221192 | tf_op jit(solution)/shard_map/ppermute | solution.py:600
  47.4 2.4 %shard_map.146.refs_0_ = f32[3,3,16,2048]{3,2,1,0:T(8,128)S(1)} custom-call(f32[3,3,16,2048]{3,2,1,0:T(8,128)S(1)} %get-tuple-element.67.refs_0_.refs_1_, f32[3,3,3,16,2048]{4,3,2,1,0:T(8,128)} %refs_1_.1, f32[3,16,2048]{2,1,0:T(8,128)S(1)} %get-tuple-element.63.refs_6_.refs_2_, f32[3,16,2048]{2,1,0:T(8,128)S(1)} %get-tuple-element.61.refs_4_.refs_3_.refs_7_, ...), custom_call_target="tpu_custom_call" | custom-call | tf_op jit(solution)/shard_map/pallas_call | solution.py:62
  49.8 0.0 collective-permute-done.6.refs_3_
  49.8 1.0 %collective-permute-done.7.refs_4_ = f32[3,3,1,2048]{3,2,1,0:T(1,128)S(1)} collective-permute-done((f32[3,3,1,2048]{3,2,1,0:T(1,128)S(1)}, f32[3,3,1,2048]{3,2,1,0:T(1,128)S(1)}, u32[]{:S(2)}, u32[]{:S(2)}) %collective-permute-start.7) | collective-permute-done | bytes 73760 | tf_op jit(solution)/shard_map/ppermute | solution.py:600
  50.8 0.0 collective-permute-done.4.refs_1_
  50.8 0.0 collective-permute-done.5.refs_2_
  50.8 1.2 %shard_map.147 = (f32[3,3,16,2048]{3,2,1,0:T(8,128)S(1)}, f32[32,1,128]{2,1,0:T(1,128)S(1)}) custom-call(f32[3,3,16,2048]{3,2,1,0:T(8,128)S(1)} %shard_map.146.refs_0_, f32[3,16,2048]{2,1,0:T(8,128)S(1)} %collective-permute-done.4.refs_1_, f32[3,16,2048]{2,1,0:T(8,128)S(1)} %collective-permute-done.5.refs_2_, ...), custom_call_target="tpu_custom_call" | custom-call | tf_op jit(solution)/shard_map/pallas_call | solution.py:62
  52.0 11.6 %all_to_all.15.refs_0_ = f32[32,1,128]{2,1,0:T(1,128)S(1)} all-to-all(f32[32,1,128]{2,1,0:T(1,128)S(1)} %get-tuple-element.72), channel_id=1, replica_groups=mesh['tile'=8,'layer'=4] {'tile','layer'}, dimensions={0} | all-to-all | bytes 32768 | tf_op jit(solution)/shard_map/all_to_all | solution.py:609
  63.6 1.7 %shard_map.148 = (f32[3,3,16,2048]{3,2,1,0:T(8,128)}, f32[3,3,16,2048]{3,2,1,0:T(8,128)}, f32[1,1]{1,0:T(1,128)}) custom-call(f32[32,1,128]{2,1,0:T(1,128)S(1)} %all_to_all.15.refs_0_, f32[3,3,16,2048]{3,2,1,0:T(8,128)S(1)} %get-tuple-element.67.refs_0_.refs_1_, f32[3,3,16,2048]{3,2,1,0:T(8,128)S(1)} %get-tuple-element.73.refs_2_, ...), custom_call_target="tpu_custom_call" | custom-call | tf_op jit(solution)/shard_map/pallas_call | solution.py:62
  (3 shorter events, 0.0 us)
Async XLA Ops:
  3.8 7.5 %collective-permute-start = (f32[7,16,2048]{2,1,0:T(8,128)S(1)}, f32[7,16,2048]{2,1,0:T(8,128)S(1)}, u32[]{:S(2)}, u32[]{:S(2)}) collective-permute-start(f32[7,16,2048]{2,1,0:T(8,128)S(1)} %get-tuple-element.41.refs_0_), channel_id=1, source_target_pairs={{0,1},{1,0},{2,3},{3,2},{4,5},{5,4},{6,7},{7,6},{8,9},{9,8},{10,11... | collective-permute-start | bytes 2752520 | tf_op jit(solution)/shard_map/ppermute | solution.py:600
  4.3 14.8 %all-to-all-start = ((f32[32,1,768]{2,1,0:T(1,128)}), f32[32,1,768]{2,1,0:T(1,128)S(1)}, u32[]{:S(2)}, u32[]{:S(2)}) async-start(f32[32,1,768]{2,1,0:T(1,128)} %get-tuple-element.40), calls=%async_computation | async-start | bytes 196608 | tf_op jit(solution)/shard_map/all_to_all | solution.py:609
  13.4 1.2 %copy-start = (f32[12,16,2048]{2,1,0:T(8,128)}, f32[12,16,2048]{2,1,0:T(8,128)S(1)}, u32[]{:S(2)}) copy-start(f32[12,16,2048]{2,1,0:T(8,128)S(1)} %get-tuple-element.51.refs_6_) | copy-start | bytes 4718596
  19.1 11.3 %copy-start.1 = (f32[256]{0:T(256)S(1)}, f32[256]{0:T(256)}, u32[]{:S(2)}) copy-start(f32[256]{0:T(256)} %param.22) | copy-start | bytes 3076
  19.1 11.3 %collective-permute-start.1 = (f32[3,16,2048]{2,1,0:T(8,128)S(1)}, f32[3,16,2048]{2,1,0:T(8,128)S(1)}, u32[]{:S(2)}, u32[]{:S(2)}) collective-permute-start(f32[3,16,2048]{2,1,0:T(8,128)S(1)} %get-tuple-element.50), channel_id=1, source_target_pairs={{0,2},{1,3},{2,0},{3,1},{4,6},{5,7},{6,4},{7,5},{8,10},{9,11},{10,... | collective-permute-start | bytes 1179656 | tf_op jit(solution)/shard_map/ppermute | solution.py:600
  24.3 10.5 %all-to-all-start.1 = ((f32[32,1,768]{2,1,0:T(1,128)}), f32[32,1,768]{2,1,0:T(1,128)S(1)}, u32[]{:S(2)}, u32[]{:S(2)}) async-start(f32[32,1,768]{2,1,0:T(1,128)} %shard_map.141), calls=%async_computation.1 | async-start | bytes 196608 | tf_op jit(solution)/shard_map/all_to_all | solution.py:609
  30.4 8.0 %collective-permute-start.2 = (f32[23,1,2048]{2,1,0:T(1,128)S(1)}, f32[23,1,2048]{2,1,0:T(1,128)S(1)}, u32[]{:S(2)}, u32[]{:S(2)}) collective-permute-start(f32[23,1,2048]{2,1,0:T(1,128)S(1)} %shard_map.143), channel_id=1, source_target_pairs={{4,8},{12,16},{20,24},{8,4},{16,12},{24,20},{5,9},{13,17},{21,25},... | collective-permute-start | bytes 565256 | tf_op jit(solution)/shard_map/ppermute | solution.py:605
  37.6 3.9 %collective-permute-start.3 = (f32[3,1,2048]{2,1,0:T(1,128)S(1)}, f32[3,1,2048]{2,1,0:T(1,128)S(1)}, u32[]{:S(2)}, u32[]{:S(2)}) collective-permute-start(f32[3,1,2048]{2,1,0:T(1,128)S(1)} %get-tuple-element.60), channel_id=1, source_target_pairs={{0,4},{4,0},{8,12},{12,8},{16,20},{20,16},{24,28},{28,24},{1,5},{5... | collective-permute-start | bytes 73736 | tf_op jit(solution)/shard_map/ppermute | solution.py:600
  42.5 8.3 %collective-permute-start.4 = (f32[3,16,2048]{2,1,0:T(8,128)S(1)}, f32[3,16,2048]{2,1,0:T(8,128)S(1)}, u32[]{:S(2)}, u32[]{:S(2)}) collective-permute-start(f32[3,16,2048]{2,1,0:T(8,128)S(1)} %get-tuple-element.68), channel_id=1, source_target_pairs={{0,1},{1,0},{2,3},{3,2},{4,5},{5,4},{6,7},{7,6},{8,9},{9,8},{10,11... | collective-permute-start | bytes 1179656 | tf_op jit(solution)/shard_map/ppermute | solution.py:600
  42.5 8.2 %collective-permute-start.5 = (f32[3,16,2048]{2,1,0:T(8,128)S(1)}, f32[3,16,2048]{2,1,0:T(8,128)S(1)}, u32[]{:S(2)}, u32[]{:S(2)}) collective-permute-start(f32[3,16,2048]{2,1,0:T(8,128)S(1)} %get-tuple-element.69), channel_id=1, source_target_pairs={{1,2},{2,1},{5,6},{6,5},{9,10},{10,9},{13,14},{14,13},{17,18},{18,... | collective-permute-start | bytes 1179656 | tf_op jit(solution)/shard_map/ppermute | solution.py:605
  43.2 6.6 %collective-permute-start.6 = (f32[3,3,1,2048]{3,2,1,0:T(1,128)S(1)}, f32[3,3,1,2048]{3,2,1,0:T(1,128)S(1)}, u32[]{:S(2)}, u32[]{:S(2)}) collective-permute-start(f32[3,3,1,2048]{3,2,1,0:T(1,128)S(1)} %get-tuple-element.70), channel_id=1, source_target_pairs={{4,8},{12,16},{20,24},{8,4},{16,12},{24,20},{5,9},{13,17},{21,25},... | collective-permute-start | bytes 221192 | tf_op jit(solution)/shard_map/ppermute | solution.py:605
  43.9 6.9 %collective-permute-start.7 = (f32[3,3,1,2048]{3,2,1,0:T(1,128)S(1)}, f32[3,3,1,2048]{3,2,1,0:T(1,128)S(1)}, u32[]{:S(2)}, u32[]{:S(2)}) collective-permute-start(f32[3,3,1,2048]{3,2,1,0:T(1,128)S(1)} %get-tuple-element.71), channel_id=1, source_target_pairs={{0,4},{4,0},{8,12},{12,8},{16,20},{20,16},{24,28},{28,24},{1,5},{5... | collective-permute-start | bytes 221192 | tf_op jit(solution)/shard_map/ppermute | solution.py:600
